TPU v7x, 512 devices: a whole 4x4x16 slice. The times are simulated.
512 devices in a mesh: cfg: 2 (over x_lo), blk: 32 (over z, core), uly: 8 (over x_hi, y).
Axes of the slice: x: 4 (x_hi: 2, x_lo: 2; x = x_hi * 2 + x_lo), y: 4, z: 16, core: 2. Of those that a mesh axis runs over, the one named last changes fastest.
Arguments:
- latent_qkv: bfloat16 [2, 12288, 3, 1536], P('cfg', ('blk', 'uly')), may hold values from -8 to 8
- text_kv: bfloat16 [2, 333, 2, 1536], P('cfg', None, None, 'uly'), may hold values from -8 to 8
- hidden_in: bfloat16 [2, 12288, 1536], P('cfg', ('blk', 'uly')), may hold values from -4 to 4
- modulation: float32 [2, 3, 1536], P('cfg'), may hold values from -4 to 4
- out_weight: bfloat16 [1536, 1536], P('uly'), may hold values from -0.875 to 0.875
- out_bias: float32 [1536], replicated, may hold values from -3 to 3
- proj_weight: bfloat16 [1536, 64], replicated, may hold values from -0.15625 to 0.15625
- proj_bias: float32 [64], replicated, may hold values from -3 to 3
- guidance: float32 [1], replicated, may hold values from 2 to 5
- sigma: float32 [1], replicated, may hold values from 0.05 to 0.2
- sample: float32 [256, 3072], P(('blk', 'uly'), 'cfg'), may hold values from -6 to 6
Outputs:
- velocity: float32 [256, 3072], P(('blk', 'uly'), 'cfg')
- denoised: float32 [256, 3072], P(('blk', 'uly'), 'cfg')
All inputs are finite; a program needn't handle non-finite values.
Results may differ from a plain program's by a relative error of at most 0.017.
Values may be sent and summed in bfloat16 or wider, within the bound.
No kernel may reach another device: no remote copies, remote signals or barrier semaphores. Data moves between devices by JAX's collectives and lax.ppermute only.
A program may use at most 64 MiB of HBM per device.

v0:
```python
import jax
import jax.numpy as jnp
from jax import lax
from jax.sharding import PartitionSpec as P

HEAD_DIM = 64


def swapped(block, axis, apart):
    count = lax.axis_size(axis)
    route = []
    for low in range(count):
        high = low | 1 << apart
        if high != low and high < count:
            route += [(low, high), (high, low)]
    return lax.ppermute(block, axis, route)


def local(
    latent_qkv,
    text_kv,
    hidden_in,
    modulation,
    out_weight,
    out_bias,
    proj_weight,
    proj_bias,
    guidance,
    sigma,
    sample,
):
    groups = lax.axis_size("uly")
    own_rows = latent_qkv[0]
    exchanged = lax.all_to_all(own_rows, "uly", split_axis=2, concat_axis=0, tiled=True)
    band_rows = exchanged.shape[0]
    group_width = exchanged.shape[2]
    group_heads = group_width // HEAD_DIM
    score_scale = HEAD_DIM ** (-0.5)
    queries = exchanged[:, 0, :].reshape(band_rows, group_heads, HEAD_DIM)
    key_values = exchanged[:, 1:, :].reshape(band_rows, 2 * group_width)
    text_pairs = text_kv[0].reshape(text_kv.shape[1], 2 * group_width)

    def absorb(carry, key_block):
        block_rows = key_block.shape[0]
        block_keys = key_block[:, :group_width].reshape(block_rows, group_heads, HEAD_DIM)
        block_values = key_block[:, group_width:].reshape(block_rows, group_heads, HEAD_DIM)
        running_max, denom_sum, weighted = carry
        scores = (
            jnp.einsum("qhd,khd->hqk", queries, block_keys, preferred_element_type=jnp.float32)
            * score_scale
        )
        new_max = jnp.maximum(running_max, jnp.max(scores, axis=-1))
        rescale = jnp.exp(running_max - new_max)
        expo = jnp.exp(scores - new_max[:, :, None])
        denom_sum = denom_sum * rescale + jnp.sum(expo, axis=-1)
        update = jnp.einsum(
            "hqk,khd->qhd",
            expo.astype(jnp.bfloat16),
            block_values,
            preferred_element_type=jnp.float32,
        )
        weighted = weighted * rescale.T[:, :, None] + update
        return (new_max, denom_sum, weighted)

    initial = (
        jnp.full((group_heads, band_rows), -jnp.inf, jnp.float32),
        jnp.zeros((group_heads, band_rows), jnp.float32),
        jnp.zeros((band_rows, group_heads, HEAD_DIM), jnp.float32),
    )
    started = absorb(initial, text_pairs)

    def scan_step(carry, key_block):
        return (absorb(carry, key_block), None)

    carry = started
    piece = lax.all_gather(key_values, "blk", axis=0, tiled=True)
    piece_rows = piece.shape[0]
    block_size = piece_rows
    while block_size > 1024 and block_size % 2 == 0:
        block_size = block_size // 2
    blocks = piece.reshape(piece_rows // block_size, block_size, 2 * group_width)
    carry, unused = lax.scan(scan_step, carry, blocks)
    running_max, denom_sum, weighted = carry
    attended = (
        (weighted / denom_sum.T[:, :, None]).astype(jnp.bfloat16).reshape(band_rows, group_width)
    )
    token_rows = band_rows // groups
    projected = lax.psum_scatter(
        jnp.dot(attended, out_weight, preferred_element_type=jnp.float32).astype(jnp.bfloat16),
        "uly",
        scatter_dimension=0,
        tiled=True,
    ).astype(jnp.float32)
    residual = hidden_in[0].astype(jnp.float32) + modulation[0, 0] * (projected + out_bias)
    middle = jnp.mean(residual, axis=-1, keepdims=True)
    centered = residual - middle
    spread = jnp.mean(centered * centered, axis=-1, keepdims=True)
    normed = centered * lax.rsqrt(spread + 1e-06) * (1.0 + modulation[0, 1]) + modulation[0, 2]
    normed = normed.astype(jnp.bfloat16)
    own_velocity = jnp.dot(normed, proj_weight, preferred_element_type=jnp.float32) + proj_bias
    latent_channels = own_velocity.shape[1] // 4
    tile = own_velocity.reshape(token_rows, 2, 2, latent_channels).transpose(1, 0, 2, 3)
    tile = tile.reshape(2, token_rows * 2 * latent_channels)
    branch = lax.axis_index("cfg")
    own_parity = lax.axis_index("uly") % 2
    partner = swapped(tile, "cfg", 0)
    conditional = jnp.where(branch == 0, tile, partner)
    unconditional = jnp.where(branch == 0, partner, tile)
    guided = unconditional + guidance[0] * (conditional - unconditional)
    outgoing = lax.dynamic_index_in_dim(guided, 1 - own_parity, 0, keepdims=False)
    incoming = swapped(outgoing, "uly", 0)
    kept = lax.dynamic_index_in_dim(guided, own_parity, 0, keepdims=False)
    result = jnp.where(branch == own_parity, kept, incoming)
    velocity = result.reshape(1, result.shape[0])
    denoised = sample - sigma[0] * velocity
    return (velocity, denoised)


def solution(mesh):
    return jax.shard_map(
        local,
        mesh=mesh,
        in_specs=(
            P("cfg", ("blk", "uly"), None, None),
            P("cfg", None, None, "uly"),
            P("cfg", ("blk", "uly"), None),
            P("cfg", None, None),
            P("uly", None),
            P(),
            P(),
            P(),
            P(),
            P(),
            P(("blk", "uly"), "cfg"),
        ),
        out_specs=(P(("blk", "uly"), "cfg"), P(("blk", "uly"), "cfg")),
        check_vma=False,
    )
```

profile of v0, /device:TPU:1, one launch (start us, length us, event | category | flops | bytes accessed | tf_op | source)
XLA Modules:
  0.0 294.7 jit_solution(944062336779766644)
XLA Ops:
  7.2 3.4 %copy.30 = bf16[1,48,3,1536]{1,2,3,0:T(4,128)(2,1)} copy(bf16[1,48,3,1536]{3,1,2,0:T(8,128)(2,1)} %param.13) | data formatting | bytes 884736 | tf_op args[0]
  10.6 1.7 bitcast_bitcast_fusion
  12.4 2.0 reshape.79
  14.4 16.0 %all_to_all.18 = bf16[8,2,13824]{2,1,0:T(2,128)(2,1)S(1)} all-to-all(bf16[8,2,13824]{2,1,0:T(2,128)(2,1)S(1)} %reshape.79), channel_id=1, replica_groups=mesh['cfg'=2,'blk'=32,'uly'=8] {'uly'}, dimensions={0} | all-to-all | bytes 884736 | tf_op jit(solution)/shard_map/all_to_all | solution.py:34
  30.4 2.0 reshape.80
  32.4 1.7 copy.31
  36.4 84.1 %all-gather.2.cloned.1.call-done = bf16[12288,384]{0,1:T(8,128)(2,1)} async-done(((bf16[384,384]{0,1:T(8,128)(2,1)}), bf16[12288,384]{0,1:T(8,128)(2,1)}) %all-gather.2.cloned.1.call-update) | async-done | bytes 9437200 | tf_op jit(solution)/shard_map/all_gather | solution.py:76
  120.4 12.7 %copy.34 = bf16[12288,384]{1,0:T(8,128)(2,1)} copy(bf16[12288,384]{0,1:T(8,128)(2,1)} %all-gather.2.cloned.1.call-done) | data formatting | bytes 18874368 | tf_op jit(solution)/shard_map/all_gather | solution.py:76
  133.1 57.3 %while.14 = (s32[]{:T(128)}, f32[3,384]{1,0:T(4,128)S(1)}, f32[3,384]{1,0:T(4,128)S(1)}, f32[384,3,64]{0,2,1:T(8,128)S(1)}, bf16[16,768,384]{2,1,0:T(8,128)(2,1)}, /*index=5*/bf16[384,3,64]{0,2,1:T(8,128)(2,1)S(1)}, s32[]{:T(128)}) while((s32[]{:T(128)}, f32[3,384]{1,0:T(4,128)S(1)}, f32[3,384]{1,0:T(4,128)S(1)}, f32[384,3,64]{0,2,1:T(8,128)S(1)}, ...), condition=%wide.region_5.6_spmd, body=%wide.region_2.5_spmd.sunk | while | flops 233721216 | bytes 15556689 | solution.py:82
  133.1 1.1 constant_dynamic-slice_fusion.2
  136.7 1.1 constant_dynamic-slice_fusion.2
  140.3 1.1 constant_dynamic-slice_fusion.2
  143.9 1.1 constant_dynamic-slice_fusion.2
  147.5 1.1 constant_dynamic-slice_fusion.2
  151.1 1.1 constant_dynamic-slice_fusion.2
  154.6 1.1 constant_dynamic-slice_fusion.2
  158.2 1.1 constant_dynamic-slice_fusion.2
  161.8 1.1 constant_dynamic-slice_fusion.2
  165.4 1.1 constant_dynamic-slice_fusion.2
  169.0 1.1 constant_dynamic-slice_fusion.2
  172.6 1.1 constant_dynamic-slice_fusion.2
  176.1 1.1 constant_dynamic-slice_fusion.2
  179.7 1.1 constant_dynamic-slice_fusion.2
  183.3 1.1 constant_dynamic-slice_fusion.2
  186.9 1.1 constant_dynamic-slice_fusion.2
  190.6 1.5 convolution_convert_fusion
  192.2 81.8 %reduce-scatter.2.cloned.1.call-done = bf16[48,1536]{1,0:T(8,128)(2,1)} async-done(((bf16[384,1536]{1,0:T(8,128)(2,1)}), bf16[48,1536]{1,0:T(8,128)(2,1)}) %reduce-scatter.2.cloned.1.call-update) | async-done | bytes 147472 | tf_op jit(solution)/shard_map/reduce_scatter | solution.py:88
  275.1 1.1 multiply_reduce_fusion
  276.2 1.2 convolution_add_fusion
  277.8 2.7 collective-permute-start
  281.1 1.1 collective-permute-done
  282.3 2.9 collective-permute-start.1
  (171 shorter events, 44.3 us)
Async XLA Ops:
  7.2 183.4 %copy-start = (bf16[192,1536]{1,0:T(8,128)(2,1)S(1)}, bf16[192,1536]{1,0:T(8,128)(2,1)}, u32[]{:S(2)}) copy-start(bf16[192,1536]{1,0:T(8,128)(2,1)} %param.17) | copy-start | bytes 1769476
  7.2 113.3 %all-gather.2.cloned.1.call-start = ((), (), s32[]{:S(2)}) async-start(), calls=%async_computation.2 | async-start | bytes 9732096 | tf_op jit(solution)/shard_map/all_gather | solution.py:76
  32.4 2.7 copy-start.2
  35.1 238.9 %reduce-scatter.2.cloned.1.call-start = ((), (), s32[]{:S(2)}) async-start(), calls=%async_computation.3 | async-start | bytes 1327104 | tf_op jit(solution)/shard_map/reduce_scatter | solution.py:88
  190.5 1.7 copy-start.4
  190.5 83.5 %copy-start.1 = (bf16[1,48,1536]{2,1,0:T(8,128)(2,1)S(1)}, bf16[1,48,1536]{2,1,0:T(8,128)(2,1)}, u32[]{:S(2)}) copy-start(bf16[1,48,1536]{2,1,0:T(8,128)(2,1)} %param.15) | copy-start | bytes 442372
  190.5 83.5 %copy-start.3 = (f32[1536]{0:T(1024)S(1)}, f32[1536]{0:T(1024)}, u32[]{:S(2)}) copy-start(f32[1536]{0:T(1024)} %param.18) | copy-start | bytes 18436
  190.5 85.7 %copy-start.6 = (bf16[1536,64]{0,1:T(8,128)(2,1)S(1)}, bf16[1536,64]{0,1:T(8,128)(2,1)}, u32[]{:S(2)}) copy-start(bf16[1536,64]{0,1:T(8,128)(2,1)} %param.19) | copy-start | bytes 589828
  190.5 85.7 %copy-start.7 = (f32[64]{0:T(128)S(1)}, f32[64]{0:T(128)}, u32[]{:S(2)}) copy-start(f32[64]{0:T(128)} %param.20) | copy-start | bytes 772
  190.6 96.7 %copy-start.5 = (f32[1,1536]{1,0:T(1,128)S(1)}, f32[1,1536]{1,0:T(1,128)}, u32[]{:S(2)}) copy-start(f32[1,1536]{1,0:T(1,128)} %param.23) | copy-start | bytes 18436
  277.8 4.4 %collective-permute-start = (f32[2,1536]{1,0:T(2,128)S(1)}, f32[2,1536]{1,0:T(2,128)S(1)}, u32[]{:S(2)}, u32[]{:S(2)}) collective-permute-start(f32[2,1536]{1,0:T(2,128)S(1)} %reshape.71), channel_id=1, source_target_pairs={{0,256},{256,0},{1,257},{257,1},{2,258},{258,2},{3,259},{259,3},{4... | collective-permute-start | bytes 36872 | tf_op jit(solution)/shard_map/ppermute | solution.py:16
  282.3 4.4 %collective-permute-start.1 = (f32[1536]{0:T(1024)S(1)}, f32[1536]{0:T(1024)S(1)}, u32[]{:S(2)}, u32[]{:S(2)}) collective-permute-start(f32[1536]{0:T(1024)S(1)} %get-tuple-element.58), channel_id=1, source_target_pairs={{0,1},{1,0},{2,3},{3,2},{4,5},{5,4},{6,7},{7,6},{8,9},{9,8},{10,11... | collective-permute-start | bytes 18440 | tf_op jit(solution)/shard_map/ppermute | solution.py:16
Sparse Core Ops, SparseCore 0:
  35.2 85.2 all-gather.1
  192.2 81.7 reduce-scatter.1
where the time goes:
time: 299 us; the launch traced here: 295 us
  waiting for transfers between devices  168 us (56%)
  local copies, waits for them, and re-layouts  48.5 us (16%)
  matrix products  27.2 us (9%)
  blocking collectives  16 us (5%)
  between operations  15.6 us (5%)
  other arithmetic  13.1 us (4%)
  starting transfers between devices  5.67 us (2%)
    all_gather x1, waiting for transfers between devices, local(): piece = lax.all_gather(key_values, 'blk', axis=0, tiled=True)  84.1 us
    reduce_scatter x1, waiting for transfers between devices, local(): lax.psum_scatter(jnp.dot(attended, out_weight, preferred_element_type=jnp...  81.8 us
    dynamic_slice x32, local copies, waits for them, and re-layouts, local(): carry, unused = lax.scan(scan_step, carry, blocks)  22.1 us
    all_to_all x1, blocking collectives, local(): lax.all_to_all(own_rows, 'uly', split_axis=2, concat_axis=0, tiled=True)  16 us
    dot_general x17, matrix products, absorb(): jnp.einsum('hqk,khd->qhd', expo.astype(jnp.bfloat16), block_values, prefe...  13 us
    all_gather x1, local copies, waits for them, and re-layouts, local(): piece = lax.all_gather(key_values, 'blk', axis=0, tiled=True)  12.7 us
    dot_general x17, matrix products, absorb(): jnp.einsum('qhd,khd->hqk', queries, block_keys, preferred_element_type=jn...  11.5 us
    reduce_sum x17, other arithmetic, absorb(): denom_sum = denom_sum * rescale + jnp.sum(expo, axis=-1)  9.72 us
  transfers between devices with their start and end apart: 4, of which 4 were waited for; matrix products, arithmetic and copies ran while one was open for 0% of the time, Pallas kernels for 0%

commit v1 on v0

v1 whole, which is shorter than its diff:
```python
import functools
import math

import jax
import jax.numpy as jnp
from jax import lax
from jax.experimental import pallas as pl
from jax.experimental.pallas import tpu as pltpu
from jax.sharding import Mesh, PartitionSpec as P

HEAD_DIM = 64
LANES = 128
ROW_TILE = 256
LOG2_SCALE = math.log2(math.e) * HEAD_DIM**-0.5
F32 = jnp.float32
BF16 = jnp.bfloat16
HEAD_AXES = ("zl", "y")
BLOCK_AXES = ("zl", "core", "xh", "y")


def params(**extra):
    return pltpu.CompilerParams(vmem_limit_bytes=32 * 1024 * 1024, **extra)


def lane_index(shape):
    return lax.broadcasted_iota(jnp.int32, shape, len(shape) - 1)


def pack_kernel(groups, heads, x_ref, out_ref):
    rows = x_ref.shape[1]
    half = rows // 2
    for group in range(groups):
        queries, pairs = [], []
        for head in range(heads):
            start = (group * heads + head) * HEAD_DIM
            cols = slice(start, start + HEAD_DIM)
            q = x_ref[0, :, cols].astype(F32)
            k = x_ref[1, :, cols].astype(F32)
            v = x_ref[2, :, cols].astype(F32)
            queries.append(jnp.concatenate([q[:half], q[half:]], axis=1))
            pairs.append(jnp.concatenate([k, v], axis=1))
        out_ref[group] = jnp.concatenate(queries + pairs, axis=0).astype(BF16)


def pack(x, groups, heads):
    rows = x.shape[1]
    return pl.pallas_call(
        functools.partial(pack_kernel, groups, heads),
        out_shape=jax.ShapeDtypeStruct((groups, heads * (rows // 2 + rows), LANES), BF16),
        compiler_params=params(),
        name="pack_heads",
    )(x)


def queries_kernel(heads, place_ref, own_ref, other_ref, out_ref, wide_ref):
    here = place_ref[0]
    cores, sources, _, half, _ = own_ref.shape
    across = sources // 2
    low = lane_index((half, LANES)) < HEAD_DIM
    for side, ref in ((here, own_ref), (1 - here, other_ref)):
        for core in range(cores):
            for source in range(sources):
                zl, y = divmod(source, across)
                first = (zl * cores + core) * 2 * across + y
                row = pl.multiple_of((first + side * across) * half, 8)
                for head in range(heads):
                    both = ref[core, source, head].astype(F32)
                    turned = pltpu.roll(both, HEAD_DIM, 1)
                    wide_ref[head, 0, pl.ds(row, half)] = jnp.where(low, both, 0.0)
                    wide_ref[head, 1, pl.ds(row, half)] = jnp.where(low, turned, 0.0)
    out_ref[...] = wide_ref[...].astype(BF16)


def unpack_queries(place, own, other):
    cores, sources, heads, half, _ = own.shape
    shape = (heads, 2, 2 * cores * sources * half, LANES)
    return pl.pallas_call(
        functools.partial(queries_kernel, heads),
        out_shape=jax.ShapeDtypeStruct(shape, BF16),
        in_specs=[
            pl.BlockSpec(memory_space=pltpu.SMEM),
            pl.BlockSpec(memory_space=pltpu.VMEM),
            pl.BlockSpec(memory_space=pltpu.VMEM),
        ],
        out_specs=pl.BlockSpec(memory_space=pltpu.VMEM),
        scratch_shapes=[pltpu.VMEM(shape, F32)],
        compiler_params=params(),
        name="unpack_queries",
    )(place, own, other)


def update(state, scores, values, flipped):
    lane = lane_index((scores[0].shape[0], LANES))
    largest = functools.reduce(jnp.maximum, [jnp.max(s, axis=1, keepdims=True) for s in scores])
    if state is not None:
        before = state[:, 32:33]
        largest = jnp.maximum(largest, before)
    offset = largest * LOG2_SCALE
    total = None
    for s, value, turn in zip(scores, values, flipped):
        weights = jnp.exp2(s * LOG2_SCALE - offset).astype(BF16)
        dims = (((1,), (1,)), ((), ())) if turn else (((1,), (0,)), ((), ()))
        term = lax.dot_general(weights, value, dims, preferred_element_type=F32)
        total = term if total is None else total + term
    if state is not None:
        total = total + state * jnp.exp2(before * LOG2_SCALE - offset)
    return jnp.where((lane >= 32) & (lane < HEAD_DIM), largest, total)


def split_block(ref, head):
    sources, _, rows, lanes = ref.shape
    block = ref[:, head].reshape(sources * rows, lanes)
    ones = jnp.ones_like(block)
    return block, jnp.where(lane_index(block.shape) < HEAD_DIM, ones, block)


def scores_of(q, block):
    return lax.dot_general(q, block, (((1,), (1,)), ((), ())), preferred_element_type=F32)


def first_kernel(heads, cut, place_ref, q_ref, block_ref, text_ref, state_ref):
    rows = 2 * q_ref.shape[2]
    for head in range(heads):
        q = q_ref[head].reshape(rows, LANES)
        block, values = split_block(block_ref, head)
        state = update(None, [scores_of(q, block)], [values], [False])
        state_ref[head] = state.reshape(state_ref.shape[1:])

    def with_text(low, high, width):
        for head in range(heads):
            q = q_ref[head].reshape(rows, LANES)
            state = state_ref[head].reshape(rows, LANES)
            features = slice(head * HEAD_DIM, (head + 1) * HEAD_DIM)
            keys = text_ref[0, features, low:high]
            values = text_ref[1, features, low:high]
            if width > high - low:
                pad = jnp.zeros((HEAD_DIM, width - (high - low)), BF16)
                keys = jnp.concatenate([keys, pad], axis=1)
                values = jnp.concatenate([values, pad], axis=1)
            stacked = jnp.concatenate([keys, values], axis=0)
            counted = jnp.concatenate([jnp.ones_like(keys), values], axis=0)
            scores = lax.dot_general(q, stacked, (((1,), (0,)), ((), ())), preferred_element_type=F32)
            scores = jnp.where(lane_index(scores.shape) < high - low, scores, -jnp.inf)
            state = update(state, [scores], [counted], [True])
            state_ref[head] = state.reshape(state_ref.shape[1:])

    count = text_ref.shape[2]

    @pl.when(place_ref[0] == 0)
    def _():
        with_text(0, cut, cut)

    @pl.when(place_ref[0] == 1)
    def _():
        with_text(cut, count, -(-(count - cut) // LANES) * LANES)


def next_kernel(heads, count, q_ref, state_ref, *refs):
    blocks, out_ref = refs[:count], refs[count]
    rows = 2 * q_ref.shape[2]
    for head in range(heads):
        q = q_ref[head].reshape(rows, LANES)
        pairs = [split_block(ref, head) for ref in blocks]
        scores = [scores_of(q, block) for block, _ in pairs]
        state = state_ref[head].reshape(rows, LANES)
        state = update(state, scores, [values for _, values in pairs], [False] * count)
        out_ref[head] = state.reshape(out_ref.shape[1:])


def last_kernel(heads, q_ref, state_ref, block_ref, out_ref):
    tile = q_ref.shape[2]
    rows = 2 * tile
    lane = lane_index((rows, LANES))
    done = []
    marks = jnp.zeros((rows, LANES), F32)
    for head in range(heads):
        q = q_ref[head].reshape(rows, LANES)
        block, values = split_block(block_ref, head)
        state = state_ref[head].reshape(rows, LANES)
        state = update(state, [scores_of(q, block)], [values], [False])
        total = state[:, 0:1]
        level = state[:, 32:33] * LOG2_SCALE + jnp.log2(total)
        coarse = level.astype(BF16).astype(F32)
        middle = (level - coarse).astype(BF16).astype(F32)
        fine = level - coarse - middle
        for place, part in enumerate((coarse, middle, fine)):
            marks = jnp.where(lane == HEAD_DIM + 3 * head + place, part, marks)
        done.append(state / total)
    low = lane < HEAD_DIM
    left = jnp.where(low, pltpu.roll(done[0], HEAD_DIM, 1), done[1]).astype(BF16)
    right = jnp.where(low, pltpu.roll(done[2], HEAD_DIM, 1), marks).astype(BF16)
    for half in range(2):
        part = slice(half * tile, (half + 1) * tile)
        out_ref[:, 2 * half * LANES : (2 * half + 1) * LANES] = left[part]
        out_ref[:, (2 * half + 1) * LANES : (2 * half + 2) * LANES] = right[part]


def attention_call(kernel, name, q, state, blocks, out, place=None, text=None):
    heads, _, rows, _ = q.shape
    tile = ROW_TILE if rows % ROW_TILE == 0 else rows
    row_spec = pl.BlockSpec((heads, 2, tile, LANES), lambda i: (0, 0, i, 0))
    whole = lambda x: pl.BlockSpec(x.shape, lambda i: (0,) * x.ndim)
    operands, specs = [], []
    if place is not None:
        operands.append(place)
        specs.append(pl.BlockSpec(memory_space=pltpu.SMEM))
    operands.append(q)
    specs.append(row_spec)
    if state is not None:
        operands.append(state)
        specs.append(row_spec)
    for block in blocks:
        operands.append(block)
        specs.append(whole(block))
    if text is not None:
        operands.append(text)
        specs.append(whole(text))
    keys = sum(b.shape[0] * b.shape[2] for b in blocks)
    pairs = heads * 2 * rows * keys
    if out == "state":
        shape = jax.ShapeDtypeStruct(q.shape, F32)
        out_spec = row_spec
    else:
        shape = jax.ShapeDtypeStruct((rows, 4 * LANES), BF16)
        out_spec = pl.BlockSpec((tile, 4 * LANES), lambda i: (i, 0))
    return pl.pallas_call(
        kernel,
        grid=(rows // tile,),
        out_shape=shape,
        in_specs=specs,
        out_specs=out_spec,
        compiler_params=params(),
        cost_estimate=pl.CostEstimate(
            flops=pairs * 4 * LANES * 2, bytes_accessed=2 * q.size * 4, transcendentals=pairs
        ),
        name=name,
    )(*operands)


def finish_kernel(
    heads, groups, partial_ref, weight_ref, hidden_ref, modulation_ref, bias_ref, final_ref, final_bias_ref, out_ref, wide_ref
):
    half = partial_ref.shape[1]
    sources = partial_ref.shape[0]
    across = groups // 2
    copies = sources // groups
    width = heads * HEAD_DIM
    low = lane_index((half, LANES)) < HEAD_DIM
    for part in range(2):
        at = part * 2 * LANES
        for group in range(groups):
            zl, y = divmod(group, across)
            members = [(zl * copies + copy) * across + y for copy in range(copies)]
            left = [partial_ref[m, :, at : at + LANES].astype(F32) for m in members]
            right = [partial_ref[m, :, at + LANES : at + 2 * LANES].astype(F32) for m in members]
            levels = [r + pltpu.roll(r, LANES - 1, 1) + pltpu.roll(r, LANES - 2, 1) for r in right]
            top = functools.reduce(jnp.maximum, levels)
            shares = [jnp.exp2(level - top) for level in levels]
            total = functools.reduce(jnp.add, shares)
            first, second = 0.0, 0.0
            for copy in range(copies):
                share = shares[copy] / total
                h0, h1, h2 = [share[:, HEAD_DIM + 3 * h : HEAD_DIM + 3 * h + 1] for h in range(3)]
                first = first + left[copy] * jnp.where(low, h0, h1)
                second = second + right[copy] * h2
            both = jnp.concatenate([first, second[:, :HEAD_DIM]], axis=1)
            wide_ref[part * half : (part + 1) * half, group * width : (group + 1) * width] = both
    attended = wide_ref[...].astype(BF16)
    weights = weight_ref.shape[0]
    projected = jnp.concatenate(
        [jnp.dot(attended, weight_ref[w], preferred_element_type=F32) for w in range(weights)], axis=1
    )
    residual = hidden_ref[...].astype(F32) + modulation_ref[0:1] * (projected + bias_ref[...])
    middle = jnp.mean(residual, axis=-1, keepdims=True)
    centered = residual - middle
    spread = jnp.mean(centered * centered, axis=-1, keepdims=True)
    normed = centered * lax.rsqrt(spread + 1e-06) * (1.0 + modulation_ref[1:2]) + modulation_ref[2:3]
    velocity = lax.dot_general(
        normed.astype(BF16), final_ref[...], (((1,), (1,)), ((), ())), preferred_element_type=F32
    )
    out_ref[...] = velocity + final_bias_ref[...]


def finish(partial, weight, hidden, modulation, bias, final_weight, final_bias, heads, groups):
    tokens, width = hidden.shape
    return pl.pallas_call(
        functools.partial(finish_kernel, heads, groups),
        out_shape=jax.ShapeDtypeStruct((tokens, final_weight.shape[0]), F32),
        scratch_shapes=[pltpu.VMEM((tokens, width), F32)],
        compiler_params=params(),
        name="project_and_norm",
    )(partial, weight, hidden, modulation, bias, final_weight, final_bias)


def local(
    latent_qkv,
    text_kv,
    hidden_in,
    modulation,
    out_weight,
    out_bias,
    proj_weight,
    proj_bias,
    guidance,
    sigma,
    sample,
):
    groups = lax.axis_size("zl") * lax.axis_size("y")
    ring = lax.axis_size("zh")
    tokens = latent_qkv.shape[1]
    half = tokens // 2
    width = latent_qkv.shape[3] // groups
    heads = width // HEAD_DIM
    zl, core, xh = (lax.axis_index(a) for a in ("zl", "core", "xh"))

    columns = out_weight.shape[1] // 2
    own_columns = lax.dynamic_slice_in_dim(out_weight, core * columns, columns, 1)
    weight = lax.all_gather(own_columns, ("core", "xh", "y"), axis=0, tiled=True)
    weight = weight.reshape(2, groups * width, columns)

    slabs = pack(latent_qkv[0].transpose(1, 0, 2), groups, heads)
    slabs = lax.all_to_all(slabs, HEAD_AXES, split_axis=0, concat_axis=0, tiled=True)
    own = slabs[:, heads * half :].reshape(groups, heads, tokens, LANES)
    up = [(i, (i + 1) % ring) for i in range(ring)]
    down = [(i, (i - 1) % ring) for i in range(ring)]
    right, left = lax.ppermute(own, "zh", up), lax.ppermute(own, "zh", down)

    packed = slabs[:, : heads * half].reshape(groups, heads, half, LANES)
    packed = lax.all_gather(packed, "core", axis=0)
    opposite = lax.ppermute(packed, "xh", [(0, 1), (1, 0)])
    q = unpack_queries(xh.reshape(1), packed, opposite)

    count = text_kv.shape[1]
    cut = min(2 * LANES, count)
    has_text = jnp.where(xh == zl, core, 2).reshape(1)
    text = text_kv[0].transpose(1, 2, 0)
    state = attention_call(
        functools.partial(first_kernel, heads, cut), "own_block", q, None, [own], "state", has_text, text
    )
    for _ in range(ring // 2 - 2):
        further_right = lax.ppermute(right, "zh", up)
        further_left = lax.ppermute(left, "zh", down)
        state = attention_call(
            functools.partial(next_kernel, heads, 2), "two_blocks", q, state, [right, left], "state"
        )
        right, left = further_right, further_left
    route = []
    for i in range(ring):
        route += [(2 * i, 2 * ((i + 1) % ring)), (2 * i + 1, 2 * ((i - 1) % ring) + 1)]
    farthest = lax.ppermute(jnp.where(core == 0, right, left), ("zh", "core"), route)
    state = attention_call(
        functools.partial(next_kernel, heads, 2), "two_blocks", q, state, [right, left], "state"
    )
    partial = attention_call(functools.partial(last_kernel, heads), "last_block", q, state, [farthest], "partial")
    partial = partial.reshape(4 * groups, half, 4 * LANES)
    partial = lax.all_to_all(partial, BLOCK_AXES, split_axis=0, concat_axis=0, tiled=True)

    velocity = finish(
        partial,
        weight,
        hidden_in[0],
        modulation[0],
        out_bias[None],
        proj_weight.T,
        proj_bias[None],
        heads,
        groups,
    )

    tiles = velocity.reshape(tokens, 2, -1).transpose(1, 0, 2).reshape(2, -1)
    branch, parity = lax.axis_index("cfg"), lax.axis_index("y") % 2
    across = lax.axis_size("y")
    same, swap = [], []
    for s in range(2):
        for y in range(across):
            a = y % 2
            same.append((s * across + y, a * across + y - a + s))
            swap.append((s * across + y, a * across + y - a + 1 - s))
    kept = lax.ppermute(lax.dynamic_index_in_dim(tiles, branch, 0, keepdims=False), ("cfg", "y"), same)
    crossed = lax.ppermute(lax.dynamic_index_in_dim(tiles, 1 - branch, 0, keepdims=False), ("cfg", "y"), swap)
    conditional = jnp.where(parity == 0, kept, crossed)
    unconditional = jnp.where(parity == 0, crossed, kept)
    guided = unconditional + guidance[0] * (conditional - unconditional)
    result = guided.reshape(1, guided.shape[0])
    denoised = sample - sigma[0] * result
    return (result, denoised)


def solution(mesh):
    sizes = dict(zip(mesh.axis_names, mesh.devices.shape))
    ring = sizes["blk"] // 4
    fine = Mesh(
        mesh.devices.reshape(sizes["cfg"], ring, 2, 2, 2, sizes["uly"] // 2),
        ("cfg", "zh", "zl", "core", "xh", "y"),
    )
    rows = ("zh", "zl", "core", "xh", "y")
    heads = ("xh", "y")
    return jax.shard_map(
        local,
        mesh=fine,
        in_specs=(
            P("cfg", rows, None, None),
            P("cfg", None, None, heads),
            P("cfg", rows, None),
            P("cfg", None, None),
            P(heads, None),
            P(),
            P(),
            P(),
            P(),
            P(),
            P(rows, "cfg"),
        ),
        out_specs=(P(rows, "cfg"), P(rows, "cfg")),
        check_vma=False,
    )
```

time: 299 us -> 158 us (0.53)
  the two profiles are of different devices: /device:TPU:1 before, /device:TPU:98 now
where the time goes in v1:
time: 158 us; the launch traced here: 157 us
  starting transfers between devices  53.3 us (34%)
  Pallas kernels  40.4 us (26%)
  waiting for transfers between devices  25.6 us (16%)
  between operations  15.7 us (10%)
  blocking collectives  15.5 us (10%)
  local copies, waits for them, and re-layouts  6.09 us (4%)
    pallas_call x5, Pallas kernels, attention_call(): pl.pallas_call(kernel, grid=(rows // tile,), out_shape=shape, in_specs=sp...  37 us
    all_to_all x1, waiting for transfers between devices, local(): lax.all_to_all(partial, BLOCK_AXES, split_axis=0, concat_axis=0, tiled=True)  14.4 us
    all_to_all x1, blocking collectives, local(): lax.all_to_all(slabs, HEAD_AXES, split_axis=0, concat_axis=0, tiled=True)  13.5 us
    all_to_all x1, starting transfers between devices, local(): lax.all_to_all(partial, BLOCK_AXES, split_axis=0, concat_axis=0, tiled=True)  11 us
    ppermute x2, starting transfers between devices, local(): further_right = lax.ppermute(right, 'zh', up)  9.2 us
    ppermute x2, starting transfers between devices, local(): further_left = lax.ppermute(left, 'zh', down)  8.56 us
    ppermute x2, starting transfers between devices, local(): right, left = (lax.ppermute(own, 'zh', up), lax.ppermute(own, 'zh', down))  8.31 us
    ppermute x1, starting transfers between devices, local(): lax.ppermute(jnp.where(core == 0, right, left), ('zh', 'core'), route)  5.89 us
  transfers between devices with their start and end apart: 12, of which 6 were waited for; matrix products, arithmetic and copies ran while one was open for 0% of the time, Pallas kernels for 24%

profile of v1, /device:TPU:98, one launch (start us, length us, event | category | flops | bytes accessed | tf_op | source)
XLA Modules:
  0.0 157.2 jit_solution(4316875887513749934)
XLA Ops:
  7.2 1.0 copy-done
  8.2 0.7 constant_dynamic-slice_fusion
  9.0 1.0 copy-done.2
  10.0 0.2 pack_heads.1
  10.2 13.5 %all_to_all.10 = bf16[8,216,128]{2,1,0:T(8,128)(2,1)S(1)} all-to-all(bf16[8,216,128]{2,1,0:T(8,128)(2,1)S(1)} %pack_heads.1), channel_id=1, replica_groups=mesh['cfg'=2,'zh'=8,'zl'=2,'core'=2,'xh'=2,'y'=4] {'zl','y'}, dimensions={0} | all-to-all | bytes 884736 | tf_op jit(solution)/shard_map/all_to_all | solution.py:322
  23.7 6.4 %collective-permute-start.1 = (bf16[8,3,48,128]{3,2,1,0:T(8,128)(2,1)S(1)}, bf16[8,3,48,128]{3,2,1,0:T(8,128)(2,1)S(1)}, u32[]{:S(2)}, u32[]{:S(2)}) collective-permute-start(bf16[8,3,48,128]{3,2,1,0:T(8,128)(2,1)S(1)} %bitcast.27), channel_id=1, source_target_pairs={{0,32},{32,64},{64,96},{96,128},{128,160},{160,192},{192,224},{224... | collective-permute-start | bytes 884744 | tf_op jit(solution)/shard_map/ppermute | solution.py:326
  30.1 1.9 %collective-permute-start.2 = (bf16[8,3,48,128]{3,2,1,0:T(8,128)(2,1)S(1)}, bf16[8,3,48,128]{3,2,1,0:T(8,128)(2,1)S(1)}, u32[]{:S(2)}, u32[]{:S(2)}) collective-permute-start(bf16[8,3,48,128]{3,2,1,0:T(8,128)(2,1)S(1)} %bitcast.28), channel_id=1, source_target_pairs={{0,224},{32,0},{64,32},{96,64},{128,96},{160,128},{192,160},{224,1... | collective-permute-start | bytes 884744 | tf_op jit(solution)/shard_map/ppermute | solution.py:326
  32.1 2.0 %all_gather.6.own_ref = bf16[2,8,3,24,128]{4,3,2,1,0:T(8,128)(2,1)S(1)} all-gather(bf16[1,8,3,24,128]{4,3,2,1,0:T(8,128)(2,1)S(1)} %bitcast.35), channel_id=1, replica_groups=mesh['cfg'=2,'zh'=8,'zl'=2,'core'=2,'xh'=2,'y'=4] {'core'}, dimensions={0}, use_global_device_ids=true | all-gather | bytes 442368 | tf_op jit(solution)/shard_map/all_gather | solution.py:329
  34.1 4.0 %collective-permute-start = (bf16[2,8,3,24,128]{4,3,2,1,0:T(8,128)(2,1)S(1)}, bf16[2,8,3,24,128]{4,3,2,1,0:T(8,128)(2,1)S(1)}, u32[]{:S(2)}, u32[]{:S(2)}) collective-permute-start(bf16[2,8,3,24,128]{4,3,2,1,0:T(8,128)(2,1)S(1)} %all_gather.6.own_ref), channel_id=1, source_target_pairs={{0,4},{4,0},{1,5},{5,1},{2,6},{6,2},{3,7},{7,3},{8,12},{12,8},{9,1... | collective-permute-start | bytes 884744 | tf_op jit(solution)/shard_map/ppermute | solution.py:330
  38.2 2.6 %collective-permute-done.1.refs_0_ = bf16[8,3,48,128]{3,2,1,0:T(8,128)(2,1)S(1)} collective-permute-done((bf16[8,3,48,128]{3,2,1,0:T(8,128)(2,1)S(1)}, bf16[8,3,48,128]{3,2,1,0:T(8,128)(2,1)S(1)}, u32[]{:S(2)}, u32[]{:S(2)}) %collective-permute-start.1) | collective-permute-done | bytes 294944 | tf_op jit(solution)/shard_map/ppermute | solution.py:326
  40.8 5.5 %collective-permute-start.3 = (bf16[8,3,48,128]{3,2,1,0:T(8,128)(2,1)S(1)}, bf16[8,3,48,128]{3,2,1,0:T(8,128)(2,1)S(1)}, u32[]{:S(2)}, u32[]{:S(2)}) collective-permute-start(bf16[8,3,48,128]{3,2,1,0:T(8,128)(2,1)S(1)} %collective-permute-done.1.refs_0_), channel_id=1, source_target_pairs={{0,32},{32,64},{64,96},{96,128},{128,160},{160,192},{192,224},{224... | collective-permute-start | bytes 884744 | tf_op jit(solution)/shard_map/ppermute | solution.py:341
  46.3 4.3 %collective-permute-start.4 = (bf16[8,3,48,128]{3,2,1,0:T(8,128)(2,1)S(1)}, bf16[8,3,48,128]{3,2,1,0:T(8,128)(2,1)S(1)}, u32[]{:S(2)}, u32[]{:S(2)}) collective-permute-start(bf16[8,3,48,128]{3,2,1,0:T(8,128)(2,1)S(1)} %collective-permute-done.2.refs_1_), channel_id=1, source_target_pairs={{0,224},{32,0},{64,32},{96,64},{128,96},{160,128},{192,160},{224,1... | collective-permute-start | bytes 884744 | tf_op jit(solution)/shard_map/ppermute | solution.py:342
  50.6 0.4 unpack_queries.1.q_ref
  51.0 4.0 %own_block.1.state_ref = f32[3,2,768,128]{3,2,1,0:T(8,128)S(1)} custom-call(s32[1]{0:T(128)} %bitcast.4.place_ref, bf16[3,2,768,128]{3,2,1,0:T(8,128)(2,1)S(1)} %unpack_queries.1.q_ref, bf16[8,3,48,128]{3,2,1,0:T(8,128)(2,1)S(1)} %bitcast.29, bf16[2,192,333]{2,1,0:T(8,128)(2,1)S(1)} %bitcast.34), custom_call_target="tpu_custom_call" | custom-call | flops 1811939328 | bytes 4718592 | tf_op jit(solution)/shard_map/own_block/pallas_call | solution.py:226
  55.0 7.3 %two_blocks.3.state_ref = f32[3,2,768,128]{3,2,1,0:T(8,128)S(1)} custom-call(bf16[3,2,768,128]{3,2,1,0:T(8,128)(2,1)S(1)} %unpack_queries.1.q_ref, f32[3,2,768,128]{3,2,1,0:T(8,128)S(1)} %own_block.1.state_ref, bf16[8,3,48,128]{3,2,1,0:T(8,128)(2,1)S(1)} %collective-permute-done.1.refs_0_, bf16[8,3,48,128]{3,2,1,0:T(8,128)(2,1)S(1)} %collective-permute-done.2.refs_1_), custom_call_target="tpu_custom_call" | custom-call | flops 3623878656 | bytes 4718592 | tf_op jit(solution)/shard_map/two_blocks/pallas_call | solution.py:226
  62.4 3.7 %collective-permute-start.5 = (bf16[8,3,48,128]{3,2,1,0:T(8,128)(2,1)S(1)}, bf16[8,3,48,128]{3,2,1,0:T(8,128)(2,1)S(1)}, u32[]{:S(2)}, u32[]{:S(2)}) collective-permute-start(bf16[8,3,48,128]{3,2,1,0:T(8,128)(2,1)S(1)} %collective-permute-done.3.refs_0_), channel_id=1, source_target_pairs={{0,32},{32,64},{64,96},{96,128},{128,160},{160,192},{192,224},{224... | collective-permute-start | bytes 884744 | tf_op jit(solution)/shard_map/ppermute | solution.py:341
  66.0 4.3 %collective-permute-start.6 = (bf16[8,3,48,128]{3,2,1,0:T(8,128)(2,1)S(1)}, bf16[8,3,48,128]{3,2,1,0:T(8,128)(2,1)S(1)}, u32[]{:S(2)}, u32[]{:S(2)}) collective-permute-start(bf16[8,3,48,128]{3,2,1,0:T(8,128)(2,1)S(1)} %collective-permute-done.4.refs_1_), channel_id=1, source_target_pairs={{0,224},{32,0},{64,32},{96,64},{128,96},{160,128},{192,160},{224,1... | collective-permute-start | bytes 884744 | tf_op jit(solution)/shard_map/ppermute | solution.py:342
  70.3 7.3 %two_blocks.4.state_ref = f32[3,2,768,128]{3,2,1,0:T(8,128)S(1)} custom-call(bf16[3,2,768,128]{3,2,1,0:T(8,128)(2,1)S(1)} %unpack_queries.1.q_ref, f32[3,2,768,128]{3,2,1,0:T(8,128)S(1)} %two_blocks.3.state_ref, bf16[8,3,48,128]{3,2,1,0:T(8,128)(2,1)S(1)} %collective-permute-done.3.refs_0_, bf16[8,3,48,128]{3,2,1,0:T(8,128)(2,1)S(1)} %collective-permute-done.4.refs_1_), custom_call_target="tpu_custom_call" | custom-call | flops 3623878656 | bytes 4718592 | tf_op jit(solution)/shard_map/two_blocks/pallas_call | solution.py:226
  77.8 0.5 collective-permute-done.6.refs_1_
  78.3 5.9 %collective-permute-start.7 = (bf16[8,3,48,128]{3,2,1,0:T(8,128)(2,1)S(1)}, bf16[8,3,48,128]{3,2,1,0:T(8,128)(2,1)S(1)}, u32[]{:S(2)}, u32[]{:S(2)}) collective-permute-start(bf16[8,3,48,128]{3,2,1,0:T(8,128)(2,1)S(1)} %broadcast_select_fusion), channel_id=1, source_target_pairs={{0,32},{8,232},{32,64},{40,8},{64,96},{72,40},{96,128},{104,72},{1... | collective-permute-start | bytes 884744 | tf_op jit(solution)/shard_map/ppermute | solution.py:350
  84.2 7.3 %two_blocks.5.state_ref = f32[3,2,768,128]{3,2,1,0:T(8,128)S(1)} custom-call(bf16[3,2,768,128]{3,2,1,0:T(8,128)(2,1)S(1)} %unpack_queries.1.q_ref, f32[3,2,768,128]{3,2,1,0:T(8,128)S(1)} %two_blocks.4.state_ref, bf16[8,3,48,128]{3,2,1,0:T(8,128)(2,1)S(1)} %collective-permute-done.5.refs_0_, bf16[8,3,48,128]{3,2,1,0:T(8,128)(2,1)S(1)} %collective-permute-done.6.refs_1_), custom_call_target="tpu_custom_call" | custom-call | flops 3623878656 | bytes 4718592 | tf_op jit(solution)/shard_map/two_blocks/pallas_call | solution.py:226
  91.6 5.8 %collective-permute-done.7.block_ref = bf16[8,3,48,128]{3,2,1,0:T(8,128)(2,1)S(1)} collective-permute-done((bf16[8,3,48,128]{3,2,1,0:T(8,128)(2,1)S(1)}, bf16[8,3,48,128]{3,2,1,0:T(8,128)(2,1)S(1)}, u32[]{:S(2)}, u32[]{:S(2)}) %collective-permute-start.7) | collective-permute-done | bytes 294944 | tf_op jit(solution)/shard_map/ppermute | solution.py:350
  97.4 11.0 %last_block.1 = bf16[768,512]{1,0:T(8,128)(2,1)} custom-call(bf16[3,2,768,128]{3,2,1,0:T(8,128)(2,1)S(1)} %unpack_queries.1.q_ref, f32[3,2,768,128]{3,2,1,0:T(8,128)S(1)} %two_blocks.5.state_ref, bf16[8,3,48,128]{3,2,1,0:T(8,128)(2,1)S(1)} %collective-permute-done.7.block_ref), custom_call_target="tpu_custom_call" | custom-call | flops 1811939328 | bytes 4718592 | tf_op jit(solution)/shard_map/last_block/pallas_call | solution.py:226
  108.4 11.0 %all-to-all-start.1 = ((bf16[32,24,512]{2,1,0:T(8,128)(2,1)}), bf16[32,24,512]{2,1,0:T(8,128)(2,1)S(1)}, u32[]{:S(2)}, u32[]{:S(2)}) async-start(bf16[32,24,512]{2,1,0:T(8,128)(2,1)} %bitcast.8), calls=%async_computation.1 | async-start | bytes 1572864 | tf_op jit(solution)/shard_map/all_to_all | solution.py:356
  119.5 14.4 %all-to-all-done.1.partial_ref = bf16[32,24,512]{2,1,0:T(8,128)(2,1)S(1)} async-done(((bf16[32,24,512]{2,1,0:T(8,128)(2,1)}), bf16[32,24,512]{2,1,0:T(8,128)(2,1)S(1)}, u32[]{:S(2)}, u32[]{:S(2)}) %all-to-all-start.1) | async-done | bytes 786464 | tf_op jit(solution)/shard_map/all_to_all | solution.py:356
  133.9 2.3 %copy-done.1 = bf16[3072,768]{1,0:T(8,128)(2,1)S(1)} copy-done((bf16[3072,768]{1,0:T(8,128)(2,1)S(1)}, bf16[3072,768]{1,0:T(8,128)(2,1)}, u32[]{:S(2)}) %copy-start.1) | copy-done | bytes 4718616
  136.2 2.9 %project_and_norm.1 = f32[48,64]{1,0:T(8,128)S(1)} custom-call(bf16[32,24,512]{2,1,0:T(8,128)(2,1)S(1)} %all-to-all-done.1.partial_ref, bf16[2,1536,768]{2,1,0:T(8,128)(2,1)S(1)} %bitcast.25, bf16[48,1536]{1,0:T(8,128)(2,1)S(1)} %bitcast.31, f32[3,1536]{1,0:T(4,128)S(1)} %bitcast.32, f32[1,1536]{1,0:T(1,128)S(1)} %broadcast_in_dim.6.bias_ref, ...), custom_call_target="tpu_custom_call" | custom-call | tf_op jit(solution)/shard_map/project_and_norm/pallas_call | solution.py:286
  139.4 3.3 %collective-permute-start.8 = (f32[1536]{0:T(1024)S(1)}, f32[1536]{0:T(1024)S(1)}, u32[]{:S(2)}, u32[]{:S(2)}) collective-permute-start(f32[1536]{0:T(1024)S(1)} %get-tuple-element.2), channel_id=1, source_target_pairs={{0,1},{1,257},{2,3},{3,259},{256,0},{257,256},{258,2},{259,258},{4... | collective-permute-start | bytes 18440 | tf_op jit(solution)/shard_map/ppermute | solution.py:380
  142.7 3.0 %collective-permute-start.9 = (f32[1536]{0:T(1024)S(1)}, f32[1536]{0:T(1024)S(1)}, u32[]{:S(2)}, u32[]{:S(2)}) collective-permute-start(f32[1536]{0:T(1024)S(1)} %get-tuple-element.3), channel_id=1, source_target_pairs={{0,0},{1,256},{2,2},{3,258},{256,1},{257,257},{258,3},{259,259},{4... | collective-permute-start | bytes 18440 | tf_op jit(solution)/shard_map/ppermute | solution.py:379
  147.0 2.1 %collective-permute-done.9 = f32[1536]{0:T(1024)S(1)} collective-permute-done((f32[1536]{0:T(1024)S(1)}, f32[1536]{0:T(1024)S(1)}, u32[]{:S(2)}, u32[]{:S(2)}) %collective-permute-start.9) | collective-permute-done | bytes 6176 | tf_op jit(solution)/shard_map/ppermute | solution.py:379
  149.2 0.6 reshape.36
  149.8 0.6 reshape_subtract_fusion
  (36 shorter events, 0.6 us)
Async XLA Ops:
  7.2 1.1 copy-start
  7.2 126.7 %all-gather.2.cloned.1.call-start = ((), (), s32[]{:S(2)}) async-start(), calls=%async_computation.2 | async-start | bytes 5013504 | tf_op jit(solution)/shard_map/all_gather | solution.py:318
  9.0 1.0 copy-start.2
  10.0 41.0 %copy-start.6 = (bf16[1,333,2,192]{1,3,2,0:T(8,128)(2,1)S(1)}, bf16[1,333,2,192]{1,3,2,0:T(8,128)(2,1)}, u32[]{:S(2)}) copy-start(bf16[1,333,2,192]{1,3,2,0:T(8,128)(2,1)} %param.12) | copy-start | bytes 767236
  23.7 17.0 %collective-permute-start.1 = (bf16[8,3,48,128]{3,2,1,0:T(8,128)(2,1)S(1)}, bf16[8,3,48,128]{3,2,1,0:T(8,128)(2,1)S(1)}, u32[]{:S(2)}, u32[]{:S(2)}) collective-permute-start(bf16[8,3,48,128]{3,2,1,0:T(8,128)(2,1)S(1)} %bitcast.27), channel_id=1, source_target_pairs={{0,32},{32,64},{64,96},{96,128},{128,160},{160,192},{192,224},{224... | collective-permute-start | bytes 884744 | tf_op jit(solution)/shard_map/ppermute | solution.py:326
  30.1 16.2 %collective-permute-start.2 = (bf16[8,3,48,128]{3,2,1,0:T(8,128)(2,1)S(1)}, bf16[8,3,48,128]{3,2,1,0:T(8,128)(2,1)S(1)}, u32[]{:S(2)}, u32[]{:S(2)}) collective-permute-start(bf16[8,3,48,128]{3,2,1,0:T(8,128)(2,1)S(1)} %bitcast.28), channel_id=1, source_target_pairs={{0,224},{32,0},{64,32},{96,64},{128,96},{160,128},{192,160},{224,1... | collective-permute-start | bytes 884744 | tf_op jit(solution)/shard_map/ppermute | solution.py:326
  34.1 16.5 %collective-permute-start = (bf16[2,8,3,24,128]{4,3,2,1,0:T(8,128)(2,1)S(1)}, bf16[2,8,3,24,128]{4,3,2,1,0:T(8,128)(2,1)S(1)}, u32[]{:S(2)}, u32[]{:S(2)}) collective-permute-start(bf16[2,8,3,24,128]{4,3,2,1,0:T(8,128)(2,1)S(1)} %all_gather.6.own_ref), channel_id=1, source_target_pairs={{0,4},{4,0},{1,5},{5,1},{2,6},{6,2},{3,7},{7,3},{8,12},{12,8},{9,1... | collective-permute-start | bytes 884744 | tf_op jit(solution)/shard_map/ppermute | solution.py:330
  40.8 21.6 %collective-permute-start.3 = (bf16[8,3,48,128]{3,2,1,0:T(8,128)(2,1)S(1)}, bf16[8,3,48,128]{3,2,1,0:T(8,128)(2,1)S(1)}, u32[]{:S(2)}, u32[]{:S(2)}) collective-permute-start(bf16[8,3,48,128]{3,2,1,0:T(8,128)(2,1)S(1)} %collective-permute-done.1.refs_0_), channel_id=1, source_target_pairs={{0,32},{32,64},{64,96},{96,128},{128,160},{160,192},{192,224},{224... | collective-permute-start | bytes 884744 | tf_op jit(solution)/shard_map/ppermute | solution.py:341
  46.3 19.7 %collective-permute-start.4 = (bf16[8,3,48,128]{3,2,1,0:T(8,128)(2,1)S(1)}, bf16[8,3,48,128]{3,2,1,0:T(8,128)(2,1)S(1)}, u32[]{:S(2)}, u32[]{:S(2)}) collective-permute-start(bf16[8,3,48,128]{3,2,1,0:T(8,128)(2,1)S(1)} %collective-permute-done.2.refs_1_), channel_id=1, source_target_pairs={{0,224},{32,0},{64,32},{96,64},{128,96},{160,128},{192,160},{224,1... | collective-permute-start | bytes 884744 | tf_op jit(solution)/shard_map/ppermute | solution.py:342
  62.4 15.4 %collective-permute-start.5 = (bf16[8,3,48,128]{3,2,1,0:T(8,128)(2,1)S(1)}, bf16[8,3,48,128]{3,2,1,0:T(8,128)(2,1)S(1)}, u32[]{:S(2)}, u32[]{:S(2)}) collective-permute-start(bf16[8,3,48,128]{3,2,1,0:T(8,128)(2,1)S(1)} %collective-permute-done.3.refs_0_), channel_id=1, source_target_pairs={{0,32},{32,64},{64,96},{96,128},{128,160},{160,192},{192,224},{224... | collective-permute-start | bytes 884744 | tf_op jit(solution)/shard_map/ppermute | solution.py:341
  66.0 12.2 %collective-permute-start.6 = (bf16[8,3,48,128]{3,2,1,0:T(8,128)(2,1)S(1)}, bf16[8,3,48,128]{3,2,1,0:T(8,128)(2,1)S(1)}, u32[]{:S(2)}, u32[]{:S(2)}) collective-permute-start(bf16[8,3,48,128]{3,2,1,0:T(8,128)(2,1)S(1)} %collective-permute-done.4.refs_1_), channel_id=1, source_target_pairs={{0,224},{32,0},{64,32},{96,64},{128,96},{160,128},{192,160},{224,1... | collective-permute-start | bytes 884744 | tf_op jit(solution)/shard_map/ppermute | solution.py:342
  78.3 19.1 %collective-permute-start.7 = (bf16[8,3,48,128]{3,2,1,0:T(8,128)(2,1)S(1)}, bf16[8,3,48,128]{3,2,1,0:T(8,128)(2,1)S(1)}, u32[]{:S(2)}, u32[]{:S(2)}) collective-permute-start(bf16[8,3,48,128]{3,2,1,0:T(8,128)(2,1)S(1)} %broadcast_select_fusion), channel_id=1, source_target_pairs={{0,32},{8,232},{32,64},{40,8},{64,96},{72,40},{96,128},{104,72},{1... | collective-permute-start | bytes 884744 | tf_op jit(solution)/shard_map/ppermute | solution.py:350
  91.5 27.9 %copy-start.7 = (f32[1,3,1536]{2,0,1:T(1,128)S(1)}, f32[1,3,1536]{2,0,1:T(1,128)}, u32[]{:S(2)}) copy-start(f32[1,3,1536]{2,0,1:T(1,128)} %param.14) | copy-start | bytes 55300
  91.6 27.9 %copy-start.8 = (f32[1536]{0:T(1024)S(1)}, f32[1536]{0:T(1024)}, u32[]{:S(2)}) copy-start(f32[1536]{0:T(1024)} %param.16) | copy-start | bytes 18436
  91.6 42.3 %copy-start.3 = (bf16[1536,64]{0,1:T(8,128)(2,1)S(1)}, bf16[1536,64]{0,1:T(8,128)(2,1)}, u32[]{:S(2)}) copy-start(bf16[1536,64]{0,1:T(8,128)(2,1)} %param.17) | copy-start | bytes 589828
  91.6 42.3 %copy-start.4 = (bf16[1,48,1536]{2,1,0:T(8,128)(2,1)S(1)}, bf16[1,48,1536]{2,1,0:T(8,128)(2,1)}, u32[]{:S(2)}) copy-start(bf16[1,48,1536]{2,1,0:T(8,128)(2,1)} %param.13) | copy-start | bytes 442372
  91.6 42.3 %copy-start.5 = (f32[64]{0:T(128)S(1)}, f32[64]{0:T(128)}, u32[]{:S(2)}) copy-start(f32[64]{0:T(128)} %param.18) | copy-start | bytes 772
  108.4 25.4 %all-to-all-start.1 = ((bf16[32,24,512]{2,1,0:T(8,128)(2,1)}), bf16[32,24,512]{2,1,0:T(8,128)(2,1)S(1)}, u32[]{:S(2)}, u32[]{:S(2)}) async-start(bf16[32,24,512]{2,1,0:T(8,128)(2,1)} %bitcast.8), calls=%async_computation.1 | async-start | bytes 1572864 | tf_op jit(solution)/shard_map/all_to_all | solution.py:356
  133.9 2.3 %copy-start.1 = (bf16[3072,768]{1,0:T(8,128)(2,1)S(1)}, bf16[3072,768]{1,0:T(8,128)(2,1)}, u32[]{:S(2)}) copy-start(bf16[3072,768]{1,0:T(8,128)(2,1)} %all-gather.2.cloned.1.call-done) | copy-start | bytes 14155780
  136.2 13.6 %copy-start.9 = (f32[1,1536]{1,0:T(1,128)S(1)}, f32[1,1536]{1,0:T(1,128)}, u32[]{:S(2)}) copy-start(f32[1,1536]{1,0:T(1,128)} %param.21) | copy-start | bytes 18436
  139.4 7.6 %collective-permute-start.8 = (f32[1536]{0:T(1024)S(1)}, f32[1536]{0:T(1024)S(1)}, u32[]{:S(2)}, u32[]{:S(2)}) collective-permute-start(f32[1536]{0:T(1024)S(1)} %get-tuple-element.2), channel_id=1, source_target_pairs={{0,1},{1,257},{2,3},{3,259},{256,0},{257,256},{258,2},{259,258},{4... | collective-permute-start | bytes 18440 | tf_op jit(solution)/shard_map/ppermute | solution.py:380
  142.7 6.4 %collective-permute-start.9 = (f32[1536]{0:T(1024)S(1)}, f32[1536]{0:T(1024)S(1)}, u32[]{:S(2)}, u32[]{:S(2)}) collective-permute-start(f32[1536]{0:T(1024)S(1)} %get-tuple-element.3), channel_id=1, source_target_pairs={{0,0},{1,256},{2,2},{3,258},{256,1},{257,257},{258,3},{259,259},{4... | collective-permute-start | bytes 18440 | tf_op jit(solution)/shard_map/ppermute | solution.py:379
Sparse Core Ops, SparseCore 0:
  11.4 75.1 all-gather.1

commit v2 on v1

--- a/solution.py
+++ b/solution.py
@@ -14,6 +14,9 @@
 LOG2_SCALE = math.log2(math.e) * HEAD_DIM**-0.5
 F32 = jnp.float32
 BF16 = jnp.bfloat16
+GUARD = HEAD_DIM + 3
+MARKS = 8
+SAFE = 2.0**100
 HEAD_AXES = ("zl", "y")
 BLOCK_AXES = ("zl", "core", "xh", "y")
 
@@ -52,11 +55,23 @@
     )(x)
 
 
+def wide_keys(block, valid=None):
+    lane = lane_index(block.shape)
+    ones = jnp.ones_like(block)
+    marked = jnp.where(lane < HEAD_DIM, block, ones)
+    if valid is not None:
+        row = lax.broadcasted_iota(jnp.int32, block.shape, 0)
+        marked = jnp.where((lane == GUARD) & (row >= valid), jnp.full_like(block, -1e30), marked)
+    return jnp.concatenate([block, marked], axis=1), jnp.where(lane < HEAD_DIM, ones, block)
+
+
 def queries_kernel(heads, place_ref, own_ref, other_ref, out_ref, wide_ref):
     here = place_ref[0]
     cores, sources, _, half, _ = own_ref.shape
     across = sources // 2
-    low = lane_index((half, LANES)) < HEAD_DIM
+    lane = lane_index((half, LANES))
+    low = lane < HEAD_DIM
+    guard = jnp.where(lane == GUARD, 1.0, 0.0)
     for side, ref in ((here, own_ref), (1 - here, other_ref)):
         for core in range(cores):
             for source in range(sources):
@@ -64,16 +79,17 @@
                 first = (zl * cores + core) * 2 * across + y
                 row = pl.multiple_of((first + side * across) * half, 8)
                 for head in range(heads):
-                    both = ref[core, source, head].astype(F32)
-                    turned = pltpu.roll(both, HEAD_DIM, 1)
-                    wide_ref[head, 0, pl.ds(row, half)] = jnp.where(low, both, 0.0)
-                    wide_ref[head, 1, pl.ds(row, half)] = jnp.where(low, turned, 0.0)
+                    both = ref[core, source, head].astype(F32) * LOG2_SCALE
+                    for part, value in enumerate((both, pltpu.roll(both, HEAD_DIM, 1))):
+                        lead = value.astype(BF16).astype(F32)
+                        wide_ref[head, part, pl.ds(row, half), 0:LANES] = jnp.where(low, lead, 0.0)
+                        wide_ref[head, part, pl.ds(row, half), LANES:] = jnp.where(low, value - lead, guard)
     out_ref[...] = wide_ref[...].astype(BF16)
 
 
 def unpack_queries(place, own, other):
     cores, sources, heads, half, _ = own.shape
-    shape = (heads, 2, 2 * cores * sources * half, LANES)
+    shape = (heads, 2, 2 * cores * sources * half, 2 * LANES)
     return pl.pallas_call(
         functools.partial(queries_kernel, heads),
         out_shape=jax.ShapeDtypeStruct(shape, BF16),
@@ -89,103 +105,109 @@
     )(place, own, other)
 
 
-def update(state, scores, values, flipped):
-    lane = lane_index((scores[0].shape[0], LANES))
-    largest = functools.reduce(jnp.maximum, [jnp.max(s, axis=1, keepdims=True) for s in scores])
-    if state is not None:
-        before = state[:, 32:33]
-        largest = jnp.maximum(largest, before)
-    offset = largest * LOG2_SCALE
-    total = None
-    for s, value, turn in zip(scores, values, flipped):
-        weights = jnp.exp2(s * LOG2_SCALE - offset).astype(BF16)
-        dims = (((1,), (1,)), ((), ())) if turn else (((1,), (0,)), ((), ()))
-        term = lax.dot_general(weights, value, dims, preferred_element_type=F32)
-        total = term if total is None else total + term
-    if state is not None:
-        total = total + state * jnp.exp2(before * LOG2_SCALE - offset)
-    return jnp.where((lane >= 32) & (lane < HEAD_DIM), largest, total)
-
-
-def split_block(ref, head):
+def rows_of(ref, head):
     sources, _, rows, lanes = ref.shape
-    block = ref[:, head].reshape(sources * rows, lanes)
-    ones = jnp.ones_like(block)
-    return block, jnp.where(lane_index(block.shape) < HEAD_DIM, ones, block)
-
-
-def scores_of(q, block):
-    return lax.dot_general(q, block, (((1,), (1,)), ((), ())), preferred_element_type=F32)
-
-
-def first_kernel(heads, cut, place_ref, q_ref, block_ref, text_ref, state_ref):
+    return ref[:, head].reshape(sources * rows, lanes)
+
+
+def scores_of(q, keys):
+    return lax.dot_general(q, keys, (((1,), (1,)), ((), ())), preferred_element_type=F32)
+
+
+def weighted(scores, values):
+    return jnp.dot(jnp.exp2(scores).astype(BF16), values, preferred_element_type=F32)
+
+
+def first_kernel(heads, valid_ref, q_ref, block_ref, text_ref, full_ref, state_ref):
     rows = 2 * q_ref.shape[2]
+    lane = lane_index((rows, LANES))
     for head in range(heads):
-        q = q_ref[head].reshape(rows, LANES)
-        block, values = split_block(block_ref, head)
-        state = update(None, [scores_of(q, block)], [values], [False])
+        q = q_ref[head].reshape(rows, 2 * LANES)
+        keys, values = wide_keys(rows_of(block_ref, head))
+        more_keys, more_values = wide_keys(text_ref[head], valid_ref[0])
+        scores = scores_of(q, jnp.concatenate([keys, more_keys], axis=0))
+        offset = jnp.max(scores, axis=1, keepdims=True)
+        state = weighted(scores - offset, jnp.concatenate([values, more_values], axis=0))
         state_ref[head] = state.reshape(state_ref.shape[1:])
-
-    def with_text(low, high, width):
-        for head in range(heads):
-            q = q_ref[head].reshape(rows, LANES)
-            state = state_ref[head].reshape(rows, LANES)
-            features = slice(head * HEAD_DIM, (head + 1) * HEAD_DIM)
-            keys = text_ref[0, features, low:high]
-            values = text_ref[1, features, low:high]
-            if width > high - low:
-                pad = jnp.zeros((HEAD_DIM, width - (high - low)), BF16)
-                keys = jnp.concatenate([keys, pad], axis=1)
-                values = jnp.concatenate([values, pad], axis=1)
-            stacked = jnp.concatenate([keys, values], axis=0)
-            counted = jnp.concatenate([jnp.ones_like(keys), values], axis=0)
-            scores = lax.dot_general(q, stacked, (((1,), (0,)), ((), ())), preferred_element_type=F32)
-            scores = jnp.where(lane_index(scores.shape) < high - low, scores, -jnp.inf)
-            state = update(state, [scores], [counted], [True])
-            state_ref[head] = state.reshape(state_ref.shape[1:])
-
-    count = text_ref.shape[2]
-
-    @pl.when(place_ref[0] == 0)
-    def _():
-        with_text(0, cut, cut)
-
-    @pl.when(place_ref[0] == 1)
-    def _():
-        with_text(cut, count, -(-(count - cut) // LANES) * LANES)
+        offset = jnp.broadcast_to(-offset, (rows, LANES))
+        coarse = offset.astype(BF16).astype(F32)
+        middle = (offset - coarse).astype(BF16).astype(F32)
+        upper = q[:, LANES:].astype(F32)
+        for place, term in enumerate((coarse, middle, offset - coarse - middle)):
+            upper = jnp.where(lane == HEAD_DIM + place, term, upper)
+        full_ref[head, :, :, :LANES] = q_ref[head, :, :, :LANES]
+        full_ref[head, :, :, LANES:] = upper.astype(BF16).reshape(state_ref.shape[1:])
 
 
 def next_kernel(heads, count, q_ref, state_ref, *refs):
     blocks, out_ref = refs[:count], refs[count]
     rows = 2 * q_ref.shape[2]
     for head in range(heads):
-        q = q_ref[head].reshape(rows, LANES)
-        pairs = [split_block(ref, head) for ref in blocks]
-        scores = [scores_of(q, block) for block, _ in pairs]
-        state = state_ref[head].reshape(rows, LANES)
-        state = update(state, scores, [values for _, values in pairs], [False] * count)
-        out_ref[head] = state.reshape(out_ref.shape[1:])
-
-
-def last_kernel(heads, q_ref, state_ref, block_ref, out_ref):
+        q = q_ref[head].reshape(rows, 2 * LANES)
+        keys, values = wide_keys(jnp.concatenate([rows_of(ref, head) for ref in blocks], axis=0))
+        state = weighted(scores_of(q, keys), values)
+        out_ref[head] = state_ref[head] + state.reshape(out_ref.shape[1:])
+
+
+def last_kernel(heads, count, valid_ref, q_ref, state_ref, block_ref, text_ref, *refs):
+    kept, out_ref, done_ref, top_ref, spare_ref, sem = refs[:count], *refs[count:]
     tile = q_ref.shape[2]
     rows = 2 * tile
     lane = lane_index((rows, LANES))
+    safe = True
+    for head in range(heads):
+        q = q_ref[head].reshape(rows, 2 * LANES)
+        keys, values = wide_keys(rows_of(block_ref, head))
+        state = weighted(scores_of(q, keys), values) + state_ref[head].reshape(rows, LANES)
+        done_ref[head] = state
+        top_ref[head] = q[:, LANES:].astype(F32)
+        largest = jnp.max(jnp.where(state[:, :HEAD_DIM] < SAFE, 0.0, 1.0))
+        safe = jnp.logical_and(safe, largest == 0.0)
+
+    @pl.when(jnp.logical_not(safe))
+    def _():
+        for at, ref in enumerate(kept):
+            copy = pltpu.make_async_copy(ref, spare_ref.at[at], sem)
+            copy.start()
+            copy.wait()
+        spare_ref[count] = block_ref[...]
+        for head in range(heads):
+            q = q_ref[head].reshape(rows, 2 * LANES)
+            spared = (lane >= HEAD_DIM) & (lane < GUARD)
+            plain = jnp.concatenate([q[:, :LANES], jnp.where(spared, jnp.zeros_like(q[:, LANES:]), q[:, LANES:])], axis=1)
+
+            def absorb(keys, values, largest, state):
+                scores = scores_of(plain, keys)
+                higher = jnp.maximum(largest, jnp.max(scores, axis=1, keepdims=True))
+                return higher, state * jnp.exp2(largest - higher) + weighted(scores - higher, values)
+
+            def step(at, carry):
+                return absorb(*wide_keys(spare_ref[at, :, head].reshape(-1, LANES)), *carry)
+
+            carry = (jnp.full((rows, 1), -1e30, F32), jnp.zeros((rows, LANES), F32))
+            carry = lax.fori_loop(0, count + 1, step, carry)
+            largest, state = absorb(*wide_keys(text_ref[head], valid_ref[0]), *carry)
+            done_ref[head] = state
+            offset = jnp.broadcast_to(-largest, (rows, LANES))
+            coarse = offset.astype(BF16).astype(F32)
+            middle = (offset - coarse).astype(BF16).astype(F32)
+            upper = jnp.zeros((rows, LANES), F32)
+            for place, term in enumerate((coarse, middle, offset - coarse - middle)):
+                upper = jnp.where(lane == HEAD_DIM + place, term, upper)
+            top_ref[head] = upper
+
+    marks = jnp.zeros((rows, LANES), F32)
     done = []
-    marks = jnp.zeros((rows, LANES), F32)
     for head in range(heads):
-        q = q_ref[head].reshape(rows, LANES)
-        block, values = split_block(block_ref, head)
-        state = state_ref[head].reshape(rows, LANES)
-        state = update(state, [scores_of(q, block)], [values], [False])
-        total = state[:, 0:1]
-        level = state[:, 32:33] * LOG2_SCALE + jnp.log2(total)
-        coarse = level.astype(BF16).astype(F32)
-        middle = (level - coarse).astype(BF16).astype(F32)
-        fine = level - coarse - middle
-        for place, part in enumerate((coarse, middle, fine)):
-            marks = jnp.where(lane == HEAD_DIM + 3 * head + place, part, marks)
+        state = done_ref[head]
+        total = pltpu.roll(state, HEAD_DIM, 1)
         done.append(state / total)
+        terms = top_ref[head] if head == 0 else pltpu.roll(top_ref[head], MARKS * head, 1)
+        place = HEAD_DIM + MARKS * head
+        lead = total.astype(BF16).astype(F32)
+        marks = jnp.where((lane >= place) & (lane < place + 3), terms, marks)
+        marks = jnp.where(lane == place + 3, lead, marks)
+        marks = jnp.where(lane == place + 4, total - lead, marks)
     low = lane < HEAD_DIM
     left = jnp.where(low, pltpu.roll(done[0], HEAD_DIM, 1), done[1]).astype(BF16)
     right = jnp.where(low, pltpu.roll(done[2], HEAD_DIM, 1), marks).astype(BF16)
@@ -195,46 +217,64 @@
         out_ref[:, (2 * half + 1) * LANES : (2 * half + 2) * LANES] = right[part]
 
 
-def attention_call(kernel, name, q, state, blocks, out, place=None, text=None):
+def attention_call(kernel, name, operands, whole, kept, out_shape, out_axes, scratch=()):
+    q = operands[-1] if len(operands[-1].shape) == 4 and operands[-1].dtype == BF16 else operands[-2]
     heads, _, rows, _ = q.shape
     tile = ROW_TILE if rows % ROW_TILE == 0 else rows
-    row_spec = pl.BlockSpec((heads, 2, tile, LANES), lambda i: (0, 0, i, 0))
-    whole = lambda x: pl.BlockSpec(x.shape, lambda i: (0,) * x.ndim)
-    operands, specs = [], []
-    if place is not None:
-        operands.append(place)
-        specs.append(pl.BlockSpec(memory_space=pltpu.SMEM))
-    operands.append(q)
-    specs.append(row_spec)
-    if state is not None:
-        operands.append(state)
-        specs.append(row_spec)
-    for block in blocks:
-        operands.append(block)
-        specs.append(whole(block))
-    if text is not None:
-        operands.append(text)
-        specs.append(whole(text))
-    keys = sum(b.shape[0] * b.shape[2] for b in blocks)
+
+    def tiled(shape, axis):
+        block = tuple(tile if d == axis else n for d, n in enumerate(shape))
+        return pl.BlockSpec(block, lambda i: tuple(i if d == axis else 0 for d in range(len(shape))))
+
+    specs = []
+    for x in operands:
+        specs.append(tiled(x.shape, 2) if x.ndim == 4 else pl.BlockSpec(memory_space=pltpu.SMEM))
+    for x in whole:
+        specs.append(pl.BlockSpec(x.shape, lambda i, n=x.ndim: (0,) * n))
+    specs += [pl.BlockSpec(memory_space=pl.ANY)] * len(kept)
+    keys = sum(x.shape[0] * x.shape[2] if x.ndim == 4 else x.shape[1] for x in whole)
     pairs = heads * 2 * rows * keys
-    if out == "state":
-        shape = jax.ShapeDtypeStruct(q.shape, F32)
-        out_spec = row_spec
-    else:
-        shape = jax.ShapeDtypeStruct((rows, 4 * LANES), BF16)
-        out_spec = pl.BlockSpec((tile, 4 * LANES), lambda i: (i, 0))
+    out_specs = [tiled(s.shape, a) for s, a in zip(out_shape, out_axes)]
     return pl.pallas_call(
         kernel,
         grid=(rows // tile,),
-        out_shape=shape,
+        out_shape=out_shape,
         in_specs=specs,
-        out_specs=out_spec,
+        out_specs=out_specs,
+        scratch_shapes=scratch,
         compiler_params=params(),
-        cost_estimate=pl.CostEstimate(
-            flops=pairs * 4 * LANES * 2, bytes_accessed=2 * q.size * 4, transcendentals=pairs
-        ),
+        cost_estimate=pl.CostEstimate(flops=pairs * 6 * LANES, bytes_accessed=4 * q.size, transcendentals=pairs),
         name=name,
-    )(*operands)
+    )(*operands, *whole, *kept)
+
+
+def state_shape(q):
+    return jax.ShapeDtypeStruct(q.shape[:3] + (LANES,), F32)
+
+
+def first_block(valid, q, block, text):
+    shapes = [jax.ShapeDtypeStruct(q.shape, BF16), state_shape(q)]
+    kernel = functools.partial(first_kernel, q.shape[0])
+    return attention_call(kernel, "own_block", [valid, q], [block, text], [], shapes, [2, 2])
+
+
+def next_blocks(q, state, blocks):
+    kernel = functools.partial(next_kernel, q.shape[0], len(blocks))
+    return attention_call(kernel, "next_blocks", [q, state], blocks, [], [state_shape(q)], [2])[0]
+
+
+def last_block(valid, q, state, block, text, kept):
+    heads, _, rows, _ = q.shape
+    tile = ROW_TILE if rows % ROW_TILE == 0 else rows
+    kernel = functools.partial(last_kernel, heads, len(kept))
+    shape = jax.ShapeDtypeStruct((rows, 4 * LANES), BF16)
+    scratch = [
+        pltpu.VMEM((heads, 2 * tile, LANES), F32),
+        pltpu.VMEM((heads, 2 * tile, LANES), F32),
+        pltpu.VMEM((len(kept) + 1,) + block.shape, BF16),
+        pltpu.SemaphoreType.DMA,
+    ]
+    return attention_call(kernel, "last_block", [valid, q, state], [block, text], kept, [shape], [0], scratch)[0]
 
 
 def finish_kernel(
@@ -253,14 +293,15 @@
             members = [(zl * copies + copy) * across + y for copy in range(copies)]
             left = [partial_ref[m, :, at : at + LANES].astype(F32) for m in members]
             right = [partial_ref[m, :, at + LANES : at + 2 * LANES].astype(F32) for m in members]
-            levels = [r + pltpu.roll(r, LANES - 1, 1) + pltpu.roll(r, LANES - 2, 1) for r in right]
+            levels = [-(r + pltpu.roll(r, LANES - 1, 1) + pltpu.roll(r, LANES - 2, 1)) for r in right]
+            counts = [pltpu.roll(r, LANES - 3, 1) + pltpu.roll(r, LANES - 4, 1) for r in right]
             top = functools.reduce(jnp.maximum, levels)
-            shares = [jnp.exp2(level - top) for level in levels]
+            shares = [count * jnp.exp2(level - top) for count, level in zip(counts, levels)]
             total = functools.reduce(jnp.add, shares)
             first, second = 0.0, 0.0
             for copy in range(copies):
                 share = shares[copy] / total
-                h0, h1, h2 = [share[:, HEAD_DIM + 3 * h : HEAD_DIM + 3 * h + 1] for h in range(3)]
+                h0, h1, h2 = [share[:, c : c + 1] for c in (HEAD_DIM, HEAD_DIM + MARKS, HEAD_DIM + 2 * MARKS)]
                 first = first + left[copy] * jnp.where(low, h0, h1)
                 second = second + right[copy] * h2
             both = jnp.concatenate([first, second[:, :HEAD_DIM]], axis=1)
@@ -331,27 +372,26 @@
     q = unpack_queries(xh.reshape(1), packed, opposite)
 
     count = text_kv.shape[1]
-    cut = min(2 * LANES, count)
-    has_text = jnp.where(xh == zl, core, 2).reshape(1)
-    text = text_kv[0].transpose(1, 2, 0)
-    state = attention_call(
-        functools.partial(first_kernel, heads, cut), "own_block", q, None, [own], "state", has_text, text
-    )
+    share = -(-count // 32) * 16
+    text = text_kv[0].reshape(count, 2, heads, HEAD_DIM).transpose(2, 0, 1, 3).reshape(heads, count, LANES)
+    text = jnp.pad(text, ((0, 0), (0, 2 * share - count), (0, 0)))
+    text = lax.dynamic_slice_in_dim(text, core * share, share, 1)
+    valid = jnp.where(xh == zl, jnp.minimum(count - core * share, share), 0).reshape(1)
+    q, state = first_block(valid, q, own, text)
+    kept = [own]
     for _ in range(ring // 2 - 2):
         further_right = lax.ppermute(right, "zh", up)
         further_left = lax.ppermute(left, "zh", down)
-        state = attention_call(
-            functools.partial(next_kernel, heads, 2), "two_blocks", q, state, [right, left], "state"
-        )
+        state = next_blocks(q, state, [right, left])
+        kept += [right, left]
         right, left = further_right, further_left
+    kept += [right, left]
     route = []
     for i in range(ring):
         route += [(2 * i, 2 * ((i + 1) % ring)), (2 * i + 1, 2 * ((i - 1) % ring) + 1)]
     farthest = lax.ppermute(jnp.where(core == 0, right, left), ("zh", "core"), route)
-    state = attention_call(
-        functools.partial(next_kernel, heads, 2), "two_blocks", q, state, [right, left], "state"
-    )
-    partial = attention_call(functools.partial(last_kernel, heads), "last_block", q, state, [farthest], "partial")
+    state = next_blocks(q, state, [right, left])
+    partial = last_block(valid, q, state, farthest, text, kept)
     partial = partial.reshape(4 * groups, half, 4 * LANES)
     partial = lax.all_to_all(partial, BLOCK_AXES, split_axis=0, concat_axis=0, tiled=True)
 

time: 158 us -> 168 us (1.063)
  the two profiles are of different devices: /device:TPU:98 before, /device:TPU:34 now
where the time goes in v2:
time: 168 us; the launch traced here: 167 us
  Pallas kernels  50.5 us (30%)
  starting transfers between devices  46.9 us (28%)
  waiting for transfers between devices  31.2 us (19%)
  between operations  15.7 us (9%)
  blocking collectives  15.5 us (9%)
  local copies, waits for them, and re-layouts  6.35 us (4%)
    pallas_call x5, Pallas kernels, attention_call(): pl.pallas_call(kernel, grid=(rows // tile,), out_shape=out_shape, in_spec...  46.2 us
    all_to_all x1, waiting for transfers between devices, local(): lax.all_to_all(partial, BLOCK_AXES, split_axis=0, concat_axis=0, tiled=True)  14.3 us
    all_to_all x1, blocking collectives, local(): lax.all_to_all(slabs, HEAD_AXES, split_axis=0, concat_axis=0, tiled=True)  13.5 us
    ppermute x2, starting transfers between devices, local(): right, left = (lax.ppermute(own, 'zh', up), lax.ppermute(own, 'zh', down))  12.9 us
    ppermute x2, starting transfers between devices, local(): further_left = lax.ppermute(left, 'zh', down)  12.6 us
    ppermute x2, waiting for transfers between devices, local(): further_right = lax.ppermute(right, 'zh', up)  6.54 us
    all_to_all x1, starting transfers between devices, local(): lax.all_to_all(partial, BLOCK_AXES, split_axis=0, concat_axis=0, tiled=True)  5.16 us
    ppermute x2, waiting for transfers between devices, local(): right, left = (lax.ppermute(own, 'zh', up), lax.ppermute(own, 'zh', down))  4.41 us
  transfers between devices with their start and end apart: 12, of which 7 were waited for; matrix products, arithmetic and copies ran while one was open for 0% of the time, Pallas kernels for 28%

profile of v2, /device:TPU:34, one launch (start us, length us, event | category | flops | bytes accessed | tf_op | source)
XLA Modules:
  0.0 166.9 jit_solution(16169117774858631992)
XLA Ops:
  7.2 1.0 copy-done
  8.2 0.7 constant_dynamic-slice_fusion
  9.0 1.0 copy-done.2
  10.2 13.5 %all_to_all.10 = bf16[8,216,128]{2,1,0:T(8,128)(2,1)S(1)} all-to-all(bf16[8,216,128]{2,1,0:T(8,128)(2,1)S(1)} %pack_heads.1), channel_id=1, replica_groups=mesh['cfg'=2,'zh'=8,'zl'=2,'core'=2,'xh'=2,'y'=4] {'zl','y'}, dimensions={0} | all-to-all | bytes 884736 | tf_op jit(solution)/shard_map/all_to_all | solution.py:363
  23.7 5.2 %collective-permute-start.1 = (bf16[8,3,48,128]{3,2,1,0:T(8,128)(2,1)S(1)}, bf16[8,3,48,128]{3,2,1,0:T(8,128)(2,1)S(1)}, u32[]{:S(2)}, u32[]{:S(2)}) collective-permute-start(bf16[8,3,48,128]{3,2,1,0:T(8,128)(2,1)S(1)} %bitcast.27), channel_id=1, source_target_pairs={{0,32},{32,64},{64,96},{96,128},{128,160},{160,192},{192,224},{224... | collective-permute-start | bytes 884744 | tf_op jit(solution)/shard_map/ppermute | solution.py:367
  28.9 7.7 %collective-permute-start.2 = (bf16[8,3,48,128]{3,2,1,0:T(8,128)(2,1)S(1)}, bf16[8,3,48,128]{3,2,1,0:T(8,128)(2,1)S(1)}, u32[]{:S(2)}, u32[]{:S(2)}) collective-permute-start(bf16[8,3,48,128]{3,2,1,0:T(8,128)(2,1)S(1)} %bitcast.28), channel_id=1, source_target_pairs={{0,224},{32,0},{64,32},{96,64},{128,96},{160,128},{192,160},{224,1... | collective-permute-start | bytes 884744 | tf_op jit(solution)/shard_map/ppermute | solution.py:367
  36.7 2.0 %all_gather.6.own_ref = bf16[2,8,3,24,128]{4,3,2,1,0:T(8,128)(2,1)S(1)} all-gather(bf16[1,8,3,24,128]{4,3,2,1,0:T(8,128)(2,1)S(1)} %bitcast.37), channel_id=1, replica_groups=mesh['cfg'=2,'zh'=8,'zl'=2,'core'=2,'xh'=2,'y'=4] {'core'}, dimensions={0}, use_global_device_ids=true | all-gather | bytes 442368 | tf_op jit(solution)/shard_map/all_gather | solution.py:370
  38.7 4.0 %collective-permute-start = (bf16[2,8,3,24,128]{4,3,2,1,0:T(8,128)(2,1)S(1)}, bf16[2,8,3,24,128]{4,3,2,1,0:T(8,128)(2,1)S(1)}, u32[]{:S(2)}, u32[]{:S(2)}) collective-permute-start(bf16[2,8,3,24,128]{4,3,2,1,0:T(8,128)(2,1)S(1)} %all_gather.6.own_ref), channel_id=1, source_target_pairs={{0,4},{4,0},{1,5},{5,1},{2,6},{6,2},{3,7},{7,3},{8,12},{12,8},{9,1... | collective-permute-start | bytes 884744 | tf_op jit(solution)/shard_map/ppermute | solution.py:371
  42.7 4.4 %collective-permute-done.1.refs_0_.refs_1_ = bf16[8,3,48,128]{3,2,1,0:T(8,128)(2,1)S(1)} collective-permute-done((bf16[8,3,48,128]{3,2,1,0:T(8,128)(2,1)S(1)}, bf16[8,3,48,128]{3,2,1,0:T(8,128)(2,1)S(1)}, u32[]{:S(2)}, u32[]{:S(2)}) %collective-permute-start.1) | collective-permute-done | bytes 294944 | tf_op jit(solution)/shard_map/ppermute | solution.py:367
  47.1 1.9 %collective-permute-start.3 = (bf16[8,3,48,128]{3,2,1,0:T(8,128)(2,1)S(1)}, bf16[8,3,48,128]{3,2,1,0:T(8,128)(2,1)S(1)}, u32[]{:S(2)}, u32[]{:S(2)}) collective-permute-start(bf16[8,3,48,128]{3,2,1,0:T(8,128)(2,1)S(1)} %collective-permute-done.1.refs_0_.refs_1_), channel_id=1, source_target_pairs={{0,32},{32,64},{64,96},{96,128},{128,160},{160,192},{192,224},{224... | collective-permute-start | bytes 884744 | tf_op jit(solution)/shard_map/ppermute | solution.py:383
  49.0 6.0 %collective-permute-start.4 = (bf16[8,3,48,128]{3,2,1,0:T(8,128)(2,1)S(1)}, bf16[8,3,48,128]{3,2,1,0:T(8,128)(2,1)S(1)}, u32[]{:S(2)}, u32[]{:S(2)}) collective-permute-start(bf16[8,3,48,128]{3,2,1,0:T(8,128)(2,1)S(1)} %collective-permute-done.2.refs_1_.refs_2_), channel_id=1, source_target_pairs={{0,224},{32,0},{64,32},{96,64},{128,96},{160,128},{192,160},{224,1... | collective-permute-start | bytes 884744 | tf_op jit(solution)/shard_map/ppermute | solution.py:384
  55.4 0.8 unpack_queries.1.q_ref
  56.2 6.5 %collective-permute-done.3.refs_0_.refs_3_ = bf16[8,3,48,128]{3,2,1,0:T(8,128)(2,1)S(1)} collective-permute-done((bf16[8,3,48,128]{3,2,1,0:T(8,128)(2,1)S(1)}, bf16[8,3,48,128]{3,2,1,0:T(8,128)(2,1)S(1)}, u32[]{:S(2)}, u32[]{:S(2)}) %collective-permute-start.3) | collective-permute-done | bytes 294944 | tf_op jit(solution)/shard_map/ppermute | solution.py:383
  62.8 1.9 %collective-permute-start.5 = (bf16[8,3,48,128]{3,2,1,0:T(8,128)(2,1)S(1)}, bf16[8,3,48,128]{3,2,1,0:T(8,128)(2,1)S(1)}, u32[]{:S(2)}, u32[]{:S(2)}) collective-permute-start(bf16[8,3,48,128]{3,2,1,0:T(8,128)(2,1)S(1)} %collective-permute-done.3.refs_0_.refs_3_), channel_id=1, source_target_pairs={{0,32},{32,64},{64,96},{96,128},{128,160},{160,192},{192,224},{224... | collective-permute-start | bytes 884744 | tf_op jit(solution)/shard_map/ppermute | solution.py:383
  64.9 6.6 %collective-permute-start.6 = (bf16[8,3,48,128]{3,2,1,0:T(8,128)(2,1)S(1)}, bf16[8,3,48,128]{3,2,1,0:T(8,128)(2,1)S(1)}, u32[]{:S(2)}, u32[]{:S(2)}) collective-permute-start(bf16[8,3,48,128]{3,2,1,0:T(8,128)(2,1)S(1)} %collective-permute-done.4.refs_1_.refs_4_), channel_id=1, source_target_pairs={{0,224},{32,0},{64,32},{96,64},{128,96},{160,128},{192,160},{224,1... | collective-permute-start | bytes 884744 | tf_op jit(solution)/shard_map/ppermute | solution.py:384
  71.5 6.3 %own_block.1 = (bf16[3,2,768,256]{3,2,1,0:T(8,128)(2,1)S(1)}, f32[3,2,768,128]{3,2,1,0:T(8,128)S(1)}) custom-call(s32[1]{0:T(128)} %bitcast.valid_ref, bf16[3,2,768,256]{3,2,1,0:T(8,128)(2,1)S(1)} %unpack_queries.1.q_ref, bf16[8,3,48,128]{3,2,1,0:T(8,128)(2,1)S(1)} %bitcast.29, bf16[3,176,128]{2,1,0:T(8,128)(2,1)S(1)} %pad_dynamic-slice_fusion.text_ref), custom_call_target="tpu_custom_call" | custom-call | flops 1981808640 | bytes 4718592 | tf_op jit(solution)/shard_map/own_block/pallas_call | solution.py:238
  77.9 4.8 %next_blocks.3.state_ref = f32[3,2,768,128]{3,2,1,0:T(8,128)S(1)} custom-call(bf16[3,2,768,256]{3,2,1,0:T(8,128)(2,1)S(1)} %get-tuple-element.4.q_ref, f32[3,2,768,128]{3,2,1,0:T(8,128)S(1)} %get-tuple-element.5.state_ref, bf16[8,3,48,128]{3,2,1,0:T(8,128)(2,1)S(1)} %collective-permute-done.1.refs_0_.refs_1_, ...), custom_call_target="tpu_custom_call" | custom-call | flops 2717908992 | bytes 4718592 | tf_op jit(solution)/shard_map/next_blocks/pallas_call | solution.py:238
  82.7 0.4 collective-permute-done.6.refs_1_.refs_6_
  83.1 2.1 %collective-permute-start.7 = (bf16[8,3,48,128]{3,2,1,0:T(8,128)(2,1)S(1)}, bf16[8,3,48,128]{3,2,1,0:T(8,128)(2,1)S(1)}, u32[]{:S(2)}, u32[]{:S(2)}) collective-permute-start(bf16[8,3,48,128]{3,2,1,0:T(8,128)(2,1)S(1)} %broadcast_select_fusion), channel_id=1, source_target_pairs={{0,32},{8,232},{32,64},{40,8},{64,96},{72,40},{96,128},{104,72},{1... | collective-permute-start | bytes 884744 | tf_op jit(solution)/shard_map/ppermute | solution.py:392
  85.2 4.8 %next_blocks.4.state_ref = f32[3,2,768,128]{3,2,1,0:T(8,128)S(1)} custom-call(bf16[3,2,768,256]{3,2,1,0:T(8,128)(2,1)S(1)} %get-tuple-element.4.q_ref, f32[3,2,768,128]{3,2,1,0:T(8,128)S(1)} %next_blocks.3.state_ref, bf16[8,3,48,128]{3,2,1,0:T(8,128)(2,1)S(1)} %collective-permute-done.3.refs_0_.refs_3_, ...), custom_call_target="tpu_custom_call" | custom-call | flops 2717908992 | bytes 4718592 | tf_op jit(solution)/shard_map/next_blocks/pallas_call | solution.py:238
  90.0 4.8 %next_blocks.5.state_ref = f32[3,2,768,128]{3,2,1,0:T(8,128)S(1)} custom-call(bf16[3,2,768,256]{3,2,1,0:T(8,128)(2,1)S(1)} %get-tuple-element.4.q_ref, f32[3,2,768,128]{3,2,1,0:T(8,128)S(1)} %next_blocks.4.state_ref, bf16[8,3,48,128]{3,2,1,0:T(8,128)(2,1)S(1)} %collective-permute-done.5.refs_0_.refs_5_, ...), custom_call_target="tpu_custom_call" | custom-call | flops 2717908992 | bytes 4718592 | tf_op jit(solution)/shard_map/next_blocks/pallas_call | solution.py:238
  94.9 2.5 %collective-permute-done.7.block_ref = bf16[8,3,48,128]{3,2,1,0:T(8,128)(2,1)S(1)} collective-permute-done((bf16[8,3,48,128]{3,2,1,0:T(8,128)(2,1)S(1)}, bf16[8,3,48,128]{3,2,1,0:T(8,128)(2,1)S(1)}, u32[]{:S(2)}, u32[]{:S(2)}) %collective-permute-start.7) | collective-permute-done | bytes 294944 | tf_op jit(solution)/shard_map/ppermute | solution.py:392
  97.4 25.4 %last_block.1 = bf16[768,512]{1,0:T(8,128)(2,1)} custom-call(s32[1]{0:T(128)} %bitcast.valid_ref, bf16[3,2,768,256]{3,2,1,0:T(8,128)(2,1)S(1)} %get-tuple-element.4.q_ref, f32[3,2,768,128]{3,2,1,0:T(8,128)S(1)} %next_blocks.5.state_ref, bf16[8,3,48,128]{3,2,1,0:T(8,128)(2,1)S(1)} %collective-permute-done.7.block_ref, ...), custom_call_target="tpu_custom_call" | custom-call | flops 1981808640 | bytes 4718592 | tf_op jit(solution)/shard_map/last_block/pallas_call | solution.py:238
  122.8 5.2 %all-to-all-start.1 = ((bf16[32,24,512]{2,1,0:T(8,128)(2,1)}), bf16[32,24,512]{2,1,0:T(8,128)(2,1)S(1)}, u32[]{:S(2)}, u32[]{:S(2)}) async-start(bf16[32,24,512]{2,1,0:T(8,128)(2,1)} %bitcast.9), calls=%async_computation.1 | async-start | bytes 1572864 | tf_op jit(solution)/shard_map/all_to_all | solution.py:396
  128.0 14.3 %all-to-all-done.1.partial_ref = bf16[32,24,512]{2,1,0:T(8,128)(2,1)S(1)} async-done(((bf16[32,24,512]{2,1,0:T(8,128)(2,1)}), bf16[32,24,512]{2,1,0:T(8,128)(2,1)S(1)}, u32[]{:S(2)}, u32[]{:S(2)}) %all-to-all-start.1) | async-done | bytes 786464 | tf_op jit(solution)/shard_map/all_to_all | solution.py:396
  142.4 2.3 %copy-done.1 = bf16[3072,768]{1,0:T(8,128)(2,1)S(1)} copy-done((bf16[3072,768]{1,0:T(8,128)(2,1)S(1)}, bf16[3072,768]{1,0:T(8,128)(2,1)}, u32[]{:S(2)}) %copy-start.1) | copy-done | bytes 4718616
  144.7 3.3 %project_and_norm.1 = f32[48,64]{1,0:T(8,128)S(1)} custom-call(bf16[32,24,512]{2,1,0:T(8,128)(2,1)S(1)} %all-to-all-done.1.partial_ref, bf16[2,1536,768]{2,1,0:T(8,128)(2,1)S(1)} %bitcast.26, bf16[48,1536]{1,0:T(8,128)(2,1)S(1)} %bitcast.33, f32[3,1536]{1,0:T(4,128)S(1)} %bitcast.34, f32[1,1536]{1,0:T(1,128)S(1)} %broadcast_in_dim.6.bias_ref, ...), custom_call_target="tpu_custom_call" | custom-call | tf_op jit(solution)/shard_map/project_and_norm/pallas_call | solution.py:327
  148.4 4.0 %collective-permute-start.8 = (f32[1536]{0:T(1024)S(1)}, f32[1536]{0:T(1024)S(1)}, u32[]{:S(2)}, u32[]{:S(2)}) collective-permute-start(f32[1536]{0:T(1024)S(1)} %get-tuple-element.6), channel_id=1, source_target_pairs={{0,1},{1,257},{2,3},{3,259},{256,0},{257,256},{258,2},{259,258},{4... | collective-permute-start | bytes 18440 | tf_op jit(solution)/shard_map/ppermute | solution.py:420
  152.4 2.3 %collective-permute-start.9 = (f32[1536]{0:T(1024)S(1)}, f32[1536]{0:T(1024)S(1)}, u32[]{:S(2)}, u32[]{:S(2)}) collective-permute-start(f32[1536]{0:T(1024)S(1)} %get-tuple-element.7), channel_id=1, source_target_pairs={{0,0},{1,256},{2,2},{3,258},{256,1},{257,257},{258,3},{259,259},{4... | collective-permute-start | bytes 18440 | tf_op jit(solution)/shard_map/ppermute | solution.py:419
  156.1 2.8 %collective-permute-done.9 = f32[1536]{0:T(1024)S(1)} collective-permute-done((f32[1536]{0:T(1024)S(1)}, f32[1536]{0:T(1024)S(1)}, u32[]{:S(2)}, u32[]{:S(2)}) %collective-permute-start.9) | collective-permute-done | bytes 6176 | tf_op jit(solution)/shard_map/ppermute | solution.py:419
  158.9 0.6 reshape.40
  159.5 0.6 reshape_subtract_fusion
  (39 shorter events, 1.2 us)
Async XLA Ops:
  7.2 1.1 copy-start
  7.2 47.9 %copy-start.6 = (bf16[1,333,2,192]{1,3,2,0:T(8,128)(2,1)S(1)}, bf16[1,333,2,192]{1,3,2,0:T(8,128)(2,1)}, u32[]{:S(2)}) copy-start(bf16[1,333,2,192]{1,3,2,0:T(8,128)(2,1)} %param.12) | copy-start | bytes 767236
  7.2 135.2 %all-gather.2.cloned.1.call-start = ((), (), s32[]{:S(2)}) async-start(), calls=%async_computation.2 | async-start | bytes 5013504 | tf_op jit(solution)/shard_map/all_gather | solution.py:359
  9.0 1.0 copy-start.2
  23.7 23.4 %collective-permute-start.1 = (bf16[8,3,48,128]{3,2,1,0:T(8,128)(2,1)S(1)}, bf16[8,3,48,128]{3,2,1,0:T(8,128)(2,1)S(1)}, u32[]{:S(2)}, u32[]{:S(2)}) collective-permute-start(bf16[8,3,48,128]{3,2,1,0:T(8,128)(2,1)S(1)} %bitcast.27), channel_id=1, source_target_pairs={{0,32},{32,64},{64,96},{96,128},{128,160},{160,192},{192,224},{224... | collective-permute-start | bytes 884744 | tf_op jit(solution)/shard_map/ppermute | solution.py:367
  28.9 20.1 %collective-permute-start.2 = (bf16[8,3,48,128]{3,2,1,0:T(8,128)(2,1)S(1)}, bf16[8,3,48,128]{3,2,1,0:T(8,128)(2,1)S(1)}, u32[]{:S(2)}, u32[]{:S(2)}) collective-permute-start(bf16[8,3,48,128]{3,2,1,0:T(8,128)(2,1)S(1)} %bitcast.28), channel_id=1, source_target_pairs={{0,224},{32,0},{64,32},{96,64},{128,96},{160,128},{192,160},{224,1... | collective-permute-start | bytes 884744 | tf_op jit(solution)/shard_map/ppermute | solution.py:367
  38.7 16.7 %collective-permute-start = (bf16[2,8,3,24,128]{4,3,2,1,0:T(8,128)(2,1)S(1)}, bf16[2,8,3,24,128]{4,3,2,1,0:T(8,128)(2,1)S(1)}, u32[]{:S(2)}, u32[]{:S(2)}) collective-permute-start(bf16[2,8,3,24,128]{4,3,2,1,0:T(8,128)(2,1)S(1)} %all_gather.6.own_ref), channel_id=1, source_target_pairs={{0,4},{4,0},{1,5},{5,1},{2,6},{6,2},{3,7},{7,3},{8,12},{12,8},{9,1... | collective-permute-start | bytes 884744 | tf_op jit(solution)/shard_map/ppermute | solution.py:371
  47.1 15.7 %collective-permute-start.3 = (bf16[8,3,48,128]{3,2,1,0:T(8,128)(2,1)S(1)}, bf16[8,3,48,128]{3,2,1,0:T(8,128)(2,1)S(1)}, u32[]{:S(2)}, u32[]{:S(2)}) collective-permute-start(bf16[8,3,48,128]{3,2,1,0:T(8,128)(2,1)S(1)} %collective-permute-done.1.refs_0_.refs_1_), channel_id=1, source_target_pairs={{0,32},{32,64},{64,96},{96,128},{128,160},{160,192},{192,224},{224... | collective-permute-start | bytes 884744 | tf_op jit(solution)/shard_map/ppermute | solution.py:383
  49.0 15.9 %collective-permute-start.4 = (bf16[8,3,48,128]{3,2,1,0:T(8,128)(2,1)S(1)}, bf16[8,3,48,128]{3,2,1,0:T(8,128)(2,1)S(1)}, u32[]{:S(2)}, u32[]{:S(2)}) collective-permute-start(bf16[8,3,48,128]{3,2,1,0:T(8,128)(2,1)S(1)} %collective-permute-done.2.refs_1_.refs_2_), channel_id=1, source_target_pairs={{0,224},{32,0},{64,32},{96,64},{128,96},{160,128},{192,160},{224,1... | collective-permute-start | bytes 884744 | tf_op jit(solution)/shard_map/ppermute | solution.py:384
  62.8 19.9 %collective-permute-start.5 = (bf16[8,3,48,128]{3,2,1,0:T(8,128)(2,1)S(1)}, bf16[8,3,48,128]{3,2,1,0:T(8,128)(2,1)S(1)}, u32[]{:S(2)}, u32[]{:S(2)}) collective-permute-start(bf16[8,3,48,128]{3,2,1,0:T(8,128)(2,1)S(1)} %collective-permute-done.3.refs_0_.refs_3_), channel_id=1, source_target_pairs={{0,32},{32,64},{64,96},{96,128},{128,160},{160,192},{192,224},{224... | collective-permute-start | bytes 884744 | tf_op jit(solution)/shard_map/ppermute | solution.py:383
  64.9 18.1 %collective-permute-start.6 = (bf16[8,3,48,128]{3,2,1,0:T(8,128)(2,1)S(1)}, bf16[8,3,48,128]{3,2,1,0:T(8,128)(2,1)S(1)}, u32[]{:S(2)}, u32[]{:S(2)}) collective-permute-start(bf16[8,3,48,128]{3,2,1,0:T(8,128)(2,1)S(1)} %collective-permute-done.4.refs_1_.refs_4_), channel_id=1, source_target_pairs={{0,224},{32,0},{64,32},{96,64},{128,96},{160,128},{192,160},{224,1... | collective-permute-start | bytes 884744 | tf_op jit(solution)/shard_map/ppermute | solution.py:384
  83.1 14.4 %collective-permute-start.7 = (bf16[8,3,48,128]{3,2,1,0:T(8,128)(2,1)S(1)}, bf16[8,3,48,128]{3,2,1,0:T(8,128)(2,1)S(1)}, u32[]{:S(2)}, u32[]{:S(2)}) collective-permute-start(bf16[8,3,48,128]{3,2,1,0:T(8,128)(2,1)S(1)} %broadcast_select_fusion), channel_id=1, source_target_pairs={{0,32},{8,232},{32,64},{40,8},{64,96},{72,40},{96,128},{104,72},{1... | collective-permute-start | bytes 884744 | tf_op jit(solution)/shard_map/ppermute | solution.py:392
  94.8 33.2 %copy-start.7 = (f32[1,3,1536]{2,0,1:T(1,128)S(1)}, f32[1,3,1536]{2,0,1:T(1,128)}, u32[]{:S(2)}) copy-start(f32[1,3,1536]{2,0,1:T(1,128)} %param.14) | copy-start | bytes 55300
  94.8 33.2 %copy-start.8 = (f32[1536]{0:T(1024)S(1)}, f32[1536]{0:T(1024)}, u32[]{:S(2)}) copy-start(f32[1536]{0:T(1024)} %param.16) | copy-start | bytes 18436
  94.8 47.5 %copy-start.3 = (bf16[1536,64]{0,1:T(8,128)(2,1)S(1)}, bf16[1536,64]{0,1:T(8,128)(2,1)}, u32[]{:S(2)}) copy-start(bf16[1536,64]{0,1:T(8,128)(2,1)} %param.17) | copy-start | bytes 589828
  94.9 47.5 %copy-start.4 = (bf16[1,48,1536]{2,1,0:T(8,128)(2,1)S(1)}, bf16[1,48,1536]{2,1,0:T(8,128)(2,1)}, u32[]{:S(2)}) copy-start(bf16[1,48,1536]{2,1,0:T(8,128)(2,1)} %param.13) | copy-start | bytes 442372
  94.9 47.5 %copy-start.5 = (f32[64]{0:T(128)S(1)}, f32[64]{0:T(128)}, u32[]{:S(2)}) copy-start(f32[64]{0:T(128)} %param.18) | copy-start | bytes 772
  122.8 19.6 %all-to-all-start.1 = ((bf16[32,24,512]{2,1,0:T(8,128)(2,1)}), bf16[32,24,512]{2,1,0:T(8,128)(2,1)S(1)}, u32[]{:S(2)}, u32[]{:S(2)}) async-start(bf16[32,24,512]{2,1,0:T(8,128)(2,1)} %bitcast.9), calls=%async_computation.1 | async-start | bytes 1572864 | tf_op jit(solution)/shard_map/all_to_all | solution.py:396
  142.4 2.3 %copy-start.1 = (bf16[3072,768]{1,0:T(8,128)(2,1)S(1)}, bf16[3072,768]{1,0:T(8,128)(2,1)}, u32[]{:S(2)}) copy-start(bf16[3072,768]{1,0:T(8,128)(2,1)} %all-gather.2.cloned.1.call-done) | copy-start | bytes 14155780
  144.7 14.7 %copy-start.9 = (f32[1,1536]{1,0:T(1,128)S(1)}, f32[1,1536]{1,0:T(1,128)}, u32[]{:S(2)}) copy-start(f32[1,1536]{1,0:T(1,128)} %param.21) | copy-start | bytes 18436
  148.4 7.6 %collective-permute-start.8 = (f32[1536]{0:T(1024)S(1)}, f32[1536]{0:T(1024)S(1)}, u32[]{:S(2)}, u32[]{:S(2)}) collective-permute-start(f32[1536]{0:T(1024)S(1)} %get-tuple-element.6), channel_id=1, source_target_pairs={{0,1},{1,257},{2,3},{3,259},{256,0},{257,256},{258,2},{259,258},{4... | collective-permute-start | bytes 18440 | tf_op jit(solution)/shard_map/ppermute | solution.py:420
  152.4 6.4 %collective-permute-start.9 = (f32[1536]{0:T(1024)S(1)}, f32[1536]{0:T(1024)S(1)}, u32[]{:S(2)}, u32[]{:S(2)}) collective-permute-start(f32[1536]{0:T(1024)S(1)} %get-tuple-element.7), channel_id=1, source_target_pairs={{0,0},{1,256},{2,2},{3,258},{256,1},{257,257},{258,3},{259,259},{4... | collective-permute-start | bytes 18440 | tf_op jit(solution)/shard_map/ppermute | solution.py:419
Sparse Core Ops, SparseCore 0:
  11.4 75.8 all-gather.1

commit v3 on v2

--- a/solution.py
+++ b/solution.py
@@ -106,8 +106,10 @@
 
 
 def rows_of(ref, head):
-    sources, _, rows, lanes = ref.shape
-    return ref[:, head].reshape(sources * rows, lanes)
+    lanes = ref.shape[-1]
+    if len(ref.shape) == 4:
+        return ref[:, head].reshape(-1, lanes)
+    return jnp.concatenate([ref[n, :, head].reshape(-1, lanes) for n in range(ref.shape[0])], axis=0)
 
 
 def scores_of(q, keys):
@@ -139,18 +141,20 @@
         full_ref[head, :, :, LANES:] = upper.astype(BF16).reshape(state_ref.shape[1:])
 
 
-def next_kernel(heads, count, q_ref, state_ref, *refs):
-    blocks, out_ref = refs[:count], refs[count]
+def next_kernel(heads, q_ref, state_ref, blocks_ref, out_ref):
     rows = 2 * q_ref.shape[2]
     for head in range(heads):
         q = q_ref[head].reshape(rows, 2 * LANES)
-        keys, values = wide_keys(jnp.concatenate([rows_of(ref, head) for ref in blocks], axis=0))
+        keys, values = wide_keys(rows_of(blocks_ref, head))
         state = weighted(scores_of(q, keys), values)
         out_ref[head] = state_ref[head] + state.reshape(out_ref.shape[1:])
 
 
 def last_kernel(heads, count, valid_ref, q_ref, state_ref, block_ref, text_ref, *refs):
     kept, out_ref, done_ref, top_ref, spare_ref, sem = refs[:count], *refs[count:]
+    parts = []
+    for ref in kept:
+        parts += [ref] if len(ref.shape) == 4 else [ref.at[n] for n in range(ref.shape[0])]
     tile = q_ref.shape[2]
     rows = 2 * tile
     lane = lane_index((rows, LANES))
@@ -166,11 +170,11 @@
 
     @pl.when(jnp.logical_not(safe))
     def _():
-        for at, ref in enumerate(kept):
+        for at, ref in enumerate(parts):
             copy = pltpu.make_async_copy(ref, spare_ref.at[at], sem)
             copy.start()
             copy.wait()
-        spare_ref[count] = block_ref[...]
+        spare_ref[len(parts)] = block_ref[...]
         for head in range(heads):
             q = q_ref[head].reshape(rows, 2 * LANES)
             spared = (lane >= HEAD_DIM) & (lane < GUARD)
@@ -185,7 +189,7 @@
                 return absorb(*wide_keys(spare_ref[at, :, head].reshape(-1, LANES)), *carry)
 
             carry = (jnp.full((rows, 1), -1e30, F32), jnp.zeros((rows, LANES), F32))
-            carry = lax.fori_loop(0, count + 1, step, carry)
+            carry = lax.fori_loop(0, len(parts) + 1, step, carry)
             largest, state = absorb(*wide_keys(text_ref[head], valid_ref[0]), *carry)
             done_ref[head] = state
             offset = jnp.broadcast_to(-largest, (rows, LANES))
@@ -232,7 +236,7 @@
     for x in whole:
         specs.append(pl.BlockSpec(x.shape, lambda i, n=x.ndim: (0,) * n))
     specs += [pl.BlockSpec(memory_space=pl.ANY)] * len(kept)
-    keys = sum(x.shape[0] * x.shape[2] if x.ndim == 4 else x.shape[1] for x in whole)
+    keys = sum(x.size // (heads * LANES) for x in whole)
     pairs = heads * 2 * rows * keys
     out_specs = [tiled(s.shape, a) for s, a in zip(out_shape, out_axes)]
     return pl.pallas_call(
@@ -259,8 +263,8 @@
 
 
 def next_blocks(q, state, blocks):
-    kernel = functools.partial(next_kernel, q.shape[0], len(blocks))
-    return attention_call(kernel, "next_blocks", [q, state], blocks, [], [state_shape(q)], [2])[0]
+    kernel = functools.partial(next_kernel, q.shape[0])
+    return attention_call(kernel, "next_blocks", [q, state], [blocks], [], [state_shape(q)], [2])[0]
 
 
 def last_block(valid, q, state, block, text, kept):
@@ -271,15 +275,35 @@
     scratch = [
         pltpu.VMEM((heads, 2 * tile, LANES), F32),
         pltpu.VMEM((heads, 2 * tile, LANES), F32),
-        pltpu.VMEM((len(kept) + 1,) + block.shape, BF16),
+        pltpu.VMEM((2 * len(kept),) + block.shape, BF16),
         pltpu.SemaphoreType.DMA,
     ]
     return attention_call(kernel, "last_block", [valid, q, state], [block, text], kept, [shape], [0], scratch)[0]
 
 
 def finish_kernel(
-    heads, groups, partial_ref, weight_ref, hidden_ref, modulation_ref, bias_ref, final_ref, final_bias_ref, out_ref, wide_ref
+    heads,
+    groups,
+    place_ref,
+    partial_ref,
+    own_weight_ref,
+    other_weight_ref,
+    hidden_ref,
+    modulation_ref,
+    bias_ref,
+    final_ref,
+    final_bias_ref,
+    out_ref,
+    wide_ref,
+    weight_ref,
+    sems,
 ):
+    copies_in = [
+        pltpu.make_async_copy(ref, weight_ref.at[n], sems.at[n])
+        for n, ref in enumerate((own_weight_ref, other_weight_ref))
+    ]
+    for copy in copies_in:
+        copy.start()
     half = partial_ref.shape[1]
     sources = partial_ref.shape[0]
     across = groups // 2
@@ -306,10 +330,22 @@
                 second = second + right[copy] * h2
             both = jnp.concatenate([first, second[:, :HEAD_DIM]], axis=1)
             wide_ref[part * half : (part + 1) * half, group * width : (group + 1) * width] = both
+    core, x, y = place_ref[0], place_ref[1], place_ref[2]
     attended = wide_ref[...].astype(BF16)
-    weights = weight_ref.shape[0]
+    for copy in copies_in:
+        copy.wait()
+    sides = []
+    for side in range(2):
+        total = 0.0
+        for group in range(groups):
+            at_x, at_y = divmod(group, across)
+            piece = lax.rem(at_y - y + across, across) * 2 + lax.rem(at_x + x, 2)
+            own = attended[:, group * width : (group + 1) * width]
+            total = total + jnp.dot(own, weight_ref[side, piece], preferred_element_type=F32)
+        sides.append(total)
+    first = core == 0
     projected = jnp.concatenate(
-        [jnp.dot(attended, weight_ref[w], preferred_element_type=F32) for w in range(weights)], axis=1
+        [jnp.where(first, sides[0], sides[1]), jnp.where(first, sides[1], sides[0])], axis=1
     )
     residual = hidden_ref[...].astype(F32) + modulation_ref[0:1] * (projected + bias_ref[...])
     middle = jnp.mean(residual, axis=-1, keepdims=True)
@@ -322,15 +358,23 @@
     out_ref[...] = velocity + final_bias_ref[...]
 
 
-def finish(partial, weight, hidden, modulation, bias, final_weight, final_bias, heads, groups):
+def finish(place, partial, own_weight, other_weight, hidden, modulation, bias, final_weight, final_bias, heads, groups):
     tokens, width = hidden.shape
+    vmem = pl.BlockSpec(memory_space=pltpu.VMEM)
+    far = pl.BlockSpec(memory_space=pl.ANY)
     return pl.pallas_call(
         functools.partial(finish_kernel, heads, groups),
         out_shape=jax.ShapeDtypeStruct((tokens, final_weight.shape[0]), F32),
-        scratch_shapes=[pltpu.VMEM((tokens, width), F32)],
+        in_specs=[pl.BlockSpec(memory_space=pltpu.SMEM), vmem, far, far, vmem, vmem, vmem, vmem, vmem],
+        out_specs=vmem,
+        scratch_shapes=[
+            pltpu.VMEM((tokens, width), F32),
+            pltpu.VMEM((2,) + own_weight.shape, BF16),
+            pltpu.SemaphoreType.DMA((2,)),
+        ],
         compiler_params=params(),
         name="project_and_norm",
-    )(partial, weight, hidden, modulation, bias, final_weight, final_bias)
+    )(place, partial, own_weight, other_weight, hidden, modulation, bias, final_weight, final_bias)
 
 
 def local(
@@ -352,24 +396,28 @@
     half = tokens // 2
     width = latent_qkv.shape[3] // groups
     heads = width // HEAD_DIM
-    zl, core, xh = (lax.axis_index(a) for a in ("zl", "core", "xh"))
-
-    columns = out_weight.shape[1] // 2
-    own_columns = lax.dynamic_slice_in_dim(out_weight, core * columns, columns, 1)
-    weight = lax.all_gather(own_columns, ("core", "xh", "y"), axis=0, tiled=True)
-    weight = weight.reshape(2, groups * width, columns)
+    across = lax.axis_size("y")
+    zl, core, xh, y = (lax.axis_index(a) for a in ("zl", "core", "xh", "y"))
+    after = lax.optimization_barrier
 
     slabs = pack(latent_qkv[0].transpose(1, 0, 2), groups, heads)
     slabs = lax.all_to_all(slabs, HEAD_AXES, split_axis=0, concat_axis=0, tiled=True)
     own = slabs[:, heads * half :].reshape(groups, heads, tokens, LANES)
-    up = [(i, (i + 1) % ring) for i in range(ring)]
-    down = [(i, (i - 1) % ring) for i in range(ring)]
-    right, left = lax.ppermute(own, "zh", up), lax.ppermute(own, "zh", down)
+    route = []
+    for i in range(ring):
+        route += [(2 * i, 2 * ((i + 1) % ring)), (2 * i + 1, 2 * ((i - 1) % ring) + 1)]
+    pass_on = lambda x: lax.ppermute(x, ("zh", "core"), route)
+    arrived = pass_on(lax.all_gather(own, "core", axis=0))
 
     packed = slabs[:, : heads * half].reshape(groups, heads, half, LANES)
     packed = lax.all_gather(packed, "core", axis=0)
     opposite = lax.ppermute(packed, "xh", [(0, 1), (1, 0)])
     q = unpack_queries(xh.reshape(1), packed, opposite)
+
+    columns = out_weight.shape[1] // 2
+    piece, _ = after((out_weight, packed))
+    piece = lax.dynamic_slice_in_dim(piece, core * columns, columns, 1)
+    pair = jnp.stack([piece, lax.ppermute(piece, "xh", [(0, 1), (1, 0)])])
 
     count = text_kv.shape[1]
     share = -(-count // 32) * 16
@@ -378,26 +426,28 @@
     text = lax.dynamic_slice_in_dim(text, core * share, share, 1)
     valid = jnp.where(xh == zl, jnp.minimum(count - core * share, share), 0).reshape(1)
     q, state = first_block(valid, q, own, text)
-    kept = [own]
+    kept = [own, arrived]
     for _ in range(ring // 2 - 2):
-        further_right = lax.ppermute(right, "zh", up)
-        further_left = lax.ppermute(left, "zh", down)
-        state = next_blocks(q, state, [right, left])
-        kept += [right, left]
-        right, left = further_right, further_left
-    kept += [right, left]
-    route = []
-    for i in range(ring):
-        route += [(2 * i, 2 * ((i + 1) % ring)), (2 * i + 1, 2 * ((i - 1) % ring) + 1)]
-    farthest = lax.ppermute(jnp.where(core == 0, right, left), ("zh", "core"), route)
-    state = next_blocks(q, state, [right, left])
+        arrived, state = after((arrived, state))
+        further = pass_on(arrived)
+        state = next_blocks(q, state, arrived)
+        arrived = further
+        kept.append(arrived)
+    arrived, state = after((arrived, state))
+    farthest = pass_on(lax.dynamic_index_in_dim(arrived, core, 0, keepdims=False))
+    turn = lambda d: lax.ppermute(pair, "y", [(i, (i - d) % across) for i in range(across)])
+    own_weight = jnp.concatenate([pair] + [turn(d) for d in range(1, across)], axis=0)
+    other_weight = lax.ppermute(own_weight, "core", [(0, 1), (1, 0)])
+    state = next_blocks(q, state, arrived)
     partial = last_block(valid, q, state, farthest, text, kept)
     partial = partial.reshape(4 * groups, half, 4 * LANES)
     partial = lax.all_to_all(partial, BLOCK_AXES, split_axis=0, concat_axis=0, tiled=True)
 
     velocity = finish(
+        jnp.stack([core, xh, y]),
         partial,
-        weight,
+        own_weight,
+        other_weight,
         hidden_in[0],
         modulation[0],
         out_bias[None],
@@ -408,8 +458,7 @@
     )
 
     tiles = velocity.reshape(tokens, 2, -1).transpose(1, 0, 2).reshape(2, -1)
-    branch, parity = lax.axis_index("cfg"), lax.axis_index("y") % 2
-    across = lax.axis_size("y")
+    branch, parity = lax.axis_index("cfg"), y % 2
     same, swap = [], []
     for s in range(2):
         for y in range(across):

time: 168 us -> 177 us (1.054)
  the two profiles are of different devices: /device:TPU:34 before, /device:TPU:40 now
where the time goes in v3:
time: 177 us; the launch traced here: 176 us
  Pallas kernels  57.9 us (33%)
  starting transfers between devices  46.6 us (26%)
  waiting for transfers between devices  28.9 us (16%)
  blocking collectives  23.4 us (13%)
  local copies, waits for them, and re-layouts  13.4 us (8%)
  other arithmetic  3.23 us (2%)
  between operations  2.42 us (1%)
    pallas_call x5, Pallas kernels, attention_call(): pl.pallas_call(kernel, grid=(rows // tile,), out_shape=out_shape, in_spec...  51.6 us
    all_to_all x1, blocking collectives, local(): lax.all_to_all(slabs, HEAD_AXES, split_axis=0, concat_axis=0, tiled=True)  13.9 us
    ppermute x4, starting transfers between devices, local(): pass_on = lambda x: lax.ppermute(x, ('zh', 'core'), route)  12.1 us
    ppermute x4, waiting for transfers between devices, local(): pass_on = lambda x: lax.ppermute(x, ('zh', 'core'), route)  12 us
    ppermute x3, starting transfers between devices, local(): lax.ppermute(pair, 'y', [(i, (i - d) % across) for i in range(across)])  10.3 us
    unnamed x33, local copies, waits for them, and re-layouts  10.1 us
    ppermute x1, waiting for transfers between devices, local(): opposite = lax.ppermute(packed, 'xh', [(0, 1), (1, 0)])  7.4 us
    all_gather x1, blocking collectives, local(): packed = lax.all_gather(packed, 'core', axis=0)  7.28 us
  transfers between devices with their start and end apart: 13, of which 5 were waited for; matrix products, arithmetic and copies ran while one was open for 5% of the time, Pallas kernels for 30%

profile of v3, /device:TPU:40, one launch (start us, length us, event | category | flops | bytes accessed | tf_op | source)
XLA Modules:
  0.0 175.9 jit_solution(10220064035126105854)
XLA Ops:
  1.8 13.9 %all_to_all.10 = bf16[8,216,128]{2,1,0:T(8,128)(2,1)S(1)} all-to-all(bf16[8,216,128]{2,1,0:T(8,128)(2,1)S(1)} %pack_heads.1), channel_id=1, replica_groups=mesh['cfg'=2,'zh'=8,'zl'=2,'core'=2,'xh'=2,'y'=4] {'zl','y'}, dimensions={0} | all-to-all | bytes 884736 | tf_op jit(solution)/shard_map/all_to_all | solution.py:404
  15.8 2.2 %all_gather.7 = bf16[2,8,3,48,128]{4,3,2,1,0:T(8,128)(2,1)S(1)} all-gather(bf16[1,8,3,48,128]{4,3,2,1,0:T(8,128)(2,1)S(1)} %bitcast.34), channel_id=1, replica_groups=mesh['cfg'=2,'zh'=8,'zl'=2,'core'=2,'xh'=2,'y'=4] {'core'}, dimensions={0}, use_global_device_ids=true | all-gather | bytes 884736 | tf_op jit(solution)/shard_map/all_gather | solution.py:410
  18.0 4.0 %collective-permute-start.1 = (bf16[2,8,3,48,128]{4,3,2,1,0:T(8,128)(2,1)S(1)}, bf16[2,8,3,48,128]{4,3,2,1,0:T(8,128)(2,1)S(1)}, u32[]{:S(2)}, u32[]{:S(2)}) collective-permute-start(bf16[2,8,3,48,128]{4,3,2,1,0:T(8,128)(2,1)S(1)} %all_gather.7), channel_id=1, source_target_pairs={{0,32},{8,232},{32,64},{40,8},{64,96},{72,40},{96,128},{104,72},{1... | collective-permute-start | bytes 1769480 | tf_op jit(solution)/shard_map/ppermute | solution.py:409
  22.0 7.3 %all_gather.6.own_ref = bf16[2,8,3,24,128]{4,3,2,1,0:T(8,128)(2,1)S(1)} all-gather(bf16[1,8,3,24,128]{4,3,2,1,0:T(8,128)(2,1)S(1)} %bitcast.44), channel_id=1, replica_groups=mesh['cfg'=2,'zh'=8,'zl'=2,'core'=2,'xh'=2,'y'=4] {'core'}, dimensions={0}, use_global_device_ids=true | all-gather | bytes 442368 | tf_op jit(solution)/shard_map/all_gather | solution.py:413
  29.3 4.9 %collective-permute-start = (bf16[2,8,3,24,128]{4,3,2,1,0:T(8,128)(2,1)S(1)}, bf16[2,8,3,24,128]{4,3,2,1,0:T(8,128)(2,1)S(1)}, u32[]{:S(2)}, u32[]{:S(2)}) collective-permute-start(bf16[2,8,3,24,128]{4,3,2,1,0:T(8,128)(2,1)S(1)} %all_gather.6.own_ref), channel_id=1, source_target_pairs={{0,4},{4,0},{1,5},{5,1},{2,6},{6,2},{3,7},{7,3},{8,12},{12,8},{9,1... | collective-permute-start | bytes 884744 | tf_op jit(solution)/shard_map/ppermute | solution.py:414
  34.6 7.4 %collective-permute-done.other_ref = bf16[2,8,3,24,128]{4,3,2,1,0:T(8,128)(2,1)S(1)} collective-permute-done((bf16[2,8,3,24,128]{4,3,2,1,0:T(8,128)(2,1)S(1)}, bf16[2,8,3,24,128]{4,3,2,1,0:T(8,128)(2,1)S(1)}, u32[]{:S(2)}, u32[]{:S(2)}) %collective-permute-start) | collective-permute-done | bytes 294944 | tf_op jit(solution)/shard_map/ppermute | solution.py:414
  42.8 6.3 %own_block.1 = (bf16[3,2,768,256]{3,2,1,0:T(8,128)(2,1)S(1)}, f32[3,2,768,128]{3,2,1,0:T(8,128)S(1)}) custom-call(s32[1]{0:T(128)} %bitcast.3.valid_ref, bf16[3,2,768,256]{3,2,1,0:T(8,128)(2,1)S(1)} %unpack_queries.1.q_ref, bf16[8,3,48,128]{3,2,1,0:T(8,128)(2,1)S(1)} %bitcast.35, bf16[3,176,128]{2,1,0:T(8,128)(2,1)S(1)} %pad_dynamic-slice_fusion.text_ref), custom_call_target="tpu_custom_call" | custom-call | flops 1981808640 | bytes 4718592 | tf_op jit(solution)/shard_map/own_block/pallas_call | solution.py:242
  49.2 1.9 %collective-permute-start.2 = (bf16[2,8,3,48,128]{4,3,2,1,0:T(8,128)(2,1)S(1)}, bf16[2,8,3,48,128]{4,3,2,1,0:T(8,128)(2,1)}, u32[]{:S(2)}, u32[]{:S(2)}) collective-permute-start(bf16[2,8,3,48,128]{4,3,2,1,0:T(8,128)(2,1)S(1)} %collective-permute-done.1.blocks_ref.refs_1_), channel_id=1, source_target_pairs={{0,32},{8,232},{32,64},{40,8},{64,96},{72,40},{96,128},{104,72},{1... | collective-permute-start | bytes 1769480 | tf_op jit(solution)/shard_map/ppermute | solution.py:409
  51.1 4.8 %next_blocks.3.state_ref = f32[3,2,768,128]{3,2,1,0:T(8,128)S(1)} custom-call(bf16[3,2,768,256]{3,2,1,0:T(8,128)(2,1)S(1)} %get-tuple-element.11.q_ref, f32[3,2,768,128]{3,2,1,0:T(8,128)S(1)} %get-tuple-element.14.state_ref, bf16[2,8,3,48,128]{4,3,2,1,0:T(8,128)(2,1)S(1)} %collective-permute-done.1.blocks_ref.refs_1_), custom_call_target="tpu_custom_call" | custom-call | flops 2717908992 | bytes 4718592 | tf_op jit(solution)/shard_map/next_blocks/pallas_call | solution.py:242
  55.9 1.4 copy-done.9
  57.4 12.0 %collective-permute-done.2.blocks_ref.refs_2_ = bf16[2,8,3,48,128]{4,3,2,1,0:T(8,128)(2,1)} collective-permute-done((bf16[2,8,3,48,128]{4,3,2,1,0:T(8,128)(2,1)S(1)}, bf16[2,8,3,48,128]{4,3,2,1,0:T(8,128)(2,1)}, u32[]{:S(2)}, u32[]{:S(2)}) %collective-permute-start.2) | collective-permute-done | bytes 589856 | tf_op jit(solution)/shard_map/ppermute | solution.py:409
  69.3 1.9 %collective-permute-start.3 = (bf16[2,8,3,48,128]{4,3,2,1,0:T(8,128)(2,1)}, bf16[2,8,3,48,128]{4,3,2,1,0:T(8,128)(2,1)}, u32[]{:S(2)}, u32[]{:S(2)}) collective-permute-start(bf16[2,8,3,48,128]{4,3,2,1,0:T(8,128)(2,1)} %collective-permute-done.2.blocks_ref.refs_2_), channel_id=1, source_target_pairs={{0,32},{8,232},{32,64},{40,8},{64,96},{72,40},{96,128},{104,72},{1... | collective-permute-start | bytes 1769480 | tf_op jit(solution)/shard_map/ppermute | solution.py:409
  72.3 4.9 %collective-permute-start.5 = (bf16[192,768]{1,0:T(8,128)(2,1)S(1)}, bf16[192,768]{1,0:T(8,128)(2,1)}, u32[]{:S(2)}, u32[]{:S(2)}) collective-permute-start(bf16[192,768]{1,0:T(8,128)(2,1)S(1)} %get-tuple-element.25), channel_id=1, source_target_pairs={{0,4},{4,0},{1,5},{5,1},{2,6},{6,2},{3,7},{7,3},{8,12},{12,8},{9,1... | collective-permute-start | bytes 884744 | tf_op jit(solution)/shard_map/ppermute | solution.py:420
  77.2 1.7 copy-done.1
  78.9 1.7 copy-done.10
  80.5 5.7 %next_blocks.4.state_ref = f32[3,2,768,128]{3,2,1,0:T(8,128)S(1)} custom-call(bf16[3,2,768,256]{3,2,1,0:T(8,128)(2,1)S(1)} %copy-done.1, f32[3,2,768,128]{3,2,1,0:T(8,128)S(1)} %copy-done.10, bf16[2,8,3,48,128]{4,3,2,1,0:T(8,128)(2,1)} %collective-permute-done.2.blocks_ref.refs_2_), custom_call_target="tpu_custom_call" | custom-call | flops 2717908992 | bytes 4718592 | tf_op jit(solution)/shard_map/next_blocks/pallas_call | solution.py:242
  87.3 4.3 %collective-permute-start.4 = (bf16[8,3,48,128]{3,2,1,0:T(8,128)(2,1)S(1)}, bf16[8,3,48,128]{3,2,1,0:T(8,128)(2,1)S(1)}, u32[]{:S(2)}, u32[]{:S(2)}) collective-permute-start(bf16[8,3,48,128]{3,2,1,0:T(8,128)(2,1)S(1)} %dynamic-slice_bitcast_fusion), channel_id=1, source_target_pairs={{0,32},{8,232},{32,64},{40,8},{64,96},{72,40},{96,128},{104,72},{1... | collective-permute-start | bytes 884744 | tf_op jit(solution)/shard_map/ppermute | solution.py:409
  91.6 1.9 %pad_maximum_fusion = bf16[2,192,768]{2,1,0:T(8,128)(2,1)} fusion(bf16[1,192,768]{2,1,0:T(8,128)(2,1)} %bitcast.15, bf16[1,192,768]{2,1,0:T(8,128)(2,1)S(1)} %bitcast.42), kind=kLoop, calls=%fused_computation | loop fusion | flops 294912 | bytes 1179648 | tf_op jit(solution)/shard_map/stack | solution.py:420
  93.5 2.6 %collective-permute-start.8 = (bf16[2,192,768]{2,1,0:T(8,128)(2,1)}, bf16[2,192,768]{2,1,0:T(8,128)(2,1)}, u32[]{:S(2)}, u32[]{:S(2)}) collective-permute-start(bf16[2,192,768]{2,1,0:T(8,128)(2,1)} %pad_maximum_fusion), channel_id=1, source_target_pairs={{0,1},{1,2},{2,3},{3,0},{4,5},{5,6},{6,7},{7,4},{8,9},{9,10},{10,1... | collective-permute-start | bytes 1769480 | tf_op jit(solution)/shard_map/ppermute | solution.py:438
  96.0 4.9 %collective-permute-start.7 = (bf16[2,192,768]{2,1,0:T(8,128)(2,1)}, bf16[2,192,768]{2,1,0:T(8,128)(2,1)}, u32[]{:S(2)}, u32[]{:S(2)}) collective-permute-start(bf16[2,192,768]{2,1,0:T(8,128)(2,1)} %pad_maximum_fusion), channel_id=1, source_target_pairs={{0,2},{1,3},{2,0},{3,1},{4,6},{5,7},{6,4},{7,5},{8,10},{9,11},{10,... | collective-permute-start | bytes 1769480 | tf_op jit(solution)/shard_map/ppermute | solution.py:438
  100.9 2.8 %collective-permute-start.6 = (bf16[2,192,768]{2,1,0:T(8,128)(2,1)}, bf16[2,192,768]{2,1,0:T(8,128)(2,1)}, u32[]{:S(2)}, u32[]{:S(2)}) collective-permute-start(bf16[2,192,768]{2,1,0:T(8,128)(2,1)} %pad_maximum_fusion), channel_id=1, source_target_pairs={{0,3},{1,0},{2,1},{3,2},{4,7},{5,4},{6,5},{7,6},{8,11},{9,8},{10,9... | collective-permute-start | bytes 1769480 | tf_op jit(solution)/shard_map/ppermute | solution.py:438
  103.7 5.8 %next_blocks.5.state_ref = f32[3,2,768,128]{3,2,1,0:T(8,128)S(1)} custom-call(bf16[3,2,768,256]{3,2,1,0:T(8,128)(2,1)S(1)} %copy-done.1, f32[3,2,768,128]{3,2,1,0:T(8,128)S(1)} %next_blocks.4.state_ref, bf16[2,8,3,48,128]{4,3,2,1,0:T(8,128)(2,1)} %collective-permute-done.3.blocks_ref.refs_3_), custom_call_target="tpu_custom_call" | custom-call | flops 2717908992 | bytes 4718592 | tf_op jit(solution)/shard_map/next_blocks/pallas_call | solution.py:242
  109.5 29.0 %last_block.1 = bf16[768,512]{1,0:T(8,128)(2,1)} custom-call(s32[1]{0:T(128)} %bitcast.3.valid_ref, bf16[3,2,768,256]{3,2,1,0:T(8,128)(2,1)S(1)} %copy-done.2, f32[3,2,768,128]{3,2,1,0:T(8,128)S(1)} %next_blocks.5.state_ref, bf16[8,3,48,128]{3,2,1,0:T(8,128)(2,1)S(1)} %collective-permute-done.4.block_ref, ...), custom_call_target="tpu_custom_call" | custom-call | flops 1981808640 | bytes 4718592 | tf_op jit(solution)/shard_map/last_block/pallas_call | solution.py:242
  138.5 6.0 %all-to-all-start.1 = ((bf16[32,24,512]{2,1,0:T(8,128)(2,1)}), bf16[32,24,512]{2,1,0:T(8,128)(2,1)S(1)}, u32[]{:S(2)}, u32[]{:S(2)}) async-start(bf16[32,24,512]{2,1,0:T(8,128)(2,1)} %bitcast.13), calls=%async_computation.1 | async-start | bytes 1572864 | tf_op jit(solution)/shard_map/all_to_all | solution.py:444
  149.0 2.1 %collective-permute-start.9 = (bf16[8,192,768]{2,1,0:T(8,128)(2,1)S(1)}, bf16[8,192,768]{2,1,0:T(8,128)(2,1)}, u32[]{:S(2)}, u32[]{:S(2)}) collective-permute-start(bf16[8,192,768]{2,1,0:T(8,128)(2,1)S(1)} %constant_dynamic-update-slice_fusion.own_weight_ref), channel_id=1, source_target_pairs={{0,8},{8,0},{1,9},{9,1},{2,10},{10,2},{3,11},{11,3},{4,12},{12,4},... | collective-permute-start | bytes 7077896 | tf_op jit(solution)/shard_map/ppermute | solution.py:440
  151.2 4.4 %collective-permute-done.9.other_weight_ref = bf16[8,192,768]{2,1,0:T(8,128)(2,1)} collective-permute-done((bf16[8,192,768]{2,1,0:T(8,128)(2,1)S(1)}, bf16[8,192,768]{2,1,0:T(8,128)(2,1)}, u32[]{:S(2)}, u32[]{:S(2)}) %collective-permute-start.9) | collective-permute-done | bytes 2359328 | tf_op jit(solution)/shard_map/ppermute | solution.py:440
  155.6 2.9 %all-to-all-done.1.partial_ref = bf16[32,24,512]{2,1,0:T(8,128)(2,1)S(1)} async-done(((bf16[32,24,512]{2,1,0:T(8,128)(2,1)}), bf16[32,24,512]{2,1,0:T(8,128)(2,1)S(1)}, u32[]{:S(2)}, u32[]{:S(2)}) %all-to-all-start.1) | async-done | bytes 786464 | tf_op jit(solution)/shard_map/all_to_all | solution.py:444
  158.5 5.3 %project_and_norm.1 = f32[48,64]{1,0:T(8,128)S(1)} custom-call(s32[3]{0:T(128)S(1)} %pad_add_fusion.place_ref, bf16[32,24,512]{2,1,0:T(8,128)(2,1)S(1)} %all-to-all-done.1.partial_ref, bf16[8,192,768]{2,1,0:T(8,128)(2,1)S(1)} %constant_dynamic-update-slice_fusion.own_weight_ref, bf16[8,192,768]{2,1,0:T(8,128)(2,1)} %collective-permute-done.9.other_weight_ref, ...), custom_call_target="tpu_custom_call" | custom-call | tf_op jit(solution)/shard_map/project_and_norm/pallas_call | solution.py:365
  164.1 3.4 %collective-permute-start.10 = (f32[1536]{0:T(1024)S(1)}, f32[1536]{0:T(1024)S(1)}, u32[]{:S(2)}, u32[]{:S(2)}) collective-permute-start(f32[1536]{0:T(1024)S(1)} %get-tuple-element.20), channel_id=1, source_target_pairs={{0,1},{1,257},{2,3},{3,259},{256,0},{257,256},{258,2},{259,258},{4... | collective-permute-start | bytes 18440 | tf_op jit(solution)/shard_map/ppermute | solution.py:469
  167.5 2.9 %collective-permute-start.11 = (f32[1536]{0:T(1024)S(1)}, f32[1536]{0:T(1024)S(1)}, u32[]{:S(2)}, u32[]{:S(2)}) collective-permute-start(f32[1536]{0:T(1024)S(1)} %get-tuple-element.21), channel_id=1, source_target_pairs={{0,0},{1,256},{2,2},{3,258},{256,1},{257,257},{258,3},{259,259},{4... | collective-permute-start | bytes 18440 | tf_op jit(solution)/shard_map/ppermute | solution.py:468
  171.8 2.2 %collective-permute-done.11 = f32[1536]{0:T(1024)S(1)} collective-permute-done((f32[1536]{0:T(1024)S(1)}, f32[1536]{0:T(1024)S(1)}, u32[]{:S(2)}, u32[]{:S(2)}) %collective-permute-start.11) | collective-permute-done | bytes 6176 | tf_op jit(solution)/shard_map/ppermute | solution.py:468
  174.6 1.3 reshape_subtract_fusion
  (55 shorter events, 9.7 us)
Async XLA Ops:
  0.6 1.0 copy-start.5
  1.6 32.6 %copy-start.11 = (bf16[1,333,2,192]{1,3,2,0:T(8,128)(2,1)S(1)}, bf16[1,333,2,192]{1,3,2,0:T(8,128)(2,1)}, u32[]{:S(2)}) copy-start(bf16[1,333,2,192]{1,3,2,0:T(8,128)(2,1)} %param.12) | copy-start | bytes 767236
  18.0 31.1 %collective-permute-start.1 = (bf16[2,8,3,48,128]{4,3,2,1,0:T(8,128)(2,1)S(1)}, bf16[2,8,3,48,128]{4,3,2,1,0:T(8,128)(2,1)S(1)}, u32[]{:S(2)}, u32[]{:S(2)}) collective-permute-start(bf16[2,8,3,48,128]{4,3,2,1,0:T(8,128)(2,1)S(1)} %all_gather.7), channel_id=1, source_target_pairs={{0,32},{8,232},{32,64},{40,8},{64,96},{72,40},{96,128},{104,72},{1... | collective-permute-start | bytes 1769480 | tf_op jit(solution)/shard_map/ppermute | solution.py:409
  29.3 12.7 %collective-permute-start = (bf16[2,8,3,24,128]{4,3,2,1,0:T(8,128)(2,1)S(1)}, bf16[2,8,3,24,128]{4,3,2,1,0:T(8,128)(2,1)S(1)}, u32[]{:S(2)}, u32[]{:S(2)}) collective-permute-start(bf16[2,8,3,24,128]{4,3,2,1,0:T(8,128)(2,1)S(1)} %all_gather.6.own_ref), channel_id=1, source_target_pairs={{0,4},{4,0},{1,5},{5,1},{2,6},{6,2},{3,7},{7,3},{8,12},{12,8},{9,1... | collective-permute-start | bytes 884744 | tf_op jit(solution)/shard_map/ppermute | solution.py:414
  49.1 6.8 %copy-start = (bf16[3,2,768,256]{3,2,1,0:T(8,128)(2,1)}, bf16[3,2,768,256]{3,2,1,0:T(8,128)(2,1)S(1)}, u32[]{:S(2)}) copy-start(bf16[3,2,768,256]{3,2,1,0:T(8,128)(2,1)S(1)} %get-tuple-element.11.q_ref) | copy-start | bytes 7077892
  49.2 6.8 %copy-start.3 = (bf16[2,8,3,48,128]{4,3,2,1,0:T(8,128)(2,1)}, bf16[2,8,3,48,128]{4,3,2,1,0:T(8,128)(2,1)S(1)}, u32[]{:S(2)}) copy-start(bf16[2,8,3,48,128]{4,3,2,1,0:T(8,128)(2,1)S(1)} %collective-permute-done.1.blocks_ref.refs_1_) | copy-start | bytes 1769476
  49.2 20.2 %collective-permute-start.2 = (bf16[2,8,3,48,128]{4,3,2,1,0:T(8,128)(2,1)S(1)}, bf16[2,8,3,48,128]{4,3,2,1,0:T(8,128)(2,1)}, u32[]{:S(2)}, u32[]{:S(2)}) collective-permute-start(bf16[2,8,3,48,128]{4,3,2,1,0:T(8,128)(2,1)S(1)} %collective-permute-done.1.blocks_ref.refs_1_), channel_id=1, source_target_pairs={{0,32},{8,232},{32,64},{40,8},{64,96},{72,40},{96,128},{104,72},{1... | collective-permute-start | bytes 1769480 | tf_op jit(solution)/shard_map/ppermute | solution.py:409
  55.9 1.4 copy-start.9
  69.3 17.0 %collective-permute-start.3 = (bf16[2,8,3,48,128]{4,3,2,1,0:T(8,128)(2,1)}, bf16[2,8,3,48,128]{4,3,2,1,0:T(8,128)(2,1)}, u32[]{:S(2)}, u32[]{:S(2)}) collective-permute-start(bf16[2,8,3,48,128]{4,3,2,1,0:T(8,128)(2,1)} %collective-permute-done.2.blocks_ref.refs_2_), channel_id=1, source_target_pairs={{0,32},{8,232},{32,64},{40,8},{64,96},{72,40},{96,128},{104,72},{1... | collective-permute-start | bytes 1769480 | tf_op jit(solution)/shard_map/ppermute | solution.py:409
  72.3 19.3 %collective-permute-start.5 = (bf16[192,768]{1,0:T(8,128)(2,1)S(1)}, bf16[192,768]{1,0:T(8,128)(2,1)}, u32[]{:S(2)}, u32[]{:S(2)}) collective-permute-start(bf16[192,768]{1,0:T(8,128)(2,1)S(1)} %get-tuple-element.25), channel_id=1, source_target_pairs={{0,4},{4,0},{1,5},{5,1},{2,6},{6,2},{3,7},{7,3},{8,12},{12,8},{9,1... | collective-permute-start | bytes 884744 | tf_op jit(solution)/shard_map/ppermute | solution.py:420
  77.2 1.7 copy-start.1
  78.9 1.7 copy-start.10
  87.3 22.2 %collective-permute-start.4 = (bf16[8,3,48,128]{3,2,1,0:T(8,128)(2,1)S(1)}, bf16[8,3,48,128]{3,2,1,0:T(8,128)(2,1)S(1)}, u32[]{:S(2)}, u32[]{:S(2)}) collective-permute-start(bf16[8,3,48,128]{3,2,1,0:T(8,128)(2,1)S(1)} %dynamic-slice_bitcast_fusion), channel_id=1, source_target_pairs={{0,32},{8,232},{32,64},{40,8},{64,96},{72,40},{96,128},{104,72},{1... | collective-permute-start | bytes 884744 | tf_op jit(solution)/shard_map/ppermute | solution.py:409
  93.4 16.1 %copy-start.2 = (bf16[3,2,768,256]{3,2,1,0:T(8,128)(2,1)S(1)}, bf16[3,2,768,256]{3,2,1,0:T(8,128)(2,1)}, u32[]{:S(2)}) copy-start(bf16[3,2,768,256]{3,2,1,0:T(8,128)(2,1)} %copy-done) | copy-start | bytes 7077892
  93.4 16.1 %copy-start.4 = (bf16[2,8,3,48,128]{4,3,2,1,0:T(8,128)(2,1)S(1)}, bf16[2,8,3,48,128]{4,3,2,1,0:T(8,128)(2,1)}, u32[]{:S(2)}) copy-start(bf16[2,8,3,48,128]{4,3,2,1,0:T(8,128)(2,1)} %copy-done.3) | copy-start | bytes 1769476
  93.5 54.4 %collective-permute-start.8 = (bf16[2,192,768]{2,1,0:T(8,128)(2,1)}, bf16[2,192,768]{2,1,0:T(8,128)(2,1)}, u32[]{:S(2)}, u32[]{:S(2)}) collective-permute-start(bf16[2,192,768]{2,1,0:T(8,128)(2,1)} %pad_maximum_fusion), channel_id=1, source_target_pairs={{0,1},{1,2},{2,3},{3,0},{4,5},{5,6},{6,7},{7,4},{8,9},{9,10},{10,1... | collective-permute-start | bytes 1769480 | tf_op jit(solution)/shard_map/ppermute | solution.py:438
  96.0 50.7 %collective-permute-start.7 = (bf16[2,192,768]{2,1,0:T(8,128)(2,1)}, bf16[2,192,768]{2,1,0:T(8,128)(2,1)}, u32[]{:S(2)}, u32[]{:S(2)}) collective-permute-start(bf16[2,192,768]{2,1,0:T(8,128)(2,1)} %pad_maximum_fusion), channel_id=1, source_target_pairs={{0,2},{1,3},{2,0},{3,1},{4,6},{5,7},{6,4},{7,5},{8,10},{9,11},{10,... | collective-permute-start | bytes 1769480 | tf_op jit(solution)/shard_map/ppermute | solution.py:438
  100.9 44.7 %collective-permute-start.6 = (bf16[2,192,768]{2,1,0:T(8,128)(2,1)}, bf16[2,192,768]{2,1,0:T(8,128)(2,1)}, u32[]{:S(2)}, u32[]{:S(2)}) collective-permute-start(bf16[2,192,768]{2,1,0:T(8,128)(2,1)} %pad_maximum_fusion), channel_id=1, source_target_pairs={{0,3},{1,0},{2,1},{3,2},{4,7},{5,4},{6,5},{7,6},{8,11},{9,8},{10,9... | collective-permute-start | bytes 1769480 | tf_op jit(solution)/shard_map/ppermute | solution.py:438
  138.5 20.0 %all-to-all-start.1 = ((bf16[32,24,512]{2,1,0:T(8,128)(2,1)}), bf16[32,24,512]{2,1,0:T(8,128)(2,1)S(1)}, u32[]{:S(2)}, u32[]{:S(2)}) async-start(bf16[32,24,512]{2,1,0:T(8,128)(2,1)} %bitcast.13), calls=%async_computation.1 | async-start | bytes 1572864 | tf_op jit(solution)/shard_map/all_to_all | solution.py:444
  144.5 6.5 %copy-start.13 = (f32[1536]{0:T(1024)S(1)}, f32[1536]{0:T(1024)}, u32[]{:S(2)}) copy-start(f32[1536]{0:T(1024)} %param.16) | copy-start | bytes 18436
  144.6 6.6 %copy-start.12 = (f32[1,3,1536]{2,0,1:T(1,128)S(1)}, f32[1,3,1536]{2,0,1:T(1,128)}, u32[]{:S(2)}) copy-start(f32[1,3,1536]{2,0,1:T(1,128)} %param.14) | copy-start | bytes 55300
  144.6 13.9 %copy-start.6 = (bf16[1536,64]{0,1:T(8,128)(2,1)S(1)}, bf16[1536,64]{0,1:T(8,128)(2,1)}, u32[]{:S(2)}) copy-start(bf16[1536,64]{0,1:T(8,128)(2,1)} %param.17) | copy-start | bytes 589828
  144.6 13.9 %copy-start.7 = (bf16[1,48,1536]{2,1,0:T(8,128)(2,1)S(1)}, bf16[1,48,1536]{2,1,0:T(8,128)(2,1)}, u32[]{:S(2)}) copy-start(bf16[1,48,1536]{2,1,0:T(8,128)(2,1)} %param.13) | copy-start | bytes 442372
  144.6 13.9 %copy-start.8 = (f32[64]{0:T(128)S(1)}, f32[64]{0:T(128)}, u32[]{:S(2)}) copy-start(f32[64]{0:T(128)} %param.18) | copy-start | bytes 772
  149.0 6.6 %collective-permute-start.9 = (bf16[8,192,768]{2,1,0:T(8,128)(2,1)S(1)}, bf16[8,192,768]{2,1,0:T(8,128)(2,1)}, u32[]{:S(2)}, u32[]{:S(2)}) collective-permute-start(bf16[8,192,768]{2,1,0:T(8,128)(2,1)S(1)} %constant_dynamic-update-slice_fusion.own_weight_ref), channel_id=1, source_target_pairs={{0,8},{8,0},{1,9},{9,1},{2,10},{10,2},{3,11},{11,3},{4,12},{12,4},... | collective-permute-start | bytes 7077896 | tf_op jit(solution)/shard_map/ppermute | solution.py:440
  164.1 7.6 %collective-permute-start.10 = (f32[1536]{0:T(1024)S(1)}, f32[1536]{0:T(1024)S(1)}, u32[]{:S(2)}, u32[]{:S(2)}) collective-permute-start(f32[1536]{0:T(1024)S(1)} %get-tuple-element.20), channel_id=1, source_target_pairs={{0,1},{1,257},{2,3},{3,259},{256,0},{257,256},{258,2},{259,258},{4... | collective-permute-start | bytes 18440 | tf_op jit(solution)/shard_map/ppermute | solution.py:469
  167.5 6.4 %collective-permute-start.11 = (f32[1536]{0:T(1024)S(1)}, f32[1536]{0:T(1024)S(1)}, u32[]{:S(2)}, u32[]{:S(2)}) collective-permute-start(f32[1536]{0:T(1024)S(1)} %get-tuple-element.21), channel_id=1, source_target_pairs={{0,0},{1,256},{2,2},{3,258},{256,1},{257,257},{258,3},{259,259},{4... | collective-permute-start | bytes 18440 | tf_op jit(solution)/shard_map/ppermute | solution.py:468

commit v4 on v3

--- a/solution.py
+++ b/solution.py
@@ -284,10 +284,8 @@
 def finish_kernel(
     heads,
     groups,
-    place_ref,
     partial_ref,
-    own_weight_ref,
-    other_weight_ref,
+    weight_ref,
     hidden_ref,
     modulation_ref,
     bias_ref,
@@ -295,15 +293,7 @@
     final_bias_ref,
     out_ref,
     wide_ref,
-    weight_ref,
-    sems,
 ):
-    copies_in = [
-        pltpu.make_async_copy(ref, weight_ref.at[n], sems.at[n])
-        for n, ref in enumerate((own_weight_ref, other_weight_ref))
-    ]
-    for copy in copies_in:
-        copy.start()
     half = partial_ref.shape[1]
     sources = partial_ref.shape[0]
     across = groups // 2
@@ -330,22 +320,9 @@
                 second = second + right[copy] * h2
             both = jnp.concatenate([first, second[:, :HEAD_DIM]], axis=1)
             wide_ref[part * half : (part + 1) * half, group * width : (group + 1) * width] = both
-    core, x, y = place_ref[0], place_ref[1], place_ref[2]
     attended = wide_ref[...].astype(BF16)
-    for copy in copies_in:
-        copy.wait()
-    sides = []
-    for side in range(2):
-        total = 0.0
-        for group in range(groups):
-            at_x, at_y = divmod(group, across)
-            piece = lax.rem(at_y - y + across, across) * 2 + lax.rem(at_x + x, 2)
-            own = attended[:, group * width : (group + 1) * width]
-            total = total + jnp.dot(own, weight_ref[side, piece], preferred_element_type=F32)
-        sides.append(total)
-    first = core == 0
     projected = jnp.concatenate(
-        [jnp.where(first, sides[0], sides[1]), jnp.where(first, sides[1], sides[0])], axis=1
+        [jnp.dot(attended, weight_ref[side], preferred_element_type=F32) for side in range(2)], axis=1
     )
     residual = hidden_ref[...].astype(F32) + modulation_ref[0:1] * (projected + bias_ref[...])
     middle = jnp.mean(residual, axis=-1, keepdims=True)
@@ -358,23 +335,15 @@
     out_ref[...] = velocity + final_bias_ref[...]
 
 
-def finish(place, partial, own_weight, other_weight, hidden, modulation, bias, final_weight, final_bias, heads, groups):
+def finish(partial, weight, hidden, modulation, bias, final_weight, final_bias, heads, groups):
     tokens, width = hidden.shape
-    vmem = pl.BlockSpec(memory_space=pltpu.VMEM)
-    far = pl.BlockSpec(memory_space=pl.ANY)
     return pl.pallas_call(
         functools.partial(finish_kernel, heads, groups),
         out_shape=jax.ShapeDtypeStruct((tokens, final_weight.shape[0]), F32),
-        in_specs=[pl.BlockSpec(memory_space=pltpu.SMEM), vmem, far, far, vmem, vmem, vmem, vmem, vmem],
-        out_specs=vmem,
-        scratch_shapes=[
-            pltpu.VMEM((tokens, width), F32),
-            pltpu.VMEM((2,) + own_weight.shape, BF16),
-            pltpu.SemaphoreType.DMA((2,)),
-        ],
+        scratch_shapes=[pltpu.VMEM((tokens, width), F32)],
         compiler_params=params(),
         name="project_and_norm",
-    )(place, partial, own_weight, other_weight, hidden, modulation, bias, final_weight, final_bias)
+    )(partial, weight, hidden, modulation, bias, final_weight, final_bias)
 
 
 def local(
@@ -407,17 +376,15 @@
     for i in range(ring):
         route += [(2 * i, 2 * ((i + 1) % ring)), (2 * i + 1, 2 * ((i - 1) % ring) + 1)]
     pass_on = lambda x: lax.ppermute(x, ("zh", "core"), route)
-    arrived = pass_on(lax.all_gather(own, "core", axis=0))
-
     packed = slabs[:, : heads * half].reshape(groups, heads, half, LANES)
-    packed = lax.all_gather(packed, "core", axis=0)
+    both, packed = after((lax.all_gather(own, "core", axis=0), lax.all_gather(packed, "core", axis=0)))
+    arrived = pass_on(both)
     opposite = lax.ppermute(packed, "xh", [(0, 1), (1, 0)])
     q = unpack_queries(xh.reshape(1), packed, opposite)
 
     columns = out_weight.shape[1] // 2
-    piece, _ = after((out_weight, packed))
-    piece = lax.dynamic_slice_in_dim(piece, core * columns, columns, 1)
-    pair = jnp.stack([piece, lax.ppermute(piece, "xh", [(0, 1), (1, 0)])])
+    piece = lax.dynamic_slice_in_dim(out_weight, core * columns, columns, 1)
+    weight = lax.all_gather(piece, ("core", "xh", "y"), axis=0, tiled=True).reshape(2, groups * width, columns)
 
     count = text_kv.shape[1]
     share = -(-count // 32) * 16
@@ -435,19 +402,14 @@
         kept.append(arrived)
     arrived, state = after((arrived, state))
     farthest = pass_on(lax.dynamic_index_in_dim(arrived, core, 0, keepdims=False))
-    turn = lambda d: lax.ppermute(pair, "y", [(i, (i - d) % across) for i in range(across)])
-    own_weight = jnp.concatenate([pair] + [turn(d) for d in range(1, across)], axis=0)
-    other_weight = lax.ppermute(own_weight, "core", [(0, 1), (1, 0)])
     state = next_blocks(q, state, arrived)
     partial = last_block(valid, q, state, farthest, text, kept)
     partial = partial.reshape(4 * groups, half, 4 * LANES)
     partial = lax.all_to_all(partial, BLOCK_AXES, split_axis=0, concat_axis=0, tiled=True)
 
     velocity = finish(
-        jnp.stack([core, xh, y]),
         partial,
-        own_weight,
-        other_weight,
+        weight,
         hidden_in[0],
         modulation[0],
         out_bias[None],

time: 177 us -> 183 us (1.034)
  the two profiles are of different devices: /device:TPU:40 before, /device:TPU:168 now
where the time goes in v4:
time: 183 us; the launch traced here: 182 us
  Pallas kernels  58.7 us (32%)
  waiting for transfers between devices  46.2 us (25%)
  starting transfers between devices  31.7 us (17%)
  blocking collectives  17.1 us (9%)
  between operations  15.6 us (9%)
  local copies, waits for them, and re-layouts  12.1 us (7%)
    pallas_call x5, Pallas kernels, attention_call(): pl.pallas_call(kernel, grid=(rows // tile,), out_shape=out_shape, in_spec...  54.4 us
    ppermute x4, waiting for transfers between devices, local(): pass_on = lambda x: lax.ppermute(x, ('zh', 'core'), route)  23.9 us
    ppermute x4, starting transfers between devices, local(): pass_on = lambda x: lax.ppermute(x, ('zh', 'core'), route)  15.5 us
    all_to_all x1, waiting for transfers between devices, local(): lax.all_to_all(partial, BLOCK_AXES, split_axis=0, concat_axis=0, tiled=True)  13.2 us
    all_to_all x1, blocking collectives, local(): lax.all_to_all(slabs, HEAD_AXES, split_axis=0, concat_axis=0, tiled=True)  12.8 us
    unnamed x23, local copies, waits for them, and re-layouts  8.42 us
    ppermute x1, waiting for transfers between devices, local(): opposite = lax.ppermute(packed, 'xh', [(0, 1), (1, 0)])  7.1 us
    ppermute x1, starting transfers between devices, local(): opposite = lax.ppermute(packed, 'xh', [(0, 1), (1, 0)])  4.93 us
  transfers between devices with their start and end apart: 9, of which 6 were waited for; matrix products, arithmetic and copies ran while one was open for 1% of the time, Pallas kernels for 30%

profile of v4, /device:TPU:168, one launch (start us, length us, event | category | flops | bytes accessed | tf_op | source)
XLA Modules:
  0.0 182.1 jit_solution(6731395923935412329)
XLA Ops:
  7.2 1.0 copy-done
  8.2 0.8 constant_dynamic-slice_fusion
  9.0 1.0 copy-done.2
  10.2 12.8 %all_to_all.10 = bf16[8,216,128]{2,1,0:T(8,128)(2,1)S(1)} all-to-all(bf16[8,216,128]{2,1,0:T(8,128)(2,1)S(1)} %pack_heads.1), channel_id=1, replica_groups=mesh['cfg'=2,'zh'=8,'zl'=2,'core'=2,'xh'=2,'y'=4] {'zl','y'}, dimensions={0} | all-to-all | bytes 884736 | tf_op jit(solution)/shard_map/all_to_all | solution.py:373
  23.0 2.0 %all_gather.10.own_ref = bf16[2,8,3,24,128]{4,3,2,1,0:T(8,128)(2,1)S(1)} all-gather(bf16[1,8,3,24,128]{4,3,2,1,0:T(8,128)(2,1)S(1)} %bitcast.39), channel_id=1, replica_groups=mesh['cfg'=2,'zh'=8,'zl'=2,'core'=2,'xh'=2,'y'=4] {'core'}, dimensions={0}, use_global_device_ids=true | all-gather | bytes 442368 | tf_op jit(solution)/shard_map/all_gather | solution.py:380
  25.0 2.3 %all_gather.9 = bf16[2,8,3,48,128]{4,3,2,1,0:T(8,128)(2,1)} all-gather(bf16[1,8,3,48,128]{4,3,2,1,0:T(8,128)(2,1)S(1)} %bitcast.30), channel_id=1, replica_groups=mesh['cfg'=2,'zh'=8,'zl'=2,'core'=2,'xh'=2,'y'=4] {'core'}, dimensions={0}, use_global_device_ids=true | all-gather | bytes 884736 | tf_op jit(solution)/shard_map/all_gather | solution.py:380
  27.4 5.2 %collective-permute-start.1 = (bf16[2,8,3,48,128]{4,3,2,1,0:T(8,128)(2,1)}, bf16[2,8,3,48,128]{4,3,2,1,0:T(8,128)(2,1)}, u32[]{:S(2)}, u32[]{:S(2)}) collective-permute-start(bf16[2,8,3,48,128]{4,3,2,1,0:T(8,128)(2,1)} %all_gather.9), channel_id=1, source_target_pairs={{0,32},{8,232},{32,64},{40,8},{64,96},{72,40},{96,128},{104,72},{1... | collective-permute-start | bytes 1769480 | tf_op jit(solution)/shard_map/ppermute | solution.py:378
  32.6 4.9 %collective-permute-start = (bf16[2,8,3,24,128]{4,3,2,1,0:T(8,128)(2,1)S(1)}, bf16[2,8,3,24,128]{4,3,2,1,0:T(8,128)(2,1)S(1)}, u32[]{:S(2)}, u32[]{:S(2)}) collective-permute-start(bf16[2,8,3,24,128]{4,3,2,1,0:T(8,128)(2,1)S(1)} %all_gather.10.own_ref), channel_id=1, source_target_pairs={{0,4},{4,0},{1,5},{5,1},{2,6},{6,2},{3,7},{7,3},{8,12},{12,8},{9,1... | collective-permute-start | bytes 884744 | tf_op jit(solution)/shard_map/ppermute | solution.py:382
  37.8 7.1 %collective-permute-done.other_ref = bf16[2,8,3,24,128]{4,3,2,1,0:T(8,128)(2,1)S(1)} collective-permute-done((bf16[2,8,3,24,128]{4,3,2,1,0:T(8,128)(2,1)S(1)}, bf16[2,8,3,24,128]{4,3,2,1,0:T(8,128)(2,1)S(1)}, u32[]{:S(2)}, u32[]{:S(2)}) %collective-permute-start) | collective-permute-done | bytes 294944 | tf_op jit(solution)/shard_map/ppermute | solution.py:382
  44.9 0.8 unpack_queries.1.q_ref
  45.7 6.3 %own_block.1 = (bf16[3,2,768,256]{3,2,1,0:T(8,128)(2,1)S(1)}, f32[3,2,768,128]{3,2,1,0:T(8,128)S(1)}) custom-call(s32[1]{0:T(128)} %bitcast.valid_ref, bf16[3,2,768,256]{3,2,1,0:T(8,128)(2,1)S(1)} %unpack_queries.1.q_ref, bf16[8,3,48,128]{3,2,1,0:T(8,128)(2,1)S(1)} %bitcast.31, bf16[3,176,128]{2,1,0:T(8,128)(2,1)S(1)} %pad_dynamic-slice_fusion.text_ref), custom_call_target="tpu_custom_call" | custom-call | flops 1981808640 | bytes 4718592 | tf_op jit(solution)/shard_map/own_block/pallas_call | solution.py:242
  52.1 4.8 %collective-permute-start.2 = (bf16[2,8,3,48,128]{4,3,2,1,0:T(8,128)(2,1)}, bf16[2,8,3,48,128]{4,3,2,1,0:T(8,128)(2,1)}, u32[]{:S(2)}, u32[]{:S(2)}) collective-permute-start(bf16[2,8,3,48,128]{4,3,2,1,0:T(8,128)(2,1)} %collective-permute-done.1.blocks_ref.refs_1_), channel_id=1, source_target_pairs={{0,32},{8,232},{32,64},{40,8},{64,96},{72,40},{96,128},{104,72},{1... | collective-permute-start | bytes 1769480 | tf_op jit(solution)/shard_map/ppermute | solution.py:378
  56.9 5.8 %next_blocks.3.state_ref = f32[3,2,768,128]{3,2,1,0:T(8,128)S(1)} custom-call(bf16[3,2,768,256]{3,2,1,0:T(8,128)(2,1)S(1)} %get-tuple-element.13.q_ref, f32[3,2,768,128]{3,2,1,0:T(8,128)S(1)} %get-tuple-element.17.state_ref, bf16[2,8,3,48,128]{4,3,2,1,0:T(8,128)(2,1)} %collective-permute-done.1.blocks_ref.refs_1_), custom_call_target="tpu_custom_call" | custom-call | flops 2717908992 | bytes 4718592 | tf_op jit(solution)/shard_map/next_blocks/pallas_call | solution.py:242
  62.7 1.4 copy-done.6
  64.1 8.5 %collective-permute-done.2.blocks_ref.refs_2_ = bf16[2,8,3,48,128]{4,3,2,1,0:T(8,128)(2,1)} collective-permute-done((bf16[2,8,3,48,128]{4,3,2,1,0:T(8,128)(2,1)}, bf16[2,8,3,48,128]{4,3,2,1,0:T(8,128)(2,1)}, u32[]{:S(2)}, u32[]{:S(2)}) %collective-permute-start.2) | collective-permute-done | bytes 589856 | tf_op jit(solution)/shard_map/ppermute | solution.py:378
  72.6 3.5 %collective-permute-start.3 = (bf16[2,8,3,48,128]{4,3,2,1,0:T(8,128)(2,1)}, bf16[2,8,3,48,128]{4,3,2,1,0:T(8,128)(2,1)}, u32[]{:S(2)}, u32[]{:S(2)}) collective-permute-start(bf16[2,8,3,48,128]{4,3,2,1,0:T(8,128)(2,1)} %collective-permute-done.2.blocks_ref.refs_2_), channel_id=1, source_target_pairs={{0,32},{8,232},{32,64},{40,8},{64,96},{72,40},{96,128},{104,72},{1... | collective-permute-start | bytes 1769480 | tf_op jit(solution)/shard_map/ppermute | solution.py:378
  76.1 1.7 copy-done.7
  77.8 5.7 %next_blocks.4.state_ref = f32[3,2,768,128]{3,2,1,0:T(8,128)S(1)} custom-call(bf16[3,2,768,256]{3,2,1,0:T(8,128)(2,1)S(1)} %get-tuple-element.13.q_ref, f32[3,2,768,128]{3,2,1,0:T(8,128)S(1)} %copy-done.7, bf16[2,8,3,48,128]{4,3,2,1,0:T(8,128)(2,1)} %collective-permute-done.2.blocks_ref.refs_2_), custom_call_target="tpu_custom_call" | custom-call | flops 2717908992 | bytes 4718592 | tf_op jit(solution)/shard_map/next_blocks/pallas_call | solution.py:242
  83.5 9.5 %collective-permute-done.3.blocks_ref.refs_3_ = bf16[2,8,3,48,128]{4,3,2,1,0:T(8,128)(2,1)} collective-permute-done((bf16[2,8,3,48,128]{4,3,2,1,0:T(8,128)(2,1)}, bf16[2,8,3,48,128]{4,3,2,1,0:T(8,128)(2,1)}, u32[]{:S(2)}, u32[]{:S(2)}) %collective-permute-start.3) | collective-permute-done | bytes 589856 | tf_op jit(solution)/shard_map/ppermute | solution.py:378
  93.0 1.0 dynamic-slice_bitcast_fusion
  94.0 2.1 %collective-permute-start.4 = (bf16[8,3,48,128]{3,2,1,0:T(8,128)(2,1)S(1)}, bf16[8,3,48,128]{3,2,1,0:T(8,128)(2,1)S(1)}, u32[]{:S(2)}, u32[]{:S(2)}) collective-permute-start(bf16[8,3,48,128]{3,2,1,0:T(8,128)(2,1)S(1)} %dynamic-slice_bitcast_fusion), channel_id=1, source_target_pairs={{0,32},{8,232},{32,64},{40,8},{64,96},{72,40},{96,128},{104,72},{1... | collective-permute-start | bytes 884744 | tf_op jit(solution)/shard_map/ppermute | solution.py:378
  96.1 5.8 %next_blocks.5.state_ref = f32[3,2,768,128]{3,2,1,0:T(8,128)S(1)} custom-call(bf16[3,2,768,256]{3,2,1,0:T(8,128)(2,1)S(1)} %get-tuple-element.13.q_ref, f32[3,2,768,128]{3,2,1,0:T(8,128)S(1)} %next_blocks.4.state_ref, bf16[2,8,3,48,128]{4,3,2,1,0:T(8,128)(2,1)} %collective-permute-done.3.blocks_ref.refs_3_), custom_call_target="tpu_custom_call" | custom-call | flops 2717908992 | bytes 4718592 | tf_op jit(solution)/shard_map/next_blocks/pallas_call | solution.py:242
  101.9 5.9 %collective-permute-done.4.block_ref = bf16[8,3,48,128]{3,2,1,0:T(8,128)(2,1)S(1)} collective-permute-done((bf16[8,3,48,128]{3,2,1,0:T(8,128)(2,1)S(1)}, bf16[8,3,48,128]{3,2,1,0:T(8,128)(2,1)S(1)}, u32[]{:S(2)}, u32[]{:S(2)}) %collective-permute-start.4) | collective-permute-done | bytes 294944 | tf_op jit(solution)/shard_map/ppermute | solution.py:378
  107.8 30.8 %last_block.1 = bf16[768,512]{1,0:T(8,128)(2,1)} custom-call(s32[1]{0:T(128)} %bitcast.valid_ref, bf16[3,2,768,256]{3,2,1,0:T(8,128)(2,1)S(1)} %get-tuple-element.13.q_ref, f32[3,2,768,128]{3,2,1,0:T(8,128)S(1)} %next_blocks.5.state_ref, bf16[8,3,48,128]{3,2,1,0:T(8,128)(2,1)S(1)} %collective-permute-done.4.block_ref, ...), custom_call_target="tpu_custom_call" | custom-call | flops 1981808640 | bytes 4718592 | tf_op jit(solution)/shard_map/last_block/pallas_call | solution.py:242
  138.6 4.9 %all-to-all-start.1 = ((bf16[32,24,512]{2,1,0:T(8,128)(2,1)}), bf16[32,24,512]{2,1,0:T(8,128)(2,1)S(1)}, u32[]{:S(2)}, u32[]{:S(2)}) async-start(bf16[32,24,512]{2,1,0:T(8,128)(2,1)} %bitcast.11), calls=%async_computation.1 | async-start | bytes 1572864 | tf_op jit(solution)/shard_map/all_to_all | solution.py:408
  144.2 13.2 %all-to-all-done.1.partial_ref = bf16[32,24,512]{2,1,0:T(8,128)(2,1)S(1)} async-done(((bf16[32,24,512]{2,1,0:T(8,128)(2,1)}), bf16[32,24,512]{2,1,0:T(8,128)(2,1)S(1)}, u32[]{:S(2)}, u32[]{:S(2)}) %all-to-all-start.1) | async-done | bytes 786464 | tf_op jit(solution)/shard_map/all_to_all | solution.py:408
  157.5 2.3 %copy-done.1 = bf16[3072,768]{1,0:T(8,128)(2,1)S(1)} copy-done((bf16[3072,768]{1,0:T(8,128)(2,1)S(1)}, bf16[3072,768]{1,0:T(8,128)(2,1)}, u32[]{:S(2)}) %copy-start.1) | copy-done | bytes 4718616
  159.8 0.9 copy-done.3
  160.7 3.3 %project_and_norm.1 = f32[48,64]{1,0:T(8,128)S(1)} custom-call(bf16[32,24,512]{2,1,0:T(8,128)(2,1)S(1)} %all-to-all-done.1.partial_ref, bf16[2,1536,768]{2,1,0:T(8,128)(2,1)S(1)} %bitcast.29, bf16[48,1536]{1,0:T(8,128)(2,1)S(1)} %bitcast.35, f32[3,1536]{1,0:T(4,128)S(1)} %bitcast.36, f32[1,1536]{1,0:T(1,128)S(1)} %broadcast_in_dim.6.bias_ref, ...), custom_call_target="tpu_custom_call" | custom-call | tf_op jit(solution)/shard_map/project_and_norm/pallas_call | solution.py:340
  164.4 3.2 %collective-permute-start.5 = (f32[1536]{0:T(1024)S(1)}, f32[1536]{0:T(1024)S(1)}, u32[]{:S(2)}, u32[]{:S(2)}) collective-permute-start(f32[1536]{0:T(1024)S(1)} %get-tuple-element.22), channel_id=1, source_target_pairs={{0,1},{1,257},{2,3},{3,259},{256,0},{257,256},{258,2},{259,258},{4... | collective-permute-start | bytes 18440 | tf_op jit(solution)/shard_map/ppermute | solution.py:431
  167.6 3.1 %collective-permute-start.6 = (f32[1536]{0:T(1024)S(1)}, f32[1536]{0:T(1024)S(1)}, u32[]{:S(2)}, u32[]{:S(2)}) collective-permute-start(f32[1536]{0:T(1024)S(1)} %get-tuple-element.23), channel_id=1, source_target_pairs={{0,0},{1,256},{2,2},{3,258},{256,1},{257,257},{258,3},{259,259},{4... | collective-permute-start | bytes 18440 | tf_op jit(solution)/shard_map/ppermute | solution.py:430
  172.0 2.0 %collective-permute-done.6 = f32[1536]{0:T(1024)S(1)} collective-permute-done((f32[1536]{0:T(1024)S(1)}, f32[1536]{0:T(1024)S(1)}, u32[]{:S(2)}, u32[]{:S(2)}) %collective-permute-start.6) | collective-permute-done | bytes 6176 | tf_op jit(solution)/shard_map/ppermute | solution.py:430
  (36 shorter events, 2.8 us)
Async XLA Ops:
  7.2 1.1 copy-start
  7.2 150.3 %all-gather.2.cloned.1.call-start = ((), (), s32[]{:S(2)}) async-start(), calls=%async_computation.2 | async-start | bytes 5013504 | tf_op jit(solution)/shard_map/all_gather | solution.py:387
  8.2 29.3 %copy-start.8 = (bf16[1,333,2,192]{1,3,2,0:T(8,128)(2,1)S(1)}, bf16[1,333,2,192]{1,3,2,0:T(8,128)(2,1)}, u32[]{:S(2)}) copy-start(bf16[1,333,2,192]{1,3,2,0:T(8,128)(2,1)} %param.12) | copy-start | bytes 767236
  9.0 1.0 copy-start.2
  27.4 24.7 %collective-permute-start.1 = (bf16[2,8,3,48,128]{4,3,2,1,0:T(8,128)(2,1)}, bf16[2,8,3,48,128]{4,3,2,1,0:T(8,128)(2,1)}, u32[]{:S(2)}, u32[]{:S(2)}) collective-permute-start(bf16[2,8,3,48,128]{4,3,2,1,0:T(8,128)(2,1)} %all_gather.9), channel_id=1, source_target_pairs={{0,32},{8,232},{32,64},{40,8},{64,96},{72,40},{96,128},{104,72},{1... | collective-permute-start | bytes 1769480 | tf_op jit(solution)/shard_map/ppermute | solution.py:378
  32.6 12.4 %collective-permute-start = (bf16[2,8,3,24,128]{4,3,2,1,0:T(8,128)(2,1)S(1)}, bf16[2,8,3,24,128]{4,3,2,1,0:T(8,128)(2,1)S(1)}, u32[]{:S(2)}, u32[]{:S(2)}) collective-permute-start(bf16[2,8,3,24,128]{4,3,2,1,0:T(8,128)(2,1)S(1)} %all_gather.10.own_ref), channel_id=1, source_target_pairs={{0,4},{4,0},{1,5},{5,1},{2,6},{6,2},{3,7},{7,3},{8,12},{12,8},{9,1... | collective-permute-start | bytes 884744 | tf_op jit(solution)/shard_map/ppermute | solution.py:382
  52.1 20.5 %collective-permute-start.2 = (bf16[2,8,3,48,128]{4,3,2,1,0:T(8,128)(2,1)}, bf16[2,8,3,48,128]{4,3,2,1,0:T(8,128)(2,1)}, u32[]{:S(2)}, u32[]{:S(2)}) collective-permute-start(bf16[2,8,3,48,128]{4,3,2,1,0:T(8,128)(2,1)} %collective-permute-done.1.blocks_ref.refs_1_), channel_id=1, source_target_pairs={{0,32},{8,232},{32,64},{40,8},{64,96},{72,40},{96,128},{104,72},{1... | collective-permute-start | bytes 1769480 | tf_op jit(solution)/shard_map/ppermute | solution.py:378
  62.7 1.5 copy-start.6
  72.6 20.4 %collective-permute-start.3 = (bf16[2,8,3,48,128]{4,3,2,1,0:T(8,128)(2,1)}, bf16[2,8,3,48,128]{4,3,2,1,0:T(8,128)(2,1)}, u32[]{:S(2)}, u32[]{:S(2)}) collective-permute-start(bf16[2,8,3,48,128]{4,3,2,1,0:T(8,128)(2,1)} %collective-permute-done.2.blocks_ref.refs_2_), channel_id=1, source_target_pairs={{0,32},{8,232},{32,64},{40,8},{64,96},{72,40},{96,128},{104,72},{1... | collective-permute-start | bytes 1769480 | tf_op jit(solution)/shard_map/ppermute | solution.py:378
  76.1 1.7 copy-start.7
  94.0 13.8 %collective-permute-start.4 = (bf16[8,3,48,128]{3,2,1,0:T(8,128)(2,1)S(1)}, bf16[8,3,48,128]{3,2,1,0:T(8,128)(2,1)S(1)}, u32[]{:S(2)}, u32[]{:S(2)}) collective-permute-start(bf16[8,3,48,128]{3,2,1,0:T(8,128)(2,1)S(1)} %dynamic-slice_bitcast_fusion), channel_id=1, source_target_pairs={{0,32},{8,232},{32,64},{40,8},{64,96},{72,40},{96,128},{104,72},{1... | collective-permute-start | bytes 884744 | tf_op jit(solution)/shard_map/ppermute | solution.py:378
  101.9 41.6 %copy-start.9 = (f32[1,3,1536]{2,0,1:T(1,128)S(1)}, f32[1,3,1536]{2,0,1:T(1,128)}, u32[]{:S(2)}) copy-start(f32[1,3,1536]{2,0,1:T(1,128)} %param.14) | copy-start | bytes 55300
  101.9 55.6 %copy-start.4 = (bf16[1,48,1536]{2,1,0:T(8,128)(2,1)S(1)}, bf16[1,48,1536]{2,1,0:T(8,128)(2,1)}, u32[]{:S(2)}) copy-start(bf16[1,48,1536]{2,1,0:T(8,128)(2,1)} %param.13) | copy-start | bytes 442372
  101.9 55.6 %copy-start.5 = (f32[64]{0:T(128)S(1)}, f32[64]{0:T(128)}, u32[]{:S(2)}) copy-start(f32[64]{0:T(128)} %param.18) | copy-start | bytes 772
  138.6 18.9 %all-to-all-start.1 = ((bf16[32,24,512]{2,1,0:T(8,128)(2,1)}), bf16[32,24,512]{2,1,0:T(8,128)(2,1)S(1)}, u32[]{:S(2)}, u32[]{:S(2)}) async-start(bf16[32,24,512]{2,1,0:T(8,128)(2,1)} %bitcast.11), calls=%async_computation.1 | async-start | bytes 1572864 | tf_op jit(solution)/shard_map/all_to_all | solution.py:408
  157.5 2.3 %copy-start.1 = (bf16[3072,768]{1,0:T(8,128)(2,1)S(1)}, bf16[3072,768]{1,0:T(8,128)(2,1)}, u32[]{:S(2)}) copy-start(bf16[3072,768]{1,0:T(8,128)(2,1)} %all-gather.2.cloned.1.call-done) | copy-start | bytes 14155780
  159.8 0.9 copy-start.3
  160.7 13.9 %copy-start.10 = (f32[1,1536]{1,0:T(1,128)S(1)}, f32[1,1536]{1,0:T(1,128)}, u32[]{:S(2)}) copy-start(f32[1,1536]{1,0:T(1,128)} %param.21) | copy-start | bytes 18436
  164.4 7.6 %collective-permute-start.5 = (f32[1536]{0:T(1024)S(1)}, f32[1536]{0:T(1024)S(1)}, u32[]{:S(2)}, u32[]{:S(2)}) collective-permute-start(f32[1536]{0:T(1024)S(1)} %get-tuple-element.22), channel_id=1, source_target_pairs={{0,1},{1,257},{2,3},{3,259},{256,0},{257,256},{258,2},{259,258},{4... | collective-permute-start | bytes 18440 | tf_op jit(solution)/shard_map/ppermute | solution.py:431
  167.6 6.4 %collective-permute-start.6 = (f32[1536]{0:T(1024)S(1)}, f32[1536]{0:T(1024)S(1)}, u32[]{:S(2)}, u32[]{:S(2)}) collective-permute-start(f32[1536]{0:T(1024)S(1)} %get-tuple-element.23), channel_id=1, source_target_pairs={{0,0},{1,256},{2,2},{3,258},{256,1},{257,257},{258,3},{259,259},{4... | collective-permute-start | bytes 18440 | tf_op jit(solution)/shard_map/ppermute | solution.py:430
Sparse Core Ops, SparseCore 0:
  11.4 75.8 all-gather.1

commit v5 on v4

--- a/solution.py
+++ b/solution.py
@@ -10,7 +10,7 @@
 
 HEAD_DIM = 64
 LANES = 128
-ROW_TILE = 256
+ROW_TILE = 768
 LOG2_SCALE = math.log2(math.e) * HEAD_DIM**-0.5
 F32 = jnp.float32
 BF16 = jnp.bfloat16
@@ -106,10 +106,7 @@
 
 
 def rows_of(ref, head):
-    lanes = ref.shape[-1]
-    if len(ref.shape) == 4:
-        return ref[:, head].reshape(-1, lanes)
-    return jnp.concatenate([ref[n, :, head].reshape(-1, lanes) for n in range(ref.shape[0])], axis=0)
+    return ref[:, head].reshape(-1, ref.shape[-1])
 
 
 def scores_of(q, keys):
@@ -141,20 +138,18 @@
         full_ref[head, :, :, LANES:] = upper.astype(BF16).reshape(state_ref.shape[1:])
 
 
-def next_kernel(heads, q_ref, state_ref, blocks_ref, out_ref):
+def next_kernel(heads, q_ref, state_ref, *refs):
+    *blocks, out_ref = refs
     rows = 2 * q_ref.shape[2]
     for head in range(heads):
         q = q_ref[head].reshape(rows, 2 * LANES)
-        keys, values = wide_keys(rows_of(blocks_ref, head))
+        keys, values = wide_keys(jnp.concatenate([rows_of(ref, head) for ref in blocks], axis=0))
         state = weighted(scores_of(q, keys), values)
         out_ref[head] = state_ref[head] + state.reshape(out_ref.shape[1:])
 
 
-def last_kernel(heads, count, valid_ref, q_ref, state_ref, block_ref, text_ref, *refs):
+def last_kernel(heads, count, valid_ref, q_ref, state_ref, block_ref, first_text_ref, text_ref, *refs):
     kept, out_ref, done_ref, top_ref, spare_ref, sem = refs[:count], *refs[count:]
-    parts = []
-    for ref in kept:
-        parts += [ref] if len(ref.shape) == 4 else [ref.at[n] for n in range(ref.shape[0])]
     tile = q_ref.shape[2]
     rows = 2 * tile
     lane = lane_index((rows, LANES))
@@ -162,7 +157,10 @@
     for head in range(heads):
         q = q_ref[head].reshape(rows, 2 * LANES)
         keys, values = wide_keys(rows_of(block_ref, head))
-        state = weighted(scores_of(q, keys), values) + state_ref[head].reshape(rows, LANES)
+        more_keys, more_values = wide_keys(text_ref[head], valid_ref[0] - first_text_ref.shape[1])
+        scores = scores_of(q, jnp.concatenate([keys, more_keys], axis=0))
+        state = weighted(scores, jnp.concatenate([values, more_values], axis=0))
+        state = state + state_ref[head].reshape(rows, LANES)
         done_ref[head] = state
         top_ref[head] = q[:, LANES:].astype(F32)
         largest = jnp.max(jnp.where(state[:, :HEAD_DIM] < SAFE, 0.0, 1.0))
@@ -170,11 +168,11 @@
 
     @pl.when(jnp.logical_not(safe))
     def _():
-        for at, ref in enumerate(parts):
+        for at, ref in enumerate(kept):
             copy = pltpu.make_async_copy(ref, spare_ref.at[at], sem)
             copy.start()
             copy.wait()
-        spare_ref[len(parts)] = block_ref[...]
+        spare_ref[count] = block_ref[...]
         for head in range(heads):
             q = q_ref[head].reshape(rows, 2 * LANES)
             spared = (lane >= HEAD_DIM) & (lane < GUARD)
@@ -189,8 +187,10 @@
                 return absorb(*wide_keys(spare_ref[at, :, head].reshape(-1, LANES)), *carry)
 
             carry = (jnp.full((rows, 1), -1e30, F32), jnp.zeros((rows, LANES), F32))
-            carry = lax.fori_loop(0, len(parts) + 1, step, carry)
-            largest, state = absorb(*wide_keys(text_ref[head], valid_ref[0]), *carry)
+            carry = lax.fori_loop(0, count + 1, step, carry)
+            carry = absorb(*wide_keys(first_text_ref[head], valid_ref[0]), *carry)
+            tail = wide_keys(text_ref[head], valid_ref[0] - first_text_ref.shape[1])
+            largest, state = absorb(*tail, *carry)
             done_ref[head] = state
             offset = jnp.broadcast_to(-largest, (rows, LANES))
             coarse = offset.astype(BF16).astype(F32)
@@ -264,10 +264,10 @@
 
 def next_blocks(q, state, blocks):
     kernel = functools.partial(next_kernel, q.shape[0])
-    return attention_call(kernel, "next_blocks", [q, state], [blocks], [], [state_shape(q)], [2])[0]
-
-
-def last_block(valid, q, state, block, text, kept):
+    return attention_call(kernel, "next_blocks", [q, state], blocks, [], [state_shape(q)], [2])[0]
+
+
+def last_block(valid, q, state, block, first_text, text, kept):
     heads, _, rows, _ = q.shape
     tile = ROW_TILE if rows % ROW_TILE == 0 else rows
     kernel = functools.partial(last_kernel, heads, len(kept))
@@ -275,10 +275,10 @@
     scratch = [
         pltpu.VMEM((heads, 2 * tile, LANES), F32),
         pltpu.VMEM((heads, 2 * tile, LANES), F32),
-        pltpu.VMEM((2 * len(kept),) + block.shape, BF16),
+        pltpu.VMEM((len(kept) + 1,) + block.shape, BF16),
         pltpu.SemaphoreType.DMA,
     ]
-    return attention_call(kernel, "last_block", [valid, q, state], [block, text], kept, [shape], [0], scratch)[0]
+    return attention_call(kernel, "last_block", [valid, q, state], [block, first_text, text], kept, [shape], [0], scratch)[0]
 
 
 def finish_kernel(
@@ -293,7 +293,11 @@
     final_bias_ref,
     out_ref,
     wide_ref,
+    held_ref,
+    sem,
 ):
+    brought = pltpu.make_async_copy(weight_ref, held_ref, sem)
+    brought.start()
     half = partial_ref.shape[1]
     sources = partial_ref.shape[0]
     across = groups // 2
@@ -321,8 +325,9 @@
             both = jnp.concatenate([first, second[:, :HEAD_DIM]], axis=1)
             wide_ref[part * half : (part + 1) * half, group * width : (group + 1) * width] = both
     attended = wide_ref[...].astype(BF16)
+    brought.wait()
     projected = jnp.concatenate(
-        [jnp.dot(attended, weight_ref[side], preferred_element_type=F32) for side in range(2)], axis=1
+        [jnp.dot(attended, held_ref[side], preferred_element_type=F32) for side in range(2)], axis=1
     )
     residual = hidden_ref[...].astype(F32) + modulation_ref[0:1] * (projected + bias_ref[...])
     middle = jnp.mean(residual, axis=-1, keepdims=True)
@@ -337,10 +342,17 @@
 
 def finish(partial, weight, hidden, modulation, bias, final_weight, final_bias, heads, groups):
     tokens, width = hidden.shape
+    vmem = pl.BlockSpec(memory_space=pltpu.VMEM)
     return pl.pallas_call(
         functools.partial(finish_kernel, heads, groups),
         out_shape=jax.ShapeDtypeStruct((tokens, final_weight.shape[0]), F32),
-        scratch_shapes=[pltpu.VMEM((tokens, width), F32)],
+        in_specs=[vmem, pl.BlockSpec(memory_space=pl.ANY), vmem, vmem, vmem, vmem, vmem],
+        out_specs=vmem,
+        scratch_shapes=[
+            pltpu.VMEM((tokens, width), F32),
+            pltpu.VMEM(weight.shape, BF16),
+            pltpu.SemaphoreType.DMA,
+        ],
         compiler_params=params(),
         name="project_and_norm",
     )(partial, weight, hidden, modulation, bias, final_weight, final_bias)
@@ -376,10 +388,12 @@
     for i in range(ring):
         route += [(2 * i, 2 * ((i + 1) % ring)), (2 * i + 1, 2 * ((i - 1) % ring) + 1)]
     pass_on = lambda x: lax.ppermute(x, ("zh", "core"), route)
+    near = pass_on(own)
+    beside = lax.ppermute(own, "core", [(0, 1), (1, 0)])
     packed = slabs[:, : heads * half].reshape(groups, heads, half, LANES)
-    both, packed = after((lax.all_gather(own, "core", axis=0), lax.all_gather(packed, "core", axis=0)))
-    arrived = pass_on(both)
+    packed = lax.all_gather(packed, "core", axis=0)
     opposite = lax.ppermute(packed, "xh", [(0, 1), (1, 0)])
+    cross = pass_on(beside)
     q = unpack_queries(xh.reshape(1), packed, opposite)
 
     columns = out_weight.shape[1] // 2
@@ -392,18 +406,24 @@
     text = jnp.pad(text, ((0, 0), (0, 2 * share - count), (0, 0)))
     text = lax.dynamic_slice_in_dim(text, core * share, share, 1)
     valid = jnp.where(xh == zl, jnp.minimum(count - core * share, share), 0).reshape(1)
-    q, state = first_block(valid, q, own, text)
-    kept = [own, arrived]
+    early, late = text[:, :LANES], text[:, LANES:]
+    q, state = first_block(valid, q, own, early)
+    kept = [own, near, cross]
+    ready = None
     for _ in range(ring // 2 - 2):
-        arrived, state = after((arrived, state))
-        further = pass_on(arrived)
-        state = next_blocks(q, state, arrived)
-        arrived = further
-        kept.append(arrived)
-    arrived, state = after((arrived, state))
-    farthest = pass_on(lax.dynamic_index_in_dim(arrived, core, 0, keepdims=False))
-    state = next_blocks(q, state, arrived)
-    partial = last_block(valid, q, state, farthest, text, kept)
+        if ready is not None:
+            near, ready = after((near, ready))
+        nearer = pass_on(near)
+        cross, state = after((cross, state))
+        crosser = pass_on(cross)
+        ready = state
+        state = next_blocks(q, state, [near, cross])
+        near, cross = nearer, crosser
+        kept += [near, cross]
+    near, ready = after((near, ready))
+    farthest = pass_on(near)
+    state = next_blocks(q, state, [near, cross])
+    partial = last_block(valid, q, state, farthest, early, late, kept)
     partial = partial.reshape(4 * groups, half, 4 * LANES)
     partial = lax.all_to_all(partial, BLOCK_AXES, split_axis=0, concat_axis=0, tiled=True)
 

time: 183 us -> 189 us (1.033)
  the two profiles are of different devices: /device:TPU:168 before, /device:TPU:1 now
where the time goes in v5:
time: 189 us; the launch traced here: 188 us
  Pallas kernels  73 us (39%)
  starting transfers between devices  57.7 us (31%)
  between operations  15.7 us (8%)
  blocking collectives  15.3 us (8%)
  waiting for transfers between devices  14.4 us (8%)
  local copies, waits for them, and re-layouts  11.1 us (6%)
    pallas_call x5, Pallas kernels, attention_call(): pl.pallas_call(kernel, grid=(rows // tile,), out_shape=out_shape, in_spec...  67.2 us
    ppermute x7, starting transfers between devices, local(): pass_on = lambda x: lax.ppermute(x, ('zh', 'core'), route)  32.6 us
    all_to_all x1, waiting for transfers between devices, local(): lax.all_to_all(partial, BLOCK_AXES, split_axis=0, concat_axis=0, tiled=True)  13.9 us
    all_to_all x1, blocking collectives, local(): lax.all_to_all(slabs, HEAD_AXES, split_axis=0, concat_axis=0, tiled=True)  13.3 us
    all_to_all x1, starting transfers between devices, local(): lax.all_to_all(partial, BLOCK_AXES, split_axis=0, concat_axis=0, tiled=True)  9.22 us
    unnamed x27, local copies, waits for them, and re-layouts  9.1 us
    ppermute x1, starting transfers between devices, local(): beside = lax.ppermute(own, 'core', [(0, 1), (1, 0)])  6.17 us
    pallas_call x1, Pallas kernels, finish(): pl.pallas_call(functools.partial(finish_kernel, heads, groups), out_shape...  4.81 us
  transfers between devices with their start and end apart: 13, of which 2 were waited for; matrix products, arithmetic and copies ran while one was open for 1% of the time, Pallas kernels for 36%

profile of v5, /device:TPU:1, one launch (start us, length us, event | category | flops | bytes accessed | tf_op | source)
XLA Modules:
  0.0 187.8 jit_solution(5183320561156209253)
XLA Ops:
  7.2 1.0 copy-done
  8.2 0.7 constant_dynamic-slice_fusion
  9.0 1.0 copy-done.2
  10.2 13.3 %all_to_all.10 = bf16[8,216,128]{2,1,0:T(8,128)(2,1)S(1)} all-to-all(bf16[8,216,128]{2,1,0:T(8,128)(2,1)S(1)} %pack_heads.1), channel_id=1, replica_groups=mesh['cfg'=2,'zh'=8,'zl'=2,'core'=2,'xh'=2,'y'=4] {'zl','y'}, dimensions={0} | all-to-all | bytes 884736 | tf_op jit(solution)/shard_map/all_to_all | solution.py:385
  23.5 6.2 %collective-permute-start.1 = (bf16[8,3,48,128]{3,2,1,0:T(8,128)(2,1)S(1)}, bf16[8,3,48,128]{3,2,1,0:T(8,128)(2,1)}, u32[]{:S(2)}, u32[]{:S(2)}) collective-permute-start(bf16[8,3,48,128]{3,2,1,0:T(8,128)(2,1)S(1)} %bitcast.27), channel_id=1, source_target_pairs={{0,8},{8,0},{1,9},{9,1},{2,10},{10,2},{3,11},{11,3},{4,12},{12,4},... | collective-permute-start | bytes 884744 | tf_op jit(solution)/shard_map/ppermute | solution.py:392
  29.7 9.5 %collective-permute-start.4 = (bf16[8,3,48,128]{3,2,1,0:T(8,128)(2,1)S(1)}, bf16[8,3,48,128]{3,2,1,0:T(8,128)(2,1)}, u32[]{:S(2)}, u32[]{:S(2)}) collective-permute-start(bf16[8,3,48,128]{3,2,1,0:T(8,128)(2,1)S(1)} %bitcast.28), channel_id=1, source_target_pairs={{0,32},{8,232},{32,64},{40,8},{64,96},{72,40},{96,128},{104,72},{1... | collective-permute-start | bytes 884744 | tf_op jit(solution)/shard_map/ppermute | solution.py:390
  39.2 2.0 %all_gather.6.own_ref = bf16[2,8,3,24,128]{4,3,2,1,0:T(8,128)(2,1)S(1)} all-gather(bf16[1,8,3,24,128]{4,3,2,1,0:T(8,128)(2,1)S(1)} %bitcast.37), channel_id=1, replica_groups=mesh['cfg'=2,'zh'=8,'zl'=2,'core'=2,'xh'=2,'y'=4] {'core'}, dimensions={0}, use_global_device_ids=true | all-gather | bytes 442368 | tf_op jit(solution)/shard_map/all_gather | solution.py:394
  41.2 4.6 %collective-permute-start = (bf16[2,8,3,24,128]{4,3,2,1,0:T(8,128)(2,1)S(1)}, bf16[2,8,3,24,128]{4,3,2,1,0:T(8,128)(2,1)S(1)}, u32[]{:S(2)}, u32[]{:S(2)}) collective-permute-start(bf16[2,8,3,24,128]{4,3,2,1,0:T(8,128)(2,1)S(1)} %all_gather.6.own_ref), channel_id=1, source_target_pairs={{0,4},{4,0},{1,5},{5,1},{2,6},{6,2},{3,7},{7,3},{8,12},{12,8},{9,1... | collective-permute-start | bytes 884744 | tf_op jit(solution)/shard_map/ppermute | solution.py:395
  45.8 3.1 %collective-permute-start.2 = (bf16[8,3,48,128]{3,2,1,0:T(8,128)(2,1)}, bf16[8,3,48,128]{3,2,1,0:T(8,128)(2,1)}, u32[]{:S(2)}, u32[]{:S(2)}) collective-permute-start(bf16[8,3,48,128]{3,2,1,0:T(8,128)(2,1)} %collective-permute-done.1), channel_id=1, source_target_pairs={{0,32},{8,232},{32,64},{40,8},{64,96},{72,40},{96,128},{104,72},{1... | collective-permute-start | bytes 884744 | tf_op jit(solution)/shard_map/ppermute | solution.py:390
  49.2 4.3 %collective-permute-start.5 = (bf16[8,3,48,128]{3,2,1,0:T(8,128)(2,1)}, bf16[8,3,48,128]{3,2,1,0:T(8,128)(2,1)}, u32[]{:S(2)}, u32[]{:S(2)}) collective-permute-start(bf16[8,3,48,128]{3,2,1,0:T(8,128)(2,1)} %collective-permute-done.4.refs_0_.refs_1_), channel_id=1, source_target_pairs={{0,32},{8,232},{32,64},{40,8},{64,96},{72,40},{96,128},{104,72},{1... | collective-permute-start | bytes 884744 | tf_op jit(solution)/shard_map/ppermute | solution.py:390
  53.6 0.8 unpack_queries.1.q_ref
  54.4 3.9 %own_block.1 = (bf16[3,2,768,256]{3,2,1,0:T(8,128)(2,1)S(1)}, f32[3,2,768,128]{3,2,1,0:T(8,128)S(1)}) custom-call(s32[1]{0:T(128)} %bitcast.valid_ref, bf16[3,2,768,256]{3,2,1,0:T(8,128)(2,1)S(1)} %unpack_queries.1.q_ref, bf16[8,3,48,128]{3,2,1,0:T(8,128)(2,1)S(1)} %bitcast.29, bf16[3,128,128]{2,1,0:T(8,128)(2,1)S(1)} %pad_dynamic-slice_fusion.text_ref.first_text_ref), custom_call_target="tpu_custom_call" | custom-call | flops 1811939328 | bytes 4718592 | tf_op jit(solution)/shard_map/own_block/pallas_call | solution.py:242
  58.3 1.4 copy-done.6
  59.8 3.1 %collective-permute-start.3 = (bf16[8,3,48,128]{3,2,1,0:T(8,128)(2,1)}, bf16[8,3,48,128]{3,2,1,0:T(8,128)(2,1)}, u32[]{:S(2)}, u32[]{:S(2)}) collective-permute-start(bf16[8,3,48,128]{3,2,1,0:T(8,128)(2,1)} %collective-permute-done.2.refs_1_.refs_2_), channel_id=1, source_target_pairs={{0,32},{8,232},{32,64},{40,8},{64,96},{72,40},{96,128},{104,72},{1... | collective-permute-start | bytes 884744 | tf_op jit(solution)/shard_map/ppermute | solution.py:390
  63.3 4.5 %collective-permute-start.6 = (bf16[8,3,48,128]{3,2,1,0:T(8,128)(2,1)}, bf16[8,3,48,128]{3,2,1,0:T(8,128)(2,1)S(1)}, u32[]{:S(2)}, u32[]{:S(2)}) collective-permute-start(bf16[8,3,48,128]{3,2,1,0:T(8,128)(2,1)} %collective-permute-done.5.refs_0_.refs_3_), channel_id=1, source_target_pairs={{0,32},{8,232},{32,64},{40,8},{64,96},{72,40},{96,128},{104,72},{1... | collective-permute-start | bytes 884744 | tf_op jit(solution)/shard_map/ppermute | solution.py:390
  67.8 1.7 copy-done.7
  69.5 5.0 %next_blocks.3.state_ref = f32[3,2,768,128]{3,2,1,0:T(8,128)S(1)} custom-call(bf16[3,2,768,256]{3,2,1,0:T(8,128)(2,1)S(1)} %get-tuple-element.10.q_ref, f32[3,2,768,128]{3,2,1,0:T(8,128)S(1)} %copy-done.7, bf16[8,3,48,128]{3,2,1,0:T(8,128)(2,1)} %collective-permute-done.4.refs_0_.refs_1_, bf16[8,3,48,128]{3,2,1,0:T(8,128)(2,1)} %collective-permute-done.2.refs_1_.refs_2_), custom_call_target="tpu_custom_call" | custom-call | flops 2717908992 | bytes 4718592 | tf_op jit(solution)/shard_map/next_blocks/pallas_call | solution.py:242
  74.5 3.9 %collective-permute-start.7 = (bf16[8,3,48,128]{3,2,1,0:T(8,128)(2,1)}, bf16[8,3,48,128]{3,2,1,0:T(8,128)(2,1)S(1)}, u32[]{:S(2)}, u32[]{:S(2)}) collective-permute-start(bf16[8,3,48,128]{3,2,1,0:T(8,128)(2,1)} %collective-permute-done.3.refs_1_.refs_4_), channel_id=1, source_target_pairs={{0,32},{8,232},{32,64},{40,8},{64,96},{72,40},{96,128},{104,72},{1... | collective-permute-start | bytes 884744 | tf_op jit(solution)/shard_map/ppermute | solution.py:390
  78.4 4.3 %collective-permute-start.8 = (bf16[8,3,48,128]{3,2,1,0:T(8,128)(2,1)S(1)}, bf16[8,3,48,128]{3,2,1,0:T(8,128)(2,1)S(1)}, u32[]{:S(2)}, u32[]{:S(2)}) collective-permute-start(bf16[8,3,48,128]{3,2,1,0:T(8,128)(2,1)S(1)} %collective-permute-done.6.refs_0_.refs_5_), channel_id=1, source_target_pairs={{0,32},{8,232},{32,64},{40,8},{64,96},{72,40},{96,128},{104,72},{1... | collective-permute-start | bytes 884744 | tf_op jit(solution)/shard_map/ppermute | solution.py:390
  82.8 5.0 %next_blocks.4.state_ref = f32[3,2,768,128]{3,2,1,0:T(8,128)S(1)} custom-call(bf16[3,2,768,256]{3,2,1,0:T(8,128)(2,1)S(1)} %get-tuple-element.10.q_ref, f32[3,2,768,128]{3,2,1,0:T(8,128)S(1)} %next_blocks.3.state_ref, bf16[8,3,48,128]{3,2,1,0:T(8,128)(2,1)} %collective-permute-done.5.refs_0_.refs_3_, ...), custom_call_target="tpu_custom_call" | custom-call | flops 2717908992 | bytes 4718592 | tf_op jit(solution)/shard_map/next_blocks/pallas_call | solution.py:242
  87.8 3.9 %next_blocks.5.state_ref = f32[3,2,768,128]{3,2,1,0:T(8,128)S(1)} custom-call(bf16[3,2,768,256]{3,2,1,0:T(8,128)(2,1)S(1)} %get-tuple-element.10.q_ref, f32[3,2,768,128]{3,2,1,0:T(8,128)S(1)} %next_blocks.4.state_ref, bf16[8,3,48,128]{3,2,1,0:T(8,128)(2,1)S(1)} %collective-permute-done.6.refs_0_.refs_5_, ...), custom_call_target="tpu_custom_call" | custom-call | flops 2717908992 | bytes 4718592 | tf_op jit(solution)/shard_map/next_blocks/pallas_call | solution.py:242
  91.7 49.4 %last_block.1 = bf16[768,512]{1,0:T(8,128)(2,1)} custom-call(s32[1]{0:T(128)} %bitcast.valid_ref, bf16[3,2,768,256]{3,2,1,0:T(8,128)(2,1)S(1)} %get-tuple-element.10.q_ref, f32[3,2,768,128]{3,2,1,0:T(8,128)S(1)} %next_blocks.5.state_ref, bf16[8,3,48,128]{3,2,1,0:T(8,128)(2,1)S(1)} %collective-permute-done.8.block_ref, ...), custom_call_target="tpu_custom_call" | custom-call | flops 1981808640 | bytes 4718592 | tf_op jit(solution)/shard_map/last_block/pallas_call | solution.py:242
  141.1 9.2 %all-to-all-start.1 = ((bf16[32,24,512]{2,1,0:T(8,128)(2,1)}), bf16[32,24,512]{2,1,0:T(8,128)(2,1)S(1)}, u32[]{:S(2)}, u32[]{:S(2)}) async-start(bf16[32,24,512]{2,1,0:T(8,128)(2,1)} %bitcast.9), calls=%async_computation.1 | async-start | bytes 1572864 | tf_op jit(solution)/shard_map/all_to_all | solution.py:428
  150.3 0.7 copy.24
  151.1 13.9 %all-to-all-done.1.partial_ref = bf16[32,24,512]{2,1,0:T(8,128)(2,1)S(1)} async-done(((bf16[32,24,512]{2,1,0:T(8,128)(2,1)}), bf16[32,24,512]{2,1,0:T(8,128)(2,1)S(1)}, u32[]{:S(2)}, u32[]{:S(2)}) %all-to-all-start.1) | async-done | bytes 786464 | tf_op jit(solution)/shard_map/all_to_all | solution.py:428
  165.0 2.3 %copy-done.1 = bf16[3072,768]{1,0:T(8,128)(2,1)S(1)} copy-done((bf16[3072,768]{1,0:T(8,128)(2,1)S(1)}, bf16[3072,768]{1,0:T(8,128)(2,1)}, u32[]{:S(2)}) %copy-start.1) | copy-done | bytes 4718616
  167.3 0.9 copy-done.4
  168.2 4.8 %project_and_norm.1 = f32[48,64]{1,0:T(8,128)S(1)} custom-call(bf16[32,24,512]{2,1,0:T(8,128)(2,1)S(1)} %all-to-all-done.1.partial_ref, bf16[2,1536,768]{2,1,0:T(8,128)(2,1)S(1)} %bitcast.26, bf16[48,1536]{1,0:T(8,128)(2,1)S(1)} %bitcast.33, f32[3,1536]{1,0:T(4,128)S(1)} %bitcast.34, f32[1,1536]{1,0:T(1,128)S(1)} %broadcast_in_dim.6.bias_ref, ...), custom_call_target="tpu_custom_call" | custom-call | tf_op jit(solution)/shard_map/project_and_norm/pallas_call | solution.py:346
  173.4 0.7 collective-permute-start.10
  174.0 4.3 %collective-permute-start.9 = (f32[1536]{0:T(1024)S(1)}, f32[1536]{0:T(1024)S(1)}, u32[]{:S(2)}, u32[]{:S(2)}) collective-permute-start(f32[1536]{0:T(1024)S(1)} %get-tuple-element.18), channel_id=1, source_target_pairs={{0,1},{1,257},{2,3},{3,259},{256,0},{257,256},{258,2},{259,258},{4... | collective-permute-start | bytes 18440 | tf_op jit(solution)/shard_map/ppermute | solution.py:451
  179.7 0.6 reshape.40
  180.3 0.6 reshape_subtract_fusion
  (47 shorter events, 1.5 us)
Async XLA Ops:
  7.2 1.1 copy-start
  7.2 41.8 %copy-start.10 = (bf16[1,333,2,192]{1,3,2,0:T(8,128)(2,1)S(1)}, bf16[1,333,2,192]{1,3,2,0:T(8,128)(2,1)}, u32[]{:S(2)}) copy-start(bf16[1,333,2,192]{1,3,2,0:T(8,128)(2,1)} %param.12) | copy-start | bytes 767236
  7.2 157.8 %all-gather.2.cloned.1.call-start = ((), (), s32[]{:S(2)}) async-start(), calls=%async_computation.2 | async-start | bytes 5013504 | tf_op jit(solution)/shard_map/all_gather | solution.py:401
  9.0 1.0 copy-start.2
  23.5 22.3 %collective-permute-start.1 = (bf16[8,3,48,128]{3,2,1,0:T(8,128)(2,1)S(1)}, bf16[8,3,48,128]{3,2,1,0:T(8,128)(2,1)}, u32[]{:S(2)}, u32[]{:S(2)}) collective-permute-start(bf16[8,3,48,128]{3,2,1,0:T(8,128)(2,1)S(1)} %bitcast.27), channel_id=1, source_target_pairs={{0,8},{8,0},{1,9},{9,1},{2,10},{10,2},{3,11},{11,3},{4,12},{12,4},... | collective-permute-start | bytes 884744 | tf_op jit(solution)/shard_map/ppermute | solution.py:392
  29.7 19.5 %collective-permute-start.4 = (bf16[8,3,48,128]{3,2,1,0:T(8,128)(2,1)S(1)}, bf16[8,3,48,128]{3,2,1,0:T(8,128)(2,1)}, u32[]{:S(2)}, u32[]{:S(2)}) collective-permute-start(bf16[8,3,48,128]{3,2,1,0:T(8,128)(2,1)S(1)} %bitcast.28), channel_id=1, source_target_pairs={{0,32},{8,232},{32,64},{40,8},{64,96},{72,40},{96,128},{104,72},{1... | collective-permute-start | bytes 884744 | tf_op jit(solution)/shard_map/ppermute | solution.py:390
  41.2 12.4 %collective-permute-start = (bf16[2,8,3,24,128]{4,3,2,1,0:T(8,128)(2,1)S(1)}, bf16[2,8,3,24,128]{4,3,2,1,0:T(8,128)(2,1)S(1)}, u32[]{:S(2)}, u32[]{:S(2)}) collective-permute-start(bf16[2,8,3,24,128]{4,3,2,1,0:T(8,128)(2,1)S(1)} %all_gather.6.own_ref), channel_id=1, source_target_pairs={{0,4},{4,0},{1,5},{5,1},{2,6},{6,2},{3,7},{7,3},{8,12},{12,8},{9,1... | collective-permute-start | bytes 884744 | tf_op jit(solution)/shard_map/ppermute | solution.py:395
  45.8 13.9 %collective-permute-start.2 = (bf16[8,3,48,128]{3,2,1,0:T(8,128)(2,1)}, bf16[8,3,48,128]{3,2,1,0:T(8,128)(2,1)}, u32[]{:S(2)}, u32[]{:S(2)}) collective-permute-start(bf16[8,3,48,128]{3,2,1,0:T(8,128)(2,1)} %collective-permute-done.1), channel_id=1, source_target_pairs={{0,32},{8,232},{32,64},{40,8},{64,96},{72,40},{96,128},{104,72},{1... | collective-permute-start | bytes 884744 | tf_op jit(solution)/shard_map/ppermute | solution.py:390
  49.2 5.2 %copy-start.8 = (bf16[3,333,128]{2,1,0:T(8,128)(2,1)}, bf16[3,333,128]{2,1,0:T(8,128)(2,1)S(1)}, u32[]{:S(2)}) copy-start(bf16[3,333,128]{2,1,0:T(8,128)(2,1)S(1)} %copy.19) | copy-start | bytes 767236
  49.2 14.1 %collective-permute-start.5 = (bf16[8,3,48,128]{3,2,1,0:T(8,128)(2,1)}, bf16[8,3,48,128]{3,2,1,0:T(8,128)(2,1)}, u32[]{:S(2)}, u32[]{:S(2)}) collective-permute-start(bf16[8,3,48,128]{3,2,1,0:T(8,128)(2,1)} %collective-permute-done.4.refs_0_.refs_1_), channel_id=1, source_target_pairs={{0,32},{8,232},{32,64},{40,8},{64,96},{72,40},{96,128},{104,72},{1... | collective-permute-start | bytes 884744 | tf_op jit(solution)/shard_map/ppermute | solution.py:390
  58.3 1.4 copy-start.6
  59.8 14.7 %collective-permute-start.3 = (bf16[8,3,48,128]{3,2,1,0:T(8,128)(2,1)}, bf16[8,3,48,128]{3,2,1,0:T(8,128)(2,1)}, u32[]{:S(2)}, u32[]{:S(2)}) collective-permute-start(bf16[8,3,48,128]{3,2,1,0:T(8,128)(2,1)} %collective-permute-done.2.refs_1_.refs_2_), channel_id=1, source_target_pairs={{0,32},{8,232},{32,64},{40,8},{64,96},{72,40},{96,128},{104,72},{1... | collective-permute-start | bytes 884744 | tf_op jit(solution)/shard_map/ppermute | solution.py:390
  63.3 15.1 %collective-permute-start.6 = (bf16[8,3,48,128]{3,2,1,0:T(8,128)(2,1)}, bf16[8,3,48,128]{3,2,1,0:T(8,128)(2,1)S(1)}, u32[]{:S(2)}, u32[]{:S(2)}) collective-permute-start(bf16[8,3,48,128]{3,2,1,0:T(8,128)(2,1)} %collective-permute-done.5.refs_0_.refs_3_), channel_id=1, source_target_pairs={{0,32},{8,232},{32,64},{40,8},{64,96},{72,40},{96,128},{104,72},{1... | collective-permute-start | bytes 884744 | tf_op jit(solution)/shard_map/ppermute | solution.py:390
  67.8 1.7 copy-start.7
  69.5 8.9 %copy-start.9 = (bf16[3,333,128]{2,1,0:T(8,128)(2,1)S(1)}, bf16[3,333,128]{2,1,0:T(8,128)(2,1)}, u32[]{:S(2)}) copy-start(bf16[3,333,128]{2,1,0:T(8,128)(2,1)} %copy-done.8) | copy-start | bytes 767236
  74.5 13.3 %collective-permute-start.7 = (bf16[8,3,48,128]{3,2,1,0:T(8,128)(2,1)}, bf16[8,3,48,128]{3,2,1,0:T(8,128)(2,1)S(1)}, u32[]{:S(2)}, u32[]{:S(2)}) collective-permute-start(bf16[8,3,48,128]{3,2,1,0:T(8,128)(2,1)} %collective-permute-done.3.refs_1_.refs_4_), channel_id=1, source_target_pairs={{0,32},{8,232},{32,64},{40,8},{64,96},{72,40},{96,128},{104,72},{1... | collective-permute-start | bytes 884744 | tf_op jit(solution)/shard_map/ppermute | solution.py:390
  78.4 13.3 %collective-permute-start.8 = (bf16[8,3,48,128]{3,2,1,0:T(8,128)(2,1)S(1)}, bf16[8,3,48,128]{3,2,1,0:T(8,128)(2,1)S(1)}, u32[]{:S(2)}, u32[]{:S(2)}) collective-permute-start(bf16[8,3,48,128]{3,2,1,0:T(8,128)(2,1)S(1)} %collective-permute-done.6.refs_0_.refs_5_), channel_id=1, source_target_pairs={{0,32},{8,232},{32,64},{40,8},{64,96},{72,40},{96,128},{104,72},{1... | collective-permute-start | bytes 884744 | tf_op jit(solution)/shard_map/ppermute | solution.py:390
  91.7 59.4 %copy-start.11 = (f32[1536]{0:T(1024)S(1)}, f32[1536]{0:T(1024)}, u32[]{:S(2)}) copy-start(f32[1536]{0:T(1024)} %param.16) | copy-start | bytes 18436
  91.7 73.3 %copy-start.3 = (bf16[1536,64]{0,1:T(8,128)(2,1)S(1)}, bf16[1536,64]{0,1:T(8,128)(2,1)}, u32[]{:S(2)}) copy-start(bf16[1536,64]{0,1:T(8,128)(2,1)} %param.17) | copy-start | bytes 589828
  91.7 73.3 %copy-start.5 = (f32[64]{0:T(128)S(1)}, f32[64]{0:T(128)}, u32[]{:S(2)}) copy-start(f32[64]{0:T(128)} %param.18) | copy-start | bytes 772
  141.1 23.9 %all-to-all-start.1 = ((bf16[32,24,512]{2,1,0:T(8,128)(2,1)}), bf16[32,24,512]{2,1,0:T(8,128)(2,1)S(1)}, u32[]{:S(2)}, u32[]{:S(2)}) async-start(bf16[32,24,512]{2,1,0:T(8,128)(2,1)} %bitcast.9), calls=%async_computation.1 | async-start | bytes 1572864 | tf_op jit(solution)/shard_map/all_to_all | solution.py:428
  165.0 2.3 %copy-start.1 = (bf16[3072,768]{1,0:T(8,128)(2,1)S(1)}, bf16[3072,768]{1,0:T(8,128)(2,1)}, u32[]{:S(2)}) copy-start(bf16[3072,768]{1,0:T(8,128)(2,1)} %all-gather.2.cloned.1.call-done) | copy-start | bytes 14155780
  167.3 0.9 copy-start.4
  168.2 12.1 %copy-start.12 = (f32[1,1536]{1,0:T(1,128)S(1)}, f32[1,1536]{1,0:T(1,128)}, u32[]{:S(2)}) copy-start(f32[1,1536]{1,0:T(1,128)} %param.21) | copy-start | bytes 18436
  173.4 6.3 %collective-permute-start.10 = (f32[1536]{0:T(1024)S(1)}, f32[1536]{0:T(1024)S(1)}, u32[]{:S(2)}, u32[]{:S(2)}) collective-permute-start(f32[1536]{0:T(1024)S(1)} %get-tuple-element.19), channel_id=1, source_target_pairs={{0,0},{1,256},{2,2},{3,258},{256,1},{257,257},{258,3},{259,259},{4... | collective-permute-start | bytes 18440 | tf_op jit(solution)/shard_map/ppermute | solution.py:450
  174.0 5.7 %collective-permute-start.9 = (f32[1536]{0:T(1024)S(1)}, f32[1536]{0:T(1024)S(1)}, u32[]{:S(2)}, u32[]{:S(2)}) collective-permute-start(f32[1536]{0:T(1024)S(1)} %get-tuple-element.18), channel_id=1, source_target_pairs={{0,1},{1,257},{2,3},{3,259},{256,0},{257,256},{258,2},{259,258},{4... | collective-permute-start | bytes 18440 | tf_op jit(solution)/shard_map/ppermute | solution.py:451
Sparse Core Ops, SparseCore 0:
  11.4 80.2 all-gather.1

commit v6 on v5

--- a/solution.py
+++ b/solution.py
@@ -117,7 +117,8 @@
     return jnp.dot(jnp.exp2(scores).astype(BF16), values, preferred_element_type=F32)
 
 
-def first_kernel(heads, valid_ref, q_ref, block_ref, text_ref, full_ref, state_ref):
+def first_kernel(heads, valid_ref, q_ref, block_ref, text_ref, full_ref, state_ref, mark_ref):
+    mark_ref[...] = jnp.zeros_like(mark_ref)
     rows = 2 * q_ref.shape[2]
     lane = lane_index((rows, LANES))
     for head in range(heads):
@@ -139,7 +140,8 @@
 
 
 def next_kernel(heads, q_ref, state_ref, *refs):
-    *blocks, out_ref = refs
+    *blocks, before_ref, out_ref, mark_ref = refs
+    mark_ref[...] = before_ref[...]
     rows = 2 * q_ref.shape[2]
     for head in range(heads):
         q = q_ref[head].reshape(rows, 2 * LANES)
@@ -227,6 +229,8 @@
     tile = ROW_TILE if rows % ROW_TILE == 0 else rows
 
     def tiled(shape, axis):
+        if axis is None:
+            return pl.BlockSpec(shape, lambda i: (0,) * len(shape))
         block = tuple(tile if d == axis else n for d, n in enumerate(shape))
         return pl.BlockSpec(block, lambda i: tuple(i if d == axis else 0 for d in range(len(shape))))
 
@@ -235,7 +239,7 @@
         specs.append(tiled(x.shape, 2) if x.ndim == 4 else pl.BlockSpec(memory_space=pltpu.SMEM))
     for x in whole:
         specs.append(pl.BlockSpec(x.shape, lambda i, n=x.ndim: (0,) * n))
-    specs += [pl.BlockSpec(memory_space=pl.ANY)] * len(kept)
+    specs += [pl.BlockSpec(memory_space=pltpu.HBM)] * len(kept)
     keys = sum(x.size // (heads * LANES) for x in whole)
     pairs = heads * 2 * rows * keys
     out_specs = [tiled(s.shape, a) for s, a in zip(out_shape, out_axes)]
@@ -256,15 +260,18 @@
     return jax.ShapeDtypeStruct(q.shape[:3] + (LANES,), F32)
 
 
+MARK = jax.ShapeDtypeStruct((8, LANES), F32)
+
+
 def first_block(valid, q, block, text):
-    shapes = [jax.ShapeDtypeStruct(q.shape, BF16), state_shape(q)]
+    shapes = [jax.ShapeDtypeStruct(q.shape, BF16), state_shape(q), MARK]
     kernel = functools.partial(first_kernel, q.shape[0])
-    return attention_call(kernel, "own_block", [valid, q], [block, text], [], shapes, [2, 2])
-
-
-def next_blocks(q, state, blocks):
+    return attention_call(kernel, "own_block", [valid, q], [block, text], [], shapes, [2, 2, None])
+
+
+def next_blocks(q, state, blocks, mark):
     kernel = functools.partial(next_kernel, q.shape[0])
-    return attention_call(kernel, "next_blocks", [q, state], blocks, [], [state_shape(q)], [2])[0]
+    return attention_call(kernel, "next_blocks", [q, state], blocks + [mark], [], [state_shape(q), MARK], [2, None])
 
 
 def last_block(valid, q, state, block, first_text, text, kept):
@@ -294,10 +301,13 @@
     out_ref,
     wide_ref,
     held_ref,
-    sem,
+    input_ref,
+    sems,
 ):
-    brought = pltpu.make_async_copy(weight_ref, held_ref, sem)
+    brought = pltpu.make_async_copy(weight_ref, held_ref, sems.at[0])
+    taken = pltpu.make_async_copy(hidden_ref, input_ref, sems.at[1])
     brought.start()
+    taken.start()
     half = partial_ref.shape[1]
     sources = partial_ref.shape[0]
     across = groups // 2
@@ -326,10 +336,11 @@
             wide_ref[part * half : (part + 1) * half, group * width : (group + 1) * width] = both
     attended = wide_ref[...].astype(BF16)
     brought.wait()
+    taken.wait()
     projected = jnp.concatenate(
         [jnp.dot(attended, held_ref[side], preferred_element_type=F32) for side in range(2)], axis=1
     )
-    residual = hidden_ref[...].astype(F32) + modulation_ref[0:1] * (projected + bias_ref[...])
+    residual = input_ref[...].astype(F32) + modulation_ref[0:1] * (projected + bias_ref[...])
     middle = jnp.mean(residual, axis=-1, keepdims=True)
     centered = residual - middle
     spread = jnp.mean(centered * centered, axis=-1, keepdims=True)
@@ -343,15 +354,17 @@
 def finish(partial, weight, hidden, modulation, bias, final_weight, final_bias, heads, groups):
     tokens, width = hidden.shape
     vmem = pl.BlockSpec(memory_space=pltpu.VMEM)
+    hbm = pl.BlockSpec(memory_space=pltpu.HBM)
     return pl.pallas_call(
         functools.partial(finish_kernel, heads, groups),
         out_shape=jax.ShapeDtypeStruct((tokens, final_weight.shape[0]), F32),
-        in_specs=[vmem, pl.BlockSpec(memory_space=pl.ANY), vmem, vmem, vmem, vmem, vmem],
+        in_specs=[vmem, hbm, hbm, vmem, vmem, vmem, vmem],
         out_specs=vmem,
         scratch_shapes=[
             pltpu.VMEM((tokens, width), F32),
             pltpu.VMEM(weight.shape, BF16),
-            pltpu.SemaphoreType.DMA,
+            pltpu.VMEM(hidden.shape, BF16),
+            pltpu.SemaphoreType.DMA((2,)),
         ],
         compiler_params=params(),
         name="project_and_norm",
@@ -383,15 +396,15 @@
 
     slabs = pack(latent_qkv[0].transpose(1, 0, 2), groups, heads)
     slabs = lax.all_to_all(slabs, HEAD_AXES, split_axis=0, concat_axis=0, tiled=True)
-    own = slabs[:, heads * half :].reshape(groups, heads, tokens, LANES)
+    packed = slabs[:, : heads * half].reshape(groups, heads, half, LANES)
+    packed = lax.all_gather(packed, "core", axis=0)
+    own, packed = after((slabs[:, heads * half :].reshape(groups, heads, tokens, LANES), packed))
     route = []
     for i in range(ring):
         route += [(2 * i, 2 * ((i + 1) % ring)), (2 * i + 1, 2 * ((i - 1) % ring) + 1)]
     pass_on = lambda x: lax.ppermute(x, ("zh", "core"), route)
     near = pass_on(own)
     beside = lax.ppermute(own, "core", [(0, 1), (1, 0)])
-    packed = slabs[:, : heads * half].reshape(groups, heads, half, LANES)
-    packed = lax.all_gather(packed, "core", axis=0)
     opposite = lax.ppermute(packed, "xh", [(0, 1), (1, 0)])
     cross = pass_on(beside)
     q = unpack_queries(xh.reshape(1), packed, opposite)
@@ -407,22 +420,20 @@
     text = lax.dynamic_slice_in_dim(text, core * share, share, 1)
     valid = jnp.where(xh == zl, jnp.minimum(count - core * share, share), 0).reshape(1)
     early, late = text[:, :LANES], text[:, LANES:]
-    q, state = first_block(valid, q, own, early)
+    q, state, mark = first_block(valid, q, own, early)
     kept = [own, near, cross]
-    ready = None
-    for _ in range(ring // 2 - 2):
-        if ready is not None:
-            near, ready = after((near, ready))
+    for step in range(ring // 2 - 2):
+        if step:
+            near, mark = after((near, mark))
         nearer = pass_on(near)
-        cross, state = after((cross, state))
+        cross, mark = after((cross, mark))
         crosser = pass_on(cross)
-        ready = state
-        state = next_blocks(q, state, [near, cross])
+        state, mark = next_blocks(q, state, [near, cross], mark)
         near, cross = nearer, crosser
         kept += [near, cross]
-    near, ready = after((near, ready))
+    near, mark = after((near, mark))
     farthest = pass_on(near)
-    state = next_blocks(q, state, [near, cross])
+    state, mark = next_blocks(q, state, [near, cross], mark)
     partial = last_block(valid, q, state, farthest, early, late, kept)
     partial = partial.reshape(4 * groups, half, 4 * LANES)
     partial = lax.all_to_all(partial, BLOCK_AXES, split_axis=0, concat_axis=0, tiled=True)
@@ -447,14 +458,13 @@
             a = y % 2
             same.append((s * across + y, a * across + y - a + s))
             swap.append((s * across + y, a * across + y - a + 1 - s))
-    kept = lax.ppermute(lax.dynamic_index_in_dim(tiles, branch, 0, keepdims=False), ("cfg", "y"), same)
-    crossed = lax.ppermute(lax.dynamic_index_in_dim(tiles, 1 - branch, 0, keepdims=False), ("cfg", "y"), swap)
+    kept = lax.ppermute(lax.dynamic_slice_in_dim(tiles, branch, 1, 0), ("cfg", "y"), same)
+    crossed = lax.ppermute(lax.dynamic_slice_in_dim(tiles, 1 - branch, 1, 0), ("cfg", "y"), swap)
     conditional = jnp.where(parity == 0, kept, crossed)
     unconditional = jnp.where(parity == 0, crossed, kept)
     guided = unconditional + guidance[0] * (conditional - unconditional)
-    result = guided.reshape(1, guided.shape[0])
-    denoised = sample - sigma[0] * result
-    return (result, denoised)
+    denoised = sample - sigma[0] * guided
+    return (guided, denoised)
 
 
 def solution(mesh):

time: 189 us -> 191 us (1.011)
  starting transfers between devices: 57.7 us -> 51 us
  blocking collectives: 15.3 us -> 19.2 us
  waiting for transfers between devices: 14.4 us -> 17.2 us
  Pallas kernels: 73 us -> 75.6 us
    ppermute x1, starting transfers between devices: 6.17 us -> 2.26 us  [local(): beside = lax.ppermute(own, 'core', [(0, 1), (1, 0)])]
    all_gather x1, blocking collectives: 2.02 us -> 5.91 us  [local(): packed = lax.all_gather(packed, 'core', axis=0)]
    all_to_all x1, starting transfers between devices: 9.22 us -> 6.18 us  [local(): lax.all_to_all(partial, BLOCK_AXES, split_axis=0, concat_axis=0, tiled=True)]
    ppermute x7, waiting for transfers between devices: 0.47 us -> 3.37 us  [local(): pass_on = lambda x: lax.ppermute(x, ('zh', 'core'), route)]
    pallas_call x5, Pallas kernels: 67.2 us -> 69.6 us  [attention_call(): pl.pallas_call(kernel, grid=(rows // tile,), out_shape=out_shape, in_spec...]
  transfers between devices with their start and end apart: 13 -> 13, of which waited for: 2 -> 3; matrix products, arithmetic and copies ran while one was open for 1% -> 1% of each run, Pallas kernels for 36% -> 37%
where the time goes in v6:
time: 191 us; the launch traced here: 190 us
  Pallas kernels  75.6 us (40%)
  starting transfers between devices  51 us (27%)
  blocking collectives  19.2 us (10%)
  waiting for transfers between devices  17.2 us (9%)
  between operations  15.7 us (8%)
  local copies, waits for them, and re-layouts  10.4 us (5%)
    pallas_call x5, Pallas kernels, attention_call(): pl.pallas_call(kernel, grid=(rows // tile,), out_shape=out_shape, in_spec...  69.6 us
    ppermute x7, starting transfers between devices, local(): pass_on = lambda x: lax.ppermute(x, ('zh', 'core'), route)  31.9 us
    all_to_all x1, waiting for transfers between devices, local(): lax.all_to_all(partial, BLOCK_AXES, split_axis=0, concat_axis=0, tiled=True)  13.8 us
    all_to_all x1, blocking collectives, local(): lax.all_to_all(slabs, HEAD_AXES, split_axis=0, concat_axis=0, tiled=True)  13.3 us
    unnamed x27, local copies, waits for them, and re-layouts  9.12 us
    all_to_all x1, starting transfers between devices, local(): lax.all_to_all(partial, BLOCK_AXES, split_axis=0, concat_axis=0, tiled=True)  6.18 us
    all_gather x1, blocking collectives, local(): packed = lax.all_gather(packed, 'core', axis=0)  5.91 us
    ppermute x1, starting transfers between devices, local(): lax.ppermute(lax.dynamic_slice_in_dim(tiles, 1 - branch, 1, 0), ('cfg', '...  5.35 us
  transfers between devices with their start and end apart: 13, of which 3 were waited for; matrix products, arithmetic and copies ran while one was open for 1% of the time, Pallas kernels for 37%

profile of v6, /device:TPU:1, one launch (start us, length us, event | category | flops | bytes accessed | tf_op | source)
XLA Modules:
  0.0 189.8 jit_solution(15966939069001442191)
XLA Ops:
  7.2 1.0 copy-done
  8.2 0.7 constant_dynamic-slice_fusion.2
  9.0 1.0 copy-done.2
  10.2 13.3 %all_to_all.10 = bf16[8,216,128]{2,1,0:T(8,128)(2,1)S(1)} all-to-all(bf16[8,216,128]{2,1,0:T(8,128)(2,1)S(1)} %pack_heads.1), channel_id=1, replica_groups=mesh['cfg'=2,'zh'=8,'zl'=2,'core'=2,'xh'=2,'y'=4] {'zl','y'}, dimensions={0} | all-to-all | bytes 884736 | tf_op jit(solution)/shard_map/all_to_all | solution.py:398
  23.5 5.9 %all_gather.6.own_ref = bf16[2,8,3,24,128]{4,3,2,1,0:T(8,128)(2,1)S(1)} all-gather(bf16[1,8,3,24,128]{4,3,2,1,0:T(8,128)(2,1)S(1)} %bitcast.37), channel_id=1, replica_groups=mesh['cfg'=2,'zh'=8,'zl'=2,'core'=2,'xh'=2,'y'=4] {'core'}, dimensions={0}, use_global_device_ids=true | all-gather | bytes 442368 | tf_op jit(solution)/shard_map/all_gather | solution.py:400
  29.4 2.3 %collective-permute-start.2 = (bf16[8,3,48,128]{3,2,1,0:T(8,128)(2,1)S(1)}, bf16[8,3,48,128]{3,2,1,0:T(8,128)(2,1)}, u32[]{:S(2)}, u32[]{:S(2)}) collective-permute-start(bf16[8,3,48,128]{3,2,1,0:T(8,128)(2,1)S(1)} %bitcast.27), channel_id=1, source_target_pairs={{0,8},{8,0},{1,9},{9,1},{2,10},{10,2},{3,11},{11,3},{4,12},{12,4},... | collective-permute-start | bytes 884744 | tf_op jit(solution)/shard_map/ppermute | solution.py:407
  31.7 9.5 %collective-permute-start.1 = (bf16[8,3,48,128]{3,2,1,0:T(8,128)(2,1)S(1)}, bf16[8,3,48,128]{3,2,1,0:T(8,128)(2,1)}, u32[]{:S(2)}, u32[]{:S(2)}) collective-permute-start(bf16[8,3,48,128]{3,2,1,0:T(8,128)(2,1)S(1)} %bitcast.28), channel_id=1, source_target_pairs={{0,32},{8,232},{32,64},{40,8},{64,96},{72,40},{96,128},{104,72},{1... | collective-permute-start | bytes 884744 | tf_op jit(solution)/shard_map/ppermute | solution.py:405
  41.2 4.7 %collective-permute-start = (bf16[2,8,3,24,128]{4,3,2,1,0:T(8,128)(2,1)S(1)}, bf16[2,8,3,24,128]{4,3,2,1,0:T(8,128)(2,1)S(1)}, u32[]{:S(2)}, u32[]{:S(2)}) collective-permute-start(bf16[2,8,3,24,128]{4,3,2,1,0:T(8,128)(2,1)S(1)} %all_gather.6.own_ref), channel_id=1, source_target_pairs={{0,4},{4,0},{1,5},{5,1},{2,6},{6,2},{3,7},{7,3},{8,12},{12,8},{9,1... | collective-permute-start | bytes 884744 | tf_op jit(solution)/shard_map/ppermute | solution.py:408
  45.8 3.1 %collective-permute-start.3 = (bf16[8,3,48,128]{3,2,1,0:T(8,128)(2,1)}, bf16[8,3,48,128]{3,2,1,0:T(8,128)(2,1)}, u32[]{:S(2)}, u32[]{:S(2)}) collective-permute-start(bf16[8,3,48,128]{3,2,1,0:T(8,128)(2,1)} %collective-permute-done.2), channel_id=1, source_target_pairs={{0,32},{8,232},{32,64},{40,8},{64,96},{72,40},{96,128},{104,72},{1... | collective-permute-start | bytes 884744 | tf_op jit(solution)/shard_map/ppermute | solution.py:405
  49.3 4.9 %collective-permute-start.4 = (bf16[8,3,48,128]{3,2,1,0:T(8,128)(2,1)}, bf16[8,3,48,128]{3,2,1,0:T(8,128)(2,1)}, u32[]{:S(2)}, u32[]{:S(2)}) collective-permute-start(bf16[8,3,48,128]{3,2,1,0:T(8,128)(2,1)} %collective-permute-done.1.refs_0_.refs_1_), channel_id=1, source_target_pairs={{0,32},{8,232},{32,64},{40,8},{64,96},{72,40},{96,128},{104,72},{1... | collective-permute-start | bytes 884744 | tf_op jit(solution)/shard_map/ppermute | solution.py:405
  54.2 0.8 unpack_queries.1.q_ref
  55.0 3.9 %own_block.1 = (bf16[3,2,768,256]{3,2,1,0:T(8,128)(2,1)S(1)}, f32[3,2,768,128]{3,2,1,0:T(8,128)S(1)}, f32[8,128]{1,0:T(8,128)S(1)}) custom-call(s32[1]{0:T(128)} %bitcast.valid_ref, bf16[3,2,768,256]{3,2,1,0:T(8,128)(2,1)S(1)} %unpack_queries.1.q_ref, bf16[8,3,48,128]{3,2,1,0:T(8,128)(2,1)S(1)} %bitcast.29, ...), custom_call_target="tpu_custom_call" | custom-call | flops 1811939328 | bytes 4718592 | tf_op jit(solution)/shard_map/own_block/pallas_call | solution.py:246
  59.0 2.2 %collective-permute-done.3.refs_1_.refs_2_ = bf16[8,3,48,128]{3,2,1,0:T(8,128)(2,1)} collective-permute-done((bf16[8,3,48,128]{3,2,1,0:T(8,128)(2,1)}, bf16[8,3,48,128]{3,2,1,0:T(8,128)(2,1)}, u32[]{:S(2)}, u32[]{:S(2)}) %collective-permute-start.3) | collective-permute-done | bytes 294944 | tf_op jit(solution)/shard_map/ppermute | solution.py:405
  61.2 3.7 %collective-permute-start.5 = (bf16[8,3,48,128]{3,2,1,0:T(8,128)(2,1)}, bf16[8,3,48,128]{3,2,1,0:T(8,128)(2,1)}, u32[]{:S(2)}, u32[]{:S(2)}) collective-permute-start(bf16[8,3,48,128]{3,2,1,0:T(8,128)(2,1)} %collective-permute-done.3.refs_1_.refs_2_), channel_id=1, source_target_pairs={{0,32},{8,232},{32,64},{40,8},{64,96},{72,40},{96,128},{104,72},{1... | collective-permute-start | bytes 884744 | tf_op jit(solution)/shard_map/ppermute | solution.py:405
  64.9 4.9 %next_blocks.3 = (f32[3,2,768,128]{3,2,1,0:T(8,128)S(1)}, f32[8,128]{1,0:T(8,128)S(1)}) custom-call(bf16[3,2,768,256]{3,2,1,0:T(8,128)(2,1)S(1)} %get-tuple-element.22.q_ref, f32[3,2,768,128]{3,2,1,0:T(8,128)S(1)} %get-tuple-element.23.state_ref, bf16[8,3,48,128]{3,2,1,0:T(8,128)(2,1)} %collective-permute-done.1.refs_0_.refs_1_, ...), custom_call_target="tpu_custom_call" | custom-call | flops 2724986880 | bytes 4718592 | tf_op jit(solution)/shard_map/next_blocks/pallas_call | solution.py:246
  69.8 1.4 copy-done.6
  71.3 3.7 %collective-permute-start.6 = (bf16[8,3,48,128]{3,2,1,0:T(8,128)(2,1)}, bf16[8,3,48,128]{3,2,1,0:T(8,128)(2,1)}, u32[]{:S(2)}, u32[]{:S(2)}) collective-permute-start(bf16[8,3,48,128]{3,2,1,0:T(8,128)(2,1)} %collective-permute-done.4.refs_0_.refs_3_), channel_id=1, source_target_pairs={{0,32},{8,232},{32,64},{40,8},{64,96},{72,40},{96,128},{104,72},{1... | collective-permute-start | bytes 884744 | tf_op jit(solution)/shard_map/ppermute | solution.py:405
  75.0 2.1 %collective-permute-start.7 = (bf16[8,3,48,128]{3,2,1,0:T(8,128)(2,1)}, bf16[8,3,48,128]{3,2,1,0:T(8,128)(2,1)S(1)}, u32[]{:S(2)}, u32[]{:S(2)}) collective-permute-start(bf16[8,3,48,128]{3,2,1,0:T(8,128)(2,1)} %collective-permute-done.5.refs_1_.refs_4_), channel_id=1, source_target_pairs={{0,32},{8,232},{32,64},{40,8},{64,96},{72,40},{96,128},{104,72},{1... | collective-permute-start | bytes 884744 | tf_op jit(solution)/shard_map/ppermute | solution.py:405
  77.1 1.7 copy-done.7
  78.7 5.0 %next_blocks.4 = (f32[3,2,768,128]{3,2,1,0:T(8,128)S(1)}, f32[8,128]{1,0:T(8,128)S(1)}) custom-call(bf16[3,2,768,256]{3,2,1,0:T(8,128)(2,1)S(1)} %get-tuple-element.22.q_ref, f32[3,2,768,128]{3,2,1,0:T(8,128)S(1)} %copy-done.7, bf16[8,3,48,128]{3,2,1,0:T(8,128)(2,1)} %collective-permute-done.4.refs_0_.refs_3_, ...), custom_call_target="tpu_custom_call" | custom-call | flops 2724986880 | bytes 4718592 | tf_op jit(solution)/shard_map/next_blocks/pallas_call | solution.py:246
  83.8 5.0 %collective-permute-start.8 = (bf16[8,3,48,128]{3,2,1,0:T(8,128)(2,1)}, bf16[8,3,48,128]{3,2,1,0:T(8,128)(2,1)S(1)}, u32[]{:S(2)}, u32[]{:S(2)}) collective-permute-start(bf16[8,3,48,128]{3,2,1,0:T(8,128)(2,1)} %collective-permute-done.6.refs_0_.refs_5_), channel_id=1, source_target_pairs={{0,32},{8,232},{32,64},{40,8},{64,96},{72,40},{96,128},{104,72},{1... | collective-permute-start | bytes 884744 | tf_op jit(solution)/shard_map/ppermute | solution.py:405
  88.8 5.4 %next_blocks.5 = (f32[3,2,768,128]{3,2,1,0:T(8,128)S(1)}, f32[8,128]{1,0:T(8,128)}) custom-call(bf16[3,2,768,256]{3,2,1,0:T(8,128)(2,1)S(1)} %get-tuple-element.22.q_ref, f32[3,2,768,128]{3,2,1,0:T(8,128)S(1)} %get-tuple-element.33.state_ref, bf16[8,3,48,128]{3,2,1,0:T(8,128)(2,1)} %collective-permute-done.6.refs_0_.refs_5_, ...), custom_call_target="tpu_custom_call" | custom-call | flops 2724986880 | bytes 4718592 | tf_op jit(solution)/shard_map/next_blocks/pallas_call | solution.py:246
  94.2 1.1 collective-permute-done.8.block_ref
  95.4 50.3 %last_block.1 = bf16[768,512]{1,0:T(8,128)(2,1)} custom-call(s32[1]{0:T(128)} %bitcast.valid_ref, bf16[3,2,768,256]{3,2,1,0:T(8,128)(2,1)S(1)} %get-tuple-element.22.q_ref, f32[3,2,768,128]{3,2,1,0:T(8,128)S(1)} %get-tuple-element.37.state_ref, bf16[8,3,48,128]{3,2,1,0:T(8,128)(2,1)S(1)} %collective-permute-done.8.block_ref, ...), custom_call_target="tpu_custom_call" | custom-call | flops 1981808640 | bytes 4718592 | tf_op jit(solution)/shard_map/last_block/pallas_call | solution.py:246
  145.6 6.2 %all-to-all-start.1 = ((bf16[32,24,512]{2,1,0:T(8,128)(2,1)}), bf16[32,24,512]{2,1,0:T(8,128)(2,1)S(1)}, u32[]{:S(2)}, u32[]{:S(2)}) async-start(bf16[32,24,512]{2,1,0:T(8,128)(2,1)} %bitcast.9), calls=%async_computation.1 | async-start | bytes 1572864 | tf_op jit(solution)/shard_map/all_to_all | solution.py:439
  151.8 0.7 copy.25
  152.6 13.8 %all-to-all-done.1.partial_ref = bf16[32,24,512]{2,1,0:T(8,128)(2,1)S(1)} async-done(((bf16[32,24,512]{2,1,0:T(8,128)(2,1)}), bf16[32,24,512]{2,1,0:T(8,128)(2,1)S(1)}, u32[]{:S(2)}, u32[]{:S(2)}) %all-to-all-start.1) | async-done | bytes 786464 | tf_op jit(solution)/shard_map/all_to_all | solution.py:439
  166.4 2.3 %copy-done.1 = bf16[3072,768]{1,0:T(8,128)(2,1)S(1)} copy-done((bf16[3072,768]{1,0:T(8,128)(2,1)S(1)}, bf16[3072,768]{1,0:T(8,128)(2,1)}, u32[]{:S(2)}) %copy-start.1) | copy-done | bytes 4718616
  168.8 0.9 copy-done.4
  169.7 5.0 %project_and_norm.1 = f32[48,64]{1,0:T(8,128)S(1)} custom-call(bf16[32,24,512]{2,1,0:T(8,128)(2,1)S(1)} %all-to-all-done.1.partial_ref, bf16[2,1536,768]{2,1,0:T(8,128)(2,1)S(1)} %bitcast.26, bf16[48,1536]{1,0:T(8,128)(2,1)S(1)} %bitcast.33, f32[3,1536]{1,0:T(4,128)S(1)} %bitcast.34, f32[1,1536]{1,0:T(1,128)S(1)} %broadcast_in_dim.6.bias_ref, ...), custom_call_target="tpu_custom_call" | custom-call | tf_op jit(solution)/shard_map/project_and_norm/pallas_call | solution.py:358
  175.0 0.7 collective-permute-start.10
  175.6 5.3 %collective-permute-start.9 = (f32[1,1536]{1,0:T(1,128)S(1)}, f32[1,1536]{1,0:T(1,128)S(1)}, u32[]{:S(2)}, u32[]{:S(2)}) collective-permute-start(f32[1,1536]{1,0:T(1,128)S(1)} %get-tuple-element.40), channel_id=1, source_target_pairs={{0,1},{1,257},{2,3},{3,259},{256,0},{257,256},{258,2},{259,258},{4... | collective-permute-start | bytes 18440 | tf_op jit(solution)/shard_map/ppermute | solution.py:462
  (45 shorter events, 1.5 us)
Async XLA Ops:
  7.2 1.1 copy-start
  7.2 41.8 %copy-start.10 = (bf16[1,333,2,192]{1,3,2,0:T(8,128)(2,1)S(1)}, bf16[1,333,2,192]{1,3,2,0:T(8,128)(2,1)}, u32[]{:S(2)}) copy-start(bf16[1,333,2,192]{1,3,2,0:T(8,128)(2,1)} %param.12) | copy-start | bytes 767236
  7.2 159.2 %all-gather.2.cloned.1.call-start = ((), (), s32[]{:S(2)}) async-start(), calls=%async_computation.2 | async-start | bytes 5013504 | tf_op jit(solution)/shard_map/all_gather | solution.py:414
  9.0 1.0 copy-start.2
  29.4 16.4 %collective-permute-start.2 = (bf16[8,3,48,128]{3,2,1,0:T(8,128)(2,1)S(1)}, bf16[8,3,48,128]{3,2,1,0:T(8,128)(2,1)}, u32[]{:S(2)}, u32[]{:S(2)}) collective-permute-start(bf16[8,3,48,128]{3,2,1,0:T(8,128)(2,1)S(1)} %bitcast.27), channel_id=1, source_target_pairs={{0,8},{8,0},{1,9},{9,1},{2,10},{10,2},{3,11},{11,3},{4,12},{12,4},... | collective-permute-start | bytes 884744 | tf_op jit(solution)/shard_map/ppermute | solution.py:407
  31.7 17.6 %collective-permute-start.1 = (bf16[8,3,48,128]{3,2,1,0:T(8,128)(2,1)S(1)}, bf16[8,3,48,128]{3,2,1,0:T(8,128)(2,1)}, u32[]{:S(2)}, u32[]{:S(2)}) collective-permute-start(bf16[8,3,48,128]{3,2,1,0:T(8,128)(2,1)S(1)} %bitcast.28), channel_id=1, source_target_pairs={{0,32},{8,232},{32,64},{40,8},{64,96},{72,40},{96,128},{104,72},{1... | collective-permute-start | bytes 884744 | tf_op jit(solution)/shard_map/ppermute | solution.py:405
  41.2 13.0 %collective-permute-start = (bf16[2,8,3,24,128]{4,3,2,1,0:T(8,128)(2,1)S(1)}, bf16[2,8,3,24,128]{4,3,2,1,0:T(8,128)(2,1)S(1)}, u32[]{:S(2)}, u32[]{:S(2)}) collective-permute-start(bf16[2,8,3,24,128]{4,3,2,1,0:T(8,128)(2,1)S(1)} %all_gather.6.own_ref), channel_id=1, source_target_pairs={{0,4},{4,0},{1,5},{5,1},{2,6},{6,2},{3,7},{7,3},{8,12},{12,8},{9,1... | collective-permute-start | bytes 884744 | tf_op jit(solution)/shard_map/ppermute | solution.py:408
  45.8 15.3 %collective-permute-start.3 = (bf16[8,3,48,128]{3,2,1,0:T(8,128)(2,1)}, bf16[8,3,48,128]{3,2,1,0:T(8,128)(2,1)}, u32[]{:S(2)}, u32[]{:S(2)}) collective-permute-start(bf16[8,3,48,128]{3,2,1,0:T(8,128)(2,1)} %collective-permute-done.2), channel_id=1, source_target_pairs={{0,32},{8,232},{32,64},{40,8},{64,96},{72,40},{96,128},{104,72},{1... | collective-permute-start | bytes 884744 | tf_op jit(solution)/shard_map/ppermute | solution.py:405
  49.2 5.8 %copy-start.8 = (bf16[3,333,128]{2,1,0:T(8,128)(2,1)}, bf16[3,333,128]{2,1,0:T(8,128)(2,1)S(1)}, u32[]{:S(2)}) copy-start(bf16[3,333,128]{2,1,0:T(8,128)(2,1)S(1)} %copy.20) | copy-start | bytes 767236
  49.3 22.0 %collective-permute-start.4 = (bf16[8,3,48,128]{3,2,1,0:T(8,128)(2,1)}, bf16[8,3,48,128]{3,2,1,0:T(8,128)(2,1)}, u32[]{:S(2)}, u32[]{:S(2)}) collective-permute-start(bf16[8,3,48,128]{3,2,1,0:T(8,128)(2,1)} %collective-permute-done.1.refs_0_.refs_1_), channel_id=1, source_target_pairs={{0,32},{8,232},{32,64},{40,8},{64,96},{72,40},{96,128},{104,72},{1... | collective-permute-start | bytes 884744 | tf_op jit(solution)/shard_map/ppermute | solution.py:405
  61.2 13.8 %collective-permute-start.5 = (bf16[8,3,48,128]{3,2,1,0:T(8,128)(2,1)}, bf16[8,3,48,128]{3,2,1,0:T(8,128)(2,1)}, u32[]{:S(2)}, u32[]{:S(2)}) collective-permute-start(bf16[8,3,48,128]{3,2,1,0:T(8,128)(2,1)} %collective-permute-done.3.refs_1_.refs_2_), channel_id=1, source_target_pairs={{0,32},{8,232},{32,64},{40,8},{64,96},{72,40},{96,128},{104,72},{1... | collective-permute-start | bytes 884744 | tf_op jit(solution)/shard_map/ppermute | solution.py:405
  69.8 1.5 copy-start.6
  71.3 12.5 %collective-permute-start.6 = (bf16[8,3,48,128]{3,2,1,0:T(8,128)(2,1)}, bf16[8,3,48,128]{3,2,1,0:T(8,128)(2,1)}, u32[]{:S(2)}, u32[]{:S(2)}) collective-permute-start(bf16[8,3,48,128]{3,2,1,0:T(8,128)(2,1)} %collective-permute-done.4.refs_0_.refs_3_), channel_id=1, source_target_pairs={{0,32},{8,232},{32,64},{40,8},{64,96},{72,40},{96,128},{104,72},{1... | collective-permute-start | bytes 884744 | tf_op jit(solution)/shard_map/ppermute | solution.py:405
  75.0 13.8 %collective-permute-start.7 = (bf16[8,3,48,128]{3,2,1,0:T(8,128)(2,1)}, bf16[8,3,48,128]{3,2,1,0:T(8,128)(2,1)S(1)}, u32[]{:S(2)}, u32[]{:S(2)}) collective-permute-start(bf16[8,3,48,128]{3,2,1,0:T(8,128)(2,1)} %collective-permute-done.5.refs_1_.refs_4_), channel_id=1, source_target_pairs={{0,32},{8,232},{32,64},{40,8},{64,96},{72,40},{96,128},{104,72},{1... | collective-permute-start | bytes 884744 | tf_op jit(solution)/shard_map/ppermute | solution.py:405
  77.1 1.7 copy-start.7
  78.7 10.0 %copy-start.9 = (bf16[3,333,128]{2,1,0:T(8,128)(2,1)S(1)}, bf16[3,333,128]{2,1,0:T(8,128)(2,1)}, u32[]{:S(2)}) copy-start(bf16[3,333,128]{2,1,0:T(8,128)(2,1)} %copy-done.8) | copy-start | bytes 767236
  83.8 11.6 %collective-permute-start.8 = (bf16[8,3,48,128]{3,2,1,0:T(8,128)(2,1)}, bf16[8,3,48,128]{3,2,1,0:T(8,128)(2,1)S(1)}, u32[]{:S(2)}, u32[]{:S(2)}) collective-permute-start(bf16[8,3,48,128]{3,2,1,0:T(8,128)(2,1)} %collective-permute-done.6.refs_0_.refs_5_), channel_id=1, source_target_pairs={{0,32},{8,232},{32,64},{40,8},{64,96},{72,40},{96,128},{104,72},{1... | collective-permute-start | bytes 884744 | tf_op jit(solution)/shard_map/ppermute | solution.py:405
  95.3 57.2 %copy-start.11 = (f32[1536]{0:T(1024)S(1)}, f32[1536]{0:T(1024)}, u32[]{:S(2)}) copy-start(f32[1536]{0:T(1024)} %param.16) | copy-start | bytes 18436
  95.4 71.1 %copy-start.3 = (bf16[1536,64]{0,1:T(8,128)(2,1)S(1)}, bf16[1536,64]{0,1:T(8,128)(2,1)}, u32[]{:S(2)}) copy-start(bf16[1536,64]{0,1:T(8,128)(2,1)} %param.17) | copy-start | bytes 589828
  95.4 71.1 %copy-start.5 = (f32[64]{0:T(128)S(1)}, f32[64]{0:T(128)}, u32[]{:S(2)}) copy-start(f32[64]{0:T(128)} %param.18) | copy-start | bytes 772
  145.6 20.8 %all-to-all-start.1 = ((bf16[32,24,512]{2,1,0:T(8,128)(2,1)}), bf16[32,24,512]{2,1,0:T(8,128)(2,1)S(1)}, u32[]{:S(2)}, u32[]{:S(2)}) async-start(bf16[32,24,512]{2,1,0:T(8,128)(2,1)} %bitcast.9), calls=%async_computation.1 | async-start | bytes 1572864 | tf_op jit(solution)/shard_map/all_to_all | solution.py:439
  166.4 2.3 %copy-start.1 = (bf16[3072,768]{1,0:T(8,128)(2,1)S(1)}, bf16[3072,768]{1,0:T(8,128)(2,1)}, u32[]{:S(2)}) copy-start(bf16[3072,768]{1,0:T(8,128)(2,1)} %all-gather.2.cloned.1.call-done) | copy-start | bytes 14155780
  168.7 0.9 copy-start.4
  169.7 12.7 %copy-start.12 = (f32[1,1536]{1,0:T(1,128)S(1)}, f32[1,1536]{1,0:T(1,128)}, u32[]{:S(2)}) copy-start(f32[1,1536]{1,0:T(1,128)} %param.21) | copy-start | bytes 18436
  175.0 7.3 %collective-permute-start.10 = (f32[1,1536]{1,0:T(1,128)S(1)}, f32[1,1536]{1,0:T(1,128)S(1)}, u32[]{:S(2)}, u32[]{:S(2)}) collective-permute-start(f32[1,1536]{1,0:T(1,128)S(1)} %get-tuple-element.41), channel_id=1, source_target_pairs={{0,0},{1,256},{2,2},{3,258},{256,1},{257,257},{258,3},{259,259},{4... | collective-permute-start | bytes 18440 | tf_op jit(solution)/shard_map/ppermute | solution.py:461
  175.6 6.7 %collective-permute-start.9 = (f32[1,1536]{1,0:T(1,128)S(1)}, f32[1,1536]{1,0:T(1,128)S(1)}, u32[]{:S(2)}, u32[]{:S(2)}) collective-permute-start(f32[1,1536]{1,0:T(1,128)S(1)} %get-tuple-element.40), channel_id=1, source_target_pairs={{0,1},{1,257},{2,3},{3,259},{256,0},{257,256},{258,2},{259,258},{4... | collective-permute-start | bytes 18440 | tf_op jit(solution)/shard_map/ppermute | solution.py:462
Sparse Core Ops, SparseCore 0:
  11.4 80.3 all-gather.1

commit v7 on v6

--- a/solution.py
+++ b/solution.py
@@ -10,7 +10,6 @@
 
 HEAD_DIM = 64
 LANES = 128
-ROW_TILE = 768
 LOG2_SCALE = math.log2(math.e) * HEAD_DIM**-0.5
 F32 = jnp.float32
 BF16 = jnp.bfloat16
@@ -21,8 +20,8 @@
 BLOCK_AXES = ("zl", "core", "xh", "y")
 
 
-def params(**extra):
-    return pltpu.CompilerParams(vmem_limit_bytes=32 * 1024 * 1024, **extra)
+def params(mib=16):
+    return pltpu.CompilerParams(vmem_limit_bytes=mib * 1024 * 1024)
 
 
 def lane_index(shape):
@@ -105,8 +104,8 @@
     )(place, own, other)
 
 
-def rows_of(ref, head):
-    return ref[:, head].reshape(-1, ref.shape[-1])
+def rows_of(ref):
+    return ref[:, 0].reshape(-1, ref.shape[-1])
 
 
 def scores_of(q, keys):
@@ -117,175 +116,160 @@
     return jnp.dot(jnp.exp2(scores).astype(BF16), values, preferred_element_type=F32)
 
 
-def first_kernel(heads, valid_ref, q_ref, block_ref, text_ref, full_ref, state_ref, mark_ref):
+def first_kernel(valid_ref, q_ref, block_ref, text_ref, full_ref, state_ref, mark_ref):
+    rows = 2 * q_ref.shape[2]
     mark_ref[...] = jnp.zeros_like(mark_ref)
-    rows = 2 * q_ref.shape[2]
-    lane = lane_index((rows, LANES))
-    for head in range(heads):
-        q = q_ref[head].reshape(rows, 2 * LANES)
-        keys, values = wide_keys(rows_of(block_ref, head))
-        more_keys, more_values = wide_keys(text_ref[head], valid_ref[0])
-        scores = scores_of(q, jnp.concatenate([keys, more_keys], axis=0))
-        offset = jnp.max(scores, axis=1, keepdims=True)
-        state = weighted(scores - offset, jnp.concatenate([values, more_values], axis=0))
-        state_ref[head] = state.reshape(state_ref.shape[1:])
-        offset = jnp.broadcast_to(-offset, (rows, LANES))
-        coarse = offset.astype(BF16).astype(F32)
-        middle = (offset - coarse).astype(BF16).astype(F32)
-        upper = q[:, LANES:].astype(F32)
-        for place, term in enumerate((coarse, middle, offset - coarse - middle)):
-            upper = jnp.where(lane == HEAD_DIM + place, term, upper)
-        full_ref[head, :, :, :LANES] = q_ref[head, :, :, :LANES]
-        full_ref[head, :, :, LANES:] = upper.astype(BF16).reshape(state_ref.shape[1:])
-
-
-def next_kernel(heads, q_ref, state_ref, *refs):
+    q = q_ref[0].reshape(rows, 2 * LANES)
+    keys, values = wide_keys(rows_of(block_ref))
+    more_keys, more_values = wide_keys(text_ref[0], valid_ref[0])
+    scores = scores_of(q, jnp.concatenate([keys, more_keys], axis=0))
+    offset = jnp.max(scores, axis=1, keepdims=True)
+    state = weighted(scores - offset, jnp.concatenate([values, more_values], axis=0))
+    state_ref[0] = state.reshape(state_ref.shape[1:])
+    full_ref[0, :, :, :LANES] = q_ref[0, :, :, :LANES]
+    upper = with_offset(q[:, LANES:].astype(F32), -offset)
+    full_ref[0, :, :, LANES:] = upper.astype(BF16).reshape(state_ref.shape[1:])
+
+
+def with_offset(upper, offset):
+    lane = lane_index(upper.shape)
+    offset = jnp.broadcast_to(offset, upper.shape)
+    coarse = offset.astype(BF16).astype(F32)
+    middle = (offset - coarse).astype(BF16).astype(F32)
+    for place, term in enumerate((coarse, middle, offset - coarse - middle)):
+        upper = jnp.where(lane == HEAD_DIM + place, term, upper)
+    return upper
+
+
+def next_kernel(q_ref, state_ref, *refs):
     *blocks, before_ref, out_ref, mark_ref = refs
     mark_ref[...] = before_ref[...]
     rows = 2 * q_ref.shape[2]
-    for head in range(heads):
-        q = q_ref[head].reshape(rows, 2 * LANES)
-        keys, values = wide_keys(jnp.concatenate([rows_of(ref, head) for ref in blocks], axis=0))
-        state = weighted(scores_of(q, keys), values)
-        out_ref[head] = state_ref[head] + state.reshape(out_ref.shape[1:])
-
-
-def last_kernel(heads, count, valid_ref, q_ref, state_ref, block_ref, first_text_ref, text_ref, *refs):
+    q = q_ref[0].reshape(rows, 2 * LANES)
+    keys, values = wide_keys(jnp.concatenate([rows_of(ref) for ref in blocks], axis=0))
+    state = weighted(scores_of(q, keys), values)
+    out_ref[0] = state_ref[0] + state.reshape(out_ref.shape[1:])
+
+
+def last_kernel(count, valid_ref, q_ref, state_ref, block_ref, first_text_ref, text_ref, *refs):
     kept, out_ref, done_ref, top_ref, spare_ref, sem = refs[:count], *refs[count:]
+    head = pl.program_id(0)
     tile = q_ref.shape[2]
     rows = 2 * tile
     lane = lane_index((rows, LANES))
-    safe = True
-    for head in range(heads):
-        q = q_ref[head].reshape(rows, 2 * LANES)
-        keys, values = wide_keys(rows_of(block_ref, head))
-        more_keys, more_values = wide_keys(text_ref[head], valid_ref[0] - first_text_ref.shape[1])
-        scores = scores_of(q, jnp.concatenate([keys, more_keys], axis=0))
-        state = weighted(scores, jnp.concatenate([values, more_values], axis=0))
-        state = state + state_ref[head].reshape(rows, LANES)
-        done_ref[head] = state
-        top_ref[head] = q[:, LANES:].astype(F32)
-        largest = jnp.max(jnp.where(state[:, :HEAD_DIM] < SAFE, 0.0, 1.0))
-        safe = jnp.logical_and(safe, largest == 0.0)
-
-    @pl.when(jnp.logical_not(safe))
+    q = q_ref[0].reshape(rows, 2 * LANES)
+    keys, values = wide_keys(rows_of(block_ref))
+    more_keys, more_values = wide_keys(text_ref[0], valid_ref[0] - first_text_ref.shape[1])
+    scores = scores_of(q, jnp.concatenate([keys, more_keys], axis=0))
+    state = weighted(scores, jnp.concatenate([values, more_values], axis=0))
+    state = state + state_ref[0].reshape(rows, LANES)
+    done_ref[head] = state
+    top_ref[head] = q[:, LANES:].astype(F32)
+    largest = jnp.max(jnp.where(state[:, :HEAD_DIM] < SAFE, 0.0, 1.0))
+
+    @pl.when(largest > 0.0)
     def _():
         for at, ref in enumerate(kept):
-            copy = pltpu.make_async_copy(ref, spare_ref.at[at], sem)
+            copy = pltpu.make_async_copy(ref.at[:, head], spare_ref.at[at], sem)
             copy.start()
             copy.wait()
-        spare_ref[count] = block_ref[...]
-        for head in range(heads):
-            q = q_ref[head].reshape(rows, 2 * LANES)
-            spared = (lane >= HEAD_DIM) & (lane < GUARD)
-            plain = jnp.concatenate([q[:, :LANES], jnp.where(spared, jnp.zeros_like(q[:, LANES:]), q[:, LANES:])], axis=1)
-
-            def absorb(keys, values, largest, state):
-                scores = scores_of(plain, keys)
-                higher = jnp.maximum(largest, jnp.max(scores, axis=1, keepdims=True))
-                return higher, state * jnp.exp2(largest - higher) + weighted(scores - higher, values)
-
-            def step(at, carry):
-                return absorb(*wide_keys(spare_ref[at, :, head].reshape(-1, LANES)), *carry)
-
-            carry = (jnp.full((rows, 1), -1e30, F32), jnp.zeros((rows, LANES), F32))
-            carry = lax.fori_loop(0, count + 1, step, carry)
-            carry = absorb(*wide_keys(first_text_ref[head], valid_ref[0]), *carry)
-            tail = wide_keys(text_ref[head], valid_ref[0] - first_text_ref.shape[1])
-            largest, state = absorb(*tail, *carry)
-            done_ref[head] = state
-            offset = jnp.broadcast_to(-largest, (rows, LANES))
-            coarse = offset.astype(BF16).astype(F32)
-            middle = (offset - coarse).astype(BF16).astype(F32)
-            upper = jnp.zeros((rows, LANES), F32)
-            for place, term in enumerate((coarse, middle, offset - coarse - middle)):
-                upper = jnp.where(lane == HEAD_DIM + place, term, upper)
-            top_ref[head] = upper
-
-    marks = jnp.zeros((rows, LANES), F32)
-    done = []
-    for head in range(heads):
-        state = done_ref[head]
-        total = pltpu.roll(state, HEAD_DIM, 1)
-        done.append(state / total)
-        terms = top_ref[head] if head == 0 else pltpu.roll(top_ref[head], MARKS * head, 1)
-        place = HEAD_DIM + MARKS * head
-        lead = total.astype(BF16).astype(F32)
-        marks = jnp.where((lane >= place) & (lane < place + 3), terms, marks)
-        marks = jnp.where(lane == place + 3, lead, marks)
-        marks = jnp.where(lane == place + 4, total - lead, marks)
-    low = lane < HEAD_DIM
-    left = jnp.where(low, pltpu.roll(done[0], HEAD_DIM, 1), done[1]).astype(BF16)
-    right = jnp.where(low, pltpu.roll(done[2], HEAD_DIM, 1), marks).astype(BF16)
-    for half in range(2):
-        part = slice(half * tile, (half + 1) * tile)
-        out_ref[:, 2 * half * LANES : (2 * half + 1) * LANES] = left[part]
-        out_ref[:, (2 * half + 1) * LANES : (2 * half + 2) * LANES] = right[part]
-
-
-def attention_call(kernel, name, operands, whole, kept, out_shape, out_axes, scratch=()):
-    q = operands[-1] if len(operands[-1].shape) == 4 and operands[-1].dtype == BF16 else operands[-2]
-    heads, _, rows, _ = q.shape
-    tile = ROW_TILE if rows % ROW_TILE == 0 else rows
-
-    def tiled(shape, axis):
-        if axis is None:
-            return pl.BlockSpec(shape, lambda i: (0,) * len(shape))
-        block = tuple(tile if d == axis else n for d, n in enumerate(shape))
-        return pl.BlockSpec(block, lambda i: tuple(i if d == axis else 0 for d in range(len(shape))))
-
-    specs = []
-    for x in operands:
-        specs.append(tiled(x.shape, 2) if x.ndim == 4 else pl.BlockSpec(memory_space=pltpu.SMEM))
-    for x in whole:
-        specs.append(pl.BlockSpec(x.shape, lambda i, n=x.ndim: (0,) * n))
-    specs += [pl.BlockSpec(memory_space=pltpu.HBM)] * len(kept)
-    keys = sum(x.size // (heads * LANES) for x in whole)
-    pairs = heads * 2 * rows * keys
-    out_specs = [tiled(s.shape, a) for s, a in zip(out_shape, out_axes)]
+        spare_ref[count] = block_ref[:, 0]
+        spared = (lane >= HEAD_DIM) & (lane < GUARD)
+        upper = jnp.where(spared, 0.0, q[:, LANES:].astype(F32)).astype(BF16)
+        plain = jnp.concatenate([q[:, :LANES], upper], axis=1)
+
+        def absorb(keys, values, largest, state):
+            scores = scores_of(plain, keys)
+            higher = jnp.maximum(largest, jnp.max(scores, axis=1, keepdims=True))
+            return higher, state * jnp.exp2(largest - higher) + weighted(scores - higher, values)
+
+        def step(at, carry):
+            return absorb(*wide_keys(spare_ref[at].reshape(-1, LANES)), *carry)
+
+        carry = (jnp.full((rows, 1), -1e30, F32), jnp.zeros((rows, LANES), F32))
+        carry = lax.fori_loop(0, count + 1, step, carry)
+        carry = absorb(*wide_keys(first_text_ref[0], valid_ref[0]), *carry)
+        tail = wide_keys(text_ref[0], valid_ref[0] - first_text_ref.shape[1])
+        largest, state = absorb(*tail, *carry)
+        done_ref[head] = state
+        top_ref[head] = with_offset(jnp.zeros((rows, LANES), F32), -largest)
+
+    @pl.when(head == pl.num_programs(0) - 1)
+    def _():
+        marks = jnp.zeros((rows, LANES), F32)
+        done = []
+        for h in range(done_ref.shape[0]):
+            state = done_ref[h]
+            total = pltpu.roll(state, HEAD_DIM, 1)
+            done.append(state / total)
+            terms = top_ref[h] if h == 0 else pltpu.roll(top_ref[h], MARKS * h, 1)
+            place = HEAD_DIM + MARKS * h
+            lead = total.astype(BF16).astype(F32)
+            marks = jnp.where((lane >= place) & (lane < place + 3), terms, marks)
+            marks = jnp.where(lane == place + 3, lead, marks)
+            marks = jnp.where(lane == place + 4, total - lead, marks)
+        low = lane < HEAD_DIM
+        left = jnp.where(low, pltpu.roll(done[0], HEAD_DIM, 1), done[1]).astype(BF16)
+        right = jnp.where(low, pltpu.roll(done[2], HEAD_DIM, 1), marks).astype(BF16)
+        for half in range(2):
+            part = slice(half * tile, (half + 1) * tile)
+            out_ref[:, 2 * half * LANES : (2 * half + 1) * LANES] = left[part]
+            out_ref[:, (2 * half + 1) * LANES : (2 * half + 2) * LANES] = right[part]
+
+
+def attention_call(kernel, name, operands, kept, out_shape, scratch=(), aliases=()):
+    heads = next(x.shape[0] for x in operands if x.ndim == 4)
+
+    def by_head(x):
+        if x.ndim == 1:
+            return pl.BlockSpec(memory_space=pltpu.SMEM)
+        axis = 1 if x.ndim == 4 and x.shape[0] != heads else 0 if x.ndim > 2 else None
+        block = tuple(1 if d == axis else n for d, n in enumerate(x.shape))
+        return pl.BlockSpec(block, lambda h: tuple(h if d == axis else 0 for d in range(x.ndim)))
+
+    specs = [by_head(x) for x in operands] + [pl.BlockSpec(memory_space=pltpu.HBM)] * len(kept)
     return pl.pallas_call(
         kernel,
-        grid=(rows // tile,),
+        grid=(heads,),
         out_shape=out_shape,
         in_specs=specs,
-        out_specs=out_specs,
+        out_specs=[by_head(x) for x in out_shape],
         scratch_shapes=scratch,
-        compiler_params=params(),
-        cost_estimate=pl.CostEstimate(flops=pairs * 6 * LANES, bytes_accessed=4 * q.size, transcendentals=pairs),
+        input_output_aliases=dict(aliases),
+        compiler_params=params(24),
+        cost_estimate=pl.CostEstimate(flops=4 * 10**9, bytes_accessed=8 * 10**6, transcendentals=3 * 10**6),
         name=name,
-    )(*operands, *whole, *kept)
+    )(*operands, *kept)
+
+
+MARK = jax.ShapeDtypeStruct((8, LANES), F32)
 
 
 def state_shape(q):
     return jax.ShapeDtypeStruct(q.shape[:3] + (LANES,), F32)
 
 
-MARK = jax.ShapeDtypeStruct((8, LANES), F32)
-
-
 def first_block(valid, q, block, text):
     shapes = [jax.ShapeDtypeStruct(q.shape, BF16), state_shape(q), MARK]
-    kernel = functools.partial(first_kernel, q.shape[0])
-    return attention_call(kernel, "own_block", [valid, q], [block, text], [], shapes, [2, 2, None])
+    return attention_call(first_kernel, "own_block", [valid, q, block, text], [], shapes)
 
 
 def next_blocks(q, state, blocks, mark):
-    kernel = functools.partial(next_kernel, q.shape[0])
-    return attention_call(kernel, "next_blocks", [q, state], blocks + [mark], [], [state_shape(q), MARK], [2, None])
+    operands = [q, state, *blocks, mark]
+    return attention_call(next_kernel, "next_blocks", operands, [], [state_shape(q), MARK], aliases=[(1, 0)])
 
 
 def last_block(valid, q, state, block, first_text, text, kept):
     heads, _, rows, _ = q.shape
-    tile = ROW_TILE if rows % ROW_TILE == 0 else rows
-    kernel = functools.partial(last_kernel, heads, len(kept))
     shape = jax.ShapeDtypeStruct((rows, 4 * LANES), BF16)
     scratch = [
-        pltpu.VMEM((heads, 2 * tile, LANES), F32),
-        pltpu.VMEM((heads, 2 * tile, LANES), F32),
-        pltpu.VMEM((len(kept) + 1,) + block.shape, BF16),
+        pltpu.VMEM((heads, 2 * rows, LANES), F32),
+        pltpu.VMEM((heads, 2 * rows, LANES), F32),
+        pltpu.VMEM((len(kept) + 1, block.shape[0]) + block.shape[2:], BF16),
         pltpu.SemaphoreType.DMA,
     ]
-    return attention_call(kernel, "last_block", [valid, q, state], [block, first_text, text], kept, [shape], [0], scratch)[0]
+    operands = [valid, q, state, block, first_text, text]
+    return attention_call(functools.partial(last_kernel, len(kept)), "last_block", operands, kept, [shape], scratch)[0]
 
 
 def finish_kernel(
@@ -337,9 +321,7 @@
     attended = wide_ref[...].astype(BF16)
     brought.wait()
     taken.wait()
-    projected = jnp.concatenate(
-        [jnp.dot(attended, held_ref[side], preferred_element_type=F32) for side in range(2)], axis=1
-    )
+    projected = jnp.dot(attended, held_ref[...], preferred_element_type=F32)
     residual = input_ref[...].astype(F32) + modulation_ref[0:1] * (projected + bias_ref[...])
     middle = jnp.mean(residual, axis=-1, keepdims=True)
     centered = residual - middle
@@ -366,7 +348,7 @@
             pltpu.VMEM(hidden.shape, BF16),
             pltpu.SemaphoreType.DMA((2,)),
         ],
-        compiler_params=params(),
+        compiler_params=params(60),
         name="project_and_norm",
     )(partial, weight, hidden, modulation, bias, final_weight, final_bias)
 
@@ -403,15 +385,14 @@
     for i in range(ring):
         route += [(2 * i, 2 * ((i + 1) % ring)), (2 * i + 1, 2 * ((i - 1) % ring) + 1)]
     pass_on = lambda x: lax.ppermute(x, ("zh", "core"), route)
-    near = pass_on(own)
     beside = lax.ppermute(own, "core", [(0, 1), (1, 0)])
+    first, beside = after((own, beside))
+    near = pass_on(first)
     opposite = lax.ppermute(packed, "xh", [(0, 1), (1, 0)])
     cross = pass_on(beside)
     q = unpack_queries(xh.reshape(1), packed, opposite)
 
-    columns = out_weight.shape[1] // 2
-    piece = lax.dynamic_slice_in_dim(out_weight, core * columns, columns, 1)
-    weight = lax.all_gather(piece, ("core", "xh", "y"), axis=0, tiled=True).reshape(2, groups * width, columns)
+    weight = lax.all_gather(out_weight, ("xh", "y"), axis=0, tiled=True)
 
     count = text_kv.shape[1]
     share = -(-count // 32) * 16

time: 191 us -> 193 us (1.010)
  starting transfers between devices: 51 us -> 59.9 us
  local copies, waits for them, and re-layouts: 10.4 us -> 4.46 us
  Pallas kernels: 75.6 us -> 72.7 us
  waiting for transfers between devices: 17.2 us -> 19.8 us
    ppermute x7, starting transfers between devices: 31.9 us -> 42.2 us  [local(): pass_on = lambda x: lax.ppermute(x, ('zh', 'core'), route)]
    unnamed x27 -> x13, local copies, waits for them, and re-layouts: 9.12 us -> 2.53 us
    pallas_call x5, Pallas kernels: 69.6 us -> 65.3 us  [attention_call(): pl.pallas_call(kernel, grid=(heads,), out_shape=out_shape, in_specs=specs...]
    ppermute x7, waiting for transfers between devices: 3.37 us -> 5.8 us  [local(): pass_on = lambda x: lax.ppermute(x, ('zh', 'core'), route)]
  transfers between devices with their start and end apart: 13 -> 13, of which waited for: 3 -> 3; matrix products, arithmetic and copies ran while one was open for 1% -> 1% of each run, Pallas kernels for 37% -> 34%
where the time goes in v7:
time: 193 us; the launch traced here: 192 us
  Pallas kernels  72.7 us (38%)
  starting transfers between devices  59.9 us (31%)
  waiting for transfers between devices  19.8 us (10%)
  blocking collectives  19.2 us (10%)
  between operations  15.7 us (8%)
  local copies, waits for them, and re-layouts  4.46 us (2%)
    pallas_call x5, Pallas kernels, attention_call(): pl.pallas_call(kernel, grid=(heads,), out_shape=out_shape, in_specs=specs...  65.3 us
    ppermute x7, starting transfers between devices, local(): pass_on = lambda x: lax.ppermute(x, ('zh', 'core'), route)  42.2 us
    all_to_all x1, waiting for transfers between devices, local(): lax.all_to_all(partial, BLOCK_AXES, split_axis=0, concat_axis=0, tiled=True)  13.4 us
    all_to_all x1, blocking collectives, local(): lax.all_to_all(slabs, HEAD_AXES, split_axis=0, concat_axis=0, tiled=True)  13.3 us
    pallas_call x1, Pallas kernels, finish(): pl.pallas_call(functools.partial(finish_kernel, heads, groups), out_shape...  6.36 us
    all_gather x1, blocking collectives, local(): packed = lax.all_gather(packed, 'core', axis=0)  5.91 us
    all_to_all x1, starting transfers between devices, local(): lax.all_to_all(partial, BLOCK_AXES, split_axis=0, concat_axis=0, tiled=True)  5.91 us
    ppermute x7, waiting for transfers between devices, local(): pass_on = lambda x: lax.ppermute(x, ('zh', 'core'), route)  5.8 us
  transfers between devices with their start and end apart: 13, of which 3 were waited for; matrix products, arithmetic and copies ran while one was open for 1% of the time, Pallas kernels for 34%

profile of v7, /device:TPU:1, one launch (start us, length us, event | category | flops | bytes accessed | tf_op | source)
XLA Modules:
  0.0 192.3 jit_solution(83556714368866957)
XLA Ops:
  7.2 0.7 all-gather.2.cloned.1.call-update
  7.9 1.0 copy-done
  9.1 13.3 %all_to_all.10 = bf16[8,216,128]{2,1,0:T(8,128)(2,1)S(1)} all-to-all(bf16[8,216,128]{2,1,0:T(8,128)(2,1)S(1)} %pack_heads.1), channel_id=1, replica_groups=mesh['cfg'=2,'zh'=8,'zl'=2,'core'=2,'xh'=2,'y'=4] {'zl','y'}, dimensions={0} | all-to-all | bytes 884736 | tf_op jit(solution)/shard_map/all_to_all | solution.py:380
  22.4 5.9 %all_gather.6.own_ref = bf16[2,8,3,24,128]{4,3,2,1,0:T(8,128)(2,1)S(1)} all-gather(bf16[1,8,3,24,128]{4,3,2,1,0:T(8,128)(2,1)S(1)} %bitcast.31), channel_id=1, replica_groups=mesh['cfg'=2,'zh'=8,'zl'=2,'core'=2,'xh'=2,'y'=4] {'core'}, dimensions={0}, use_global_device_ids=true | all-gather | bytes 442368 | tf_op jit(solution)/shard_map/all_gather | solution.py:382
  28.3 2.3 %collective-permute-start.1 = (bf16[8,3,48,128]{3,2,1,0:T(8,128)(2,1)S(1)}, bf16[8,3,48,128]{3,2,1,0:T(8,128)(2,1)S(1)}, u32[]{:S(2)}, u32[]{:S(2)}) collective-permute-start(bf16[8,3,48,128]{3,2,1,0:T(8,128)(2,1)S(1)} %bitcast.26), channel_id=1, source_target_pairs={{0,8},{8,0},{1,9},{9,1},{2,10},{10,2},{3,11},{11,3},{4,12},{12,4},... | collective-permute-start | bytes 884744 | tf_op jit(solution)/shard_map/ppermute | solution.py:388
  30.6 3.5 %collective-permute-start = (bf16[2,8,3,24,128]{4,3,2,1,0:T(8,128)(2,1)S(1)}, bf16[2,8,3,24,128]{4,3,2,1,0:T(8,128)(2,1)S(1)}, u32[]{:S(2)}, u32[]{:S(2)}) collective-permute-start(bf16[2,8,3,24,128]{4,3,2,1,0:T(8,128)(2,1)S(1)} %all_gather.6.own_ref), channel_id=1, source_target_pairs={{0,4},{4,0},{1,5},{5,1},{2,6},{6,2},{3,7},{7,3},{8,12},{12,8},{9,1... | collective-permute-start | bytes 884744 | tf_op jit(solution)/shard_map/ppermute | solution.py:391
  34.1 0.2 copy.23
  34.4 10.7 %collective-permute-start.3 = (bf16[8,3,48,128]{3,2,1,0:T(8,128)(2,1)S(1)}, bf16[8,3,48,128]{3,2,1,0:T(8,128)(2,1)S(1)}, u32[]{:S(2)}, u32[]{:S(2)}) collective-permute-start(bf16[8,3,48,128]{3,2,1,0:T(8,128)(2,1)S(1)} %collective-permute-done.1), channel_id=1, source_target_pairs={{0,32},{8,232},{32,64},{40,8},{64,96},{72,40},{96,128},{104,72},{1... | collective-permute-start | bytes 884744 | tf_op jit(solution)/shard_map/ppermute | solution.py:387
  45.1 3.1 %collective-permute-start.2 = (bf16[8,3,48,128]{3,2,1,0:T(8,128)(2,1)S(1)}, bf16[8,3,48,128]{3,2,1,0:T(8,128)(2,1)S(1)}, u32[]{:S(2)}, u32[]{:S(2)}) collective-permute-start(bf16[8,3,48,128]{3,2,1,0:T(8,128)(2,1)S(1)} %bitcast.27), channel_id=1, source_target_pairs={{0,32},{8,232},{32,64},{40,8},{64,96},{72,40},{96,128},{104,72},{1... | collective-permute-start | bytes 884744 | tf_op jit(solution)/shard_map/ppermute | solution.py:387
  48.2 0.8 unpack_queries.1.q_ref
  49.0 5.4 %own_block.1 = (bf16[3,2,768,256]{3,2,1,0:T(8,128)(2,1)S(1)}, f32[3,2,768,128]{3,2,1,0:T(8,128)S(1)}, f32[8,128]{1,0:T(8,128)S(1)}) custom-call(s32[1]{0:T(128)} %bitcast.valid_ref, bf16[3,2,768,256]{3,2,1,0:T(8,128)(2,1)S(1)} %unpack_queries.1.q_ref, bf16[8,3,48,128]{3,2,1,0:T(8,128)(2,1)S(1)} %bitcast.28, ...), custom_call_target="tpu_custom_call" | custom-call | flops 4000000000 | bytes 8000000 | tf_op jit(solution)/shard_map/own_block/pallas_call | solution.py:231
  54.4 9.4 %collective-permute-start.5 = (bf16[8,3,48,128]{3,2,1,0:T(8,128)(2,1)S(1)}, bf16[8,3,48,128]{3,2,1,0:T(8,128)(2,1)S(1)}, u32[]{:S(2)}, u32[]{:S(2)}) collective-permute-start(bf16[8,3,48,128]{3,2,1,0:T(8,128)(2,1)S(1)} %collective-permute-done.3.refs_1_.refs_2_), channel_id=1, source_target_pairs={{0,32},{8,232},{32,64},{40,8},{64,96},{72,40},{96,128},{104,72},{1... | collective-permute-start | bytes 884744 | tf_op jit(solution)/shard_map/ppermute | solution.py:387
  63.8 4.0 %collective-permute-start.4 = (bf16[8,3,48,128]{3,2,1,0:T(8,128)(2,1)S(1)}, bf16[8,3,48,128]{3,2,1,0:T(8,128)(2,1)S(1)}, u32[]{:S(2)}, u32[]{:S(2)}) collective-permute-start(bf16[8,3,48,128]{3,2,1,0:T(8,128)(2,1)S(1)} %collective-permute-done.2.refs_0_.refs_1_), channel_id=1, source_target_pairs={{0,32},{8,232},{32,64},{40,8},{64,96},{72,40},{96,128},{104,72},{1... | collective-permute-start | bytes 884744 | tf_op jit(solution)/shard_map/ppermute | solution.py:387
  67.9 4.5 %next_blocks.3 = (f32[3,2,768,128]{3,2,1,0:T(8,128)S(1)}, f32[8,128]{1,0:T(8,128)S(1)}) custom-call(bf16[3,2,768,256]{3,2,1,0:T(8,128)(2,1)S(1)} %get-tuple-element.24.q_ref, f32[3,2,768,128]{3,2,1,0:T(8,128)S(1)} %get-tuple-element.25.state_ref, bf16[8,3,48,128]{3,2,1,0:T(8,128)(2,1)S(1)} %collective-permute-done.2.refs_0_.refs_1_, ...), custom_call_target="tpu_custom_call", output_to_operand_aliasing={{0}: (1, {})} | custom-call | flops 4000000000 | bytes 8000000 | tf_op jit(solution)/shard_map/next_blocks/pallas_call | solution.py:231
  72.4 4.5 %collective-permute-done.4.refs_0_.refs_3_ = bf16[8,3,48,128]{3,2,1,0:T(8,128)(2,1)S(1)} collective-permute-done((bf16[8,3,48,128]{3,2,1,0:T(8,128)(2,1)S(1)}, bf16[8,3,48,128]{3,2,1,0:T(8,128)(2,1)S(1)}, u32[]{:S(2)}, u32[]{:S(2)}) %collective-permute-start.4) | collective-permute-done | bytes 294944 | tf_op jit(solution)/shard_map/ppermute | solution.py:387
  76.9 5.9 %collective-permute-start.6 = (bf16[8,3,48,128]{3,2,1,0:T(8,128)(2,1)S(1)}, bf16[8,3,48,128]{3,2,1,0:T(8,128)(2,1)S(1)}, u32[]{:S(2)}, u32[]{:S(2)}) collective-permute-start(bf16[8,3,48,128]{3,2,1,0:T(8,128)(2,1)S(1)} %collective-permute-done.4.refs_0_.refs_3_), channel_id=1, source_target_pairs={{0,32},{8,232},{32,64},{40,8},{64,96},{72,40},{96,128},{104,72},{1... | collective-permute-start | bytes 884744 | tf_op jit(solution)/shard_map/ppermute | solution.py:387
  82.9 3.1 %collective-permute-start.7 = (bf16[8,3,48,128]{3,2,1,0:T(8,128)(2,1)S(1)}, bf16[8,3,48,128]{3,2,1,0:T(8,128)(2,1)S(1)}, u32[]{:S(2)}, u32[]{:S(2)}) collective-permute-start(bf16[8,3,48,128]{3,2,1,0:T(8,128)(2,1)S(1)} %collective-permute-done.5.refs_1_.refs_4_), channel_id=1, source_target_pairs={{0,32},{8,232},{32,64},{40,8},{64,96},{72,40},{96,128},{104,72},{1... | collective-permute-start | bytes 884744 | tf_op jit(solution)/shard_map/ppermute | solution.py:387
  86.0 4.5 %next_blocks.4 = (f32[3,2,768,128]{3,2,1,0:T(8,128)S(1)}, f32[8,128]{1,0:T(8,128)S(1)}) custom-call(bf16[3,2,768,256]{3,2,1,0:T(8,128)(2,1)S(1)} %get-tuple-element.24.q_ref, f32[3,2,768,128]{3,2,1,0:T(8,128)S(1)} %get-tuple-element.31.state_ref, bf16[8,3,48,128]{3,2,1,0:T(8,128)(2,1)S(1)} %collective-permute-done.4.refs_0_.refs_3_, ...), custom_call_target="tpu_custom_call", output_to_operand_aliasing={{0}: (1, {})} | custom-call | flops 4000000000 | bytes 8000000 | tf_op jit(solution)/shard_map/next_blocks/pallas_call | solution.py:231
  90.5 6.0 %collective-permute-start.8 = (bf16[8,3,48,128]{3,2,1,0:T(8,128)(2,1)S(1)}, bf16[8,3,48,128]{3,2,1,0:T(8,128)(2,1)S(1)}, u32[]{:S(2)}, u32[]{:S(2)}) collective-permute-start(bf16[8,3,48,128]{3,2,1,0:T(8,128)(2,1)S(1)} %collective-permute-done.6.refs_0_.refs_5_), channel_id=1, source_target_pairs={{0,32},{8,232},{32,64},{40,8},{64,96},{72,40},{96,128},{104,72},{1... | collective-permute-start | bytes 884744 | tf_op jit(solution)/shard_map/ppermute | solution.py:387
  96.6 1.2 collective-permute-done.7.refs_1_.refs_6_
  97.8 5.0 %next_blocks.5 = (f32[3,2,768,128]{3,2,1,0:T(8,128)S(1)}, f32[8,128]{1,0:T(8,128)}) custom-call(bf16[3,2,768,256]{3,2,1,0:T(8,128)(2,1)S(1)} %get-tuple-element.24.q_ref, f32[3,2,768,128]{3,2,1,0:T(8,128)S(1)} %get-tuple-element.37.state_ref, bf16[8,3,48,128]{3,2,1,0:T(8,128)(2,1)S(1)} %collective-permute-done.6.refs_0_.refs_5_, ...), custom_call_target="tpu_custom_call", output_to_operand_aliasing={{0}: (1, {})} | custom-call | flops 4000000000 | bytes 8000000 | tf_op jit(solution)/shard_map/next_blocks/pallas_call | solution.py:231
  102.9 45.8 %last_block.1 = bf16[768,512]{1,0:T(8,128)(2,1)} custom-call(s32[1]{0:T(128)} %bitcast.valid_ref, bf16[3,2,768,256]{3,2,1,0:T(8,128)(2,1)S(1)} %get-tuple-element.24.q_ref, f32[3,2,768,128]{3,2,1,0:T(8,128)S(1)} %get-tuple-element.41.state_ref, bf16[8,3,48,128]{3,2,1,0:T(8,128)(2,1)S(1)} %collective-permute-done.8.block_ref, ...), custom_call_target="tpu_custom_call" | custom-call | flops 4000000000 | bytes 8000000 | tf_op jit(solution)/shard_map/last_block/pallas_call | solution.py:231
  148.7 5.9 %all-to-all-start.1 = ((bf16[32,24,512]{2,1,0:T(8,128)(2,1)}), bf16[32,24,512]{2,1,0:T(8,128)(2,1)S(1)}, u32[]{:S(2)}, u32[]{:S(2)}) async-start(bf16[32,24,512]{2,1,0:T(8,128)(2,1)} %bitcast.9), calls=%async_computation.1 | async-start | bytes 1572864 | tf_op jit(solution)/shard_map/all_to_all | solution.py:420
  154.6 0.6 copy.28
  155.2 0.6 broadcast_in_dim.6.bias_ref
  155.8 13.4 %all-to-all-done.1.partial_ref = bf16[32,24,512]{2,1,0:T(8,128)(2,1)S(1)} async-done(((bf16[32,24,512]{2,1,0:T(8,128)(2,1)}), bf16[32,24,512]{2,1,0:T(8,128)(2,1)S(1)}, u32[]{:S(2)}, u32[]{:S(2)}) %all-to-all-start.1) | async-done | bytes 786464 | tf_op jit(solution)/shard_map/all_to_all | solution.py:420
  169.2 0.9 copy-done.1
  170.1 6.4 %project_and_norm.1 = f32[48,64]{1,0:T(8,128)} custom-call(bf16[32,24,512]{2,1,0:T(8,128)(2,1)} %copy-done.1, bf16[1536,1536]{1,0:T(8,128)(2,1)} %all-gather.2.cloned.1.call-done.weight_ref, bf16[48,1536]{1,0:T(8,128)(2,1)} %bitcast.34, f32[3,1536]{1,0:T(4,128)} %bitcast.36, f32[1,1536]{1,0:T(1,128)} %broadcast_in_dim.6.bias_ref, bf16[64,1536]{1,0:T(8,128)(2,1)} %bitcast.33, ...), custom_call_target="tpu_custom_call" | custom-call | tf_op jit(solution)/shard_map/project_and_norm/pallas_call | solution.py:340
  176.5 0.8 copy.24
  177.5 0.7 collective-permute-start.10
  178.2 5.3 %collective-permute-start.9 = (f32[1,1536]{1,0:T(1,128)S(1)}, f32[1,1536]{1,0:T(1,128)S(1)}, u32[]{:S(2)}, u32[]{:S(2)}) collective-permute-start(f32[1,1536]{1,0:T(1,128)S(1)} %get-tuple-element.44), channel_id=1, source_target_pairs={{0,1},{1,257},{2,3},{3,259},{256,0},{257,256},{258,2},{259,258},{4... | collective-permute-start | bytes 18440 | tf_op jit(solution)/shard_map/ppermute | solution.py:443
  184.8 0.6 multiply_subtract_fusion
  (30 shorter events, 0.6 us)
Async XLA Ops:
  7.2 26.9 %copy-start.2 = (bf16[1,333,2,192]{1,3,2,0:T(8,128)(2,1)S(1)}, bf16[1,333,2,192]{1,3,2,0:T(8,128)(2,1)}, u32[]{:S(2)}) copy-start(bf16[1,333,2,192]{1,3,2,0:T(8,128)(2,1)} %param.12) | copy-start | bytes 767236
  7.2 162.0 %all-gather.2.cloned.1.call-start = ((), (), s32[]{:S(2)}) async-start(), calls=%async_computation.2 | async-start | bytes 5308416 | tf_op jit(solution)/shard_map/all_gather | solution.py:395
  7.9 1.0 copy-start
  28.3 6.1 %collective-permute-start.1 = (bf16[8,3,48,128]{3,2,1,0:T(8,128)(2,1)S(1)}, bf16[8,3,48,128]{3,2,1,0:T(8,128)(2,1)S(1)}, u32[]{:S(2)}, u32[]{:S(2)}) collective-permute-start(bf16[8,3,48,128]{3,2,1,0:T(8,128)(2,1)S(1)} %bitcast.26), channel_id=1, source_target_pairs={{0,8},{8,0},{1,9},{9,1},{2,10},{10,2},{3,11},{11,3},{4,12},{12,4},... | collective-permute-start | bytes 884744 | tf_op jit(solution)/shard_map/ppermute | solution.py:388
  30.6 17.6 %collective-permute-start = (bf16[2,8,3,24,128]{4,3,2,1,0:T(8,128)(2,1)S(1)}, bf16[2,8,3,24,128]{4,3,2,1,0:T(8,128)(2,1)S(1)}, u32[]{:S(2)}, u32[]{:S(2)}) collective-permute-start(bf16[2,8,3,24,128]{4,3,2,1,0:T(8,128)(2,1)S(1)} %all_gather.6.own_ref), channel_id=1, source_target_pairs={{0,4},{4,0},{1,5},{5,1},{2,6},{6,2},{3,7},{7,3},{8,12},{12,8},{9,1... | collective-permute-start | bytes 884744 | tf_op jit(solution)/shard_map/ppermute | solution.py:391
  34.4 20.0 %collective-permute-start.3 = (bf16[8,3,48,128]{3,2,1,0:T(8,128)(2,1)S(1)}, bf16[8,3,48,128]{3,2,1,0:T(8,128)(2,1)S(1)}, u32[]{:S(2)}, u32[]{:S(2)}) collective-permute-start(bf16[8,3,48,128]{3,2,1,0:T(8,128)(2,1)S(1)} %collective-permute-done.1), channel_id=1, source_target_pairs={{0,32},{8,232},{32,64},{40,8},{64,96},{72,40},{96,128},{104,72},{1... | collective-permute-start | bytes 884744 | tf_op jit(solution)/shard_map/ppermute | solution.py:387
  45.1 18.7 %collective-permute-start.2 = (bf16[8,3,48,128]{3,2,1,0:T(8,128)(2,1)S(1)}, bf16[8,3,48,128]{3,2,1,0:T(8,128)(2,1)S(1)}, u32[]{:S(2)}, u32[]{:S(2)}) collective-permute-start(bf16[8,3,48,128]{3,2,1,0:T(8,128)(2,1)S(1)} %bitcast.27), channel_id=1, source_target_pairs={{0,32},{8,232},{32,64},{40,8},{64,96},{72,40},{96,128},{104,72},{1... | collective-permute-start | bytes 884744 | tf_op jit(solution)/shard_map/ppermute | solution.py:387
  54.4 22.5 %collective-permute-start.5 = (bf16[8,3,48,128]{3,2,1,0:T(8,128)(2,1)S(1)}, bf16[8,3,48,128]{3,2,1,0:T(8,128)(2,1)S(1)}, u32[]{:S(2)}, u32[]{:S(2)}) collective-permute-start(bf16[8,3,48,128]{3,2,1,0:T(8,128)(2,1)S(1)} %collective-permute-done.3.refs_1_.refs_2_), channel_id=1, source_target_pairs={{0,32},{8,232},{32,64},{40,8},{64,96},{72,40},{96,128},{104,72},{1... | collective-permute-start | bytes 884744 | tf_op jit(solution)/shard_map/ppermute | solution.py:387
  63.8 13.1 %collective-permute-start.4 = (bf16[8,3,48,128]{3,2,1,0:T(8,128)(2,1)S(1)}, bf16[8,3,48,128]{3,2,1,0:T(8,128)(2,1)S(1)}, u32[]{:S(2)}, u32[]{:S(2)}) collective-permute-start(bf16[8,3,48,128]{3,2,1,0:T(8,128)(2,1)S(1)} %collective-permute-done.2.refs_0_.refs_1_), channel_id=1, source_target_pairs={{0,32},{8,232},{32,64},{40,8},{64,96},{72,40},{96,128},{104,72},{1... | collective-permute-start | bytes 884744 | tf_op jit(solution)/shard_map/ppermute | solution.py:387
  76.9 13.6 %collective-permute-start.6 = (bf16[8,3,48,128]{3,2,1,0:T(8,128)(2,1)S(1)}, bf16[8,3,48,128]{3,2,1,0:T(8,128)(2,1)S(1)}, u32[]{:S(2)}, u32[]{:S(2)}) collective-permute-start(bf16[8,3,48,128]{3,2,1,0:T(8,128)(2,1)S(1)} %collective-permute-done.4.refs_0_.refs_3_), channel_id=1, source_target_pairs={{0,32},{8,232},{32,64},{40,8},{64,96},{72,40},{96,128},{104,72},{1... | collective-permute-start | bytes 884744 | tf_op jit(solution)/shard_map/ppermute | solution.py:387
  82.9 14.9 %collective-permute-start.7 = (bf16[8,3,48,128]{3,2,1,0:T(8,128)(2,1)S(1)}, bf16[8,3,48,128]{3,2,1,0:T(8,128)(2,1)S(1)}, u32[]{:S(2)}, u32[]{:S(2)}) collective-permute-start(bf16[8,3,48,128]{3,2,1,0:T(8,128)(2,1)S(1)} %collective-permute-done.5.refs_1_.refs_4_), channel_id=1, source_target_pairs={{0,32},{8,232},{32,64},{40,8},{64,96},{72,40},{96,128},{104,72},{1... | collective-permute-start | bytes 884744 | tf_op jit(solution)/shard_map/ppermute | solution.py:387
  90.5 12.3 %collective-permute-start.8 = (bf16[8,3,48,128]{3,2,1,0:T(8,128)(2,1)S(1)}, bf16[8,3,48,128]{3,2,1,0:T(8,128)(2,1)S(1)}, u32[]{:S(2)}, u32[]{:S(2)}) collective-permute-start(bf16[8,3,48,128]{3,2,1,0:T(8,128)(2,1)S(1)} %collective-permute-done.6.refs_0_.refs_5_), channel_id=1, source_target_pairs={{0,32},{8,232},{32,64},{40,8},{64,96},{72,40},{96,128},{104,72},{1... | collective-permute-start | bytes 884744 | tf_op jit(solution)/shard_map/ppermute | solution.py:387
  102.9 51.7 %copy-start.3 = (f32[1,3,1536]{2,0,1:T(1,128)S(1)}, f32[1,3,1536]{2,0,1:T(1,128)}, u32[]{:S(2)}) copy-start(f32[1,3,1536]{2,0,1:T(1,128)} %param.14) | copy-start | bytes 55300
  102.9 52.4 %copy-start.4 = (f32[1536]{0:T(1024)S(1)}, f32[1536]{0:T(1024)}, u32[]{:S(2)}) copy-start(f32[1536]{0:T(1024)} %param.16) | copy-start | bytes 18436
  148.7 20.5 %all-to-all-start.1 = ((bf16[32,24,512]{2,1,0:T(8,128)(2,1)}), bf16[32,24,512]{2,1,0:T(8,128)(2,1)S(1)}, u32[]{:S(2)}, u32[]{:S(2)}) async-start(bf16[32,24,512]{2,1,0:T(8,128)(2,1)} %bitcast.9), calls=%async_computation.1 | async-start | bytes 1572864 | tf_op jit(solution)/shard_map/all_to_all | solution.py:420
  169.2 0.9 copy-start.1
  170.1 14.7 %copy-start.5 = (f32[1,1536]{1,0:T(1,128)S(1)}, f32[1,1536]{1,0:T(1,128)}, u32[]{:S(2)}) copy-start(f32[1,1536]{1,0:T(1,128)} %param.21) | copy-start | bytes 18436
  177.5 7.3 %collective-permute-start.10 = (f32[1,1536]{1,0:T(1,128)S(1)}, f32[1,1536]{1,0:T(1,128)S(1)}, u32[]{:S(2)}, u32[]{:S(2)}) collective-permute-start(f32[1,1536]{1,0:T(1,128)S(1)} %get-tuple-element.45), channel_id=1, source_target_pairs={{0,0},{1,256},{2,2},{3,258},{256,1},{257,257},{258,3},{259,259},{4... | collective-permute-start | bytes 18440 | tf_op jit(solution)/shard_map/ppermute | solution.py:442
  178.2 6.6 %collective-permute-start.9 = (f32[1,1536]{1,0:T(1,128)S(1)}, f32[1,1536]{1,0:T(1,128)S(1)}, u32[]{:S(2)}, u32[]{:S(2)}) collective-permute-start(f32[1,1536]{1,0:T(1,128)S(1)} %get-tuple-element.44), channel_id=1, source_target_pairs={{0,1},{1,257},{2,3},{3,259},{256,0},{257,256},{258,2},{259,258},{4... | collective-permute-start | bytes 18440 | tf_op jit(solution)/shard_map/ppermute | solution.py:443
Sparse Core Ops, SparseCore 0:
  11.2 101.1 all-gather.1

commit v8 on v6

--- a/solution.py
+++ b/solution.py
@@ -21,8 +21,8 @@
 BLOCK_AXES = ("zl", "core", "xh", "y")
 
 
-def params(**extra):
-    return pltpu.CompilerParams(vmem_limit_bytes=32 * 1024 * 1024, **extra)
+def params(mib=32):
+    return pltpu.CompilerParams(vmem_limit_bytes=mib * 1024 * 1024)
 
 
 def lane_index(shape):
@@ -139,15 +139,14 @@
         full_ref[head, :, :, LANES:] = upper.astype(BF16).reshape(state_ref.shape[1:])
 
 
-def next_kernel(heads, q_ref, state_ref, *refs):
+def next_kernel(q_ref, state_ref, *refs):
     *blocks, before_ref, out_ref, mark_ref = refs
     mark_ref[...] = before_ref[...]
     rows = 2 * q_ref.shape[2]
-    for head in range(heads):
-        q = q_ref[head].reshape(rows, 2 * LANES)
-        keys, values = wide_keys(jnp.concatenate([rows_of(ref, head) for ref in blocks], axis=0))
-        state = weighted(scores_of(q, keys), values)
-        out_ref[head] = state_ref[head] + state.reshape(out_ref.shape[1:])
+    q = q_ref[0].reshape(rows, 2 * LANES)
+    keys, values = wide_keys(jnp.concatenate([rows_of(ref, 0) for ref in blocks], axis=0))
+    state = weighted(scores_of(q, keys), values)
+    out_ref[0] = state_ref[0] + state.reshape(out_ref.shape[1:])
 
 
 def last_kernel(heads, count, valid_ref, q_ref, state_ref, block_ref, first_text_ref, text_ref, *refs):
@@ -270,8 +269,22 @@
 
 
 def next_blocks(q, state, blocks, mark):
-    kernel = functools.partial(next_kernel, q.shape[0])
-    return attention_call(kernel, "next_blocks", [q, state], blocks + [mark], [], [state_shape(q), MARK], [2, None])
+    heads, _, rows, _ = q.shape
+    step = lambda x: pl.BlockSpec((1,) + x.shape[1:], lambda h: (h, 0, 0, 0))
+    block_step = lambda x: pl.BlockSpec((x.shape[0], 1) + x.shape[2:], lambda h: (0, h, 0, 0))
+    mark_spec = pl.BlockSpec(mark.shape, lambda h: (0, 0))
+    pairs = heads * 2 * rows * sum(x.size // (heads * LANES) for x in blocks)
+    return pl.pallas_call(
+        next_kernel,
+        grid=(heads,),
+        out_shape=[state_shape(q), MARK],
+        in_specs=[step(q), step(state), *map(block_step, blocks), mark_spec],
+        out_specs=[step(state), mark_spec],
+        input_output_aliases={1: 0},
+        compiler_params=params(16),
+        cost_estimate=pl.CostEstimate(flops=pairs * 6 * LANES, bytes_accessed=4 * q.size, transcendentals=pairs),
+        name="next_blocks",
+    )(q, state, *blocks, mark)
 
 
 def last_block(valid, q, state, block, first_text, text, kept):
@@ -300,14 +313,7 @@
     final_bias_ref,
     out_ref,
     wide_ref,
-    held_ref,
-    input_ref,
-    sems,
 ):
-    brought = pltpu.make_async_copy(weight_ref, held_ref, sems.at[0])
-    taken = pltpu.make_async_copy(hidden_ref, input_ref, sems.at[1])
-    brought.start()
-    taken.start()
     half = partial_ref.shape[1]
     sources = partial_ref.shape[0]
     across = groups // 2
@@ -335,12 +341,10 @@
             both = jnp.concatenate([first, second[:, :HEAD_DIM]], axis=1)
             wide_ref[part * half : (part + 1) * half, group * width : (group + 1) * width] = both
     attended = wide_ref[...].astype(BF16)
-    brought.wait()
-    taken.wait()
     projected = jnp.concatenate(
-        [jnp.dot(attended, held_ref[side], preferred_element_type=F32) for side in range(2)], axis=1
+        [jnp.dot(attended, weight_ref[side], preferred_element_type=F32) for side in range(2)], axis=1
     )
-    residual = input_ref[...].astype(F32) + modulation_ref[0:1] * (projected + bias_ref[...])
+    residual = hidden_ref[...].astype(F32) + modulation_ref[0:1] * (projected + bias_ref[...])
     middle = jnp.mean(residual, axis=-1, keepdims=True)
     centered = residual - middle
     spread = jnp.mean(centered * centered, axis=-1, keepdims=True)
@@ -353,20 +357,11 @@
 
 def finish(partial, weight, hidden, modulation, bias, final_weight, final_bias, heads, groups):
     tokens, width = hidden.shape
-    vmem = pl.BlockSpec(memory_space=pltpu.VMEM)
-    hbm = pl.BlockSpec(memory_space=pltpu.HBM)
     return pl.pallas_call(
         functools.partial(finish_kernel, heads, groups),
         out_shape=jax.ShapeDtypeStruct((tokens, final_weight.shape[0]), F32),
-        in_specs=[vmem, hbm, hbm, vmem, vmem, vmem, vmem],
-        out_specs=vmem,
-        scratch_shapes=[
-            pltpu.VMEM((tokens, width), F32),
-            pltpu.VMEM(weight.shape, BF16),
-            pltpu.VMEM(hidden.shape, BF16),
-            pltpu.SemaphoreType.DMA((2,)),
-        ],
-        compiler_params=params(),
+        scratch_shapes=[pltpu.VMEM((tokens, width), F32)],
+        compiler_params=params(16),
         name="project_and_norm",
     )(partial, weight, hidden, modulation, bias, final_weight, final_bias)
 
@@ -435,7 +430,7 @@
     farthest = pass_on(near)
     state, mark = next_blocks(q, state, [near, cross], mark)
     partial = last_block(valid, q, state, farthest, early, late, kept)
-    partial = partial.reshape(4 * groups, half, 4 * LANES)
+    partial, weight = after((partial.reshape(4 * groups, half, 4 * LANES), weight))
     partial = lax.all_to_all(partial, BLOCK_AXES, split_axis=0, concat_axis=0, tiled=True)
 
     velocity = finish(

time: 191 us -> 191 us (level)
  local copies, waits for them, and re-layouts: 10.4 us -> 13.6 us
    pallas_call x0 -> x3, Pallas kernels: none -> 16.8 us  [next_blocks(): pl.pallas_call(next_kernel, grid=(heads,), out_shape=[state_shape(q), MAR...]
    pallas_call x5 -> x2, Pallas kernels: 69.6 us -> 54 us  [attention_call(): pl.pallas_call(kernel, grid=(rows // tile,), out_shape=out_shape, in_spec...]
    unnamed x27 -> x31, local copies, waits for them, and re-layouts: 9.12 us -> 12.2 us
  transfers between devices with their start and end apart: 13 -> 13, of which waited for: 3 -> 2; matrix products, arithmetic and copies ran while one was open for 1% -> 1% of each run, Pallas kernels for 37% -> 38%
where the time goes in v8:
time: 191 us; the launch traced here: 190 us
  Pallas kernels  75.1 us (39%)
  starting transfers between devices  50.1 us (26%)
  blocking collectives  19.2 us (10%)
  waiting for transfers between devices  16.1 us (8%)
  between operations  15.7 us (8%)
  local copies, waits for them, and re-layouts  13.6 us (7%)
    pallas_call x2, Pallas kernels, attention_call(): pl.pallas_call(kernel, grid=(rows // tile,), out_shape=out_shape, in_spec...  54 us
    ppermute x7, starting transfers between devices, local(): pass_on = lambda x: lax.ppermute(x, ('zh', 'core'), route)  31.5 us
    pallas_call x3, Pallas kernels, next_blocks(): pl.pallas_call(next_kernel, grid=(heads,), out_shape=[state_shape(q), MAR...  16.8 us
    all_to_all x1, waiting for transfers between devices, local(): lax.all_to_all(partial, BLOCK_AXES, split_axis=0, concat_axis=0, tiled=True)  13.8 us
    all_to_all x1, blocking collectives, local(): lax.all_to_all(slabs, HEAD_AXES, split_axis=0, concat_axis=0, tiled=True)  13.3 us
    unnamed x31, local copies, waits for them, and re-layouts  12.2 us
    all_gather x1, blocking collectives, local(): packed = lax.all_gather(packed, 'core', axis=0)  5.91 us
    all_to_all x1, starting transfers between devices, local(): lax.all_to_all(partial, BLOCK_AXES, split_axis=0, concat_axis=0, tiled=True)  5.63 us
  transfers between devices with their start and end apart: 13, of which 2 were waited for; matrix products, arithmetic and copies ran while one was open for 1% of the time, Pallas kernels for 38%

profile of v8, /device:TPU:1, one launch (start us, length us, event | category | flops | bytes accessed | tf_op | source)
XLA Modules:
  0.0 190.4 jit_solution(2633930188659407897)
XLA Ops:
  7.2 1.0 copy-done
  8.2 0.7 constant_dynamic-slice_fusion.2
  9.0 1.0 copy-done.6
  10.2 13.3 %all_to_all.10 = bf16[8,216,128]{2,1,0:T(8,128)(2,1)S(1)} all-to-all(bf16[8,216,128]{2,1,0:T(8,128)(2,1)S(1)} %pack_heads.1), channel_id=1, replica_groups=mesh['cfg'=2,'zh'=8,'zl'=2,'core'=2,'xh'=2,'y'=4] {'zl','y'}, dimensions={0} | all-to-all | bytes 884736 | tf_op jit(solution)/shard_map/all_to_all | solution.py:393
  23.5 5.9 %all_gather.6.own_ref = bf16[2,8,3,24,128]{4,3,2,1,0:T(8,128)(2,1)S(1)} all-gather(bf16[1,8,3,24,128]{4,3,2,1,0:T(8,128)(2,1)S(1)} %bitcast.37), channel_id=1, replica_groups=mesh['cfg'=2,'zh'=8,'zl'=2,'core'=2,'xh'=2,'y'=4] {'core'}, dimensions={0}, use_global_device_ids=true | all-gather | bytes 442368 | tf_op jit(solution)/shard_map/all_gather | solution.py:395
  29.4 2.3 %collective-permute-start.2 = (bf16[8,3,48,128]{3,2,1,0:T(8,128)(2,1)S(1)}, bf16[8,3,48,128]{3,2,1,0:T(8,128)(2,1)}, u32[]{:S(2)}, u32[]{:S(2)}) collective-permute-start(bf16[8,3,48,128]{3,2,1,0:T(8,128)(2,1)S(1)} %bitcast.27), channel_id=1, source_target_pairs={{0,8},{8,0},{1,9},{9,1},{2,10},{10,2},{3,11},{11,3},{4,12},{12,4},... | collective-permute-start | bytes 884744 | tf_op jit(solution)/shard_map/ppermute | solution.py:402
  31.7 9.5 %collective-permute-start.1 = (bf16[8,3,48,128]{3,2,1,0:T(8,128)(2,1)S(1)}, bf16[8,3,48,128]{3,2,1,0:T(8,128)(2,1)}, u32[]{:S(2)}, u32[]{:S(2)}) collective-permute-start(bf16[8,3,48,128]{3,2,1,0:T(8,128)(2,1)S(1)} %bitcast.28), channel_id=1, source_target_pairs={{0,32},{8,232},{32,64},{40,8},{64,96},{72,40},{96,128},{104,72},{1... | collective-permute-start | bytes 884744 | tf_op jit(solution)/shard_map/ppermute | solution.py:400
  41.2 4.7 %collective-permute-start = (bf16[2,8,3,24,128]{4,3,2,1,0:T(8,128)(2,1)S(1)}, bf16[2,8,3,24,128]{4,3,2,1,0:T(8,128)(2,1)S(1)}, u32[]{:S(2)}, u32[]{:S(2)}) collective-permute-start(bf16[2,8,3,24,128]{4,3,2,1,0:T(8,128)(2,1)S(1)} %all_gather.6.own_ref), channel_id=1, source_target_pairs={{0,4},{4,0},{1,5},{5,1},{2,6},{6,2},{3,7},{7,3},{8,12},{12,8},{9,1... | collective-permute-start | bytes 884744 | tf_op jit(solution)/shard_map/ppermute | solution.py:403
  45.9 3.1 %collective-permute-start.3 = (bf16[8,3,48,128]{3,2,1,0:T(8,128)(2,1)}, bf16[8,3,48,128]{3,2,1,0:T(8,128)(2,1)}, u32[]{:S(2)}, u32[]{:S(2)}) collective-permute-start(bf16[8,3,48,128]{3,2,1,0:T(8,128)(2,1)} %collective-permute-done.2), channel_id=1, source_target_pairs={{0,32},{8,232},{32,64},{40,8},{64,96},{72,40},{96,128},{104,72},{1... | collective-permute-start | bytes 884744 | tf_op jit(solution)/shard_map/ppermute | solution.py:400
  49.3 4.9 %collective-permute-start.4 = (bf16[8,3,48,128]{3,2,1,0:T(8,128)(2,1)}, bf16[8,3,48,128]{3,2,1,0:T(8,128)(2,1)}, u32[]{:S(2)}, u32[]{:S(2)}) collective-permute-start(bf16[8,3,48,128]{3,2,1,0:T(8,128)(2,1)} %collective-permute-done.1.refs_0_.refs_1_), channel_id=1, source_target_pairs={{0,32},{8,232},{32,64},{40,8},{64,96},{72,40},{96,128},{104,72},{1... | collective-permute-start | bytes 884744 | tf_op jit(solution)/shard_map/ppermute | solution.py:400
  54.2 0.8 unpack_queries.1.q_ref
  55.0 3.9 %own_block.1 = (bf16[3,2,768,256]{3,2,1,0:T(8,128)(2,1)S(1)}, f32[3,2,768,128]{3,2,1,0:T(8,128)S(1)}, f32[8,128]{1,0:T(8,128)S(1)}) custom-call(s32[1]{0:T(128)} %bitcast.valid_ref, bf16[3,2,768,256]{3,2,1,0:T(8,128)(2,1)S(1)} %unpack_queries.1.q_ref, bf16[8,3,48,128]{3,2,1,0:T(8,128)(2,1)S(1)} %bitcast.29, ...), custom_call_target="tpu_custom_call" | custom-call | flops 1811939328 | bytes 4718592 | tf_op jit(solution)/shard_map/own_block/pallas_call | solution.py:245
  59.0 2.2 %collective-permute-done.3.refs_1_.refs_2_ = bf16[8,3,48,128]{3,2,1,0:T(8,128)(2,1)} collective-permute-done((bf16[8,3,48,128]{3,2,1,0:T(8,128)(2,1)}, bf16[8,3,48,128]{3,2,1,0:T(8,128)(2,1)}, u32[]{:S(2)}, u32[]{:S(2)}) %collective-permute-start.3) | collective-permute-done | bytes 294944 | tf_op jit(solution)/shard_map/ppermute | solution.py:400
  61.2 3.7 %collective-permute-start.5 = (bf16[8,3,48,128]{3,2,1,0:T(8,128)(2,1)}, bf16[8,3,48,128]{3,2,1,0:T(8,128)(2,1)}, u32[]{:S(2)}, u32[]{:S(2)}) collective-permute-start(bf16[8,3,48,128]{3,2,1,0:T(8,128)(2,1)} %collective-permute-done.3.refs_1_.refs_2_), channel_id=1, source_target_pairs={{0,32},{8,232},{32,64},{40,8},{64,96},{72,40},{96,128},{104,72},{1... | collective-permute-start | bytes 884744 | tf_op jit(solution)/shard_map/ppermute | solution.py:400
  64.9 5.4 %next_blocks.3 = (f32[3,2,768,128]{3,2,1,0:T(8,128)S(1)}, f32[8,128]{1,0:T(8,128)S(1)}) custom-call(bf16[3,2,768,256]{3,2,1,0:T(8,128)(2,1)S(1)} %get-tuple-element.24.q_ref, f32[3,2,768,128]{3,2,1,0:T(8,128)S(1)} %get-tuple-element.25.state_ref, bf16[8,3,48,128]{3,2,1,0:T(8,128)(2,1)} %collective-permute-done.1.refs_0_.refs_1_, ...), custom_call_target="tpu_custom_call", output_to_operand_aliasing={{0}: (1, {})} | custom-call | flops 2717908992 | bytes 4718592 | tf_op jit(solution)/shard_map/next_blocks/pallas_call | solution.py:277
  70.4 1.4 copy-done.2
  71.8 3.7 %collective-permute-start.6 = (bf16[8,3,48,128]{3,2,1,0:T(8,128)(2,1)}, bf16[8,3,48,128]{3,2,1,0:T(8,128)(2,1)}, u32[]{:S(2)}, u32[]{:S(2)}) collective-permute-start(bf16[8,3,48,128]{3,2,1,0:T(8,128)(2,1)} %collective-permute-done.4.refs_0_.refs_3_), channel_id=1, source_target_pairs={{0,32},{8,232},{32,64},{40,8},{64,96},{72,40},{96,128},{104,72},{1... | collective-permute-start | bytes 884744 | tf_op jit(solution)/shard_map/ppermute | solution.py:400
  75.5 1.9 %collective-permute-start.7 = (bf16[8,3,48,128]{3,2,1,0:T(8,128)(2,1)}, bf16[8,3,48,128]{3,2,1,0:T(8,128)(2,1)S(1)}, u32[]{:S(2)}, u32[]{:S(2)}) collective-permute-start(bf16[8,3,48,128]{3,2,1,0:T(8,128)(2,1)} %collective-permute-done.5.refs_1_.refs_4_), channel_id=1, source_target_pairs={{0,32},{8,232},{32,64},{40,8},{64,96},{72,40},{96,128},{104,72},{1... | collective-permute-start | bytes 884744 | tf_op jit(solution)/shard_map/ppermute | solution.py:400
  77.4 1.7 copy-done.3
  79.1 5.5 %next_blocks.4 = (f32[3,2,768,128]{3,2,1,0:T(8,128)S(1)}, f32[8,128]{1,0:T(8,128)S(1)}) custom-call(bf16[3,2,768,256]{3,2,1,0:T(8,128)(2,1)S(1)} %get-tuple-element.24.q_ref, f32[3,2,768,128]{3,2,1,0:T(8,128)S(1)} %copy-done.3, bf16[8,3,48,128]{3,2,1,0:T(8,128)(2,1)} %collective-permute-done.4.refs_0_.refs_3_, ...), custom_call_target="tpu_custom_call", output_to_operand_aliasing={{0}: (1, {})} | custom-call | flops 2717908992 | bytes 4718592 | tf_op jit(solution)/shard_map/next_blocks/pallas_call | solution.py:277
  84.6 4.8 %collective-permute-start.8 = (bf16[8,3,48,128]{3,2,1,0:T(8,128)(2,1)}, bf16[8,3,48,128]{3,2,1,0:T(8,128)(2,1)S(1)}, u32[]{:S(2)}, u32[]{:S(2)}) collective-permute-start(bf16[8,3,48,128]{3,2,1,0:T(8,128)(2,1)} %collective-permute-done.6.refs_0_.refs_5_), channel_id=1, source_target_pairs={{0,32},{8,232},{32,64},{40,8},{64,96},{72,40},{96,128},{104,72},{1... | collective-permute-start | bytes 884744 | tf_op jit(solution)/shard_map/ppermute | solution.py:400
  89.4 5.9 %next_blocks.5 = (f32[3,2,768,128]{3,2,1,0:T(8,128)S(1)}, f32[8,128]{1,0:T(8,128)}) custom-call(bf16[3,2,768,256]{3,2,1,0:T(8,128)(2,1)S(1)} %get-tuple-element.24.q_ref, f32[3,2,768,128]{3,2,1,0:T(8,128)S(1)} %get-tuple-element.35.state_ref, bf16[8,3,48,128]{3,2,1,0:T(8,128)(2,1)} %collective-permute-done.6.refs_0_.refs_5_, ...), custom_call_target="tpu_custom_call", output_to_operand_aliasing={{0}: (1, {})} | custom-call | flops 2717908992 | bytes 4718592 | tf_op jit(solution)/shard_map/next_blocks/pallas_call | solution.py:277
  95.3 1.4 copy-done.4
  96.7 1.7 copy-done.5
  98.4 50.1 %last_block.1 = bf16[768,512]{1,0:T(8,128)(2,1)} custom-call(s32[1]{0:T(128)} %bitcast.valid_ref, bf16[3,2,768,256]{3,2,1,0:T(8,128)(2,1)S(1)} %get-tuple-element.24.q_ref, f32[3,2,768,128]{3,2,1,0:T(8,128)S(1)} %copy-done.5, bf16[8,3,48,128]{3,2,1,0:T(8,128)(2,1)S(1)} %collective-permute-done.8.block_ref, ...), custom_call_target="tpu_custom_call" | custom-call | flops 1981808640 | bytes 4718592 | tf_op jit(solution)/shard_map/last_block/pallas_call | solution.py:245
  148.5 5.6 %all-to-all-start.1 = ((bf16[32,24,512]{2,1,0:T(8,128)(2,1)}), bf16[32,24,512]{2,1,0:T(8,128)(2,1)S(1)}, u32[]{:S(2)}, u32[]{:S(2)}) async-start(bf16[32,24,512]{2,1,0:T(8,128)(2,1)} %bitcast.9), calls=%async_computation.1 | async-start | bytes 1572864 | tf_op jit(solution)/shard_map/all_to_all | solution.py:434
  154.1 0.7 copy.28
  154.9 13.8 %all-to-all-done.1.partial_ref = bf16[32,24,512]{2,1,0:T(8,128)(2,1)S(1)} async-done(((bf16[32,24,512]{2,1,0:T(8,128)(2,1)}), bf16[32,24,512]{2,1,0:T(8,128)(2,1)S(1)}, u32[]{:S(2)}, u32[]{:S(2)}) %all-to-all-start.1) | async-done | bytes 786464 | tf_op jit(solution)/shard_map/all_to_all | solution.py:434
  168.7 2.3 %copy-done.1 = bf16[3072,768]{1,0:T(8,128)(2,1)S(1)} copy-done((bf16[3072,768]{1,0:T(8,128)(2,1)S(1)}, bf16[3072,768]{1,0:T(8,128)(2,1)}, u32[]{:S(2)}) %copy-start.1) | copy-done | bytes 4718616
  171.1 0.9 copy-done.8
  172.0 3.3 %project_and_norm.1 = f32[48,64]{1,0:T(8,128)S(1)} custom-call(bf16[32,24,512]{2,1,0:T(8,128)(2,1)S(1)} %all-to-all-done.1.partial_ref, bf16[2,1536,768]{2,1,0:T(8,128)(2,1)S(1)} %bitcast.26, bf16[48,1536]{1,0:T(8,128)(2,1)S(1)} %bitcast.33, f32[3,1536]{1,0:T(4,128)S(1)} %bitcast.34, f32[1,1536]{1,0:T(1,128)S(1)} %broadcast_in_dim.6.bias_ref, ...), custom_call_target="tpu_custom_call" | custom-call | tf_op jit(solution)/shard_map/project_and_norm/pallas_call | solution.py:360
  176.3 5.3 %collective-permute-start.9 = (f32[1,1536]{1,0:T(1,128)S(1)}, f32[1,1536]{1,0:T(1,128)S(1)}, u32[]{:S(2)}, u32[]{:S(2)}) collective-permute-start(f32[1,1536]{1,0:T(1,128)S(1)} %get-tuple-element.44), channel_id=1, source_target_pairs={{0,1},{1,257},{2,3},{3,259},{256,0},{257,256},{258,2},{259,258},{4... | collective-permute-start | bytes 18440 | tf_op jit(solution)/shard_map/ppermute | solution.py:457
  (49 shorter events, 2.3 us)
Async XLA Ops:
  7.2 1.1 copy-start
  7.2 41.8 %copy-start.12 = (bf16[1,333,2,192]{1,3,2,0:T(8,128)(2,1)S(1)}, bf16[1,333,2,192]{1,3,2,0:T(8,128)(2,1)}, u32[]{:S(2)}) copy-start(bf16[1,333,2,192]{1,3,2,0:T(8,128)(2,1)} %param.12) | copy-start | bytes 767236
  7.2 141.3 %all-gather.2.cloned.1.call-start = ((), (), s32[]{:S(2)}) async-start(), calls=%async_computation.2 | async-start | bytes 5013504 | tf_op jit(solution)/shard_map/all_gather | solution.py:409
  9.0 1.0 copy-start.6
  29.4 16.4 %collective-permute-start.2 = (bf16[8,3,48,128]{3,2,1,0:T(8,128)(2,1)S(1)}, bf16[8,3,48,128]{3,2,1,0:T(8,128)(2,1)}, u32[]{:S(2)}, u32[]{:S(2)}) collective-permute-start(bf16[8,3,48,128]{3,2,1,0:T(8,128)(2,1)S(1)} %bitcast.27), channel_id=1, source_target_pairs={{0,8},{8,0},{1,9},{9,1},{2,10},{10,2},{3,11},{11,3},{4,12},{12,4},... | collective-permute-start | bytes 884744 | tf_op jit(solution)/shard_map/ppermute | solution.py:402
  31.7 17.6 %collective-permute-start.1 = (bf16[8,3,48,128]{3,2,1,0:T(8,128)(2,1)S(1)}, bf16[8,3,48,128]{3,2,1,0:T(8,128)(2,1)}, u32[]{:S(2)}, u32[]{:S(2)}) collective-permute-start(bf16[8,3,48,128]{3,2,1,0:T(8,128)(2,1)S(1)} %bitcast.28), channel_id=1, source_target_pairs={{0,32},{8,232},{32,64},{40,8},{64,96},{72,40},{96,128},{104,72},{1... | collective-permute-start | bytes 884744 | tf_op jit(solution)/shard_map/ppermute | solution.py:400
  41.2 13.0 %collective-permute-start = (bf16[2,8,3,24,128]{4,3,2,1,0:T(8,128)(2,1)S(1)}, bf16[2,8,3,24,128]{4,3,2,1,0:T(8,128)(2,1)S(1)}, u32[]{:S(2)}, u32[]{:S(2)}) collective-permute-start(bf16[2,8,3,24,128]{4,3,2,1,0:T(8,128)(2,1)S(1)} %all_gather.6.own_ref), channel_id=1, source_target_pairs={{0,4},{4,0},{1,5},{5,1},{2,6},{6,2},{3,7},{7,3},{8,12},{12,8},{9,1... | collective-permute-start | bytes 884744 | tf_op jit(solution)/shard_map/ppermute | solution.py:403
  45.9 15.3 %collective-permute-start.3 = (bf16[8,3,48,128]{3,2,1,0:T(8,128)(2,1)}, bf16[8,3,48,128]{3,2,1,0:T(8,128)(2,1)}, u32[]{:S(2)}, u32[]{:S(2)}) collective-permute-start(bf16[8,3,48,128]{3,2,1,0:T(8,128)(2,1)} %collective-permute-done.2), channel_id=1, source_target_pairs={{0,32},{8,232},{32,64},{40,8},{64,96},{72,40},{96,128},{104,72},{1... | collective-permute-start | bytes 884744 | tf_op jit(solution)/shard_map/ppermute | solution.py:400
  49.2 5.8 %copy-start.10 = (bf16[3,333,128]{2,1,0:T(8,128)(2,1)}, bf16[3,333,128]{2,1,0:T(8,128)(2,1)S(1)}, u32[]{:S(2)}) copy-start(bf16[3,333,128]{2,1,0:T(8,128)(2,1)S(1)} %copy.23) | copy-start | bytes 767236
  49.3 22.5 %collective-permute-start.4 = (bf16[8,3,48,128]{3,2,1,0:T(8,128)(2,1)}, bf16[8,3,48,128]{3,2,1,0:T(8,128)(2,1)}, u32[]{:S(2)}, u32[]{:S(2)}) collective-permute-start(bf16[8,3,48,128]{3,2,1,0:T(8,128)(2,1)} %collective-permute-done.1.refs_0_.refs_1_), channel_id=1, source_target_pairs={{0,32},{8,232},{32,64},{40,8},{64,96},{72,40},{96,128},{104,72},{1... | collective-permute-start | bytes 884744 | tf_op jit(solution)/shard_map/ppermute | solution.py:400
  61.2 14.3 %collective-permute-start.5 = (bf16[8,3,48,128]{3,2,1,0:T(8,128)(2,1)}, bf16[8,3,48,128]{3,2,1,0:T(8,128)(2,1)}, u32[]{:S(2)}, u32[]{:S(2)}) collective-permute-start(bf16[8,3,48,128]{3,2,1,0:T(8,128)(2,1)} %collective-permute-done.3.refs_1_.refs_2_), channel_id=1, source_target_pairs={{0,32},{8,232},{32,64},{40,8},{64,96},{72,40},{96,128},{104,72},{1... | collective-permute-start | bytes 884744 | tf_op jit(solution)/shard_map/ppermute | solution.py:400
  70.4 1.4 copy-start.2
  71.8 12.8 %collective-permute-start.6 = (bf16[8,3,48,128]{3,2,1,0:T(8,128)(2,1)}, bf16[8,3,48,128]{3,2,1,0:T(8,128)(2,1)}, u32[]{:S(2)}, u32[]{:S(2)}) collective-permute-start(bf16[8,3,48,128]{3,2,1,0:T(8,128)(2,1)} %collective-permute-done.4.refs_0_.refs_3_), channel_id=1, source_target_pairs={{0,32},{8,232},{32,64},{40,8},{64,96},{72,40},{96,128},{104,72},{1... | collective-permute-start | bytes 884744 | tf_op jit(solution)/shard_map/ppermute | solution.py:400
  75.5 13.9 %collective-permute-start.7 = (bf16[8,3,48,128]{3,2,1,0:T(8,128)(2,1)}, bf16[8,3,48,128]{3,2,1,0:T(8,128)(2,1)S(1)}, u32[]{:S(2)}, u32[]{:S(2)}) collective-permute-start(bf16[8,3,48,128]{3,2,1,0:T(8,128)(2,1)} %collective-permute-done.5.refs_1_.refs_4_), channel_id=1, source_target_pairs={{0,32},{8,232},{32,64},{40,8},{64,96},{72,40},{96,128},{104,72},{1... | collective-permute-start | bytes 884744 | tf_op jit(solution)/shard_map/ppermute | solution.py:400
  77.4 1.7 copy-start.3
  79.1 10.3 %copy-start.11 = (bf16[3,333,128]{2,1,0:T(8,128)(2,1)S(1)}, bf16[3,333,128]{2,1,0:T(8,128)(2,1)}, u32[]{:S(2)}) copy-start(bf16[3,333,128]{2,1,0:T(8,128)(2,1)} %copy-done.10) | copy-start | bytes 767236
  84.6 12.2 %collective-permute-start.8 = (bf16[8,3,48,128]{3,2,1,0:T(8,128)(2,1)}, bf16[8,3,48,128]{3,2,1,0:T(8,128)(2,1)S(1)}, u32[]{:S(2)}, u32[]{:S(2)}) collective-permute-start(bf16[8,3,48,128]{3,2,1,0:T(8,128)(2,1)} %collective-permute-done.6.refs_0_.refs_5_), channel_id=1, source_target_pairs={{0,32},{8,232},{32,64},{40,8},{64,96},{72,40},{96,128},{104,72},{1... | collective-permute-start | bytes 884744 | tf_op jit(solution)/shard_map/ppermute | solution.py:400
  95.3 1.4 copy-start.4
  96.7 1.7 copy-start.5
  98.4 56.5 %copy-start.13 = (f32[1536]{0:T(1024)S(1)}, f32[1536]{0:T(1024)}, u32[]{:S(2)}) copy-start(f32[1536]{0:T(1024)} %param.16) | copy-start | bytes 18436
  98.4 70.3 %copy-start.7 = (bf16[1536,64]{0,1:T(8,128)(2,1)S(1)}, bf16[1536,64]{0,1:T(8,128)(2,1)}, u32[]{:S(2)}) copy-start(bf16[1536,64]{0,1:T(8,128)(2,1)} %param.17) | copy-start | bytes 589828
  98.4 70.3 %copy-start.9 = (f32[64]{0:T(128)S(1)}, f32[64]{0:T(128)}, u32[]{:S(2)}) copy-start(f32[64]{0:T(128)} %param.18) | copy-start | bytes 772
  148.5 20.2 %all-to-all-start.1 = ((bf16[32,24,512]{2,1,0:T(8,128)(2,1)}), bf16[32,24,512]{2,1,0:T(8,128)(2,1)S(1)}, u32[]{:S(2)}, u32[]{:S(2)}) async-start(bf16[32,24,512]{2,1,0:T(8,128)(2,1)} %bitcast.9), calls=%async_computation.1 | async-start | bytes 1572864 | tf_op jit(solution)/shard_map/all_to_all | solution.py:434
  168.7 2.3 %copy-start.1 = (bf16[3072,768]{1,0:T(8,128)(2,1)S(1)}, bf16[3072,768]{1,0:T(8,128)(2,1)}, u32[]{:S(2)}) copy-start(bf16[3072,768]{1,0:T(8,128)(2,1)} %all-gather.2.cloned.1.call-done) | copy-start | bytes 14155780
  171.1 0.9 copy-start.8
  172.0 11.0 %copy-start.14 = (f32[1,1536]{1,0:T(1,128)S(1)}, f32[1,1536]{1,0:T(1,128)}, u32[]{:S(2)}) copy-start(f32[1,1536]{1,0:T(1,128)} %param.21) | copy-start | bytes 18436
  175.6 7.3 %collective-permute-start.10 = (f32[1,1536]{1,0:T(1,128)S(1)}, f32[1,1536]{1,0:T(1,128)S(1)}, u32[]{:S(2)}, u32[]{:S(2)}) collective-permute-start(f32[1,1536]{1,0:T(1,128)S(1)} %get-tuple-element.45), channel_id=1, source_target_pairs={{0,0},{1,256},{2,2},{3,258},{256,1},{257,257},{258,3},{259,259},{4... | collective-permute-start | bytes 18440 | tf_op jit(solution)/shard_map/ppermute | solution.py:456
  176.3 6.6 %collective-permute-start.9 = (f32[1,1536]{1,0:T(1,128)S(1)}, f32[1,1536]{1,0:T(1,128)S(1)}, u32[]{:S(2)}, u32[]{:S(2)}) collective-permute-start(f32[1,1536]{1,0:T(1,128)S(1)} %get-tuple-element.44), channel_id=1, source_target_pairs={{0,1},{1,257},{2,3},{3,259},{256,0},{257,256},{258,2},{259,258},{4... | collective-permute-start | bytes 18440 | tf_op jit(solution)/shard_map/ppermute | solution.py:457
Sparse Core Ops, SparseCore 0:
  11.4 80.3 all-gather.1

commit v9 on v7

--- a/solution.py
+++ b/solution.py
@@ -284,14 +284,7 @@
     final_bias_ref,
     out_ref,
     wide_ref,
-    held_ref,
-    input_ref,
-    sems,
 ):
-    brought = pltpu.make_async_copy(weight_ref, held_ref, sems.at[0])
-    taken = pltpu.make_async_copy(hidden_ref, input_ref, sems.at[1])
-    brought.start()
-    taken.start()
     half = partial_ref.shape[1]
     sources = partial_ref.shape[0]
     across = groups // 2
@@ -319,10 +312,8 @@
             both = jnp.concatenate([first, second[:, :HEAD_DIM]], axis=1)
             wide_ref[part * half : (part + 1) * half, group * width : (group + 1) * width] = both
     attended = wide_ref[...].astype(BF16)
-    brought.wait()
-    taken.wait()
-    projected = jnp.dot(attended, held_ref[...], preferred_element_type=F32)
-    residual = input_ref[...].astype(F32) + modulation_ref[0:1] * (projected + bias_ref[...])
+    projected = jnp.dot(attended, weight_ref[...], preferred_element_type=F32)
+    residual = hidden_ref[...].astype(F32) + modulation_ref[0:1] * (projected + bias_ref[...])
     middle = jnp.mean(residual, axis=-1, keepdims=True)
     centered = residual - middle
     spread = jnp.mean(centered * centered, axis=-1, keepdims=True)
@@ -335,20 +326,11 @@
 
 def finish(partial, weight, hidden, modulation, bias, final_weight, final_bias, heads, groups):
     tokens, width = hidden.shape
-    vmem = pl.BlockSpec(memory_space=pltpu.VMEM)
-    hbm = pl.BlockSpec(memory_space=pltpu.HBM)
     return pl.pallas_call(
         functools.partial(finish_kernel, heads, groups),
         out_shape=jax.ShapeDtypeStruct((tokens, final_weight.shape[0]), F32),
-        in_specs=[vmem, hbm, hbm, vmem, vmem, vmem, vmem],
-        out_specs=vmem,
-        scratch_shapes=[
-            pltpu.VMEM((tokens, width), F32),
-            pltpu.VMEM(weight.shape, BF16),
-            pltpu.VMEM(hidden.shape, BF16),
-            pltpu.SemaphoreType.DMA((2,)),
-        ],
-        compiler_params=params(60),
+        scratch_shapes=[pltpu.VMEM((tokens, width), F32)],
+        compiler_params=params(),
         name="project_and_norm",
     )(partial, weight, hidden, modulation, bias, final_weight, final_bias)
 
@@ -378,16 +360,15 @@
 
     slabs = pack(latent_qkv[0].transpose(1, 0, 2), groups, heads)
     slabs = lax.all_to_all(slabs, HEAD_AXES, split_axis=0, concat_axis=0, tiled=True)
-    packed = slabs[:, : heads * half].reshape(groups, heads, half, LANES)
-    packed = lax.all_gather(packed, "core", axis=0)
-    own, packed = after((slabs[:, heads * half :].reshape(groups, heads, tokens, LANES), packed))
+    own = slabs[:, heads * half :].reshape(groups, heads, tokens, LANES)
     route = []
     for i in range(ring):
         route += [(2 * i, 2 * ((i + 1) % ring)), (2 * i + 1, 2 * ((i - 1) % ring) + 1)]
     pass_on = lambda x: lax.ppermute(x, ("zh", "core"), route)
     beside = lax.ppermute(own, "core", [(0, 1), (1, 0)])
-    first, beside = after((own, beside))
-    near = pass_on(first)
+    near = pass_on(own)
+    packed = slabs[:, : heads * half].reshape(groups, heads, half, LANES)
+    packed = lax.all_gather(packed, "core", axis=0)
     opposite = lax.ppermute(packed, "xh", [(0, 1), (1, 0)])
     cross = pass_on(beside)
     q = unpack_queries(xh.reshape(1), packed, opposite)

time: 193 us -> 182 us (0.943)
  blocking collectives: 19.2 us -> 15.3 us
  Pallas kernels: 72.7 us -> 69.7 us
  starting transfers between devices: 59.9 us -> 57.6 us
    ppermute x7, starting transfers between devices: 42.2 us -> 34.2 us  [local(): pass_on = lambda x: lax.ppermute(x, ('zh', 'core'), route)]
    ppermute x1, starting transfers between devices: 2.26 us -> 6.17 us  [local(): beside = lax.ppermute(own, 'core', [(0, 1), (1, 0)])]
    all_gather x1, blocking collectives: 5.91 us -> 2.02 us  [local(): packed = lax.all_gather(packed, 'core', axis=0)]
    pallas_call x1, Pallas kernels: 6.36 us -> 3.33 us  [finish(): pl.pallas_call(functools.partial(finish_kernel, heads, groups), out_shape...]
    ppermute x7, waiting for transfers between devices: 5.8 us -> 3.48 us  [local(): pass_on = lambda x: lax.ppermute(x, ('zh', 'core'), route)]
  transfers between devices with their start and end apart: 13 -> 13, of which waited for: 3 -> 4; matrix products, arithmetic and copies ran while one was open for 1% -> 0% of each run, Pallas kernels for 34% -> 37%
where the time goes in v9:
time: 182 us
  Pallas kernels  69.7 us (38%)
  starting transfers between devices  57.6 us (32%)
  waiting for transfers between devices  18.7 us (10%)
  between operations  15.7 us (9%)
  blocking collectives  15.3 us (8%)
  local copies, waits for them, and re-layouts  4.02 us (2%)
    pallas_call x5, Pallas kernels, attention_call(): pl.pallas_call(kernel, grid=(heads,), out_shape=out_shape, in_specs=specs...  65.4 us
    ppermute x7, starting transfers between devices, local(): pass_on = lambda x: lax.ppermute(x, ('zh', 'core'), route)  34.2 us
    all_to_all x1, waiting for transfers between devices, local(): lax.all_to_all(partial, BLOCK_AXES, split_axis=0, concat_axis=0, tiled=True)  14.5 us
    all_to_all x1, blocking collectives, local(): lax.all_to_all(slabs, HEAD_AXES, split_axis=0, concat_axis=0, tiled=True)  13.3 us
    all_to_all x1, starting transfers between devices, local(): lax.all_to_all(partial, BLOCK_AXES, split_axis=0, concat_axis=0, tiled=True)  7.25 us
    ppermute x1, starting transfers between devices, local(): beside = lax.ppermute(own, 'core', [(0, 1), (1, 0)])  6.17 us
    ppermute x1, starting transfers between devices, local(): lax.ppermute(lax.dynamic_slice_in_dim(tiles, 1 - branch, 1, 0), ('cfg', '...  4.7 us
    ppermute x1, starting transfers between devices, local(): opposite = lax.ppermute(packed, 'xh', [(0, 1), (1, 0)])  4.64 us
  transfers between devices with their start and end apart: 13, of which 4 were waited for; matrix products, arithmetic and copies ran while one was open for 0% of the time, Pallas kernels for 37%

profile of v9, /device:TPU:1, one launch (start us, length us, event | category | flops | bytes accessed | tf_op | source)
XLA Modules:
  0.0 181.6 jit_solution(4078476534230031440)
XLA Ops:
  7.2 0.7 all-gather.2.cloned.1.call-update
  7.9 1.0 copy-done.1
  8.9 0.2 pack_heads.1
  9.1 13.3 %all_to_all.10 = bf16[8,216,128]{2,1,0:T(8,128)(2,1)S(1)} all-to-all(bf16[8,216,128]{2,1,0:T(8,128)(2,1)S(1)} %pack_heads.1), channel_id=1, replica_groups=mesh['cfg'=2,'zh'=8,'zl'=2,'core'=2,'xh'=2,'y'=4] {'zl','y'}, dimensions={0} | all-to-all | bytes 884736 | tf_op jit(solution)/shard_map/all_to_all | solution.py:362
  22.4 6.2 %collective-permute-start.2 = (bf16[8,3,48,128]{3,2,1,0:T(8,128)(2,1)S(1)}, bf16[8,3,48,128]{3,2,1,0:T(8,128)(2,1)S(1)}, u32[]{:S(2)}, u32[]{:S(2)}) collective-permute-start(bf16[8,3,48,128]{3,2,1,0:T(8,128)(2,1)S(1)} %bitcast.26), channel_id=1, source_target_pairs={{0,8},{8,0},{1,9},{9,1},{2,10},{10,2},{3,11},{11,3},{4,12},{12,4},... | collective-permute-start | bytes 884744 | tf_op jit(solution)/shard_map/ppermute | solution.py:368
  28.6 9.5 %collective-permute-start.1 = (bf16[8,3,48,128]{3,2,1,0:T(8,128)(2,1)S(1)}, bf16[8,3,48,128]{3,2,1,0:T(8,128)(2,1)S(1)}, u32[]{:S(2)}, u32[]{:S(2)}) collective-permute-start(bf16[8,3,48,128]{3,2,1,0:T(8,128)(2,1)S(1)} %bitcast.27), channel_id=1, source_target_pairs={{0,32},{8,232},{32,64},{40,8},{64,96},{72,40},{96,128},{104,72},{1... | collective-permute-start | bytes 884744 | tf_op jit(solution)/shard_map/ppermute | solution.py:367
  38.1 2.0 %all_gather.6.own_ref = bf16[2,8,3,24,128]{4,3,2,1,0:T(8,128)(2,1)S(1)} all-gather(bf16[1,8,3,24,128]{4,3,2,1,0:T(8,128)(2,1)S(1)} %bitcast.35), channel_id=1, replica_groups=mesh['cfg'=2,'zh'=8,'zl'=2,'core'=2,'xh'=2,'y'=4] {'core'}, dimensions={0}, use_global_device_ids=true | all-gather | bytes 442368 | tf_op jit(solution)/shard_map/all_gather | solution.py:371
  40.1 4.6 %collective-permute-start = (bf16[2,8,3,24,128]{4,3,2,1,0:T(8,128)(2,1)S(1)}, bf16[2,8,3,24,128]{4,3,2,1,0:T(8,128)(2,1)S(1)}, u32[]{:S(2)}, u32[]{:S(2)}) collective-permute-start(bf16[2,8,3,24,128]{4,3,2,1,0:T(8,128)(2,1)S(1)} %all_gather.6.own_ref), channel_id=1, source_target_pairs={{0,4},{4,0},{1,5},{5,1},{2,6},{6,2},{3,7},{7,3},{8,12},{12,8},{9,1... | collective-permute-start | bytes 884744 | tf_op jit(solution)/shard_map/ppermute | solution.py:372
  44.8 0.2 copy.23
  45.1 3.1 %collective-permute-start.3 = (bf16[8,3,48,128]{3,2,1,0:T(8,128)(2,1)S(1)}, bf16[8,3,48,128]{3,2,1,0:T(8,128)(2,1)S(1)}, u32[]{:S(2)}, u32[]{:S(2)}) collective-permute-start(bf16[8,3,48,128]{3,2,1,0:T(8,128)(2,1)S(1)} %collective-permute-done.2), channel_id=1, source_target_pairs={{0,32},{8,232},{32,64},{40,8},{64,96},{72,40},{96,128},{104,72},{1... | collective-permute-start | bytes 884744 | tf_op jit(solution)/shard_map/ppermute | solution.py:367
  48.2 4.3 %collective-permute-start.4 = (bf16[8,3,48,128]{3,2,1,0:T(8,128)(2,1)S(1)}, bf16[8,3,48,128]{3,2,1,0:T(8,128)(2,1)S(1)}, u32[]{:S(2)}, u32[]{:S(2)}) collective-permute-start(bf16[8,3,48,128]{3,2,1,0:T(8,128)(2,1)S(1)} %collective-permute-done.1.refs_0_.refs_1_), channel_id=1, source_target_pairs={{0,32},{8,232},{32,64},{40,8},{64,96},{72,40},{96,128},{104,72},{1... | collective-permute-start | bytes 884744 | tf_op jit(solution)/shard_map/ppermute | solution.py:367
  52.5 0.8 unpack_queries.1.q_ref
  53.3 5.3 %own_block.1 = (bf16[3,2,768,256]{3,2,1,0:T(8,128)(2,1)S(1)}, f32[3,2,768,128]{3,2,1,0:T(8,128)S(1)}, f32[8,128]{1,0:T(8,128)S(1)}) custom-call(s32[1]{0:T(128)} %bitcast.valid_ref, bf16[3,2,768,256]{3,2,1,0:T(8,128)(2,1)S(1)} %unpack_queries.1.q_ref, bf16[8,3,48,128]{3,2,1,0:T(8,128)(2,1)S(1)} %bitcast.28, ...), custom_call_target="tpu_custom_call" | custom-call | flops 4000000000 | bytes 8000000 | tf_op jit(solution)/shard_map/own_block/pallas_call | solution.py:231
  58.7 0.5 collective-permute-done.3.refs_1_.refs_2_
  59.2 4.6 %collective-permute-start.5 = (bf16[8,3,48,128]{3,2,1,0:T(8,128)(2,1)S(1)}, bf16[8,3,48,128]{3,2,1,0:T(8,128)(2,1)S(1)}, u32[]{:S(2)}, u32[]{:S(2)}) collective-permute-start(bf16[8,3,48,128]{3,2,1,0:T(8,128)(2,1)S(1)} %collective-permute-done.3.refs_1_.refs_2_), channel_id=1, source_target_pairs={{0,32},{8,232},{32,64},{40,8},{64,96},{72,40},{96,128},{104,72},{1... | collective-permute-start | bytes 884744 | tf_op jit(solution)/shard_map/ppermute | solution.py:367
  63.8 4.6 %next_blocks.3 = (f32[3,2,768,128]{3,2,1,0:T(8,128)S(1)}, f32[8,128]{1,0:T(8,128)S(1)}) custom-call(bf16[3,2,768,256]{3,2,1,0:T(8,128)(2,1)S(1)} %get-tuple-element.18.q_ref, f32[3,2,768,128]{3,2,1,0:T(8,128)S(1)} %get-tuple-element.19.state_ref, bf16[8,3,48,128]{3,2,1,0:T(8,128)(2,1)S(1)} %collective-permute-done.1.refs_0_.refs_1_, ...), custom_call_target="tpu_custom_call", output_to_operand_aliasing={{0}: (1, {})} | custom-call | flops 4000000000 | bytes 8000000 | tf_op jit(solution)/shard_map/next_blocks/pallas_call | solution.py:231
  68.4 3.8 %collective-permute-start.6 = (bf16[8,3,48,128]{3,2,1,0:T(8,128)(2,1)S(1)}, bf16[8,3,48,128]{3,2,1,0:T(8,128)(2,1)S(1)}, u32[]{:S(2)}, u32[]{:S(2)}) collective-permute-start(bf16[8,3,48,128]{3,2,1,0:T(8,128)(2,1)S(1)} %collective-permute-done.4.refs_0_.refs_3_), channel_id=1, source_target_pairs={{0,32},{8,232},{32,64},{40,8},{64,96},{72,40},{96,128},{104,72},{1... | collective-permute-start | bytes 884744 | tf_op jit(solution)/shard_map/ppermute | solution.py:367
  72.2 5.0 %collective-permute-start.7 = (bf16[8,3,48,128]{3,2,1,0:T(8,128)(2,1)S(1)}, bf16[8,3,48,128]{3,2,1,0:T(8,128)(2,1)S(1)}, u32[]{:S(2)}, u32[]{:S(2)}) collective-permute-start(bf16[8,3,48,128]{3,2,1,0:T(8,128)(2,1)S(1)} %collective-permute-done.5.refs_1_.refs_4_), channel_id=1, source_target_pairs={{0,32},{8,232},{32,64},{40,8},{64,96},{72,40},{96,128},{104,72},{1... | collective-permute-start | bytes 884744 | tf_op jit(solution)/shard_map/ppermute | solution.py:367
  77.2 4.6 %next_blocks.4 = (f32[3,2,768,128]{3,2,1,0:T(8,128)S(1)}, f32[8,128]{1,0:T(8,128)S(1)}) custom-call(bf16[3,2,768,256]{3,2,1,0:T(8,128)(2,1)S(1)} %get-tuple-element.18.q_ref, f32[3,2,768,128]{3,2,1,0:T(8,128)S(1)} %get-tuple-element.23.state_ref, bf16[8,3,48,128]{3,2,1,0:T(8,128)(2,1)S(1)} %collective-permute-done.4.refs_0_.refs_3_, ...), custom_call_target="tpu_custom_call", output_to_operand_aliasing={{0}: (1, {})} | custom-call | flops 4000000000 | bytes 8000000 | tf_op jit(solution)/shard_map/next_blocks/pallas_call | solution.py:231
  81.8 3.9 %collective-permute-start.8 = (bf16[8,3,48,128]{3,2,1,0:T(8,128)(2,1)S(1)}, bf16[8,3,48,128]{3,2,1,0:T(8,128)(2,1)S(1)}, u32[]{:S(2)}, u32[]{:S(2)}) collective-permute-start(bf16[8,3,48,128]{3,2,1,0:T(8,128)(2,1)S(1)} %collective-permute-done.6.refs_0_.refs_5_), channel_id=1, source_target_pairs={{0,32},{8,232},{32,64},{40,8},{64,96},{72,40},{96,128},{104,72},{1... | collective-permute-start | bytes 884744 | tf_op jit(solution)/shard_map/ppermute | solution.py:367
  85.8 0.9 collective-permute-done.7.refs_1_.refs_6_
  86.7 5.0 %next_blocks.5 = (f32[3,2,768,128]{3,2,1,0:T(8,128)S(1)}, f32[8,128]{1,0:T(8,128)}) custom-call(bf16[3,2,768,256]{3,2,1,0:T(8,128)(2,1)S(1)} %get-tuple-element.18.q_ref, f32[3,2,768,128]{3,2,1,0:T(8,128)S(1)} %get-tuple-element.29.state_ref, bf16[8,3,48,128]{3,2,1,0:T(8,128)(2,1)S(1)} %collective-permute-done.6.refs_0_.refs_5_, ...), custom_call_target="tpu_custom_call", output_to_operand_aliasing={{0}: (1, {})} | custom-call | flops 4000000000 | bytes 8000000 | tf_op jit(solution)/shard_map/next_blocks/pallas_call | solution.py:231
  91.7 2.0 %collective-permute-done.8.block_ref = bf16[8,3,48,128]{3,2,1,0:T(8,128)(2,1)S(1)} collective-permute-done((bf16[8,3,48,128]{3,2,1,0:T(8,128)(2,1)S(1)}, bf16[8,3,48,128]{3,2,1,0:T(8,128)(2,1)S(1)}, u32[]{:S(2)}, u32[]{:S(2)}) %collective-permute-start.8) | collective-permute-done | bytes 294944 | tf_op jit(solution)/shard_map/ppermute | solution.py:367
  93.8 45.9 %last_block.1 = bf16[768,512]{1,0:T(8,128)(2,1)} custom-call(s32[1]{0:T(128)} %bitcast.valid_ref, bf16[3,2,768,256]{3,2,1,0:T(8,128)(2,1)S(1)} %get-tuple-element.18.q_ref, f32[3,2,768,128]{3,2,1,0:T(8,128)S(1)} %get-tuple-element.33.state_ref, bf16[8,3,48,128]{3,2,1,0:T(8,128)(2,1)S(1)} %collective-permute-done.8.block_ref, ...), custom_call_target="tpu_custom_call" | custom-call | flops 4000000000 | bytes 8000000 | tf_op jit(solution)/shard_map/last_block/pallas_call | solution.py:231
  139.6 7.3 %all-to-all-start.1 = ((bf16[32,24,512]{2,1,0:T(8,128)(2,1)}), bf16[32,24,512]{2,1,0:T(8,128)(2,1)S(1)}, u32[]{:S(2)}, u32[]{:S(2)}) async-start(bf16[32,24,512]{2,1,0:T(8,128)(2,1)} %bitcast.9), calls=%async_computation.1 | async-start | bytes 1572864 | tf_op jit(solution)/shard_map/all_to_all | solution.py:401
  146.9 14.5 %all-to-all-done.1.partial_ref = bf16[32,24,512]{2,1,0:T(8,128)(2,1)S(1)} async-done(((bf16[32,24,512]{2,1,0:T(8,128)(2,1)}), bf16[32,24,512]{2,1,0:T(8,128)(2,1)S(1)}, u32[]{:S(2)}, u32[]{:S(2)}) %all-to-all-start.1) | async-done | bytes 786464 | tf_op jit(solution)/shard_map/all_to_all | solution.py:401
  161.5 2.3 %copy-done = bf16[1536,1536]{1,0:T(8,128)(2,1)S(1)} copy-done((bf16[1536,1536]{1,0:T(8,128)(2,1)S(1)}, bf16[1536,1536]{1,0:T(8,128)(2,1)}, u32[]{:S(2)}) %copy-start) | copy-done | bytes 4718616
  163.8 3.3 %project_and_norm.1 = f32[48,64]{1,0:T(8,128)S(1)} custom-call(bf16[32,24,512]{2,1,0:T(8,128)(2,1)S(1)} %all-to-all-done.1.partial_ref, bf16[1536,1536]{1,0:T(8,128)(2,1)S(1)} %copy-done, bf16[48,1536]{1,0:T(8,128)(2,1)S(1)} %bitcast.31, f32[3,1536]{1,0:T(4,128)S(1)} %bitcast.32, f32[1,1536]{1,0:T(1,128)S(1)} %broadcast_in_dim.6.bias_ref, ...), custom_call_target="tpu_custom_call" | custom-call | tf_op jit(solution)/shard_map/project_and_norm/pallas_call | solution.py:329
  167.1 0.1 copy.24
  167.5 0.7 collective-permute-start.10
  168.1 4.7 %collective-permute-start.9 = (f32[1,1536]{1,0:T(1,128)S(1)}, f32[1,1536]{1,0:T(1,128)S(1)}, u32[]{:S(2)}, u32[]{:S(2)}) collective-permute-start(f32[1,1536]{1,0:T(1,128)S(1)} %get-tuple-element.36), channel_id=1, source_target_pairs={{0,1},{1,257},{2,3},{3,259},{256,0},{257,256},{258,2},{259,258},{4... | collective-permute-start | bytes 18440 | tf_op jit(solution)/shard_map/ppermute | solution.py:424
  174.2 0.6 multiply_subtract_fusion
  (36 shorter events, 0.4 us)
Async XLA Ops:
  7.2 37.6 %copy-start.5 = (bf16[1,333,2,192]{1,3,2,0:T(8,128)(2,1)S(1)}, bf16[1,333,2,192]{1,3,2,0:T(8,128)(2,1)}, u32[]{:S(2)}) copy-start(bf16[1,333,2,192]{1,3,2,0:T(8,128)(2,1)} %param.12) | copy-start | bytes 767236
  7.2 154.3 %all-gather.2.cloned.1.call-start = ((), (), s32[]{:S(2)}) async-start(), calls=%async_computation.2 | async-start | bytes 5308416 | tf_op jit(solution)/shard_map/all_gather | solution.py:376
  7.9 1.0 copy-start.1
  22.4 22.7 %collective-permute-start.2 = (bf16[8,3,48,128]{3,2,1,0:T(8,128)(2,1)S(1)}, bf16[8,3,48,128]{3,2,1,0:T(8,128)(2,1)S(1)}, u32[]{:S(2)}, u32[]{:S(2)}) collective-permute-start(bf16[8,3,48,128]{3,2,1,0:T(8,128)(2,1)S(1)} %bitcast.26), channel_id=1, source_target_pairs={{0,8},{8,0},{1,9},{9,1},{2,10},{10,2},{3,11},{11,3},{4,12},{12,4},... | collective-permute-start | bytes 884744 | tf_op jit(solution)/shard_map/ppermute | solution.py:368
  28.6 19.6 %collective-permute-start.1 = (bf16[8,3,48,128]{3,2,1,0:T(8,128)(2,1)S(1)}, bf16[8,3,48,128]{3,2,1,0:T(8,128)(2,1)S(1)}, u32[]{:S(2)}, u32[]{:S(2)}) collective-permute-start(bf16[8,3,48,128]{3,2,1,0:T(8,128)(2,1)S(1)} %bitcast.27), channel_id=1, source_target_pairs={{0,32},{8,232},{32,64},{40,8},{64,96},{72,40},{96,128},{104,72},{1... | collective-permute-start | bytes 884744 | tf_op jit(solution)/shard_map/ppermute | solution.py:367
  40.1 12.4 %collective-permute-start = (bf16[2,8,3,24,128]{4,3,2,1,0:T(8,128)(2,1)S(1)}, bf16[2,8,3,24,128]{4,3,2,1,0:T(8,128)(2,1)S(1)}, u32[]{:S(2)}, u32[]{:S(2)}) collective-permute-start(bf16[2,8,3,24,128]{4,3,2,1,0:T(8,128)(2,1)S(1)} %all_gather.6.own_ref), channel_id=1, source_target_pairs={{0,4},{4,0},{1,5},{5,1},{2,6},{6,2},{3,7},{7,3},{8,12},{12,8},{9,1... | collective-permute-start | bytes 884744 | tf_op jit(solution)/shard_map/ppermute | solution.py:372
  45.1 14.1 %collective-permute-start.3 = (bf16[8,3,48,128]{3,2,1,0:T(8,128)(2,1)S(1)}, bf16[8,3,48,128]{3,2,1,0:T(8,128)(2,1)S(1)}, u32[]{:S(2)}, u32[]{:S(2)}) collective-permute-start(bf16[8,3,48,128]{3,2,1,0:T(8,128)(2,1)S(1)} %collective-permute-done.2), channel_id=1, source_target_pairs={{0,32},{8,232},{32,64},{40,8},{64,96},{72,40},{96,128},{104,72},{1... | collective-permute-start | bytes 884744 | tf_op jit(solution)/shard_map/ppermute | solution.py:367
  48.2 20.2 %collective-permute-start.4 = (bf16[8,3,48,128]{3,2,1,0:T(8,128)(2,1)S(1)}, bf16[8,3,48,128]{3,2,1,0:T(8,128)(2,1)S(1)}, u32[]{:S(2)}, u32[]{:S(2)}) collective-permute-start(bf16[8,3,48,128]{3,2,1,0:T(8,128)(2,1)S(1)} %collective-permute-done.1.refs_0_.refs_1_), channel_id=1, source_target_pairs={{0,32},{8,232},{32,64},{40,8},{64,96},{72,40},{96,128},{104,72},{1... | collective-permute-start | bytes 884744 | tf_op jit(solution)/shard_map/ppermute | solution.py:367
  59.2 13.0 %collective-permute-start.5 = (bf16[8,3,48,128]{3,2,1,0:T(8,128)(2,1)S(1)}, bf16[8,3,48,128]{3,2,1,0:T(8,128)(2,1)S(1)}, u32[]{:S(2)}, u32[]{:S(2)}) collective-permute-start(bf16[8,3,48,128]{3,2,1,0:T(8,128)(2,1)S(1)} %collective-permute-done.3.refs_1_.refs_2_), channel_id=1, source_target_pairs={{0,32},{8,232},{32,64},{40,8},{64,96},{72,40},{96,128},{104,72},{1... | collective-permute-start | bytes 884744 | tf_op jit(solution)/shard_map/ppermute | solution.py:367
  68.4 13.4 %collective-permute-start.6 = (bf16[8,3,48,128]{3,2,1,0:T(8,128)(2,1)S(1)}, bf16[8,3,48,128]{3,2,1,0:T(8,128)(2,1)S(1)}, u32[]{:S(2)}, u32[]{:S(2)}) collective-permute-start(bf16[8,3,48,128]{3,2,1,0:T(8,128)(2,1)S(1)} %collective-permute-done.4.refs_0_.refs_3_), channel_id=1, source_target_pairs={{0,32},{8,232},{32,64},{40,8},{64,96},{72,40},{96,128},{104,72},{1... | collective-permute-start | bytes 884744 | tf_op jit(solution)/shard_map/ppermute | solution.py:367
  72.2 14.5 %collective-permute-start.7 = (bf16[8,3,48,128]{3,2,1,0:T(8,128)(2,1)S(1)}, bf16[8,3,48,128]{3,2,1,0:T(8,128)(2,1)S(1)}, u32[]{:S(2)}, u32[]{:S(2)}) collective-permute-start(bf16[8,3,48,128]{3,2,1,0:T(8,128)(2,1)S(1)} %collective-permute-done.5.refs_1_.refs_4_), channel_id=1, source_target_pairs={{0,32},{8,232},{32,64},{40,8},{64,96},{72,40},{96,128},{104,72},{1... | collective-permute-start | bytes 884744 | tf_op jit(solution)/shard_map/ppermute | solution.py:367
  81.8 11.9 %collective-permute-start.8 = (bf16[8,3,48,128]{3,2,1,0:T(8,128)(2,1)S(1)}, bf16[8,3,48,128]{3,2,1,0:T(8,128)(2,1)S(1)}, u32[]{:S(2)}, u32[]{:S(2)}) collective-permute-start(bf16[8,3,48,128]{3,2,1,0:T(8,128)(2,1)S(1)} %collective-permute-done.6.refs_0_.refs_5_), channel_id=1, source_target_pairs={{0,32},{8,232},{32,64},{40,8},{64,96},{72,40},{96,128},{104,72},{1... | collective-permute-start | bytes 884744 | tf_op jit(solution)/shard_map/ppermute | solution.py:367
  93.7 53.2 %copy-start.6 = (f32[1,3,1536]{2,0,1:T(1,128)S(1)}, f32[1,3,1536]{2,0,1:T(1,128)}, u32[]{:S(2)}) copy-start(f32[1,3,1536]{2,0,1:T(1,128)} %param.14) | copy-start | bytes 55300
  93.7 53.2 %copy-start.7 = (f32[1536]{0:T(1024)S(1)}, f32[1536]{0:T(1024)}, u32[]{:S(2)}) copy-start(f32[1536]{0:T(1024)} %param.16) | copy-start | bytes 18436
  93.7 67.7 %copy-start.2 = (bf16[1536,64]{0,1:T(8,128)(2,1)S(1)}, bf16[1536,64]{0,1:T(8,128)(2,1)}, u32[]{:S(2)}) copy-start(bf16[1536,64]{0,1:T(8,128)(2,1)} %param.17) | copy-start | bytes 589828
  93.7 67.7 %copy-start.3 = (bf16[1,48,1536]{2,1,0:T(8,128)(2,1)S(1)}, bf16[1,48,1536]{2,1,0:T(8,128)(2,1)}, u32[]{:S(2)}) copy-start(bf16[1,48,1536]{2,1,0:T(8,128)(2,1)} %param.13) | copy-start | bytes 442372
  93.7 67.7 %copy-start.4 = (f32[64]{0:T(128)S(1)}, f32[64]{0:T(128)}, u32[]{:S(2)}) copy-start(f32[64]{0:T(128)} %param.18) | copy-start | bytes 772
  139.6 21.8 %all-to-all-start.1 = ((bf16[32,24,512]{2,1,0:T(8,128)(2,1)}), bf16[32,24,512]{2,1,0:T(8,128)(2,1)S(1)}, u32[]{:S(2)}, u32[]{:S(2)}) async-start(bf16[32,24,512]{2,1,0:T(8,128)(2,1)} %bitcast.9), calls=%async_computation.1 | async-start | bytes 1572864 | tf_op jit(solution)/shard_map/all_to_all | solution.py:401
  161.5 2.3 %copy-start = (bf16[1536,1536]{1,0:T(8,128)(2,1)S(1)}, bf16[1536,1536]{1,0:T(8,128)(2,1)}, u32[]{:S(2)}) copy-start(bf16[1536,1536]{1,0:T(8,128)(2,1)} %all-gather.2.cloned.1.call-done.weight_ref) | copy-start | bytes 14155780
  163.8 10.4 %copy-start.8 = (f32[1,1536]{1,0:T(1,128)S(1)}, f32[1,1536]{1,0:T(1,128)}, u32[]{:S(2)}) copy-start(f32[1,1536]{1,0:T(1,128)} %param.21) | copy-start | bytes 18436
  167.5 6.7 %collective-permute-start.10 = (f32[1,1536]{1,0:T(1,128)S(1)}, f32[1,1536]{1,0:T(1,128)S(1)}, u32[]{:S(2)}, u32[]{:S(2)}) collective-permute-start(f32[1,1536]{1,0:T(1,128)S(1)} %get-tuple-element.37), channel_id=1, source_target_pairs={{0,0},{1,256},{2,2},{3,258},{256,1},{257,257},{258,3},{259,259},{4... | collective-permute-start | bytes 18440 | tf_op jit(solution)/shard_map/ppermute | solution.py:423
  168.1 6.0 %collective-permute-start.9 = (f32[1,1536]{1,0:T(1,128)S(1)}, f32[1,1536]{1,0:T(1,128)S(1)}, u32[]{:S(2)}, u32[]{:S(2)}) collective-permute-start(f32[1,1536]{1,0:T(1,128)S(1)} %get-tuple-element.36), channel_id=1, source_target_pairs={{0,1},{1,257},{2,3},{3,259},{256,0},{257,256},{258,2},{259,258},{4... | collective-permute-start | bytes 18440 | tf_op jit(solution)/shard_map/ppermute | solution.py:424
Sparse Core Ops, SparseCore 0:
  11.2 101.5 all-gather.1

commit v10 on v9

--- a/solution.py
+++ b/solution.py
@@ -16,6 +16,7 @@
 GUARD = HEAD_DIM + 3
 MARKS = 8
 SAFE = 2.0**100
+PIECES = 4
 HEAD_AXES = ("zl", "y")
 BLOCK_AXES = ("zl", "core", "xh", "y")
 
@@ -284,7 +285,16 @@
     final_bias_ref,
     out_ref,
     wide_ref,
+    held_ref,
+    sems,
 ):
+    depth = held_ref.shape[1]
+    copies_in = [
+        pltpu.make_async_copy(weight_ref.at[pl.ds(n * depth, depth)], held_ref.at[n], sems.at[n])
+        for n in range(held_ref.shape[0])
+    ]
+    for copy in copies_in:
+        copy.start()
     half = partial_ref.shape[1]
     sources = partial_ref.shape[0]
     across = groups // 2
@@ -312,7 +322,11 @@
             both = jnp.concatenate([first, second[:, :HEAD_DIM]], axis=1)
             wide_ref[part * half : (part + 1) * half, group * width : (group + 1) * width] = both
     attended = wide_ref[...].astype(BF16)
-    projected = jnp.dot(attended, weight_ref[...], preferred_element_type=F32)
+    projected = 0.0
+    for n, copy in enumerate(copies_in):
+        copy.wait()
+        part = attended[:, n * depth : (n + 1) * depth]
+        projected = projected + jnp.dot(part, held_ref[n], preferred_element_type=F32)
     residual = hidden_ref[...].astype(F32) + modulation_ref[0:1] * (projected + bias_ref[...])
     middle = jnp.mean(residual, axis=-1, keepdims=True)
     centered = residual - middle
@@ -326,10 +340,17 @@
 
 def finish(partial, weight, hidden, modulation, bias, final_weight, final_bias, heads, groups):
     tokens, width = hidden.shape
+    vmem = pl.BlockSpec(memory_space=pltpu.VMEM)
     return pl.pallas_call(
         functools.partial(finish_kernel, heads, groups),
         out_shape=jax.ShapeDtypeStruct((tokens, final_weight.shape[0]), F32),
-        scratch_shapes=[pltpu.VMEM((tokens, width), F32)],
+        in_specs=[vmem, pl.BlockSpec(memory_space=pltpu.HBM), vmem, vmem, vmem, vmem, vmem],
+        out_specs=vmem,
+        scratch_shapes=[
+            pltpu.VMEM((tokens, width), F32),
+            pltpu.VMEM((PIECES, weight.shape[0] // PIECES, weight.shape[1]), BF16),
+            pltpu.SemaphoreType.DMA((PIECES,)),
+        ],
         compiler_params=params(),
         name="project_and_norm",
     )(partial, weight, hidden, modulation, bias, final_weight, final_bias)
@@ -402,7 +423,7 @@
 
     velocity = finish(
         partial,
-        weight,
+        pltpu.with_memory_space_constraint(weight, pltpu.HBM),
         hidden_in[0],
         modulation[0],
         out_bias[None],

time: 182 us -> 183 us (level)
  Pallas kernels: 69.7 us -> 72.5 us
  local copies, waits for them, and re-layouts: 4.02 us -> 1.66 us
    pallas_call x1, Pallas kernels: 3.33 us -> 6.12 us  [finish(): pl.pallas_call(functools.partial(finish_kernel, heads, groups), out_shape...]
    unnamed x19 -> x17, local copies, waits for them, and re-layouts: 3.37 us -> 1.05 us
  transfers between devices with their start and end apart: 13 -> 13, of which waited for: 4 -> 4; matrix products, arithmetic and copies ran while one was open for 0% -> 0% of each run, Pallas kernels for 37% -> 36%
where the time goes in v10:
time: 183 us; the launch traced here: 182 us
  Pallas kernels  72.5 us (40%)
  starting transfers between devices  57.6 us (31%)
  waiting for transfers between devices  18.7 us (10%)
  between operations  15.7 us (9%)
  blocking collectives  15.3 us (8%)
    pallas_call x5, Pallas kernels, attention_call(): pl.pallas_call(kernel, grid=(heads,), out_shape=out_shape, in_specs=specs...  65.4 us
    ppermute x7, starting transfers between devices, local(): pass_on = lambda x: lax.ppermute(x, ('zh', 'core'), route)  34.2 us
    all_to_all x1, waiting for transfers between devices, local(): lax.all_to_all(partial, BLOCK_AXES, split_axis=0, concat_axis=0, tiled=True)  14.5 us
    all_to_all x1, blocking collectives, local(): lax.all_to_all(slabs, HEAD_AXES, split_axis=0, concat_axis=0, tiled=True)  13.3 us
    all_to_all x1, starting transfers between devices, local(): lax.all_to_all(partial, BLOCK_AXES, split_axis=0, concat_axis=0, tiled=True)  7.25 us
    ppermute x1, starting transfers between devices, local(): beside = lax.ppermute(own, 'core', [(0, 1), (1, 0)])  6.17 us
    pallas_call x1, Pallas kernels, finish(): pl.pallas_call(functools.partial(finish_kernel, heads, groups), out_shape...  6.12 us
    ppermute x1, starting transfers between devices, local(): lax.ppermute(lax.dynamic_slice_in_dim(tiles, 1 - branch, 1, 0), ('cfg', '...  4.7 us
  transfers between devices with their start and end apart: 13, of which 4 were waited for; matrix products, arithmetic and copies ran while one was open for 0% of the time, Pallas kernels for 36%

profile of v10, /device:TPU:1, one launch (start us, length us, event | category | flops | bytes accessed | tf_op | source)
XLA Modules:
  0.0 182.1 jit_solution(15770474939438273994)
XLA Ops:
  7.2 0.7 all-gather.2.cloned.1.call-update
  7.9 1.0 copy-done
  8.9 0.2 pack_heads.1
  9.1 13.3 %all_to_all.10 = bf16[8,216,128]{2,1,0:T(8,128)(2,1)S(1)} all-to-all(bf16[8,216,128]{2,1,0:T(8,128)(2,1)S(1)} %pack_heads.1), channel_id=1, replica_groups=mesh['cfg'=2,'zh'=8,'zl'=2,'core'=2,'xh'=2,'y'=4] {'zl','y'}, dimensions={0} | all-to-all | bytes 884736 | tf_op jit(solution)/shard_map/all_to_all | solution.py:383
  22.4 6.2 %collective-permute-start.2 = (bf16[8,3,48,128]{3,2,1,0:T(8,128)(2,1)S(1)}, bf16[8,3,48,128]{3,2,1,0:T(8,128)(2,1)S(1)}, u32[]{:S(2)}, u32[]{:S(2)}) collective-permute-start(bf16[8,3,48,128]{3,2,1,0:T(8,128)(2,1)S(1)} %bitcast.26), channel_id=1, source_target_pairs={{0,8},{8,0},{1,9},{9,1},{2,10},{10,2},{3,11},{11,3},{4,12},{12,4},... | collective-permute-start | bytes 884744 | tf_op jit(solution)/shard_map/ppermute | solution.py:389
  28.6 9.5 %collective-permute-start.1 = (bf16[8,3,48,128]{3,2,1,0:T(8,128)(2,1)S(1)}, bf16[8,3,48,128]{3,2,1,0:T(8,128)(2,1)S(1)}, u32[]{:S(2)}, u32[]{:S(2)}) collective-permute-start(bf16[8,3,48,128]{3,2,1,0:T(8,128)(2,1)S(1)} %bitcast.27), channel_id=1, source_target_pairs={{0,32},{8,232},{32,64},{40,8},{64,96},{72,40},{96,128},{104,72},{1... | collective-permute-start | bytes 884744 | tf_op jit(solution)/shard_map/ppermute | solution.py:388
  38.1 2.0 %all_gather.6.own_ref = bf16[2,8,3,24,128]{4,3,2,1,0:T(8,128)(2,1)S(1)} all-gather(bf16[1,8,3,24,128]{4,3,2,1,0:T(8,128)(2,1)S(1)} %bitcast.35), channel_id=1, replica_groups=mesh['cfg'=2,'zh'=8,'zl'=2,'core'=2,'xh'=2,'y'=4] {'core'}, dimensions={0}, use_global_device_ids=true | all-gather | bytes 442368 | tf_op jit(solution)/shard_map/all_gather | solution.py:392
  40.1 4.6 %collective-permute-start = (bf16[2,8,3,24,128]{4,3,2,1,0:T(8,128)(2,1)S(1)}, bf16[2,8,3,24,128]{4,3,2,1,0:T(8,128)(2,1)S(1)}, u32[]{:S(2)}, u32[]{:S(2)}) collective-permute-start(bf16[2,8,3,24,128]{4,3,2,1,0:T(8,128)(2,1)S(1)} %all_gather.6.own_ref), channel_id=1, source_target_pairs={{0,4},{4,0},{1,5},{5,1},{2,6},{6,2},{3,7},{7,3},{8,12},{12,8},{9,1... | collective-permute-start | bytes 884744 | tf_op jit(solution)/shard_map/ppermute | solution.py:393
  44.8 0.2 copy.23
  45.1 3.1 %collective-permute-start.3 = (bf16[8,3,48,128]{3,2,1,0:T(8,128)(2,1)S(1)}, bf16[8,3,48,128]{3,2,1,0:T(8,128)(2,1)S(1)}, u32[]{:S(2)}, u32[]{:S(2)}) collective-permute-start(bf16[8,3,48,128]{3,2,1,0:T(8,128)(2,1)S(1)} %collective-permute-done.2), channel_id=1, source_target_pairs={{0,32},{8,232},{32,64},{40,8},{64,96},{72,40},{96,128},{104,72},{1... | collective-permute-start | bytes 884744 | tf_op jit(solution)/shard_map/ppermute | solution.py:388
  48.2 4.3 %collective-permute-start.4 = (bf16[8,3,48,128]{3,2,1,0:T(8,128)(2,1)S(1)}, bf16[8,3,48,128]{3,2,1,0:T(8,128)(2,1)S(1)}, u32[]{:S(2)}, u32[]{:S(2)}) collective-permute-start(bf16[8,3,48,128]{3,2,1,0:T(8,128)(2,1)S(1)} %collective-permute-done.1.refs_0_.refs_1_), channel_id=1, source_target_pairs={{0,32},{8,232},{32,64},{40,8},{64,96},{72,40},{96,128},{104,72},{1... | collective-permute-start | bytes 884744 | tf_op jit(solution)/shard_map/ppermute | solution.py:388
  52.5 0.8 unpack_queries.1.q_ref
  53.3 5.3 %own_block.1 = (bf16[3,2,768,256]{3,2,1,0:T(8,128)(2,1)S(1)}, f32[3,2,768,128]{3,2,1,0:T(8,128)S(1)}, f32[8,128]{1,0:T(8,128)S(1)}) custom-call(s32[1]{0:T(128)} %bitcast.valid_ref, bf16[3,2,768,256]{3,2,1,0:T(8,128)(2,1)S(1)} %unpack_queries.1.q_ref, bf16[8,3,48,128]{3,2,1,0:T(8,128)(2,1)S(1)} %bitcast.28, ...), custom_call_target="tpu_custom_call" | custom-call | flops 4000000000 | bytes 8000000 | tf_op jit(solution)/shard_map/own_block/pallas_call | solution.py:232
  58.7 0.5 collective-permute-done.3.refs_1_.refs_2_
  59.2 4.6 %collective-permute-start.5 = (bf16[8,3,48,128]{3,2,1,0:T(8,128)(2,1)S(1)}, bf16[8,3,48,128]{3,2,1,0:T(8,128)(2,1)S(1)}, u32[]{:S(2)}, u32[]{:S(2)}) collective-permute-start(bf16[8,3,48,128]{3,2,1,0:T(8,128)(2,1)S(1)} %collective-permute-done.3.refs_1_.refs_2_), channel_id=1, source_target_pairs={{0,32},{8,232},{32,64},{40,8},{64,96},{72,40},{96,128},{104,72},{1... | collective-permute-start | bytes 884744 | tf_op jit(solution)/shard_map/ppermute | solution.py:388
  63.8 4.6 %next_blocks.3 = (f32[3,2,768,128]{3,2,1,0:T(8,128)S(1)}, f32[8,128]{1,0:T(8,128)S(1)}) custom-call(bf16[3,2,768,256]{3,2,1,0:T(8,128)(2,1)S(1)} %get-tuple-element.18.q_ref, f32[3,2,768,128]{3,2,1,0:T(8,128)S(1)} %get-tuple-element.19.state_ref, bf16[8,3,48,128]{3,2,1,0:T(8,128)(2,1)S(1)} %collective-permute-done.1.refs_0_.refs_1_, ...), custom_call_target="tpu_custom_call", output_to_operand_aliasing={{0}: (1, {})} | custom-call | flops 4000000000 | bytes 8000000 | tf_op jit(solution)/shard_map/next_blocks/pallas_call | solution.py:232
  68.4 3.8 %collective-permute-start.6 = (bf16[8,3,48,128]{3,2,1,0:T(8,128)(2,1)S(1)}, bf16[8,3,48,128]{3,2,1,0:T(8,128)(2,1)S(1)}, u32[]{:S(2)}, u32[]{:S(2)}) collective-permute-start(bf16[8,3,48,128]{3,2,1,0:T(8,128)(2,1)S(1)} %collective-permute-done.4.refs_0_.refs_3_), channel_id=1, source_target_pairs={{0,32},{8,232},{32,64},{40,8},{64,96},{72,40},{96,128},{104,72},{1... | collective-permute-start | bytes 884744 | tf_op jit(solution)/shard_map/ppermute | solution.py:388
  72.2 5.0 %collective-permute-start.7 = (bf16[8,3,48,128]{3,2,1,0:T(8,128)(2,1)S(1)}, bf16[8,3,48,128]{3,2,1,0:T(8,128)(2,1)S(1)}, u32[]{:S(2)}, u32[]{:S(2)}) collective-permute-start(bf16[8,3,48,128]{3,2,1,0:T(8,128)(2,1)S(1)} %collective-permute-done.5.refs_1_.refs_4_), channel_id=1, source_target_pairs={{0,32},{8,232},{32,64},{40,8},{64,96},{72,40},{96,128},{104,72},{1... | collective-permute-start | bytes 884744 | tf_op jit(solution)/shard_map/ppermute | solution.py:388
  77.2 4.6 %next_blocks.4 = (f32[3,2,768,128]{3,2,1,0:T(8,128)S(1)}, f32[8,128]{1,0:T(8,128)S(1)}) custom-call(bf16[3,2,768,256]{3,2,1,0:T(8,128)(2,1)S(1)} %get-tuple-element.18.q_ref, f32[3,2,768,128]{3,2,1,0:T(8,128)S(1)} %get-tuple-element.23.state_ref, bf16[8,3,48,128]{3,2,1,0:T(8,128)(2,1)S(1)} %collective-permute-done.4.refs_0_.refs_3_, ...), custom_call_target="tpu_custom_call", output_to_operand_aliasing={{0}: (1, {})} | custom-call | flops 4000000000 | bytes 8000000 | tf_op jit(solution)/shard_map/next_blocks/pallas_call | solution.py:232
  81.8 3.9 %collective-permute-start.8 = (bf16[8,3,48,128]{3,2,1,0:T(8,128)(2,1)S(1)}, bf16[8,3,48,128]{3,2,1,0:T(8,128)(2,1)S(1)}, u32[]{:S(2)}, u32[]{:S(2)}) collective-permute-start(bf16[8,3,48,128]{3,2,1,0:T(8,128)(2,1)S(1)} %collective-permute-done.6.refs_0_.refs_5_), channel_id=1, source_target_pairs={{0,32},{8,232},{32,64},{40,8},{64,96},{72,40},{96,128},{104,72},{1... | collective-permute-start | bytes 884744 | tf_op jit(solution)/shard_map/ppermute | solution.py:388
  85.8 0.9 collective-permute-done.7.refs_1_.refs_6_
  86.7 5.0 %next_blocks.5 = (f32[3,2,768,128]{3,2,1,0:T(8,128)S(1)}, f32[8,128]{1,0:T(8,128)}) custom-call(bf16[3,2,768,256]{3,2,1,0:T(8,128)(2,1)S(1)} %get-tuple-element.18.q_ref, f32[3,2,768,128]{3,2,1,0:T(8,128)S(1)} %get-tuple-element.29.state_ref, bf16[8,3,48,128]{3,2,1,0:T(8,128)(2,1)S(1)} %collective-permute-done.6.refs_0_.refs_5_, ...), custom_call_target="tpu_custom_call", output_to_operand_aliasing={{0}: (1, {})} | custom-call | flops 4000000000 | bytes 8000000 | tf_op jit(solution)/shard_map/next_blocks/pallas_call | solution.py:232
  91.7 2.0 %collective-permute-done.8.block_ref = bf16[8,3,48,128]{3,2,1,0:T(8,128)(2,1)S(1)} collective-permute-done((bf16[8,3,48,128]{3,2,1,0:T(8,128)(2,1)S(1)}, bf16[8,3,48,128]{3,2,1,0:T(8,128)(2,1)S(1)}, u32[]{:S(2)}, u32[]{:S(2)}) %collective-permute-start.8) | collective-permute-done | bytes 294944 | tf_op jit(solution)/shard_map/ppermute | solution.py:388
  93.8 45.9 %last_block.1 = bf16[768,512]{1,0:T(8,128)(2,1)} custom-call(s32[1]{0:T(128)} %bitcast.valid_ref, bf16[3,2,768,256]{3,2,1,0:T(8,128)(2,1)S(1)} %get-tuple-element.18.q_ref, f32[3,2,768,128]{3,2,1,0:T(8,128)S(1)} %get-tuple-element.33.state_ref, bf16[8,3,48,128]{3,2,1,0:T(8,128)(2,1)S(1)} %collective-permute-done.8.block_ref, ...), custom_call_target="tpu_custom_call" | custom-call | flops 4000000000 | bytes 8000000 | tf_op jit(solution)/shard_map/last_block/pallas_call | solution.py:232
  139.6 7.3 %all-to-all-start.1 = ((bf16[32,24,512]{2,1,0:T(8,128)(2,1)}), bf16[32,24,512]{2,1,0:T(8,128)(2,1)S(1)}, u32[]{:S(2)}, u32[]{:S(2)}) async-start(bf16[32,24,512]{2,1,0:T(8,128)(2,1)} %bitcast.9), calls=%async_computation.1 | async-start | bytes 1572864 | tf_op jit(solution)/shard_map/all_to_all | solution.py:422
  146.9 14.5 %all-to-all-done.1.partial_ref = bf16[32,24,512]{2,1,0:T(8,128)(2,1)S(1)} async-done(((bf16[32,24,512]{2,1,0:T(8,128)(2,1)}), bf16[32,24,512]{2,1,0:T(8,128)(2,1)S(1)}, u32[]{:S(2)}, u32[]{:S(2)}) %all-to-all-start.1) | async-done | bytes 786464 | tf_op jit(solution)/shard_map/all_to_all | solution.py:422
  161.5 6.1 %project_and_norm.1 = f32[48,64]{1,0:T(8,128)S(1)} custom-call(bf16[32,24,512]{2,1,0:T(8,128)(2,1)S(1)} %all-to-all-done.1.partial_ref, bf16[1536,1536]{1,0:T(8,128)(2,1)} %all-gather.2.cloned.1.call-done.weight_ref, bf16[48,1536]{1,0:T(8,128)(2,1)S(1)} %bitcast.31, f32[3,1536]{1,0:T(4,128)S(1)} %bitcast.32, f32[1,1536]{1,0:T(1,128)S(1)} %broadcast_in_dim.6.bias_ref, ...), custom_call_target="tpu_custom_call" | custom-call | tf_op jit(solution)/shard_map/project_and_norm/pallas_call | solution.py:344
  167.7 0.1 copy.25
  167.8 0.1 reshape.31
  167.9 0.7 collective-permute-start.10
  168.6 4.7 %collective-permute-start.9 = (f32[1,1536]{1,0:T(1,128)S(1)}, f32[1,1536]{1,0:T(1,128)S(1)}, u32[]{:S(2)}, u32[]{:S(2)}) collective-permute-start(f32[1,1536]{1,0:T(1,128)S(1)} %get-tuple-element.36), channel_id=1, source_target_pairs={{0,1},{1,257},{2,3},{3,259},{256,0},{257,256},{258,2},{259,258},{4... | collective-permute-start | bytes 18440 | tf_op jit(solution)/shard_map/ppermute | solution.py:445
  174.6 0.6 multiply_subtract_fusion
  (34 shorter events, 0.3 us)
Async XLA Ops:
  7.2 37.6 %copy-start.4 = (bf16[1,333,2,192]{1,3,2,0:T(8,128)(2,1)S(1)}, bf16[1,333,2,192]{1,3,2,0:T(8,128)(2,1)}, u32[]{:S(2)}) copy-start(bf16[1,333,2,192]{1,3,2,0:T(8,128)(2,1)} %param.12) | copy-start | bytes 767236
  7.2 154.3 %all-gather.2.cloned.1.call-start = ((), (), s32[]{:S(2)}) async-start(), calls=%async_computation.2 | async-start | bytes 5308416 | tf_op jit(solution)/shard_map/all_gather | solution.py:397
  7.9 1.0 copy-start
  22.4 22.7 %collective-permute-start.2 = (bf16[8,3,48,128]{3,2,1,0:T(8,128)(2,1)S(1)}, bf16[8,3,48,128]{3,2,1,0:T(8,128)(2,1)S(1)}, u32[]{:S(2)}, u32[]{:S(2)}) collective-permute-start(bf16[8,3,48,128]{3,2,1,0:T(8,128)(2,1)S(1)} %bitcast.26), channel_id=1, source_target_pairs={{0,8},{8,0},{1,9},{9,1},{2,10},{10,2},{3,11},{11,3},{4,12},{12,4},... | collective-permute-start | bytes 884744 | tf_op jit(solution)/shard_map/ppermute | solution.py:389
  28.6 19.6 %collective-permute-start.1 = (bf16[8,3,48,128]{3,2,1,0:T(8,128)(2,1)S(1)}, bf16[8,3,48,128]{3,2,1,0:T(8,128)(2,1)S(1)}, u32[]{:S(2)}, u32[]{:S(2)}) collective-permute-start(bf16[8,3,48,128]{3,2,1,0:T(8,128)(2,1)S(1)} %bitcast.27), channel_id=1, source_target_pairs={{0,32},{8,232},{32,64},{40,8},{64,96},{72,40},{96,128},{104,72},{1... | collective-permute-start | bytes 884744 | tf_op jit(solution)/shard_map/ppermute | solution.py:388
  40.1 12.4 %collective-permute-start = (bf16[2,8,3,24,128]{4,3,2,1,0:T(8,128)(2,1)S(1)}, bf16[2,8,3,24,128]{4,3,2,1,0:T(8,128)(2,1)S(1)}, u32[]{:S(2)}, u32[]{:S(2)}) collective-permute-start(bf16[2,8,3,24,128]{4,3,2,1,0:T(8,128)(2,1)S(1)} %all_gather.6.own_ref), channel_id=1, source_target_pairs={{0,4},{4,0},{1,5},{5,1},{2,6},{6,2},{3,7},{7,3},{8,12},{12,8},{9,1... | collective-permute-start | bytes 884744 | tf_op jit(solution)/shard_map/ppermute | solution.py:393
  45.1 14.1 %collective-permute-start.3 = (bf16[8,3,48,128]{3,2,1,0:T(8,128)(2,1)S(1)}, bf16[8,3,48,128]{3,2,1,0:T(8,128)(2,1)S(1)}, u32[]{:S(2)}, u32[]{:S(2)}) collective-permute-start(bf16[8,3,48,128]{3,2,1,0:T(8,128)(2,1)S(1)} %collective-permute-done.2), channel_id=1, source_target_pairs={{0,32},{8,232},{32,64},{40,8},{64,96},{72,40},{96,128},{104,72},{1... | collective-permute-start | bytes 884744 | tf_op jit(solution)/shard_map/ppermute | solution.py:388
  48.2 20.2 %collective-permute-start.4 = (bf16[8,3,48,128]{3,2,1,0:T(8,128)(2,1)S(1)}, bf16[8,3,48,128]{3,2,1,0:T(8,128)(2,1)S(1)}, u32[]{:S(2)}, u32[]{:S(2)}) collective-permute-start(bf16[8,3,48,128]{3,2,1,0:T(8,128)(2,1)S(1)} %collective-permute-done.1.refs_0_.refs_1_), channel_id=1, source_target_pairs={{0,32},{8,232},{32,64},{40,8},{64,96},{72,40},{96,128},{104,72},{1... | collective-permute-start | bytes 884744 | tf_op jit(solution)/shard_map/ppermute | solution.py:388
  59.2 13.0 %collective-permute-start.5 = (bf16[8,3,48,128]{3,2,1,0:T(8,128)(2,1)S(1)}, bf16[8,3,48,128]{3,2,1,0:T(8,128)(2,1)S(1)}, u32[]{:S(2)}, u32[]{:S(2)}) collective-permute-start(bf16[8,3,48,128]{3,2,1,0:T(8,128)(2,1)S(1)} %collective-permute-done.3.refs_1_.refs_2_), channel_id=1, source_target_pairs={{0,32},{8,232},{32,64},{40,8},{64,96},{72,40},{96,128},{104,72},{1... | collective-permute-start | bytes 884744 | tf_op jit(solution)/shard_map/ppermute | solution.py:388
  68.4 13.4 %collective-permute-start.6 = (bf16[8,3,48,128]{3,2,1,0:T(8,128)(2,1)S(1)}, bf16[8,3,48,128]{3,2,1,0:T(8,128)(2,1)S(1)}, u32[]{:S(2)}, u32[]{:S(2)}) collective-permute-start(bf16[8,3,48,128]{3,2,1,0:T(8,128)(2,1)S(1)} %collective-permute-done.4.refs_0_.refs_3_), channel_id=1, source_target_pairs={{0,32},{8,232},{32,64},{40,8},{64,96},{72,40},{96,128},{104,72},{1... | collective-permute-start | bytes 884744 | tf_op jit(solution)/shard_map/ppermute | solution.py:388
  72.2 14.5 %collective-permute-start.7 = (bf16[8,3,48,128]{3,2,1,0:T(8,128)(2,1)S(1)}, bf16[8,3,48,128]{3,2,1,0:T(8,128)(2,1)S(1)}, u32[]{:S(2)}, u32[]{:S(2)}) collective-permute-start(bf16[8,3,48,128]{3,2,1,0:T(8,128)(2,1)S(1)} %collective-permute-done.5.refs_1_.refs_4_), channel_id=1, source_target_pairs={{0,32},{8,232},{32,64},{40,8},{64,96},{72,40},{96,128},{104,72},{1... | collective-permute-start | bytes 884744 | tf_op jit(solution)/shard_map/ppermute | solution.py:388
  81.8 11.9 %collective-permute-start.8 = (bf16[8,3,48,128]{3,2,1,0:T(8,128)(2,1)S(1)}, bf16[8,3,48,128]{3,2,1,0:T(8,128)(2,1)S(1)}, u32[]{:S(2)}, u32[]{:S(2)}) collective-permute-start(bf16[8,3,48,128]{3,2,1,0:T(8,128)(2,1)S(1)} %collective-permute-done.6.refs_0_.refs_5_), channel_id=1, source_target_pairs={{0,32},{8,232},{32,64},{40,8},{64,96},{72,40},{96,128},{104,72},{1... | collective-permute-start | bytes 884744 | tf_op jit(solution)/shard_map/ppermute | solution.py:388
  93.7 53.2 %copy-start.5 = (f32[1,3,1536]{2,0,1:T(1,128)S(1)}, f32[1,3,1536]{2,0,1:T(1,128)}, u32[]{:S(2)}) copy-start(f32[1,3,1536]{2,0,1:T(1,128)} %param.14) | copy-start | bytes 55300
  93.7 53.2 %copy-start.6 = (f32[1536]{0:T(1024)S(1)}, f32[1536]{0:T(1024)}, u32[]{:S(2)}) copy-start(f32[1536]{0:T(1024)} %param.16) | copy-start | bytes 18436
  93.7 67.7 %copy-start.1 = (bf16[1536,64]{0,1:T(8,128)(2,1)S(1)}, bf16[1536,64]{0,1:T(8,128)(2,1)}, u32[]{:S(2)}) copy-start(bf16[1536,64]{0,1:T(8,128)(2,1)} %param.17) | copy-start | bytes 589828
  93.7 67.7 %copy-start.2 = (bf16[1,48,1536]{2,1,0:T(8,128)(2,1)S(1)}, bf16[1,48,1536]{2,1,0:T(8,128)(2,1)}, u32[]{:S(2)}) copy-start(bf16[1,48,1536]{2,1,0:T(8,128)(2,1)} %param.13) | copy-start | bytes 442372
  93.7 67.7 %copy-start.3 = (f32[64]{0:T(128)S(1)}, f32[64]{0:T(128)}, u32[]{:S(2)}) copy-start(f32[64]{0:T(128)} %param.18) | copy-start | bytes 772
  139.6 21.8 %all-to-all-start.1 = ((bf16[32,24,512]{2,1,0:T(8,128)(2,1)}), bf16[32,24,512]{2,1,0:T(8,128)(2,1)S(1)}, u32[]{:S(2)}, u32[]{:S(2)}) async-start(bf16[32,24,512]{2,1,0:T(8,128)(2,1)} %bitcast.9), calls=%async_computation.1 | async-start | bytes 1572864 | tf_op jit(solution)/shard_map/all_to_all | solution.py:422
  161.5 13.1 %copy-start.7 = (f32[1,1536]{1,0:T(1,128)S(1)}, f32[1,1536]{1,0:T(1,128)}, u32[]{:S(2)}) copy-start(f32[1,1536]{1,0:T(1,128)} %param.21) | copy-start | bytes 18436
  167.9 6.7 %collective-permute-start.10 = (f32[1,1536]{1,0:T(1,128)S(1)}, f32[1,1536]{1,0:T(1,128)S(1)}, u32[]{:S(2)}, u32[]{:S(2)}) collective-permute-start(f32[1,1536]{1,0:T(1,128)S(1)} %get-tuple-element.37), channel_id=1, source_target_pairs={{0,0},{1,256},{2,2},{3,258},{256,1},{257,257},{258,3},{259,259},{4... | collective-permute-start | bytes 18440 | tf_op jit(solution)/shard_map/ppermute | solution.py:444
  168.6 6.0 %collective-permute-start.9 = (f32[1,1536]{1,0:T(1,128)S(1)}, f32[1,1536]{1,0:T(1,128)S(1)}, u32[]{:S(2)}, u32[]{:S(2)}) collective-permute-start(f32[1,1536]{1,0:T(1,128)S(1)} %get-tuple-element.36), channel_id=1, source_target_pairs={{0,1},{1,257},{2,3},{3,259},{256,0},{257,256},{258,2},{259,258},{4... | collective-permute-start | bytes 18440 | tf_op jit(solution)/shard_map/ppermute | solution.py:445
Sparse Core Ops, SparseCore 0:
  11.2 101.5 all-gather.1

commit v11 on v9

--- a/solution.py
+++ b/solution.py
@@ -65,20 +65,20 @@
 
 
 def queries_kernel(heads, place_ref, own_ref, other_ref, out_ref, wide_ref):
-    here = place_ref[0]
+    here, here_core = place_ref[0], place_ref[1]
     cores, sources, _, half, _ = own_ref.shape
     across = sources // 2
     lane = lane_index((half, LANES))
     low = lane < HEAD_DIM
     guard = jnp.where(lane == GUARD, 1.0, 0.0)
     for side, ref in ((here, own_ref), (1 - here, other_ref)):
-        for core in range(cores):
+        for slot, core in enumerate((here_core, 1 - here_core)):
             for source in range(sources):
                 zl, y = divmod(source, across)
                 first = (zl * cores + core) * 2 * across + y
                 row = pl.multiple_of((first + side * across) * half, 8)
                 for head in range(heads):
-                    both = ref[core, source, head].astype(F32) * LOG2_SCALE
+                    both = ref[slot, source, head].astype(F32) * LOG2_SCALE
                     for part, value in enumerate((both, pltpu.roll(both, HEAD_DIM, 1))):
                         lead = value.astype(BF16).astype(F32)
                         wide_ref[head, part, pl.ds(row, half), 0:LANES] = jnp.where(low, lead, 0.0)
@@ -365,13 +365,15 @@
     for i in range(ring):
         route += [(2 * i, 2 * ((i + 1) % ring)), (2 * i + 1, 2 * ((i - 1) % ring) + 1)]
     pass_on = lambda x: lax.ppermute(x, ("zh", "core"), route)
-    beside = lax.ppermute(own, "core", [(0, 1), (1, 0)])
+    other_slabs = lax.ppermute(slabs, "core", [(0, 1), (1, 0)])
+    beside = other_slabs[:, heads * half :].reshape(groups, heads, tokens, LANES)
     near = pass_on(own)
-    packed = slabs[:, : heads * half].reshape(groups, heads, half, LANES)
-    packed = lax.all_gather(packed, "core", axis=0)
+    packed = jnp.stack([slabs[:, : heads * half], other_slabs[:, : heads * half]])
+    packed = packed.reshape(2, groups, heads, half, LANES)
     opposite = lax.ppermute(packed, "xh", [(0, 1), (1, 0)])
     cross = pass_on(beside)
-    q = unpack_queries(xh.reshape(1), packed, opposite)
+    opposite, cross = after((opposite, cross))
+    q = unpack_queries(jnp.stack([xh, core]), packed, opposite)
 
     weight = lax.all_gather(out_weight, ("xh", "y"), axis=0, tiled=True)
 

time: 182 us -> 183 us (level)
  waiting for transfers between devices: 18.7 us -> 24.3 us
  starting transfers between devices: 57.6 us -> 54 us
  blocking collectives: 15.3 us -> 13.3 us
    ppermute x7, waiting for transfers between devices: 3.48 us -> 8.93 us  [local(): pass_on = lambda x: lax.ppermute(x, ('zh', 'core'), route)]
    ppermute x7, starting transfers between devices: 34.2 us -> 31.4 us  [local(): pass_on = lambda x: lax.ppermute(x, ('zh', 'core'), route)]
    all_gather x1 -> x0, blocking collectives: 2.02 us -> none  [local(): packed = lax.all_gather(packed, 'core', axis=0)]
  transfers between devices with their start and end apart: 13 -> 13, of which waited for: 4 -> 5; matrix products, arithmetic and copies ran while one was open for 0% -> 0% of each run, Pallas kernels for 37% -> 37%
where the time goes in v11:
time: 183 us; the launch traced here: 182 us
  Pallas kernels  70.2 us (38%)
  starting transfers between devices  54 us (30%)
  waiting for transfers between devices  24.3 us (13%)
  between operations  15.7 us (9%)
  blocking collectives  13.3 us (7%)
  local copies, waits for them, and re-layouts  4.04 us (2%)
    pallas_call x5, Pallas kernels, attention_call(): pl.pallas_call(kernel, grid=(heads,), out_shape=out_shape, in_specs=specs...  65.4 us
    ppermute x7, starting transfers between devices, local(): pass_on = lambda x: lax.ppermute(x, ('zh', 'core'), route)  31.4 us
    all_to_all x1, waiting for transfers between devices, local(): lax.all_to_all(partial, BLOCK_AXES, split_axis=0, concat_axis=0, tiled=True)  14.6 us
    all_to_all x1, blocking collectives, local(): lax.all_to_all(slabs, HEAD_AXES, split_axis=0, concat_axis=0, tiled=True)  13.3 us
    ppermute x7, waiting for transfers between devices, local(): pass_on = lambda x: lax.ppermute(x, ('zh', 'core'), route)  8.93 us
    all_to_all x1, starting transfers between devices, local(): lax.all_to_all(partial, BLOCK_AXES, split_axis=0, concat_axis=0, tiled=True)  6.84 us
    ppermute x1, starting transfers between devices, local(): other_slabs = lax.ppermute(slabs, 'core', [(0, 1), (1, 0)])  6.15 us
    ppermute x1, starting transfers between devices, local(): opposite = lax.ppermute(packed, 'xh', [(0, 1), (1, 0)])  4.65 us
  transfers between devices with their start and end apart: 13, of which 5 were waited for; matrix products, arithmetic and copies ran while one was open for 0% of the time, Pallas kernels for 37%

profile of v11, /device:TPU:1, one launch (start us, length us, event | category | flops | bytes accessed | tf_op | source)
XLA Modules:
  0.0 182.3 jit_solution(8662177418173023972)
XLA Ops:
  7.2 0.7 all-gather.2.cloned.1.call-update
  7.9 1.0 copy-done.1
  8.9 0.2 pack_heads.1
  9.1 13.3 %all_to_all.10 = bf16[8,216,128]{2,1,0:T(8,128)(2,1)S(1)} all-to-all(bf16[8,216,128]{2,1,0:T(8,128)(2,1)S(1)} %pack_heads.1), channel_id=1, replica_groups=mesh['cfg'=2,'zh'=8,'zl'=2,'core'=2,'xh'=2,'y'=4] {'zl','y'}, dimensions={0} | all-to-all | bytes 884736 | tf_op jit(solution)/shard_map/all_to_all | solution.py:362
  22.4 6.2 %collective-permute-start = (bf16[8,216,128]{2,1,0:T(8,128)(2,1)S(1)}, bf16[8,216,128]{2,1,0:T(8,128)(2,1)S(1)}, u32[]{:S(2)}, u32[]{:S(2)}) collective-permute-start(bf16[8,216,128]{2,1,0:T(8,128)(2,1)S(1)} %all_to_all.10), channel_id=1, source_target_pairs={{0,8},{8,0},{1,9},{9,1},{2,10},{10,2},{3,11},{11,3},{4,12},{12,4},... | collective-permute-start | bytes 1327112 | tf_op jit(solution)/shard_map/ppermute | solution.py:368
  28.6 0.2 copy.19
  28.9 9.5 %collective-permute-start.3 = (bf16[8,3,48,128]{3,2,1,0:T(8,128)(2,1)S(1)}, bf16[8,3,48,128]{3,2,1,0:T(8,128)(2,1)S(1)}, u32[]{:S(2)}, u32[]{:S(2)}) collective-permute-start(bf16[8,3,48,128]{3,2,1,0:T(8,128)(2,1)S(1)} %bitcast.29), channel_id=1, source_target_pairs={{0,32},{8,232},{32,64},{40,8},{64,96},{72,40},{96,128},{104,72},{1... | collective-permute-start | bytes 884744 | tf_op jit(solution)/shard_map/ppermute | solution.py:367
  38.4 4.7 %collective-permute-start.1 = (bf16[2,8,3,24,128]{4,3,2,1,0:T(8,128)(2,1)S(1)}, bf16[2,8,3,24,128]{4,3,2,1,0:T(8,128)(2,1)S(1)}, u32[]{:S(2)}, u32[]{:S(2)}) collective-permute-start(bf16[2,8,3,24,128]{4,3,2,1,0:T(8,128)(2,1)S(1)} %pad_maximum_fusion.own_ref), channel_id=1, source_target_pairs={{0,4},{4,0},{1,5},{5,1},{2,6},{6,2},{3,7},{7,3},{8,12},{12,8},{9,1... | collective-permute-start | bytes 884744 | tf_op jit(solution)/shard_map/ppermute | solution.py:373
  43.1 3.1 %collective-permute-start.2 = (bf16[8,3,48,128]{3,2,1,0:T(8,128)(2,1)S(1)}, bf16[8,3,48,128]{3,2,1,0:T(8,128)(2,1)S(1)}, u32[]{:S(2)}, u32[]{:S(2)}) collective-permute-start(bf16[8,3,48,128]{3,2,1,0:T(8,128)(2,1)S(1)} %bitcast.40), channel_id=1, source_target_pairs={{0,32},{8,232},{32,64},{40,8},{64,96},{72,40},{96,128},{104,72},{1... | collective-permute-start | bytes 884744 | tf_op jit(solution)/shard_map/ppermute | solution.py:367
  46.4 5.1 %collective-permute-start.4 = (bf16[8,3,48,128]{3,2,1,0:T(8,128)(2,1)S(1)}, bf16[8,3,48,128]{3,2,1,0:T(8,128)(2,1)S(1)}, u32[]{:S(2)}, u32[]{:S(2)}) collective-permute-start(bf16[8,3,48,128]{3,2,1,0:T(8,128)(2,1)S(1)} %collective-permute-done.3.refs_0_.refs_1_), channel_id=1, source_target_pairs={{0,32},{8,232},{32,64},{40,8},{64,96},{72,40},{96,128},{104,72},{1... | collective-permute-start | bytes 884744 | tf_op jit(solution)/shard_map/ppermute | solution.py:367
  51.5 6.7 %collective-permute-done.2.refs_1_.refs_2_ = bf16[8,3,48,128]{3,2,1,0:T(8,128)(2,1)S(1)} collective-permute-done((bf16[8,3,48,128]{3,2,1,0:T(8,128)(2,1)S(1)}, bf16[8,3,48,128]{3,2,1,0:T(8,128)(2,1)S(1)}, u32[]{:S(2)}, u32[]{:S(2)}) %collective-permute-start.2) | collective-permute-done | bytes 294944 | tf_op jit(solution)/shard_map/ppermute | solution.py:367
  58.1 1.3 unpack_queries.1.q_ref
  59.5 5.3 %own_block.1 = (bf16[3,2,768,256]{3,2,1,0:T(8,128)(2,1)S(1)}, f32[3,2,768,128]{3,2,1,0:T(8,128)S(1)}, f32[8,128]{1,0:T(8,128)S(1)}) custom-call(s32[1]{0:T(128)} %bitcast.valid_ref, bf16[3,2,768,256]{3,2,1,0:T(8,128)(2,1)S(1)} %unpack_queries.1.q_ref, bf16[8,3,48,128]{3,2,1,0:T(8,128)(2,1)S(1)} %bitcast.30, ...), custom_call_target="tpu_custom_call" | custom-call | flops 4000000000 | bytes 8000000 | tf_op jit(solution)/shard_map/own_block/pallas_call | solution.py:231
  64.8 3.7 %collective-permute-start.5 = (bf16[8,3,48,128]{3,2,1,0:T(8,128)(2,1)S(1)}, bf16[8,3,48,128]{3,2,1,0:T(8,128)(2,1)S(1)}, u32[]{:S(2)}, u32[]{:S(2)}) collective-permute-start(bf16[8,3,48,128]{3,2,1,0:T(8,128)(2,1)S(1)} %collective-permute-done.2.refs_1_.refs_2_), channel_id=1, source_target_pairs={{0,32},{8,232},{32,64},{40,8},{64,96},{72,40},{96,128},{104,72},{1... | collective-permute-start | bytes 884744 | tf_op jit(solution)/shard_map/ppermute | solution.py:367
  68.5 4.6 %next_blocks.3 = (f32[3,2,768,128]{3,2,1,0:T(8,128)S(1)}, f32[8,128]{1,0:T(8,128)S(1)}) custom-call(bf16[3,2,768,256]{3,2,1,0:T(8,128)(2,1)S(1)} %get-tuple-element.21.q_ref, f32[3,2,768,128]{3,2,1,0:T(8,128)S(1)} %get-tuple-element.22.state_ref, bf16[8,3,48,128]{3,2,1,0:T(8,128)(2,1)S(1)} %collective-permute-done.3.refs_0_.refs_1_, ...), custom_call_target="tpu_custom_call", output_to_operand_aliasing={{0}: (1, {})} | custom-call | flops 4000000000 | bytes 8000000 | tf_op jit(solution)/shard_map/next_blocks/pallas_call | solution.py:231
  73.1 3.7 %collective-permute-start.6 = (bf16[8,3,48,128]{3,2,1,0:T(8,128)(2,1)S(1)}, bf16[8,3,48,128]{3,2,1,0:T(8,128)(2,1)S(1)}, u32[]{:S(2)}, u32[]{:S(2)}) collective-permute-start(bf16[8,3,48,128]{3,2,1,0:T(8,128)(2,1)S(1)} %collective-permute-done.4.refs_0_.refs_3_), channel_id=1, source_target_pairs={{0,32},{8,232},{32,64},{40,8},{64,96},{72,40},{96,128},{104,72},{1... | collective-permute-start | bytes 884744 | tf_op jit(solution)/shard_map/ppermute | solution.py:367
  76.8 1.9 %collective-permute-start.7 = (bf16[8,3,48,128]{3,2,1,0:T(8,128)(2,1)S(1)}, bf16[8,3,48,128]{3,2,1,0:T(8,128)(2,1)S(1)}, u32[]{:S(2)}, u32[]{:S(2)}) collective-permute-start(bf16[8,3,48,128]{3,2,1,0:T(8,128)(2,1)S(1)} %collective-permute-done.5.refs_1_.refs_4_), channel_id=1, source_target_pairs={{0,32},{8,232},{32,64},{40,8},{64,96},{72,40},{96,128},{104,72},{1... | collective-permute-start | bytes 884744 | tf_op jit(solution)/shard_map/ppermute | solution.py:367
  78.7 4.6 %next_blocks.4 = (f32[3,2,768,128]{3,2,1,0:T(8,128)S(1)}, f32[8,128]{1,0:T(8,128)S(1)}) custom-call(bf16[3,2,768,256]{3,2,1,0:T(8,128)(2,1)S(1)} %get-tuple-element.21.q_ref, f32[3,2,768,128]{3,2,1,0:T(8,128)S(1)} %get-tuple-element.27.state_ref, bf16[8,3,48,128]{3,2,1,0:T(8,128)(2,1)S(1)} %collective-permute-done.4.refs_0_.refs_3_, ...), custom_call_target="tpu_custom_call", output_to_operand_aliasing={{0}: (1, {})} | custom-call | flops 4000000000 | bytes 8000000 | tf_op jit(solution)/shard_map/next_blocks/pallas_call | solution.py:231
  83.3 1.8 collective-permute-done.6.refs_0_.refs_5_
  85.1 4.5 %collective-permute-start.8 = (bf16[8,3,48,128]{3,2,1,0:T(8,128)(2,1)S(1)}, bf16[8,3,48,128]{3,2,1,0:T(8,128)(2,1)S(1)}, u32[]{:S(2)}, u32[]{:S(2)}) collective-permute-start(bf16[8,3,48,128]{3,2,1,0:T(8,128)(2,1)S(1)} %collective-permute-done.6.refs_0_.refs_5_), channel_id=1, source_target_pairs={{0,32},{8,232},{32,64},{40,8},{64,96},{72,40},{96,128},{104,72},{1... | collective-permute-start | bytes 884744 | tf_op jit(solution)/shard_map/ppermute | solution.py:367
  89.6 5.0 %next_blocks.5 = (f32[3,2,768,128]{3,2,1,0:T(8,128)S(1)}, f32[8,128]{1,0:T(8,128)}) custom-call(bf16[3,2,768,256]{3,2,1,0:T(8,128)(2,1)S(1)} %get-tuple-element.21.q_ref, f32[3,2,768,128]{3,2,1,0:T(8,128)S(1)} %get-tuple-element.33.state_ref, bf16[8,3,48,128]{3,2,1,0:T(8,128)(2,1)S(1)} %collective-permute-done.6.refs_0_.refs_5_, ...), custom_call_target="tpu_custom_call", output_to_operand_aliasing={{0}: (1, {})} | custom-call | flops 4000000000 | bytes 8000000 | tf_op jit(solution)/shard_map/next_blocks/pallas_call | solution.py:231
  94.6 0.5 collective-permute-done.8.block_ref
  95.1 45.9 %last_block.1 = bf16[768,512]{1,0:T(8,128)(2,1)} custom-call(s32[1]{0:T(128)} %bitcast.valid_ref, bf16[3,2,768,256]{3,2,1,0:T(8,128)(2,1)S(1)} %get-tuple-element.21.q_ref, f32[3,2,768,128]{3,2,1,0:T(8,128)S(1)} %get-tuple-element.37.state_ref, bf16[8,3,48,128]{3,2,1,0:T(8,128)(2,1)S(1)} %collective-permute-done.8.block_ref, ...), custom_call_target="tpu_custom_call" | custom-call | flops 4000000000 | bytes 8000000 | tf_op jit(solution)/shard_map/last_block/pallas_call | solution.py:231
  141.0 6.8 %all-to-all-start.1 = ((bf16[32,24,512]{2,1,0:T(8,128)(2,1)}), bf16[32,24,512]{2,1,0:T(8,128)(2,1)S(1)}, u32[]{:S(2)}, u32[]{:S(2)}) async-start(bf16[32,24,512]{2,1,0:T(8,128)(2,1)} %bitcast.12), calls=%async_computation.1 | async-start | bytes 1572864 | tf_op jit(solution)/shard_map/all_to_all | solution.py:403
  147.9 14.6 %all-to-all-done.1.partial_ref = bf16[32,24,512]{2,1,0:T(8,128)(2,1)S(1)} async-done(((bf16[32,24,512]{2,1,0:T(8,128)(2,1)}), bf16[32,24,512]{2,1,0:T(8,128)(2,1)S(1)}, u32[]{:S(2)}, u32[]{:S(2)}) %all-to-all-start.1) | async-done | bytes 786464 | tf_op jit(solution)/shard_map/all_to_all | solution.py:403
  162.5 2.3 %copy-done = bf16[1536,1536]{1,0:T(8,128)(2,1)S(1)} copy-done((bf16[1536,1536]{1,0:T(8,128)(2,1)S(1)}, bf16[1536,1536]{1,0:T(8,128)(2,1)}, u32[]{:S(2)}) %copy-start) | copy-done | bytes 4718616
  164.8 3.3 %project_and_norm.1 = f32[48,64]{1,0:T(8,128)S(1)} custom-call(bf16[32,24,512]{2,1,0:T(8,128)(2,1)S(1)} %all-to-all-done.1.partial_ref, bf16[1536,1536]{1,0:T(8,128)(2,1)S(1)} %copy-done, bf16[48,1536]{1,0:T(8,128)(2,1)S(1)} %bitcast.33, f32[3,1536]{1,0:T(4,128)S(1)} %bitcast.34, f32[1,1536]{1,0:T(1,128)S(1)} %broadcast_in_dim.6.bias_ref, ...), custom_call_target="tpu_custom_call" | custom-call | tf_op jit(solution)/shard_map/project_and_norm/pallas_call | solution.py:329
  168.1 0.1 copy.20
  168.3 0.1 reshape.36
  168.5 0.7 collective-permute-start.10
  169.1 4.3 %collective-permute-start.9 = (f32[1,1536]{1,0:T(1,128)S(1)}, f32[1,1536]{1,0:T(1,128)S(1)}, u32[]{:S(2)}, u32[]{:S(2)}) collective-permute-start(f32[1,1536]{1,0:T(1,128)S(1)} %get-tuple-element.40), channel_id=1, source_target_pairs={{0,1},{1,257},{2,3},{3,259},{256,0},{257,256},{258,2},{259,258},{4... | collective-permute-start | bytes 18440 | tf_op jit(solution)/shard_map/ppermute | solution.py:426
  174.8 0.6 multiply_subtract_fusion
  (39 shorter events, 0.5 us)
Async XLA Ops:
  7.2 21.4 %copy-start.5 = (bf16[1,333,2,192]{1,3,2,0:T(8,128)(2,1)S(1)}, bf16[1,333,2,192]{1,3,2,0:T(8,128)(2,1)}, u32[]{:S(2)}) copy-start(bf16[1,333,2,192]{1,3,2,0:T(8,128)(2,1)} %param.12) | copy-start | bytes 767236
  7.2 155.3 %all-gather.2.cloned.1.call-start = ((), (), s32[]{:S(2)}) async-start(), calls=%async_computation.2 | async-start | bytes 5308416 | tf_op jit(solution)/shard_map/all_gather | solution.py:378
  7.9 1.0 copy-start.1
  22.4 16.0 %collective-permute-start = (bf16[8,216,128]{2,1,0:T(8,128)(2,1)S(1)}, bf16[8,216,128]{2,1,0:T(8,128)(2,1)S(1)}, u32[]{:S(2)}, u32[]{:S(2)}) collective-permute-start(bf16[8,216,128]{2,1,0:T(8,128)(2,1)S(1)} %all_to_all.10), channel_id=1, source_target_pairs={{0,8},{8,0},{1,9},{9,1},{2,10},{10,2},{3,11},{11,3},{4,12},{12,4},... | collective-permute-start | bytes 1327112 | tf_op jit(solution)/shard_map/ppermute | solution.py:368
  28.9 17.5 %collective-permute-start.3 = (bf16[8,3,48,128]{3,2,1,0:T(8,128)(2,1)S(1)}, bf16[8,3,48,128]{3,2,1,0:T(8,128)(2,1)S(1)}, u32[]{:S(2)}, u32[]{:S(2)}) collective-permute-start(bf16[8,3,48,128]{3,2,1,0:T(8,128)(2,1)S(1)} %bitcast.29), channel_id=1, source_target_pairs={{0,32},{8,232},{32,64},{40,8},{64,96},{72,40},{96,128},{104,72},{1... | collective-permute-start | bytes 884744 | tf_op jit(solution)/shard_map/ppermute | solution.py:367
  38.4 13.0 %collective-permute-start.1 = (bf16[2,8,3,24,128]{4,3,2,1,0:T(8,128)(2,1)S(1)}, bf16[2,8,3,24,128]{4,3,2,1,0:T(8,128)(2,1)S(1)}, u32[]{:S(2)}, u32[]{:S(2)}) collective-permute-start(bf16[2,8,3,24,128]{4,3,2,1,0:T(8,128)(2,1)S(1)} %pad_maximum_fusion.own_ref), channel_id=1, source_target_pairs={{0,4},{4,0},{1,5},{5,1},{2,6},{6,2},{3,7},{7,3},{8,12},{12,8},{9,1... | collective-permute-start | bytes 884744 | tf_op jit(solution)/shard_map/ppermute | solution.py:373
  43.1 15.0 %collective-permute-start.2 = (bf16[8,3,48,128]{3,2,1,0:T(8,128)(2,1)S(1)}, bf16[8,3,48,128]{3,2,1,0:T(8,128)(2,1)S(1)}, u32[]{:S(2)}, u32[]{:S(2)}) collective-permute-start(bf16[8,3,48,128]{3,2,1,0:T(8,128)(2,1)S(1)} %bitcast.40), channel_id=1, source_target_pairs={{0,32},{8,232},{32,64},{40,8},{64,96},{72,40},{96,128},{104,72},{1... | collective-permute-start | bytes 884744 | tf_op jit(solution)/shard_map/ppermute | solution.py:367
  46.4 26.8 %collective-permute-start.4 = (bf16[8,3,48,128]{3,2,1,0:T(8,128)(2,1)S(1)}, bf16[8,3,48,128]{3,2,1,0:T(8,128)(2,1)S(1)}, u32[]{:S(2)}, u32[]{:S(2)}) collective-permute-start(bf16[8,3,48,128]{3,2,1,0:T(8,128)(2,1)S(1)} %collective-permute-done.3.refs_0_.refs_1_), channel_id=1, source_target_pairs={{0,32},{8,232},{32,64},{40,8},{64,96},{72,40},{96,128},{104,72},{1... | collective-permute-start | bytes 884744 | tf_op jit(solution)/shard_map/ppermute | solution.py:367
  64.8 12.0 %collective-permute-start.5 = (bf16[8,3,48,128]{3,2,1,0:T(8,128)(2,1)S(1)}, bf16[8,3,48,128]{3,2,1,0:T(8,128)(2,1)S(1)}, u32[]{:S(2)}, u32[]{:S(2)}) collective-permute-start(bf16[8,3,48,128]{3,2,1,0:T(8,128)(2,1)S(1)} %collective-permute-done.2.refs_1_.refs_2_), channel_id=1, source_target_pairs={{0,32},{8,232},{32,64},{40,8},{64,96},{72,40},{96,128},{104,72},{1... | collective-permute-start | bytes 884744 | tf_op jit(solution)/shard_map/ppermute | solution.py:367
  73.1 12.0 %collective-permute-start.6 = (bf16[8,3,48,128]{3,2,1,0:T(8,128)(2,1)S(1)}, bf16[8,3,48,128]{3,2,1,0:T(8,128)(2,1)S(1)}, u32[]{:S(2)}, u32[]{:S(2)}) collective-permute-start(bf16[8,3,48,128]{3,2,1,0:T(8,128)(2,1)S(1)} %collective-permute-done.4.refs_0_.refs_3_), channel_id=1, source_target_pairs={{0,32},{8,232},{32,64},{40,8},{64,96},{72,40},{96,128},{104,72},{1... | collective-permute-start | bytes 884744 | tf_op jit(solution)/shard_map/ppermute | solution.py:367
  76.8 12.8 %collective-permute-start.7 = (bf16[8,3,48,128]{3,2,1,0:T(8,128)(2,1)S(1)}, bf16[8,3,48,128]{3,2,1,0:T(8,128)(2,1)S(1)}, u32[]{:S(2)}, u32[]{:S(2)}) collective-permute-start(bf16[8,3,48,128]{3,2,1,0:T(8,128)(2,1)S(1)} %collective-permute-done.5.refs_1_.refs_4_), channel_id=1, source_target_pairs={{0,32},{8,232},{32,64},{40,8},{64,96},{72,40},{96,128},{104,72},{1... | collective-permute-start | bytes 884744 | tf_op jit(solution)/shard_map/ppermute | solution.py:367
  85.1 10.0 %collective-permute-start.8 = (bf16[8,3,48,128]{3,2,1,0:T(8,128)(2,1)S(1)}, bf16[8,3,48,128]{3,2,1,0:T(8,128)(2,1)S(1)}, u32[]{:S(2)}, u32[]{:S(2)}) collective-permute-start(bf16[8,3,48,128]{3,2,1,0:T(8,128)(2,1)S(1)} %collective-permute-done.6.refs_0_.refs_5_), channel_id=1, source_target_pairs={{0,32},{8,232},{32,64},{40,8},{64,96},{72,40},{96,128},{104,72},{1... | collective-permute-start | bytes 884744 | tf_op jit(solution)/shard_map/ppermute | solution.py:367
  95.1 52.7 %copy-start.6 = (f32[1,3,1536]{2,0,1:T(1,128)S(1)}, f32[1,3,1536]{2,0,1:T(1,128)}, u32[]{:S(2)}) copy-start(f32[1,3,1536]{2,0,1:T(1,128)} %param.14) | copy-start | bytes 55300
  95.1 52.8 %copy-start.7 = (f32[1536]{0:T(1024)S(1)}, f32[1536]{0:T(1024)}, u32[]{:S(2)}) copy-start(f32[1536]{0:T(1024)} %param.16) | copy-start | bytes 18436
  95.1 67.4 %copy-start.2 = (bf16[1536,64]{0,1:T(8,128)(2,1)S(1)}, bf16[1536,64]{0,1:T(8,128)(2,1)}, u32[]{:S(2)}) copy-start(bf16[1536,64]{0,1:T(8,128)(2,1)} %param.17) | copy-start | bytes 589828
  95.1 67.4 %copy-start.3 = (bf16[1,48,1536]{2,1,0:T(8,128)(2,1)S(1)}, bf16[1,48,1536]{2,1,0:T(8,128)(2,1)}, u32[]{:S(2)}) copy-start(bf16[1,48,1536]{2,1,0:T(8,128)(2,1)} %param.13) | copy-start | bytes 442372
  95.1 67.4 %copy-start.4 = (f32[64]{0:T(128)S(1)}, f32[64]{0:T(128)}, u32[]{:S(2)}) copy-start(f32[64]{0:T(128)} %param.18) | copy-start | bytes 772
  141.0 21.5 %all-to-all-start.1 = ((bf16[32,24,512]{2,1,0:T(8,128)(2,1)}), bf16[32,24,512]{2,1,0:T(8,128)(2,1)S(1)}, u32[]{:S(2)}, u32[]{:S(2)}) async-start(bf16[32,24,512]{2,1,0:T(8,128)(2,1)} %bitcast.12), calls=%async_computation.1 | async-start | bytes 1572864 | tf_op jit(solution)/shard_map/all_to_all | solution.py:403
  162.5 2.3 %copy-start = (bf16[1536,1536]{1,0:T(8,128)(2,1)S(1)}, bf16[1536,1536]{1,0:T(8,128)(2,1)}, u32[]{:S(2)}) copy-start(bf16[1536,1536]{1,0:T(8,128)(2,1)} %all-gather.2.cloned.1.call-done.weight_ref) | copy-start | bytes 14155780
  164.8 10.0 %copy-start.8 = (f32[1,1536]{1,0:T(1,128)S(1)}, f32[1,1536]{1,0:T(1,128)}, u32[]{:S(2)}) copy-start(f32[1,1536]{1,0:T(1,128)} %param.21) | copy-start | bytes 18436
  168.5 6.3 %collective-permute-start.10 = (f32[1,1536]{1,0:T(1,128)S(1)}, f32[1,1536]{1,0:T(1,128)S(1)}, u32[]{:S(2)}, u32[]{:S(2)}) collective-permute-start(f32[1,1536]{1,0:T(1,128)S(1)} %get-tuple-element.41), channel_id=1, source_target_pairs={{0,0},{1,256},{2,2},{3,258},{256,1},{257,257},{258,3},{259,259},{4... | collective-permute-start | bytes 18440 | tf_op jit(solution)/shard_map/ppermute | solution.py:425
  169.1 5.7 %collective-permute-start.9 = (f32[1,1536]{1,0:T(1,128)S(1)}, f32[1,1536]{1,0:T(1,128)S(1)}, u32[]{:S(2)}, u32[]{:S(2)}) collective-permute-start(f32[1,1536]{1,0:T(1,128)S(1)} %get-tuple-element.40), channel_id=1, source_target_pairs={{0,1},{1,257},{2,3},{3,259},{256,0},{257,256},{258,2},{259,258},{4... | collective-permute-start | bytes 18440 | tf_op jit(solution)/shard_map/ppermute | solution.py:426
Sparse Core Ops, SparseCore 0:
  11.2 101.3 all-gather.1

commit v12 on v9

--- a/solution.py
+++ b/solution.py
@@ -397,7 +397,7 @@
     farthest = pass_on(near)
     state, mark = next_blocks(q, state, [near, cross], mark)
     partial = last_block(valid, q, state, farthest, early, late, kept)
-    partial = partial.reshape(4 * groups, half, 4 * LANES)
+    partial, weight = after((partial.reshape(4 * groups, half, 4 * LANES), weight))
     partial = lax.all_to_all(partial, BLOCK_AXES, split_axis=0, concat_axis=0, tiled=True)
 
     velocity = finish(

time: 182 us -> 182 us (level)
  no operation moved by 1% of the time
where the time goes in v12:
time: 182 us
  Pallas kernels  69.7 us (38%)
  starting transfers between devices  57.6 us (32%)
  waiting for transfers between devices  18.7 us (10%)
  between operations  15.7 us (9%)
  blocking collectives  15.3 us (8%)
  local copies, waits for them, and re-layouts  4.02 us (2%)
    pallas_call x5, Pallas kernels, attention_call(): pl.pallas_call(kernel, grid=(heads,), out_shape=out_shape, in_specs=specs...  65.4 us
    ppermute x7, starting transfers between devices, local(): pass_on = lambda x: lax.ppermute(x, ('zh', 'core'), route)  34.2 us
    all_to_all x1, waiting for transfers between devices, local(): lax.all_to_all(partial, BLOCK_AXES, split_axis=0, concat_axis=0, tiled=True)  14.5 us
    all_to_all x1, blocking collectives, local(): lax.all_to_all(slabs, HEAD_AXES, split_axis=0, concat_axis=0, tiled=True)  13.3 us
    all_to_all x1, starting transfers between devices, local(): lax.all_to_all(partial, BLOCK_AXES, split_axis=0, concat_axis=0, tiled=True)  7.25 us
    ppermute x1, starting transfers between devices, local(): beside = lax.ppermute(own, 'core', [(0, 1), (1, 0)])  6.17 us
    ppermute x1, starting transfers between devices, local(): lax.ppermute(lax.dynamic_slice_in_dim(tiles, 1 - branch, 1, 0), ('cfg', '...  4.7 us
    ppermute x1, starting transfers between devices, local(): opposite = lax.ppermute(packed, 'xh', [(0, 1), (1, 0)])  4.64 us
  transfers between devices with their start and end apart: 13, of which 4 were waited for; matrix products, arithmetic and copies ran while one was open for 0% of the time, Pallas kernels for 37%

profile of v12, /device:TPU:1, one launch (start us, length us, event | category | flops | bytes accessed | tf_op | source)
XLA Modules:
  0.0 181.7 jit_solution(3594857436597391497)
XLA Ops:
  7.2 0.7 all-gather.2.cloned.1.call-update
  7.9 1.0 copy-done.1
  8.9 0.2 pack_heads.1
  9.1 13.3 %all_to_all.10 = bf16[8,216,128]{2,1,0:T(8,128)(2,1)S(1)} all-to-all(bf16[8,216,128]{2,1,0:T(8,128)(2,1)S(1)} %pack_heads.1), channel_id=1, replica_groups=mesh['cfg'=2,'zh'=8,'zl'=2,'core'=2,'xh'=2,'y'=4] {'zl','y'}, dimensions={0} | all-to-all | bytes 884736 | tf_op jit(solution)/shard_map/all_to_all | solution.py:362
  22.4 6.2 %collective-permute-start.2 = (bf16[8,3,48,128]{3,2,1,0:T(8,128)(2,1)S(1)}, bf16[8,3,48,128]{3,2,1,0:T(8,128)(2,1)S(1)}, u32[]{:S(2)}, u32[]{:S(2)}) collective-permute-start(bf16[8,3,48,128]{3,2,1,0:T(8,128)(2,1)S(1)} %bitcast.26), channel_id=1, source_target_pairs={{0,8},{8,0},{1,9},{9,1},{2,10},{10,2},{3,11},{11,3},{4,12},{12,4},... | collective-permute-start | bytes 884744 | tf_op jit(solution)/shard_map/ppermute | solution.py:368
  28.6 9.5 %collective-permute-start.1 = (bf16[8,3,48,128]{3,2,1,0:T(8,128)(2,1)S(1)}, bf16[8,3,48,128]{3,2,1,0:T(8,128)(2,1)S(1)}, u32[]{:S(2)}, u32[]{:S(2)}) collective-permute-start(bf16[8,3,48,128]{3,2,1,0:T(8,128)(2,1)S(1)} %bitcast.27), channel_id=1, source_target_pairs={{0,32},{8,232},{32,64},{40,8},{64,96},{72,40},{96,128},{104,72},{1... | collective-permute-start | bytes 884744 | tf_op jit(solution)/shard_map/ppermute | solution.py:367
  38.1 2.0 %all_gather.6.own_ref = bf16[2,8,3,24,128]{4,3,2,1,0:T(8,128)(2,1)S(1)} all-gather(bf16[1,8,3,24,128]{4,3,2,1,0:T(8,128)(2,1)S(1)} %bitcast.35), channel_id=1, replica_groups=mesh['cfg'=2,'zh'=8,'zl'=2,'core'=2,'xh'=2,'y'=4] {'core'}, dimensions={0}, use_global_device_ids=true | all-gather | bytes 442368 | tf_op jit(solution)/shard_map/all_gather | solution.py:371
  40.1 4.6 %collective-permute-start = (bf16[2,8,3,24,128]{4,3,2,1,0:T(8,128)(2,1)S(1)}, bf16[2,8,3,24,128]{4,3,2,1,0:T(8,128)(2,1)S(1)}, u32[]{:S(2)}, u32[]{:S(2)}) collective-permute-start(bf16[2,8,3,24,128]{4,3,2,1,0:T(8,128)(2,1)S(1)} %all_gather.6.own_ref), channel_id=1, source_target_pairs={{0,4},{4,0},{1,5},{5,1},{2,6},{6,2},{3,7},{7,3},{8,12},{12,8},{9,1... | collective-permute-start | bytes 884744 | tf_op jit(solution)/shard_map/ppermute | solution.py:372
  44.8 0.2 copy.23
  45.1 3.1 %collective-permute-start.3 = (bf16[8,3,48,128]{3,2,1,0:T(8,128)(2,1)S(1)}, bf16[8,3,48,128]{3,2,1,0:T(8,128)(2,1)S(1)}, u32[]{:S(2)}, u32[]{:S(2)}) collective-permute-start(bf16[8,3,48,128]{3,2,1,0:T(8,128)(2,1)S(1)} %collective-permute-done.2), channel_id=1, source_target_pairs={{0,32},{8,232},{32,64},{40,8},{64,96},{72,40},{96,128},{104,72},{1... | collective-permute-start | bytes 884744 | tf_op jit(solution)/shard_map/ppermute | solution.py:367
  48.2 4.3 %collective-permute-start.4 = (bf16[8,3,48,128]{3,2,1,0:T(8,128)(2,1)S(1)}, bf16[8,3,48,128]{3,2,1,0:T(8,128)(2,1)S(1)}, u32[]{:S(2)}, u32[]{:S(2)}) collective-permute-start(bf16[8,3,48,128]{3,2,1,0:T(8,128)(2,1)S(1)} %collective-permute-done.1.refs_0_.refs_1_), channel_id=1, source_target_pairs={{0,32},{8,232},{32,64},{40,8},{64,96},{72,40},{96,128},{104,72},{1... | collective-permute-start | bytes 884744 | tf_op jit(solution)/shard_map/ppermute | solution.py:367
  52.5 0.8 unpack_queries.1.q_ref
  53.3 5.3 %own_block.1 = (bf16[3,2,768,256]{3,2,1,0:T(8,128)(2,1)S(1)}, f32[3,2,768,128]{3,2,1,0:T(8,128)S(1)}, f32[8,128]{1,0:T(8,128)S(1)}) custom-call(s32[1]{0:T(128)} %bitcast.valid_ref, bf16[3,2,768,256]{3,2,1,0:T(8,128)(2,1)S(1)} %unpack_queries.1.q_ref, bf16[8,3,48,128]{3,2,1,0:T(8,128)(2,1)S(1)} %bitcast.28, ...), custom_call_target="tpu_custom_call" | custom-call | flops 4000000000 | bytes 8000000 | tf_op jit(solution)/shard_map/own_block/pallas_call | solution.py:231
  58.7 0.5 collective-permute-done.3.refs_1_.refs_2_
  59.2 4.6 %collective-permute-start.5 = (bf16[8,3,48,128]{3,2,1,0:T(8,128)(2,1)S(1)}, bf16[8,3,48,128]{3,2,1,0:T(8,128)(2,1)S(1)}, u32[]{:S(2)}, u32[]{:S(2)}) collective-permute-start(bf16[8,3,48,128]{3,2,1,0:T(8,128)(2,1)S(1)} %collective-permute-done.3.refs_1_.refs_2_), channel_id=1, source_target_pairs={{0,32},{8,232},{32,64},{40,8},{64,96},{72,40},{96,128},{104,72},{1... | collective-permute-start | bytes 884744 | tf_op jit(solution)/shard_map/ppermute | solution.py:367
  63.8 4.6 %next_blocks.3 = (f32[3,2,768,128]{3,2,1,0:T(8,128)S(1)}, f32[8,128]{1,0:T(8,128)S(1)}) custom-call(bf16[3,2,768,256]{3,2,1,0:T(8,128)(2,1)S(1)} %get-tuple-element.20.q_ref, f32[3,2,768,128]{3,2,1,0:T(8,128)S(1)} %get-tuple-element.21.state_ref, bf16[8,3,48,128]{3,2,1,0:T(8,128)(2,1)S(1)} %collective-permute-done.1.refs_0_.refs_1_, ...), custom_call_target="tpu_custom_call", output_to_operand_aliasing={{0}: (1, {})} | custom-call | flops 4000000000 | bytes 8000000 | tf_op jit(solution)/shard_map/next_blocks/pallas_call | solution.py:231
  68.4 3.8 %collective-permute-start.6 = (bf16[8,3,48,128]{3,2,1,0:T(8,128)(2,1)S(1)}, bf16[8,3,48,128]{3,2,1,0:T(8,128)(2,1)S(1)}, u32[]{:S(2)}, u32[]{:S(2)}) collective-permute-start(bf16[8,3,48,128]{3,2,1,0:T(8,128)(2,1)S(1)} %collective-permute-done.4.refs_0_.refs_3_), channel_id=1, source_target_pairs={{0,32},{8,232},{32,64},{40,8},{64,96},{72,40},{96,128},{104,72},{1... | collective-permute-start | bytes 884744 | tf_op jit(solution)/shard_map/ppermute | solution.py:367
  72.2 5.0 %collective-permute-start.7 = (bf16[8,3,48,128]{3,2,1,0:T(8,128)(2,1)S(1)}, bf16[8,3,48,128]{3,2,1,0:T(8,128)(2,1)S(1)}, u32[]{:S(2)}, u32[]{:S(2)}) collective-permute-start(bf16[8,3,48,128]{3,2,1,0:T(8,128)(2,1)S(1)} %collective-permute-done.5.refs_1_.refs_4_), channel_id=1, source_target_pairs={{0,32},{8,232},{32,64},{40,8},{64,96},{72,40},{96,128},{104,72},{1... | collective-permute-start | bytes 884744 | tf_op jit(solution)/shard_map/ppermute | solution.py:367
  77.2 4.6 %next_blocks.4 = (f32[3,2,768,128]{3,2,1,0:T(8,128)S(1)}, f32[8,128]{1,0:T(8,128)S(1)}) custom-call(bf16[3,2,768,256]{3,2,1,0:T(8,128)(2,1)S(1)} %get-tuple-element.20.q_ref, f32[3,2,768,128]{3,2,1,0:T(8,128)S(1)} %get-tuple-element.25.state_ref, bf16[8,3,48,128]{3,2,1,0:T(8,128)(2,1)S(1)} %collective-permute-done.4.refs_0_.refs_3_, ...), custom_call_target="tpu_custom_call", output_to_operand_aliasing={{0}: (1, {})} | custom-call | flops 4000000000 | bytes 8000000 | tf_op jit(solution)/shard_map/next_blocks/pallas_call | solution.py:231
  81.8 3.9 %collective-permute-start.8 = (bf16[8,3,48,128]{3,2,1,0:T(8,128)(2,1)S(1)}, bf16[8,3,48,128]{3,2,1,0:T(8,128)(2,1)S(1)}, u32[]{:S(2)}, u32[]{:S(2)}) collective-permute-start(bf16[8,3,48,128]{3,2,1,0:T(8,128)(2,1)S(1)} %collective-permute-done.6.refs_0_.refs_5_), channel_id=1, source_target_pairs={{0,32},{8,232},{32,64},{40,8},{64,96},{72,40},{96,128},{104,72},{1... | collective-permute-start | bytes 884744 | tf_op jit(solution)/shard_map/ppermute | solution.py:367
  85.8 0.9 collective-permute-done.7.refs_1_.refs_6_
  86.7 5.0 %next_blocks.5 = (f32[3,2,768,128]{3,2,1,0:T(8,128)S(1)}, f32[8,128]{1,0:T(8,128)}) custom-call(bf16[3,2,768,256]{3,2,1,0:T(8,128)(2,1)S(1)} %get-tuple-element.20.q_ref, f32[3,2,768,128]{3,2,1,0:T(8,128)S(1)} %get-tuple-element.31.state_ref, bf16[8,3,48,128]{3,2,1,0:T(8,128)(2,1)S(1)} %collective-permute-done.6.refs_0_.refs_5_, ...), custom_call_target="tpu_custom_call", output_to_operand_aliasing={{0}: (1, {})} | custom-call | flops 4000000000 | bytes 8000000 | tf_op jit(solution)/shard_map/next_blocks/pallas_call | solution.py:231
  91.7 2.0 %collective-permute-done.8.block_ref = bf16[8,3,48,128]{3,2,1,0:T(8,128)(2,1)S(1)} collective-permute-done((bf16[8,3,48,128]{3,2,1,0:T(8,128)(2,1)S(1)}, bf16[8,3,48,128]{3,2,1,0:T(8,128)(2,1)S(1)}, u32[]{:S(2)}, u32[]{:S(2)}) %collective-permute-start.8) | collective-permute-done | bytes 294944 | tf_op jit(solution)/shard_map/ppermute | solution.py:367
  93.8 45.9 %last_block.1 = bf16[768,512]{1,0:T(8,128)(2,1)} custom-call(s32[1]{0:T(128)} %bitcast.valid_ref, bf16[3,2,768,256]{3,2,1,0:T(8,128)(2,1)S(1)} %get-tuple-element.20.q_ref, f32[3,2,768,128]{3,2,1,0:T(8,128)S(1)} %get-tuple-element.35.state_ref, bf16[8,3,48,128]{3,2,1,0:T(8,128)(2,1)S(1)} %collective-permute-done.8.block_ref, ...), custom_call_target="tpu_custom_call" | custom-call | flops 4000000000 | bytes 8000000 | tf_op jit(solution)/shard_map/last_block/pallas_call | solution.py:231
  139.7 7.3 %all-to-all-start.1 = ((bf16[32,24,512]{2,1,0:T(8,128)(2,1)}), bf16[32,24,512]{2,1,0:T(8,128)(2,1)S(1)}, u32[]{:S(2)}, u32[]{:S(2)}) async-start(bf16[32,24,512]{2,1,0:T(8,128)(2,1)} %bitcast.9), calls=%async_computation.1 | async-start | bytes 1572864 | tf_op jit(solution)/shard_map/all_to_all | solution.py:401
  147.0 14.5 %all-to-all-done.1.partial_ref = bf16[32,24,512]{2,1,0:T(8,128)(2,1)S(1)} async-done(((bf16[32,24,512]{2,1,0:T(8,128)(2,1)}), bf16[32,24,512]{2,1,0:T(8,128)(2,1)S(1)}, u32[]{:S(2)}, u32[]{:S(2)}) %all-to-all-start.1) | async-done | bytes 786464 | tf_op jit(solution)/shard_map/all_to_all | solution.py:401
  161.5 2.3 %copy-done = bf16[1536,1536]{1,0:T(8,128)(2,1)S(1)} copy-done((bf16[1536,1536]{1,0:T(8,128)(2,1)S(1)}, bf16[1536,1536]{1,0:T(8,128)(2,1)}, u32[]{:S(2)}) %copy-start) | copy-done | bytes 4718616
  163.8 3.3 %project_and_norm.1 = f32[48,64]{1,0:T(8,128)S(1)} custom-call(bf16[32,24,512]{2,1,0:T(8,128)(2,1)S(1)} %all-to-all-done.1.partial_ref, bf16[1536,1536]{1,0:T(8,128)(2,1)S(1)} %copy-done, bf16[48,1536]{1,0:T(8,128)(2,1)S(1)} %bitcast.31, f32[3,1536]{1,0:T(4,128)S(1)} %bitcast.32, f32[1,1536]{1,0:T(1,128)S(1)} %broadcast_in_dim.6.bias_ref, ...), custom_call_target="tpu_custom_call" | custom-call | tf_op jit(solution)/shard_map/project_and_norm/pallas_call | solution.py:329
  167.2 0.1 copy.24
  167.5 0.7 collective-permute-start.10
  168.2 4.7 %collective-permute-start.9 = (f32[1,1536]{1,0:T(1,128)S(1)}, f32[1,1536]{1,0:T(1,128)S(1)}, u32[]{:S(2)}, u32[]{:S(2)}) collective-permute-start(f32[1,1536]{1,0:T(1,128)S(1)} %get-tuple-element.40), channel_id=1, source_target_pairs={{0,1},{1,257},{2,3},{3,259},{256,0},{257,256},{258,2},{259,258},{4... | collective-permute-start | bytes 18440 | tf_op jit(solution)/shard_map/ppermute | solution.py:424
  174.2 0.6 multiply_subtract_fusion
  (36 shorter events, 0.5 us)
Async XLA Ops:
  7.2 37.6 %copy-start.5 = (bf16[1,333,2,192]{1,3,2,0:T(8,128)(2,1)S(1)}, bf16[1,333,2,192]{1,3,2,0:T(8,128)(2,1)}, u32[]{:S(2)}) copy-start(bf16[1,333,2,192]{1,3,2,0:T(8,128)(2,1)} %param.12) | copy-start | bytes 767236
  7.2 132.5 %all-gather.2.cloned.1.call-start = ((), (), s32[]{:S(2)}) async-start(), calls=%async_computation.2 | async-start | bytes 5308416 | tf_op jit(solution)/shard_map/all_gather | solution.py:376
  7.9 1.0 copy-start.1
  22.4 22.7 %collective-permute-start.2 = (bf16[8,3,48,128]{3,2,1,0:T(8,128)(2,1)S(1)}, bf16[8,3,48,128]{3,2,1,0:T(8,128)(2,1)S(1)}, u32[]{:S(2)}, u32[]{:S(2)}) collective-permute-start(bf16[8,3,48,128]{3,2,1,0:T(8,128)(2,1)S(1)} %bitcast.26), channel_id=1, source_target_pairs={{0,8},{8,0},{1,9},{9,1},{2,10},{10,2},{3,11},{11,3},{4,12},{12,4},... | collective-permute-start | bytes 884744 | tf_op jit(solution)/shard_map/ppermute | solution.py:368
  28.6 19.6 %collective-permute-start.1 = (bf16[8,3,48,128]{3,2,1,0:T(8,128)(2,1)S(1)}, bf16[8,3,48,128]{3,2,1,0:T(8,128)(2,1)S(1)}, u32[]{:S(2)}, u32[]{:S(2)}) collective-permute-start(bf16[8,3,48,128]{3,2,1,0:T(8,128)(2,1)S(1)} %bitcast.27), channel_id=1, source_target_pairs={{0,32},{8,232},{32,64},{40,8},{64,96},{72,40},{96,128},{104,72},{1... | collective-permute-start | bytes 884744 | tf_op jit(solution)/shard_map/ppermute | solution.py:367
  40.1 12.4 %collective-permute-start = (bf16[2,8,3,24,128]{4,3,2,1,0:T(8,128)(2,1)S(1)}, bf16[2,8,3,24,128]{4,3,2,1,0:T(8,128)(2,1)S(1)}, u32[]{:S(2)}, u32[]{:S(2)}) collective-permute-start(bf16[2,8,3,24,128]{4,3,2,1,0:T(8,128)(2,1)S(1)} %all_gather.6.own_ref), channel_id=1, source_target_pairs={{0,4},{4,0},{1,5},{5,1},{2,6},{6,2},{3,7},{7,3},{8,12},{12,8},{9,1... | collective-permute-start | bytes 884744 | tf_op jit(solution)/shard_map/ppermute | solution.py:372
  45.1 14.1 %collective-permute-start.3 = (bf16[8,3,48,128]{3,2,1,0:T(8,128)(2,1)S(1)}, bf16[8,3,48,128]{3,2,1,0:T(8,128)(2,1)S(1)}, u32[]{:S(2)}, u32[]{:S(2)}) collective-permute-start(bf16[8,3,48,128]{3,2,1,0:T(8,128)(2,1)S(1)} %collective-permute-done.2), channel_id=1, source_target_pairs={{0,32},{8,232},{32,64},{40,8},{64,96},{72,40},{96,128},{104,72},{1... | collective-permute-start | bytes 884744 | tf_op jit(solution)/shard_map/ppermute | solution.py:367
  48.2 20.2 %collective-permute-start.4 = (bf16[8,3,48,128]{3,2,1,0:T(8,128)(2,1)S(1)}, bf16[8,3,48,128]{3,2,1,0:T(8,128)(2,1)S(1)}, u32[]{:S(2)}, u32[]{:S(2)}) collective-permute-start(bf16[8,3,48,128]{3,2,1,0:T(8,128)(2,1)S(1)} %collective-permute-done.1.refs_0_.refs_1_), channel_id=1, source_target_pairs={{0,32},{8,232},{32,64},{40,8},{64,96},{72,40},{96,128},{104,72},{1... | collective-permute-start | bytes 884744 | tf_op jit(solution)/shard_map/ppermute | solution.py:367
  59.2 13.0 %collective-permute-start.5 = (bf16[8,3,48,128]{3,2,1,0:T(8,128)(2,1)S(1)}, bf16[8,3,48,128]{3,2,1,0:T(8,128)(2,1)S(1)}, u32[]{:S(2)}, u32[]{:S(2)}) collective-permute-start(bf16[8,3,48,128]{3,2,1,0:T(8,128)(2,1)S(1)} %collective-permute-done.3.refs_1_.refs_2_), channel_id=1, source_target_pairs={{0,32},{8,232},{32,64},{40,8},{64,96},{72,40},{96,128},{104,72},{1... | collective-permute-start | bytes 884744 | tf_op jit(solution)/shard_map/ppermute | solution.py:367
  68.4 13.4 %collective-permute-start.6 = (bf16[8,3,48,128]{3,2,1,0:T(8,128)(2,1)S(1)}, bf16[8,3,48,128]{3,2,1,0:T(8,128)(2,1)S(1)}, u32[]{:S(2)}, u32[]{:S(2)}) collective-permute-start(bf16[8,3,48,128]{3,2,1,0:T(8,128)(2,1)S(1)} %collective-permute-done.4.refs_0_.refs_3_), channel_id=1, source_target_pairs={{0,32},{8,232},{32,64},{40,8},{64,96},{72,40},{96,128},{104,72},{1... | collective-permute-start | bytes 884744 | tf_op jit(solution)/shard_map/ppermute | solution.py:367
  72.2 14.5 %collective-permute-start.7 = (bf16[8,3,48,128]{3,2,1,0:T(8,128)(2,1)S(1)}, bf16[8,3,48,128]{3,2,1,0:T(8,128)(2,1)S(1)}, u32[]{:S(2)}, u32[]{:S(2)}) collective-permute-start(bf16[8,3,48,128]{3,2,1,0:T(8,128)(2,1)S(1)} %collective-permute-done.5.refs_1_.refs_4_), channel_id=1, source_target_pairs={{0,32},{8,232},{32,64},{40,8},{64,96},{72,40},{96,128},{104,72},{1... | collective-permute-start | bytes 884744 | tf_op jit(solution)/shard_map/ppermute | solution.py:367
  81.8 11.9 %collective-permute-start.8 = (bf16[8,3,48,128]{3,2,1,0:T(8,128)(2,1)S(1)}, bf16[8,3,48,128]{3,2,1,0:T(8,128)(2,1)S(1)}, u32[]{:S(2)}, u32[]{:S(2)}) collective-permute-start(bf16[8,3,48,128]{3,2,1,0:T(8,128)(2,1)S(1)} %collective-permute-done.6.refs_0_.refs_5_), channel_id=1, source_target_pairs={{0,32},{8,232},{32,64},{40,8},{64,96},{72,40},{96,128},{104,72},{1... | collective-permute-start | bytes 884744 | tf_op jit(solution)/shard_map/ppermute | solution.py:367
  93.7 53.2 %copy-start.6 = (f32[1,3,1536]{2,0,1:T(1,128)S(1)}, f32[1,3,1536]{2,0,1:T(1,128)}, u32[]{:S(2)}) copy-start(f32[1,3,1536]{2,0,1:T(1,128)} %param.14) | copy-start | bytes 55300
  93.7 53.2 %copy-start.7 = (f32[1536]{0:T(1024)S(1)}, f32[1536]{0:T(1024)}, u32[]{:S(2)}) copy-start(f32[1536]{0:T(1024)} %param.16) | copy-start | bytes 18436
  93.7 67.8 %copy-start.2 = (bf16[1536,64]{0,1:T(8,128)(2,1)S(1)}, bf16[1536,64]{0,1:T(8,128)(2,1)}, u32[]{:S(2)}) copy-start(bf16[1536,64]{0,1:T(8,128)(2,1)} %param.17) | copy-start | bytes 589828
  93.7 67.8 %copy-start.3 = (bf16[1,48,1536]{2,1,0:T(8,128)(2,1)S(1)}, bf16[1,48,1536]{2,1,0:T(8,128)(2,1)}, u32[]{:S(2)}) copy-start(bf16[1,48,1536]{2,1,0:T(8,128)(2,1)} %param.13) | copy-start | bytes 442372
  93.7 67.8 %copy-start.4 = (f32[64]{0:T(128)S(1)}, f32[64]{0:T(128)}, u32[]{:S(2)}) copy-start(f32[64]{0:T(128)} %param.18) | copy-start | bytes 772
  139.7 21.8 %all-to-all-start.1 = ((bf16[32,24,512]{2,1,0:T(8,128)(2,1)}), bf16[32,24,512]{2,1,0:T(8,128)(2,1)S(1)}, u32[]{:S(2)}, u32[]{:S(2)}) async-start(bf16[32,24,512]{2,1,0:T(8,128)(2,1)} %bitcast.9), calls=%async_computation.1 | async-start | bytes 1572864 | tf_op jit(solution)/shard_map/all_to_all | solution.py:401
  161.5 2.3 %copy-start = (bf16[1536,1536]{1,0:T(8,128)(2,1)S(1)}, bf16[1536,1536]{1,0:T(8,128)(2,1)}, u32[]{:S(2)}) copy-start(bf16[1536,1536]{1,0:T(8,128)(2,1)} %all-gather.2.cloned.1.call-done.weight_ref) | copy-start | bytes 14155780
  163.8 10.4 %copy-start.8 = (f32[1,1536]{1,0:T(1,128)S(1)}, f32[1,1536]{1,0:T(1,128)}, u32[]{:S(2)}) copy-start(f32[1,1536]{1,0:T(1,128)} %param.21) | copy-start | bytes 18436
  167.5 6.7 %collective-permute-start.10 = (f32[1,1536]{1,0:T(1,128)S(1)}, f32[1,1536]{1,0:T(1,128)S(1)}, u32[]{:S(2)}, u32[]{:S(2)}) collective-permute-start(f32[1,1536]{1,0:T(1,128)S(1)} %get-tuple-element.41), channel_id=1, source_target_pairs={{0,0},{1,256},{2,2},{3,258},{256,1},{257,257},{258,3},{259,259},{4... | collective-permute-start | bytes 18440 | tf_op jit(solution)/shard_map/ppermute | solution.py:423
  168.2 6.0 %collective-permute-start.9 = (f32[1,1536]{1,0:T(1,128)S(1)}, f32[1,1536]{1,0:T(1,128)S(1)}, u32[]{:S(2)}, u32[]{:S(2)}) collective-permute-start(f32[1,1536]{1,0:T(1,128)S(1)} %get-tuple-element.40), channel_id=1, source_target_pairs={{0,1},{1,257},{2,3},{3,259},{256,0},{257,256},{258,2},{259,258},{4... | collective-permute-start | bytes 18440 | tf_op jit(solution)/shard_map/ppermute | solution.py:424
Sparse Core Ops, SparseCore 0:
  11.2 101.5 all-gather.1
